TPU v7x, 32 devices: a whole 2x2x4 slice. The times are simulated.
32 devices in a mesh: fsdp: 8 (over z, y), tp: 4 (over x, core).
Axes of the slice: x: 2, y: 2, z: 4, core: 2. Of those that a mesh axis runs over, the one named last changes fastest.
Arguments:
- tokens: bfloat16 [2, 3072, 1600], P(None, ('fsdp', 'tp')), may hold values from -6 to 6
- qkv_weight: bfloat16 [2, 1600, 4800], P(None, 'fsdp'), may hold values from -0.15625 to 0.15625
- query_bias: bfloat16 [2, 1600], P(None, 'fsdp'), may hold values from -3 to 3
- value_bias: bfloat16 [2, 1600], P(None, 'fsdp'), may hold values from -3 to 3
- out_weight: bfloat16 [2, 1600, 1600], P(None, 'fsdp'), may hold values from -0.625 to 0.625
- out_bias: bfloat16 [2, 1600], P(None, 'fsdp'), may hold values from -3 to 3
- fc_weight: bfloat16 [2, 1600, 6400], P(None, 'fsdp', 'tp'), may hold values from -0.15625 to 0.15625
- fc_bias: bfloat16 [2, 4, 1600], P(None, 'tp', 'fsdp'), may hold values from -3 to 3
- proj_weight: bfloat16 [2, 6400, 1600], P(None, 'tp', 'fsdp'), may hold values from -0.109375 to 0.109375
- proj_bias: bfloat16 [2, 1600], P(None, 'fsdp'), may hold values from -3 to 3
- first_gain: bfloat16 [2, 1600], P(None, 'fsdp'), may hold values from 0.5 to 1.5
- first_bias: bfloat16 [2, 1600], P(None, 'fsdp'), may hold values from -3 to 3
- second_gain: bfloat16 [2, 1600], P(None, 'fsdp'), may hold values from 0.5 to 1.5
- second_bias: bfloat16 [2, 1600], P(None, 'fsdp'), may hold values from -3 to 3
- out_grad: bfloat16 [2, 3072, 1600], P(None, ('fsdp', 'tp')), may hold values from -6 to 6
Outputs:
- out_tokens: bfloat16 [2, 3072, 1600], P(None, ('fsdp', 'tp'))
- tokens_grad: float32 [2, 3072, 1600], P(None, ('fsdp', 'tp'))
- qkv_weight_grad: float32 [2, 1600, 4800], P(None, 'fsdp')
- query_bias_grad: float32 [2, 1600], P(None, 'fsdp')
- value_bias_grad: float32 [2, 1600], P(None, 'fsdp')
- out_weight_grad: float32 [2, 1600, 1600], P(None, 'fsdp')
- out_bias_grad: float32 [2, 1600], P(None, 'fsdp')
- fc_weight_grad: float32 [2, 1600, 6400], P(None, 'fsdp', 'tp')
- fc_bias_grad: float32 [2, 4, 1600], P(None, 'tp', 'fsdp')
- proj_weight_grad: float32 [2, 6400, 1600], P(None, 'tp', 'fsdp')
- proj_bias_grad: float32 [2, 1600], P(None, 'fsdp')
- first_gain_grad: float32 [2, 1600], P(None, 'fsdp')
- first_bias_grad: float32 [2, 1600], P(None, 'fsdp')
- second_gain_grad: float32 [2, 1600], P(None, 'fsdp')
- second_bias_grad: float32 [2, 1600], P(None, 'fsdp')
All inputs are finite; a program needn't handle non-finite values.
Results may differ from a plain program's by a relative error of at most 0.018.
Values may be sent and summed in bfloat16 or wider, within the bound.
A program may use at most 384 MiB of HBM per device.

v0:
```python
import jax
import jax.numpy as jnp
from jax import lax
from jax.sharding import PartitionSpec as P

D = 1600
HEADS = 25
HEAD = 64
GROUP = 8
PROMPT_DEV = 128
CONT_LEN = 256
MICRO = 2
LAYERS = 2
PROMPT = 1024


norm_eps = 1e-05


def swapped(value, axis, bit):
    mask = 2**bit
    pairs = [(source, source ^ mask) for source in range(lax.axis_size(axis))]
    return lax.ppermute(value, axis, pairs)


def layer_norm(x, gain, bias):
    centred = x - jnp.mean(x, -1, keepdims=True)
    spread = jnp.mean(centred * centred, -1, keepdims=True)
    return centred * lax.rsqrt(spread + norm_eps) * gain + bias


def gelu_tanh(value):
    return jax.nn.gelu(value, approximate=True)


def key_mask(rows, member):
    query_at = rows[:, None]
    key_at = lax.broadcasted_iota(jnp.int32, (1, PROMPT + CONT_LEN), 1)
    in_prompt = query_at < PROMPT_DEV
    prompt_pos = member * PROMPT_DEV + query_at
    cont_pos = query_at - PROMPT_DEV
    prompt_ok = in_prompt & (key_at <= prompt_pos)
    cont_ok = jnp.logical_not(in_prompt) & ((key_at < PROMPT) | (key_at - PROMPT <= cont_pos))
    return prompt_ok | cont_ok


def mat_t(left, right):
    return lax.dot_general(
        left, right, (((0,), (0,)), ((), ())), preferred_element_type=jnp.float32
    )


def mat_rt(left, right):
    return lax.dot_general(
        left, right, (((1,), (1,)), ((), ())), preferred_element_type=jnp.float32
    )


def head_scores(query, keys, rows, member):
    heads_q = query.reshape(query.shape[0], HEADS, HEAD)
    heads_k = keys.reshape(keys.shape[0], HEADS, HEAD)
    scores = jnp.einsum(
        "rhd,khd->hrk", heads_q, heads_k, preferred_element_type=jnp.float32
    ) * HEAD ** (-0.5)
    return jnp.where(key_mask(rows, member)[None], scores, -1e30)


def share_prompt(stacked, member):
    current = stacked
    for level in range(GROUP.bit_length() - 1):
        partner = swapped(current, "fsdp", level)
        upper_side = member >> level & 1 == 1
        current = jnp.where(
            upper_side,
            jnp.concatenate([partner, current], axis=1),
            jnp.concatenate([current, partner], axis=1),
        )
    return current


def sum_prompt(stacked, member):
    current = stacked
    for level in reversed(range(GROUP.bit_length() - 1)):
        half_rows = current.shape[1] // 2
        lower_half = current[:, :half_rows]
        upper_half = current[:, half_rows:]
        upper_side = member >> level & 1 == 1
        staying = jnp.where(upper_side, upper_half, lower_half)
        leaving = jnp.where(upper_side, lower_half, upper_half)
        current = staying + swapped(leaving.astype(jnp.bfloat16), "fsdp", level).astype(
            leaving.dtype
        )
    return current


def forward_layer(x, full, member, rows):
    w_qkv, w_out, w_fc, w_proj, b_fc, vectors = full
    vecs = vectors.astype(jnp.float32)
    row_count = x.shape[0]
    normed = layer_norm(x, vecs[0], vecs[1]).astype(jnp.bfloat16)
    projected = jnp.dot(normed, w_qkv, preferred_element_type=jnp.float32)
    query = (projected[:, :D] + vecs[2]).astype(jnp.bfloat16)
    key = projected[:, D : 2 * D].astype(jnp.bfloat16)
    value = (projected[:, 2 * D :] + vecs[3]).astype(jnp.bfloat16)
    block_keys, block_values, normed_all = (
        lax.all_gather(key, "tp", axis=0, tiled=True),
        lax.all_gather(value, "tp", axis=0, tiled=True),
        lax.all_gather(normed, "tp", axis=0, tiled=True),
    )
    prompt_all = share_prompt(
        jnp.stack([block_keys[:PROMPT_DEV], block_values[:PROMPT_DEV]]), member
    )
    keys = jnp.concatenate([prompt_all[0], block_keys[PROMPT_DEV:]], axis=0)
    values = jnp.concatenate([prompt_all[1], block_values[PROMPT_DEV:]], axis=0)
    masked = head_scores(query, keys, rows, member)
    top = jnp.max(masked, -1, keepdims=True)
    expo = jnp.exp(masked - top)
    total = jnp.sum(expo, -1, keepdims=True)
    probs = (expo / total).astype(jnp.bfloat16)
    logsum = top + jnp.log(total)
    heads_v = values.reshape(values.shape[0], HEADS, HEAD)
    mixed = jnp.einsum("hrk,khd->rhd", probs, heads_v, preferred_element_type=jnp.float32)
    mixed = mixed.reshape(row_count, D).astype(jnp.bfloat16)
    x_mid = x + (jnp.dot(mixed, w_out, preferred_element_type=jnp.float32) + vecs[4])
    second = layer_norm(x_mid, vecs[5], vecs[6]).astype(jnp.bfloat16)
    second_all, mixed_all = (
        lax.all_gather(second, "tp", axis=0, tiled=True),
        lax.all_gather(mixed, "tp", axis=0, tiled=True),
    )
    hidden_pre = jnp.dot(second_all, w_fc, preferred_element_type=jnp.float32) + b_fc[0].astype(
        jnp.float32
    )
    hidden = gelu_tanh(hidden_pre).astype(jnp.bfloat16)
    partial_out = jnp.dot(hidden, w_proj, preferred_element_type=jnp.float32)
    summed = lax.psum_scatter(
        partial_out.astype(jnp.bfloat16), "tp", scatter_dimension=0, tiled=True
    ).astype(jnp.float32)
    x_next = x_mid + summed + vecs[7]
    saved = (
        x,
        normed_all,
        query,
        keys,
        values,
        logsum,
        mixed_all,
        x_mid,
        second_all,
        hidden_pre,
        hidden,
    )
    return (x_next, saved)


def backward_layer(grad_x, full, saved, member, rows):
    w_qkv, w_out, w_fc, w_proj, b_fc, vectors = full
    vecs = vectors.astype(jnp.float32)
    x, normed_all, query, keys, values, logsum, mixed_all, x_mid, second_all, hidden_pre, hidden = (
        saved
    )
    row_count = x.shape[0]
    grad_branch = grad_x.astype(jnp.bfloat16)
    grad_proj_bias = jnp.sum(grad_branch.astype(jnp.float32), 0)
    branch_all = lax.all_gather(grad_branch, "tp", axis=0, tiled=True)
    grad_proj = mat_t(hidden, branch_all)
    grad_hidden = mat_rt(branch_all, w_proj)
    gelu_out, gelu_back = jax.vjp(gelu_tanh, hidden_pre)
    grad_pre = gelu_back(grad_hidden)[0].astype(jnp.bfloat16)
    grad_fc = mat_t(second_all, grad_pre)
    grad_fc_bias = jnp.sum(grad_pre.astype(jnp.float32), 0)[None]
    second_part = mat_rt(grad_pre, w_fc)
    grad_second = lax.psum_scatter(
        second_part.astype(jnp.bfloat16), "tp", scatter_dimension=0, tiled=True
    ).astype(jnp.float32)
    norm_out, norm_back = jax.vjp(layer_norm, x_mid, vecs[5], vecs[6])
    grad_from_norm, grad_gain_two, grad_bias_two = norm_back(grad_second)
    grad_mid = grad_x + grad_from_norm
    grad_attn = grad_mid.astype(jnp.bfloat16)
    grad_out_bias = jnp.sum(grad_attn.astype(jnp.float32), 0)
    grad_mixed = mat_rt(grad_attn, w_out).astype(jnp.bfloat16)
    masked = head_scores(query, keys, rows, member)
    probs = jnp.exp(masked - logsum)
    heads_q = query.reshape(row_count, HEADS, HEAD)
    heads_k = keys.reshape(keys.shape[0], HEADS, HEAD)
    heads_v = values.reshape(values.shape[0], HEADS, HEAD)
    grad_heads = grad_mixed.reshape(row_count, HEADS, HEAD)
    grad_values = jnp.einsum(
        "hrk,rhd->khd", probs.astype(jnp.bfloat16), grad_heads, preferred_element_type=jnp.float32
    )
    grad_probs = jnp.einsum("rhd,khd->hrk", grad_heads, heads_v, preferred_element_type=jnp.float32)
    inner = jnp.sum(probs * grad_probs, -1, keepdims=True)
    grad_scores = (probs * (grad_probs - inner)).astype(jnp.bfloat16)
    grad_query = jnp.einsum(
        "hrk,khd->rhd", grad_scores, heads_k, preferred_element_type=jnp.float32
    ) * HEAD ** (-0.5)
    grad_keys = jnp.einsum(
        "hrk,rhd->khd", grad_scores, heads_q, preferred_element_type=jnp.float32
    ) * HEAD ** (-0.5)
    grad_keys = grad_keys.reshape(keys.shape[0], D)
    grad_values = grad_values.reshape(values.shape[0], D)
    own_prompt = sum_prompt(jnp.stack([grad_keys[:PROMPT], grad_values[:PROMPT]]), member)
    local_keys = jnp.concatenate([own_prompt[0], grad_keys[PROMPT:]], axis=0)
    local_values = jnp.concatenate([own_prompt[1], grad_values[PROMPT:]], axis=0)
    own_keys, own_values = (
        lax.psum_scatter(
            local_keys.astype(jnp.bfloat16), "tp", scatter_dimension=0, tiled=True
        ).astype(jnp.float32),
        lax.psum_scatter(
            local_values.astype(jnp.bfloat16), "tp", scatter_dimension=0, tiled=True
        ).astype(jnp.float32),
    )
    grad_qkv = jnp.concatenate(
        [grad_query.reshape(row_count, D), own_keys, own_values], axis=1
    ).astype(jnp.bfloat16)
    qkv_cols, attn_cols = (
        lax.all_to_all(grad_qkv, "tp", split_axis=1, concat_axis=0, tiled=True),
        lax.all_to_all(grad_attn, "tp", split_axis=1, concat_axis=0, tiled=True),
    )
    grad_qkv_weight = mat_t(normed_all, qkv_cols)
    grad_out = mat_t(mixed_all, attn_cols)
    column_sums = jnp.sum(grad_qkv.astype(jnp.float32), 0)
    grad_normed = mat_rt(grad_qkv, w_qkv)
    first_out, first_back = jax.vjp(layer_norm, x, vecs[0], vecs[1])
    grad_from_first, grad_gain_one, grad_bias_one = first_back(grad_normed)
    grad_in = grad_mid + grad_from_first
    vector_grads = jnp.stack(
        [
            grad_gain_one,
            grad_bias_one,
            column_sums[:D],
            column_sums[2 * D :],
            grad_out_bias,
            grad_gain_two,
            grad_bias_two,
            grad_proj_bias,
        ]
    )
    return (grad_in, (grad_qkv_weight, grad_out, grad_fc, grad_proj, grad_fc_bias, vector_grads))


def local(
    tokens,
    qkv_weight,
    query_bias,
    value_bias,
    out_weight,
    out_bias,
    fc_weight,
    fc_bias,
    proj_weight,
    proj_bias,
    first_gain,
    first_bias,
    second_gain,
    second_bias,
    out_grad,
):
    row_count = tokens.shape[1]
    rows = lax.axis_index("tp") * row_count + lax.iota(jnp.int32, row_count)
    member = lax.axis_index("fsdp") % GROUP

    def layer_vectors(layer):
        return jnp.stack(
            [
                first_gain[layer],
                first_bias[layer],
                query_bias[layer],
                value_bias[layer],
                out_bias[layer],
                second_gain[layer],
                second_bias[layer],
                proj_bias[layer],
            ]
        )

    totals = [None] * LAYERS
    outputs = []
    input_grads = []
    for micro in range(MICRO):
        state = tokens[micro].astype(jnp.float32)
        saves = []
        for layer in range(LAYERS):
            full = (
                lax.all_gather(qkv_weight[layer], "fsdp", axis=0, tiled=True),
                lax.all_gather(out_weight[layer], "fsdp", axis=0, tiled=True),
                lax.all_gather(fc_weight[layer], "fsdp", axis=0, tiled=True),
                lax.all_gather(proj_weight[layer], "fsdp", axis=1, tiled=True),
                lax.all_gather(fc_bias[layer], "fsdp", axis=1, tiled=True),
                lax.all_gather(layer_vectors(layer), "fsdp", axis=1, tiled=True),
            )
            state, saved = forward_layer(state, full, member, rows)
            saves.append(saved)
        outputs.append(state.astype(jnp.bfloat16))
        grad_state = out_grad[micro].astype(jnp.float32)
        for layer in reversed(range(LAYERS)):
            full = (
                lax.all_gather(qkv_weight[layer], "fsdp", axis=0, tiled=True),
                lax.all_gather(out_weight[layer], "fsdp", axis=0, tiled=True),
                lax.all_gather(fc_weight[layer], "fsdp", axis=0, tiled=True),
                lax.all_gather(proj_weight[layer], "fsdp", axis=1, tiled=True),
                lax.all_gather(fc_bias[layer], "fsdp", axis=1, tiled=True),
                lax.all_gather(layer_vectors(layer), "fsdp", axis=1, tiled=True),
            )
            grad_state, layer_grads = backward_layer(grad_state, full, saves[layer], member, rows)
            if totals[layer] is None:
                totals[layer] = layer_grads
            else:
                totals[layer] = tuple((a + b for a, b in zip(totals[layer], layer_grads)))
        input_grads.append(grad_state)
    stacked = [jnp.stack([totals[layer][index] for layer in range(LAYERS)]) for index in range(6)]
    qkv_part, out_part, fc_part, proj_part, fc_bias_part, vector_part = (
        lax.psum_scatter(
            stacked[0].astype(jnp.bfloat16), "fsdp", scatter_dimension=1, tiled=True
        ).astype(jnp.float32),
        lax.psum_scatter(
            stacked[1].astype(jnp.bfloat16), "fsdp", scatter_dimension=1, tiled=True
        ).astype(jnp.float32),
        lax.psum_scatter(
            stacked[2].astype(jnp.bfloat16), "fsdp", scatter_dimension=1, tiled=True
        ).astype(jnp.float32),
        lax.psum_scatter(
            stacked[3].astype(jnp.bfloat16), "fsdp", scatter_dimension=2, tiled=True
        ).astype(jnp.float32),
        lax.psum_scatter(
            stacked[4].astype(jnp.bfloat16), "fsdp", scatter_dimension=2, tiled=True
        ).astype(jnp.float32),
        lax.psum_scatter(
            stacked[5].astype(jnp.bfloat16), "fsdp", scatter_dimension=2, tiled=True
        ).astype(jnp.float32),
    )
    qkv_sum, out_sum = (
        lax.all_gather(qkv_part.astype(jnp.bfloat16), "tp", axis=2, tiled=True).astype(
            qkv_part.dtype
        ),
        lax.all_gather(out_part.astype(jnp.bfloat16), "tp", axis=2, tiled=True).astype(
            out_part.dtype
        ),
    )
    vector_sum = lax.psum(vector_part, "tp")
    return (
        jnp.stack(outputs),
        jnp.stack(input_grads),
        qkv_sum,
        vector_sum[:, 2],
        vector_sum[:, 3],
        out_sum,
        vector_sum[:, 4],
        fc_part,
        fc_bias_part,
        proj_part,
        vector_sum[:, 7],
        vector_sum[:, 0],
        vector_sum[:, 1],
        vector_sum[:, 5],
        vector_sum[:, 6],
    )


def solution(mesh):
    in_specs = (
        P(None, ("fsdp", "tp"), None),
        P(None, "fsdp", None),
        P(None, "fsdp"),
        P(None, "fsdp"),
        P(None, "fsdp", None),
        P(None, "fsdp"),
        P(None, "fsdp", "tp"),
        P(None, "tp", "fsdp"),
        P(None, "tp", "fsdp"),
        P(None, "fsdp"),
        P(None, "fsdp"),
        P(None, "fsdp"),
        P(None, "fsdp"),
        P(None, "fsdp"),
        P(None, ("fsdp", "tp"), None),
    )
    out_specs = (
        P(None, ("fsdp", "tp"), None),
        P(None, ("fsdp", "tp"), None),
        P(None, "fsdp", None),
        P(None, "fsdp"),
        P(None, "fsdp"),
        P(None, "fsdp", None),
        P(None, "fsdp"),
        P(None, "fsdp", "tp"),
        P(None, "tp", "fsdp"),
        P(None, "tp", "fsdp"),
        P(None, "fsdp"),
        P(None, "fsdp"),
        P(None, "fsdp"),
        P(None, "fsdp"),
        P(None, "fsdp"),
    )
    return jax.shard_map(local, mesh=mesh, in_specs=in_specs, out_specs=out_specs, check_vma=False)
```

profile of v0, /device:TPU:9, one launch (start us, length us, event | category | flops | bytes accessed | tf_op | source)
XLA Modules:
  0.0 4573.6 jit_solution(690851291029238529)
XLA Ops:
  14.1 22.2 all-gather.12
  38.7 185.1 %all-gather.97.cloned.1.call-done = bf16[1,1600,4800]{2,1,0:T(8,128)(2,1)} async-done(((bf16[1,200,4800]{2,1,0:T(8,128)(2,1)}), bf16[1,1600,4800]{2,1,0:T(8,128)(2,1)}) %all-gather.97.cloned.1.call-update) | async-done | bytes 15360016 | tf_op jit(solution)/shard_map/all_gather | solution.py:284
  247.6 13.8 all-gather.51.cloned.1.call-done
  262.5 19.1 all-gather.49.cloned.1.call-done
  284.6 17.0 all-gather.63.cloned.1.call-done
  327.0 25.8 collective-permute-done.6
  379.6 85.7 %collective-permute-done.7 = bf16[2,256,1600]{1,2,0:T(8,128)(2,1)} collective-permute-done((bf16[2,256,1600]{1,2,0:T(8,128)(2,1)}, bf16[2,256,1600]{1,2,0:T(8,128)(2,1)}, u32[]{:S(2)}, u32[]{:S(2)}) %collective-permute-start.7) | collective-permute-done | bytes 1638432 | tf_op jit(solution)/shard_map/ppermute | solution.py:23
  508.8 143.0 %collective-permute-done.2 = bf16[2,512,1600]{1,2,0:T(8,128)(2,1)} collective-permute-done((bf16[2,512,1600]{1,2,0:T(8,128)(2,1)}, bf16[2,512,1600]{1,2,0:T(8,128)(2,1)}, u32[]{:S(2)}, u32[]{:S(2)}) %collective-permute-start.2) | collective-permute-done | bytes 3276832 | tf_op jit(solution)/shard_map/ppermute | solution.py:23
  666.5 55.5 %collective-permute-done.8 = bf16[2,512,1600]{1,2,0:T(8,128)(2,1)} collective-permute-done((bf16[2,512,1600]{1,2,0:T(8,128)(2,1)}, bf16[2,512,1600]{1,2,0:T(8,128)(2,1)}, u32[]{:S(2)}, u32[]{:S(2)}) %collective-permute-start.8) | collective-permute-done | bytes 3276832 | tf_op jit(solution)/shard_map/ppermute | solution.py:23
  802.2 17.6 all-reduce.9
  827.2 79.1 %all-gather.103.cloned.1.call-done = bf16[1,1600,1600]{1,2,0:T(8,128)(2,1)} async-done(((bf16[1,1600,200]{1,2,0:T(8,128)(2,1)}), bf16[1,1600,1600]{1,2,0:T(8,128)(2,1)}) %all-gather.103.cloned.1.call-update) | async-done | bytes 5120016 | tf_op jit(solution)/shard_map/all_gather | solution.py:287
  913.9 13.1 all-gather.65.cloned.1.call-done
  942.6 21.7 all-gather.13
  965.0 20.8 reduce-scatter.25.cloned.1.call-done
  988.5 210.5 %all-gather.105.cloned.1.call-done = bf16[1,1600,4800]{2,1,0:T(8,128)(2,1)} async-done(((bf16[1,200,4800]{2,1,0:T(8,128)(2,1)}), bf16[1,1600,4800]{2,1,0:T(8,128)(2,1)}) %all-gather.105.cloned.1.call-update) | async-done | bytes 15360016 | tf_op jit(solution)/shard_map/all_gather | solution.py:284
  1222.4 14.3 all-gather.57.cloned.1.call-done
  1237.8 19.0 all-gather.55.cloned.1.call-done
  1259.8 17.0 all-gather.69.cloned.1.call-done
  1299.8 25.8 collective-permute-done.9
  1354.8 85.2 %collective-permute-done.10 = bf16[2,256,1600]{1,2,0:T(8,128)(2,1)} collective-permute-done((bf16[2,256,1600]{1,2,0:T(8,128)(2,1)}, bf16[2,256,1600]{1,2,0:T(8,128)(2,1)}, u32[]{:S(2)}, u32[]{:S(2)}) %collective-permute-start.10) | collective-permute-done | bytes 1638432 | tf_op jit(solution)/shard_map/ppermute | solution.py:23
  1475.3 153.4 %collective-permute-done.5 = bf16[2,512,1600]{1,2,0:T(8,128)(2,1)} collective-permute-done((bf16[2,512,1600]{1,2,0:T(8,128)(2,1)}, bf16[2,512,1600]{1,2,0:T(8,128)(2,1)}, u32[]{:S(2)}, u32[]{:S(2)}) %collective-permute-start.5) | collective-permute-done | bytes 3276832 | tf_op jit(solution)/shard_map/ppermute | solution.py:23
  1643.5 55.5 %collective-permute-done.11 = bf16[2,512,1600]{1,2,0:T(8,128)(2,1)} collective-permute-done((bf16[2,512,1600]{1,2,0:T(8,128)(2,1)}, bf16[2,512,1600]{1,2,0:T(8,128)(2,1)}, u32[]{:S(2)}, u32[]{:S(2)}) %collective-permute-start.11) | collective-permute-done | bytes 3276832 | tf_op jit(solution)/shard_map/ppermute | solution.py:23
  1779.2 17.9 all-gather.71.cloned.1.call-done
  1816.7 87.0 %all-gather.111.cloned.1.call-done = bf16[1,1600,1600]{1,2,0:T(8,128)(2,1)} async-done(((bf16[1,1600,200]{1,2,0:T(8,128)(2,1)}), bf16[1,1600,1600]{1,2,0:T(8,128)(2,1)}) %all-gather.111.cloned.1.call-update) | async-done | bytes 5120016 | tf_op jit(solution)/shard_map/all_gather | solution.py:287
  1976.0 26.2 reduce-scatter.29.cloned.1.call-done
  2004.4 26.6 reduce-scatter.23.cloned.1.call-done
  2031.0 29.1 reduce-scatter.27.cloned.1.call-done
  2108.6 140.8 %collective-permute-done.18 = bf16[2,512,1600]{1,2,0:T(8,128)(2,1)} collective-permute-done((bf16[2,512,1600]{1,2,0:T(8,128)(2,1)S(1)}, bf16[2,512,1600]{1,2,0:T(8,128)(2,1)}, u32[]{:S(2)}, u32[]{:S(2)}) %collective-permute-start.18) | collective-permute-done | bytes 3276832 | tf_op jit(solution)/shard_map/ppermute | solution.py:23
  2253.7 36.5 collective-permute-done.19
  2295.8 15.0 collective-permute-done.20
  2328.9 16.6 reduce-scatter.43.cloned.1.call-done
  2345.5 29.0 reduce-scatter.45.cloned.1.call-done
  2435.5 140.8 %collective-permute-done.12 = bf16[2,512,1600]{1,2,0:T(8,128)(2,1)} collective-permute-done((bf16[2,512,1600]{1,2,0:T(8,128)(2,1)S(1)}, bf16[2,512,1600]{1,2,0:T(8,128)(2,1)}, u32[]{:S(2)}, u32[]{:S(2)}) %collective-permute-start.12) | collective-permute-done | bytes 3276832 | tf_op jit(solution)/shard_map/ppermute | solution.py:23
  2580.6 36.5 collective-permute-done.13
  2620.1 16.3 collective-permute-done.14
  2650.2 18.9 reduce-scatter.31.cloned.1.call-done
  2669.1 29.1 reduce-scatter.33.cloned.1.call-done
  2767.5 29.6 reduce-scatter.35.cloned.1.call-done
  2881.7 112.8 %collective-permute-done.15 = bf16[2,512,1600]{1,2,0:T(8,128)(2,1)} collective-permute-done((bf16[2,512,1600]{1,2,0:T(8,128)(2,1)}, bf16[2,512,1600]{1,2,0:T(8,128)(2,1)}, u32[]{:S(2)}, u32[]{:S(2)}) %collective-permute-start.15) | collective-permute-done | bytes 3276832 | tf_op jit(solution)/shard_map/ppermute | solution.py:23
  3006.7 29.9 collective-permute-done.16
  3068.6 131.0 %collective-permute-done.21 = bf16[2,512,1600]{1,2,0:T(8,128)(2,1)} collective-permute-done((bf16[2,512,1600]{1,2,0:T(8,128)(2,1)}, bf16[2,512,1600]{1,2,0:T(8,128)(2,1)}, u32[]{:S(2)}, u32[]{:S(2)}) %collective-permute-start.21) | collective-permute-done | bytes 3276832 | tf_op jit(solution)/shard_map/ppermute | solution.py:23
  3211.0 35.3 collective-permute-done.22
  3412.0 31.6 copy.358
  3511.8 22.9 copy.344
  3562.3 916.3 %all-reduce.13.cloned.1.call-done = (bf16[2,1600,1200]{2,0,1:T(2,128)(2,1)}, bf16[2,1600,400]{1,2,0:T(8,128)(2,1)}, bf16[2,1600,1600]{2,1,0:T(8,128)(2,1)}, bf16[2,1600,1600]{1,0,2:T(2,128)(2,1)}) async-done(((bf16[2,1600,1200]{2,0,1:T(2,128)(2,1)}, bf16[2,1600,400]{1,2,0:T(8,128)(2,1)}, bf16[2,1600,1600]{2,1,0:T(8,128)(2,1)}, bf16[2,1600,1600]{1,0,2:T(2,128)(2,1)}), (bf16[2,1600,1200]{2,0,1:T(2,128)(2,1)}, ...) | async-done | bytes 30720016
  4492.4 27.7 all-reduce.8
  4520.2 17.7 psum.7
  4552.4 13.9 copy.359
  (1103 shorter events, 1217.5 us)
Async XLA Ops:
  7.3 216.5 %all-gather.97.cloned.1.call-start = ((), (), s32[]{:S(2)}) async-start(), calls=%async_computation.64 | async-start | bytes 17510400 | tf_op jit(solution)/shard_map/all_gather | solution.py:284
  11.7 249.7 %all-gather.51.cloned.1.call-start = ((), (), s32[]{:S(2)}) async-start(), calls=%async_computation.25 | async-start | bytes 1597440 | tf_op jit(solution)/shard_map/all_gather | solution.py:107
  245.1 76.6 %all-gather.61.cloned.1.call-start = ((), (), s32[]{:S(2)}) async-start(), calls=%async_computation.32 | async-start | bytes 1597440 | tf_op jit(solution)/shard_map/all_gather | solution.py:106
  246.0 528.2 %all-gather.99.cloned.1.call-start = ((), (), s32[]{:S(2)}) async-start(), calls=%async_computation.65 | async-start | bytes 5990400 | tf_op jit(solution)/shard_map/all_gather | solution.py:285
  247.3 572.4 %all-gather.101.cloned.1.call-start = ((), (), s32[]{:S(2)}) async-start(), calls=%async_computation.66 | async-start | bytes 5990400 | tf_op jit(solution)/shard_map/all_gather | solution.py:286
  359.4 105.9 %collective-permute-start.7 = (bf16[2,256,1600]{1,2,0:T(8,128)(2,1)}, bf16[2,256,1600]{1,2,0:T(8,128)(2,1)}, u32[]{:S(2)}, u32[]{:S(2)}) collective-permute-start(bf16[2,256,1600]{1,2,0:T(8,128)(2,1)} %copy.291), channel_id=1, source_target_pairs={{0,8},{4,12},{8,0},{12,4},{16,24},{20,28},{24,16},{28,20},{1,9},{5... | collective-permute-start | bytes 4915208 | tf_op jit(solution)/shard_map/ppermute | solution.py:23
  373.1 278.7 %collective-permute-start.2 = (bf16[2,512,1600]{1,2,0:T(8,128)(2,1)}, bf16[2,512,1600]{1,2,0:T(8,128)(2,1)}, u32[]{:S(2)}, u32[]{:S(2)}) collective-permute-start(bf16[2,512,1600]{1,2,0:T(8,128)(2,1)} %copy.265), channel_id=1, source_target_pairs={{0,16},{4,20},{8,24},{12,28},{16,0},{20,4},{24,8},{28,12},{1,17},{... | collective-permute-start | bytes 9830408 | tf_op jit(solution)/shard_map/ppermute | solution.py:23
  479.5 242.5 %collective-permute-start.8 = (bf16[2,512,1600]{1,2,0:T(8,128)(2,1)}, bf16[2,512,1600]{1,2,0:T(8,128)(2,1)}, u32[]{:S(2)}, u32[]{:S(2)}) collective-permute-start(bf16[2,512,1600]{1,2,0:T(8,128)(2,1)} %copy.294), channel_id=1, source_target_pairs={{0,16},{4,20},{8,24},{12,28},{16,0},{20,4},{24,8},{28,12},{1,17},{... | collective-permute-start | bytes 9830408 | tf_op jit(solution)/shard_map/ppermute | solution.py:23
  487.1 332.6 %all-gather.53.cloned.1.call-start = ((), (), s32[]{:S(2)}) async-start(), calls=%async_computation.26 | async-start | bytes 1597440 | tf_op jit(solution)/shard_map/all_gather | solution.py:127
  797.2 109.1 %all-gather.103.cloned.1.call-start = ((), (), s32[]{:S(2)}) async-start(), calls=%async_computation.67 | async-start | bytes 5990400 | tf_op jit(solution)/shard_map/all_gather | solution.py:287
  799.8 127.3 %all-gather.65.cloned.1.call-start = ((), (), s32[]{:S(2)}) async-start(), calls=%async_computation.34 | async-start | bytes 1597440 | tf_op jit(solution)/shard_map/all_gather | solution.py:127
  800.4 164.6 %reduce-scatter.21.cloned.1.call-start = ((), (), s32[]{:S(2)}) async-start(), calls=%async_computation.27 | async-start | bytes 1597440 | tf_op jit(solution)/shard_map/reduce_scatter | solution.py:135
  941.6 257.5 %all-gather.105.cloned.1.call-start = ((), (), s32[]{:S(2)}) async-start(), calls=%async_computation.68 | async-start | bytes 17510400 | tf_op jit(solution)/shard_map/all_gather | solution.py:284
  942.4 294.4 %all-gather.57.cloned.1.call-start = ((), (), s32[]{:S(2)}) async-start(), calls=%async_computation.29 | async-start | bytes 1597440 | tf_op jit(solution)/shard_map/all_gather | solution.py:107
  1220.4 75.9 %all-gather.67.cloned.1.call-start = ((), (), s32[]{:S(2)}) async-start(), calls=%async_computation.36 | async-start | bytes 1597440 | tf_op jit(solution)/shard_map/all_gather | solution.py:106
  1221.3 530.0 %all-gather.107.cloned.1.call-start = ((), (), s32[]{:S(2)}) async-start(), calls=%async_computation.69 | async-start | bytes 5990400 | tf_op jit(solution)/shard_map/all_gather | solution.py:285
  1221.9 557.3 %all-gather.109.cloned.1.call-start = ((), (), s32[]{:S(2)}) async-start(), calls=%async_computation.70 | async-start | bytes 5990400 | tf_op jit(solution)/shard_map/all_gather | solution.py:286
  1330.2 109.8 %collective-permute-start.10 = (bf16[2,256,1600]{1,2,0:T(8,128)(2,1)}, bf16[2,256,1600]{1,2,0:T(8,128)(2,1)}, u32[]{:S(2)}, u32[]{:S(2)}) collective-permute-start(bf16[2,256,1600]{1,2,0:T(8,128)(2,1)} %copy.305), channel_id=1, source_target_pairs={{0,8},{4,12},{8,0},{12,4},{16,24},{20,28},{24,16},{28,20},{1,9},{5... | collective-permute-start | bytes 4915208 | tf_op jit(solution)/shard_map/ppermute | solution.py:23
  1349.4 279.4 %collective-permute-start.5 = (bf16[2,512,1600]{1,2,0:T(8,128)(2,1)}, bf16[2,512,1600]{1,2,0:T(8,128)(2,1)}, u32[]{:S(2)}, u32[]{:S(2)}) collective-permute-start(bf16[2,512,1600]{1,2,0:T(8,128)(2,1)} %copy.280), channel_id=1, source_target_pairs={{0,16},{4,20},{8,24},{12,28},{16,0},{20,4},{24,8},{28,12},{1,17},{... | collective-permute-start | bytes 9830408 | tf_op jit(solution)/shard_map/ppermute | solution.py:23
  1454.0 244.9 %collective-permute-start.11 = (bf16[2,512,1600]{1,2,0:T(8,128)(2,1)}, bf16[2,512,1600]{1,2,0:T(8,128)(2,1)}, u32[]{:S(2)}, u32[]{:S(2)}) collective-permute-start(bf16[2,512,1600]{1,2,0:T(8,128)(2,1)} %copy.308), channel_id=1, source_target_pairs={{0,16},{4,20},{8,24},{12,28},{16,0},{20,4},{24,8},{28,12},{1,17},{... | collective-permute-start | bytes 9830408 | tf_op jit(solution)/shard_map/ppermute | solution.py:23
  1454.1 343.0 %all-gather.71.cloned.1.call-start = ((), (), s32[]{:S(2)}) async-start(), calls=%async_computation.38 | async-start | bytes 1597440 | tf_op jit(solution)/shard_map/all_gather | solution.py:127
  1777.1 126.6 %all-gather.111.cloned.1.call-start = ((), (), s32[]{:S(2)}) async-start(), calls=%async_computation.71 | async-start | bytes 5990400 | tf_op jit(solution)/shard_map/all_gather | solution.py:287
  1777.8 146.8 %all-gather.59.cloned.1.call-start = ((), (), s32[]{:S(2)}) async-start(), calls=%async_computation.30 | async-start | bytes 1597440 | tf_op jit(solution)/shard_map/all_gather | solution.py:127
  1778.6 165.5 %all-gather.113.cloned.1.call-start = ((), (), s32[]{:S(2)}) async-start(), calls=%async_computation.72 | async-start | bytes 1597440 | tf_op jit(solution)/shard_map/all_gather | solution.py:164
  1779.1 196.8 %reduce-scatter.41.cloned.1.call-start = ((), (), s32[]{:S(2)}) async-start(), calls=%async_computation.47 | async-start | bytes 1597440 | tf_op jit(solution)/shard_map/reduce_scatter | solution.py:172
  1920.2 82.0 %reduce-scatter.29.cloned.1.call-start = ((), (), s32[]{:S(2)}) async-start(), calls=%async_computation.40 | async-start | bytes 1597440 | tf_op jit(solution)/shard_map/reduce_scatter | solution.py:172
  1968.4 91.7 %reduce-scatter.27.cloned.1.call-start = ((), (), s32[]{:S(2)}) async-start(), calls=%async_computation.39 | async-start | bytes 1597440 | tf_op jit(solution)/shard_map/reduce_scatter | solution.py:135
  1975.9 369.6 %reduce-scatter.43.cloned.1.call-start = ((), (), s32[]{:S(2)}) async-start(), calls=%async_computation.48 | async-start | bytes 1597440 | tf_op jit(solution)/shard_map/reduce_scatter | solution.py:205
  2106.4 143.0 %collective-permute-start.18 = (bf16[2,512,1600]{1,2,0:T(8,128)(2,1)S(1)}, bf16[2,512,1600]{1,2,0:T(8,128)(2,1)}, u32[]{:S(2)}, u32[]{:S(2)}) collective-permute-start(bf16[2,512,1600]{1,2,0:T(8,128)(2,1)S(1)} %select_convert_fusion.1), channel_id=1, source_target_pairs={{0,16},{4,20},{8,24},{12,28},{16,0},{20,4},{24,8},{28,12},{1,17},{... | collective-permute-start | bytes 9830408 | tf_op jit(solution)/shard_map/ppermute | solution.py:23
  2321.9 347.3 %reduce-scatter.31.cloned.1.call-start = ((), (), s32[]{:S(2)}) async-start(), calls=%async_computation.41 | async-start | bytes 1597440 | tf_op jit(solution)/shard_map/reduce_scatter | solution.py:205
  2433.3 143.0 %collective-permute-start.12 = (bf16[2,512,1600]{1,2,0:T(8,128)(2,1)S(1)}, bf16[2,512,1600]{1,2,0:T(8,128)(2,1)}, u32[]{:S(2)}, u32[]{:S(2)}) collective-permute-start(bf16[2,512,1600]{1,2,0:T(8,128)(2,1)S(1)} %select_convert_fusion.3), channel_id=1, source_target_pairs={{0,16},{4,20},{8,24},{12,28},{16,0},{20,4},{24,8},{28,12},{1,17},{... | collective-permute-start | bytes 9830408 | tf_op jit(solution)/shard_map/ppermute | solution.py:23
  2650.1 88.2 %all-gather.73.cloned.1.call-start = ((), (), s32[]{:S(2)}) async-start(), calls=%async_computation.43 | async-start | bytes 1597440 | tf_op jit(solution)/shard_map/all_gather | solution.py:164
  2755.1 585.9 %all-gather.91.cloned.1.call-start = ((), (), s32[]{:S(2)}) async-start(), calls=%async_computation.61 | async-start | bytes 1597440 | tf_op jit(solution)/shard_map/all_gather | solution.py:128
  2756.1 593.9 %all-gather.93.cloned.1.call-start = ((), (), s32[]{:S(2)}) async-start(), calls=%async_computation.62 | async-start | bytes 1597440 | tf_op jit(solution)/shard_map/all_gather | solution.py:128
  2757.1 596.2 %all-gather.81.cloned.1.call-start = ((), (), s32[]{:S(2)}) async-start(), calls=%async_computation.56 | async-start | bytes 1597440 | tf_op jit(solution)/shard_map/all_gather | solution.py:108
  2757.7 602.8 %all-gather.83.cloned.1.call-start = ((), (), s32[]{:S(2)}) async-start(), calls=%async_computation.57 | async-start | bytes 1597440 | tf_op jit(solution)/shard_map/all_gather | solution.py:108
  2851.3 143.2 %collective-permute-start.15 = (bf16[2,512,1600]{1,2,0:T(8,128)(2,1)}, bf16[2,512,1600]{1,2,0:T(8,128)(2,1)}, u32[]{:S(2)}, u32[]{:S(2)}) collective-permute-start(bf16[2,512,1600]{1,2,0:T(8,128)(2,1)} %select_convert_fusion.2), channel_id=1, source_target_pairs={{0,16},{4,20},{8,24},{12,28},{16,0},{20,4},{24,8},{28,12},{1,17},{... | collective-permute-start | bytes 9830408 | tf_op jit(solution)/shard_map/ppermute | solution.py:23
  2853.4 605.7 %reduce-scatter.37.cloned.1.call-start = ((), (), s32[]{:S(2)}) async-start(), calls=%async_computation.45 | async-start | bytes 1597440 | tf_op jit(solution)/shard_map/reduce_scatter | solution.py:205
  3055.4 144.2 %collective-permute-start.21 = (bf16[2,512,1600]{1,2,0:T(8,128)(2,1)}, bf16[2,512,1600]{1,2,0:T(8,128)(2,1)}, u32[]{:S(2)}, u32[]{:S(2)}) collective-permute-start(bf16[2,512,1600]{1,2,0:T(8,128)(2,1)} %select_convert_fusion), channel_id=1, source_target_pairs={{0,16},{4,20},{8,24},{12,28},{16,0},{20,4},{24,8},{28,12},{1,17},{... | collective-permute-start | bytes 9830408 | tf_op jit(solution)/shard_map/ppermute | solution.py:23
  3064.7 394.5 %reduce-scatter.39.cloned.1.call-start = ((), (), s32[]{:S(2)}) async-start(), calls=%async_computation.46 | async-start | bytes 1597440 | tf_op jit(solution)/shard_map/reduce_scatter | solution.py:208
  3068.5 405.4 %all-gather.87.cloned.1.call-start = ((), (), s32[]{:S(2)}) async-start(), calls=%async_computation.59 | async-start | bytes 1597440 | tf_op jit(solution)/shard_map/all_gather | solution.py:128
  3211.0 265.4 %all-gather.89.cloned.1.call-start = ((), (), s32[]{:S(2)}) async-start(), calls=%async_computation.60 | async-start | bytes 1597440 | tf_op jit(solution)/shard_map/all_gather | solution.py:128
  3253.6 226.2 %reduce-scatter.49.cloned.1.call-start = ((), (), s32[]{:S(2)}) async-start(), calls=%async_computation.52 | async-start | bytes 1597440 | tf_op jit(solution)/shard_map/reduce_scatter | solution.py:205
  3274.8 205.0 %reduce-scatter.51.cloned.1.call-start = ((), (), s32[]{:S(2)}) async-start(), calls=%async_computation.53 | async-start | bytes 1597440 | tf_op jit(solution)/shard_map/reduce_scatter | solution.py:208
  3281.4 209.1 %all-gather.77.cloned.1.call-start = ((), (), s32[]{:S(2)}) async-start(), calls=%async_computation.54 | async-start | bytes 1597440 | tf_op jit(solution)/shard_map/all_gather | solution.py:108
  3282.0 215.7 %all-gather.79.cloned.1.call-start = ((), (), s32[]{:S(2)}) async-start(), calls=%async_computation.55 | async-start | bytes 1597440 | tf_op jit(solution)/shard_map/all_gather | solution.py:108
  3487.3 991.2 %all-reduce.13.cloned.1.call-start = ((), (), s32[]{:S(2)}) async-start(), calls=%async_computation.74 | async-start | bytes 64307200
  3534.9 1014.6 %all-gather.95.cloned.1.call-start = ((), (), s32[]{:S(2)}) async-start(), calls=%async_computation.63 | async-start | bytes 2048000 | tf_op jit(solution)/shard_map/all_gather | solution.py:335
  (283 other events, 11084.2 us)
Sparse Core Ops, SparseCore 0:
  11.8 211.8 all-gather.96
  242.6 18.8 all-gather.50
  263.5 18.0 all-gather.48
  283.6 17.9 all-gather.62
  303.6 17.9 all-gather.60
  323.7 144.1 all-gather.98
  487.3 288.2 all-gather.100
  797.4 21.4 all-gather.52
  821.6 84.6 all-gather.102
  908.3 18.7 all-gather.64
  930.2 25.9 reduce-scatter.20
  959.4 26.3 reduce-scatter.24
  988.5 210.5 all-gather.104
  1217.9 18.8 all-gather.56
  1238.7 18.0 all-gather.54
  1258.8 17.9 all-gather.68
  1278.2 17.9 all-gather.66
  1298.3 262.5 all-gather.106
  1563.2 190.0 all-gather.108
  1776.2 20.8 all-gather.70
  1818.9 84.7 all-gather.110
  1905.8 18.7 all-gather.58
  1947.2 25.9 reduce-scatter.40
  1975.8 26.3 reduce-scatter.28
  2004.6 26.3 reduce-scatter.22
  2033.8 26.3 reduce-scatter.26
  2316.5 28.9 reduce-scatter.42
  2348.1 26.3 reduce-scatter.44
  2640.1 28.9 reduce-scatter.30
  2671.9 26.3 reduce-scatter.32
  2699.7 18.4 all-gather.74
  2720.3 18.0 all-gather.72
  2741.5 25.9 reduce-scatter.46
  2770.7 26.3 reduce-scatter.34
  2798.5 18.3 all-gather.90
  2818.5 17.9 all-gather.92
  2857.5 18.0 all-gather.82
  3064.8 26.0 reduce-scatter.36
  3093.7 26.3 reduce-scatter.38
  3211.1 18.3 all-gather.86
  3253.7 20.3 all-gather.88
  3277.1 28.2 reduce-scatter.48
  3308.0 30.0 reduce-scatter.50
  3339.6 23.8 all-gather.76
  3364.9 18.3 all-gather.78
  3534.9 943.6 all-reduce.12
  4480.8 21.3 all-gather.94
  4504.3 38.8 all-gather.84
  (3 shorter events, 53.8 us)
where the time goes:
time: 4590 us; the launch traced here: 4570 us
  waiting for transfers between devices  3270 us (71%)
  matrix products  480 us (10%)
  local copies, waits for them, and re-layouts  412 us (9%)
  other arithmetic  202 us (4%)
  blocking collectives  107 us (2%)
  starting transfers between devices  79.6 us (2%)
    ppermute x24, waiting for transfers between devices, swapped(): return lax.ppermute(value, axis, pairs)  1350 us
    unnamed x52, waiting for transfers between devices  923 us
    all_gather x2, waiting for transfers between devices, local(): lax.all_gather(qkv_weight[layer], 'fsdp', axis=0, tiled=True)  396 us
    all_gather x2, waiting for transfers between devices, local(): lax.all_gather(proj_weight[layer], 'fsdp', axis=1, tiled=True)  166 us
    dot_general x16, matrix products, mat_rt(): lax.dot_general(left, right, (((1,), (1,)), ((), ())), preferred_element_...  126 us
    dot_general x16, matrix products, mat_t(): lax.dot_general(left, right, (((0,), (0,)), ((), ())), preferred_element_...  91.9 us
  transfers between devices with their start and end apart: 83, of which 56 were waited for; matrix products, arithmetic and copies ran while one was open for 18% of the time, Pallas kernels for 0%

commit v1 on v0

v1 whole, which is shorter than its diff:
```python
import functools

import jax
import jax.numpy as jnp
from jax import lax
from jax.experimental import pallas as pl
from jax.experimental.pallas import tpu as pltpu
from jax.sharding import PartitionSpec as P

D = 1600
HEADS = 25
HEAD = 64
GROUP = 8
PROMPT_DEV = 128
CONT_LEN = 256
TOK_DEV = 384
MICRO = 2
LAYERS = 2
PROMPT = 1024
KEYS = PROMPT + CONT_LEN
CHUNK = 128

f32 = jnp.float32
bf16 = jnp.bfloat16
norm_eps = 1e-05
NN = (((1,), (0,)), ((), ()))
NT = (((1,), (1,)), ((), ()))
TN = (((0,), (0,)), ((), ()))


def mm(left, right, dims=NN):
    return lax.dot_general(left, right, dims, preferred_element_type=f32)


def swapped(value, axis, mask):
    pairs = [(source, source ^ mask) for source in range(lax.axis_size(axis))]
    return lax.ppermute(value, axis, pairs)


def layer_norm(x, gain, bias):
    centred = x - jnp.mean(x, -1, keepdims=True)
    spread = jnp.mean(centred * centred, -1, keepdims=True)
    return centred * lax.rsqrt(spread + norm_eps) * gain + bias


def gelu_tanh(value):
    return jax.nn.gelu(value, approximate=True)


def by_offset(stacked, index):
    return jnp.take(stacked, index ^ jnp.arange(stacked.shape[0]), axis=0)


def tp_gather(value):
    n = lax.axis_size("tp")
    held = value[None]
    mask = n // 2
    order = [0]
    while mask:
        held = jnp.concatenate([held, swapped(held, "tp", mask)], axis=0)
        order = order + [o ^ mask for o in order]
        mask //= 2
    place = [order.index(k) for k in range(n)]
    held = jnp.stack([held[p] for p in place])
    return by_offset(held, lax.axis_index("tp"))


def tp_scatter(parts):
    held = by_offset(parts, lax.axis_index("tp"))
    mask = 1
    while mask < lax.axis_size("tp"):
        arrived = swapped(held[1::2].astype(bf16), "tp", mask)
        held = held[0::2].astype(f32) + arrived.astype(f32)
        mask *= 2
    return held[0]


def group_gather(value, member):
    along = [value] + [swapped(value, "fsdp", k) for k in (2, 4, 6)]
    across = [swapped(piece, "fsdp", 1) for piece in along]
    stacked = jnp.stack([piece for pair in zip(along, across) for piece in pair])
    return by_offset(stacked, member)


def group_scatter(parts, member):
    held = by_offset(parts, member)
    arrived = swapped(held[1::2], "fsdp", 1)
    summed = held[0::2].astype(f32) + arrived.astype(f32)
    total = summed[0]
    for k in (1, 2, 3):
        total = total + swapped(summed[k].astype(bf16), "fsdp", 2 * k).astype(f32)
    return total


def key_limit(member):
    row = lax.broadcasted_iota(jnp.int32, (1, TOK_DEV), 1)
    return jnp.where(row < PROMPT_DEV, member * PROMPT_DEV + row, PROMPT - PROMPT_DEV + row)


def half_of(value, half):
    lane = lax.broadcasted_iota(jnp.int32, value.shape, 1)
    return jnp.where((lane >= HEAD * half) & (lane < HEAD * (half + 1)), value, jnp.zeros_like(value))


def fold(value, op):
    return op(value.reshape(value.shape[0] // 8, 8, value.shape[1]), axis=0)


N_PROMPT_CHUNKS = PROMPT // CHUNK
N_CONT_CHUNKS = CONT_LEN // CHUNK


def over_keys(body, prompt_ref, own_ref, carry):
    def prompt_step(c, carry):
        at = pl.ds(pl.multiple_of(c * CHUNK, CHUNK), CHUNK)
        return body(c, lambda refs: refs[0][0, at, :], carry)

    def own_step(c, carry):
        at = pl.ds(pl.multiple_of(PROMPT_DEV + c * CHUNK, CHUNK), CHUNK)
        return body(N_PROMPT_CHUNKS + c, lambda refs: refs[1][0, at, :], carry)

    carry = lax.fori_loop(0, N_PROMPT_CHUNKS, prompt_step, carry)
    return lax.fori_loop(0, N_CONT_CHUNKS, own_step, carry)


def attn_fwd_kernel(q_ref, kp_ref, vp_ref, k_ref, v_ref, out_ref, lse_ref, s_ref, p_ref, o_ref):
    member = lax.rem(lax.axis_index("fsdp"), GROUP)
    limit = key_limit(member)
    sub = lax.broadcasted_iota(jnp.int32, (CHUNK, TOK_DEV), 0)
    pair = pl.program_id(1)

    def head(half):
        qh = half_of(q_ref[0], half)

        def first(c, load, top):
            s = mm(load((kp_ref, k_ref)), qh, NT)
            s = jnp.where(sub + c * CHUNK <= limit, s, -1e30)
            s_ref[pl.ds(pl.multiple_of(c * CHUNK, CHUNK), CHUNK), :] = s
            return jnp.maximum(top, fold(s, jnp.max))

        top = over_keys(first, kp_ref, k_ref, jnp.full((8, TOK_DEV), -1e30, f32))
        top = jnp.max(top, axis=0, keepdims=True)

        def second(c, total):
            at = pl.ds(pl.multiple_of(c * CHUNK, CHUNK), CHUNK)
            p = jnp.exp(s_ref[at, :] - top)
            p_ref[at, :] = p.astype(bf16)
            return total + fold(p, jnp.sum)

        total = lax.fori_loop(0, KEYS // CHUNK, second, jnp.zeros((8, TOK_DEV), f32))
        total = jnp.sum(total, axis=0, keepdims=True)
        out = mm(vp_ref[0], p_ref[:PROMPT, :], TN) + mm(v_ref[0, PROMPT_DEV:, :], p_ref[PROMPT:, :], TN)
        rows = slice(HEAD * half, HEAD * (half + 1))
        o_ref[rows, :] = out[rows, :] / total
        lse_ref[0, 0, half : half + 1, :] = top + jnp.log(total)

    head(0)

    @pl.when(pair < HEAD_PAIRS - 1)
    def _():
        head(1)

    @pl.when(pair == HEAD_PAIRS - 1)
    def _():
        o_ref[HEAD:, :] = jnp.zeros((HEAD, TOK_DEV), f32)

    out_ref[0] = o_ref[...].T.astype(bf16)


HEAD_PAIRS = 4
WIDE = HEAD_PAIRS * 2 * HEAD


def pair_spec(rows):
    return pl.BlockSpec((1, rows, 2 * HEAD), lambda m, h: (m, 0, h))


LSE_SPEC = pl.BlockSpec((1, 1, 8, TOK_DEV), lambda m, h: (m, h, 0, 0))


def attn_fwd(query, keys_p, values_p, key, value):
    return pl.pallas_call(
        attn_fwd_kernel,
        grid=(MICRO, HEAD_PAIRS),
        out_shape=(
            jax.ShapeDtypeStruct((MICRO, TOK_DEV, WIDE), bf16),
            jax.ShapeDtypeStruct((MICRO, HEAD_PAIRS, 8, TOK_DEV), f32),
        ),
        in_specs=[pair_spec(TOK_DEV), pair_spec(PROMPT), pair_spec(PROMPT), pair_spec(TOK_DEV), pair_spec(TOK_DEV)],
        out_specs=(pair_spec(TOK_DEV), LSE_SPEC),
        scratch_shapes=[
            pltpu.VMEM((KEYS, TOK_DEV), f32),
            pltpu.VMEM((KEYS, TOK_DEV), bf16),
            pltpu.VMEM((2 * HEAD, TOK_DEV), f32),
        ],
        compiler_params=pltpu.CompilerParams(vmem_limit_bytes=32 * 2**20),
        cost_estimate=pl.CostEstimate(
            flops=2 * 7 * MICRO * TOK_DEV * KEYS * 256 * 2, bytes_accessed=16 * 2**20, transcendentals=0
        ),
    )(query, keys_p, values_p, key, value)


def attn_bwd_kernel(
    q_ref, kp_ref, vp_ref, k_ref, v_ref, g_ref, lse_ref,
    dq_ref, dkp_ref, dvp_ref, dkc_ref, dvc_ref, p_ref, dp_ref, ds_ref, o_ref,
):
    member = lax.rem(lax.axis_index("fsdp"), GROUP)
    limit = key_limit(member)
    sub = lax.broadcasted_iota(jnp.int32, (CHUNK, TOK_DEV), 0)
    pair = pl.program_id(1)

    def put(ref, at, value, half):
        if half:
            value = value + ref[0, at, :].astype(f32)
        ref[0, at, :] = value.astype(ref.dtype)

    def head(half):
        qh = half_of(q_ref[0], half)
        gh = half_of(g_ref[0], half)
        lse = lse_ref[0, 0, half : half + 1, :]

        def first(c, load, inner):
            at = pl.ds(pl.multiple_of(c * CHUNK, CHUNK), CHUNK)
            s = mm(load((kp_ref, k_ref)), qh, NT)
            p = jnp.exp(jnp.where(sub + c * CHUNK <= limit, s, -1e30) - lse)
            dp = mm(load((vp_ref, v_ref)), gh, NT)
            p_ref[at, :] = p
            dp_ref[at, :] = dp
            return inner + fold(p * dp, jnp.sum)

        inner = over_keys(first, kp_ref, k_ref, jnp.zeros((8, TOK_DEV), f32))
        inner = jnp.sum(inner, axis=0, keepdims=True)

        def second(c, base, dk_ref, dv_ref):
            at = pl.ds(pl.multiple_of(base + c * CHUNK, CHUNK), CHUNK)
            to = pl.ds(pl.multiple_of(c * CHUNK, CHUNK), CHUNK)
            p = p_ref[at, :]
            ds = (p * (dp_ref[at, :] - inner)).astype(bf16)
            ds_ref[at, :] = ds
            put(dv_ref, to, mm(p.astype(bf16), gh), half)
            put(dk_ref, to, mm(ds, qh), half)

        @pl.loop(0, N_PROMPT_CHUNKS)
        def _(c):
            second(c, 0, dkp_ref, dvp_ref)

        @pl.loop(0, N_CONT_CHUNKS)
        def _(c):
            second(c, PROMPT, dkc_ref, dvc_ref)

        dq = mm(kp_ref[0], ds_ref[:PROMPT, :], TN) + mm(k_ref[0, PROMPT_DEV:, :], ds_ref[PROMPT:, :], TN)
        rows = slice(HEAD * half, HEAD * (half + 1))
        o_ref[rows, :] = dq[rows, :] * HEAD ** (-0.5)

    head(0)

    @pl.when(pair < HEAD_PAIRS - 1)
    def _():
        head(1)

    @pl.when(pair == HEAD_PAIRS - 1)
    def _():
        o_ref[HEAD:, :] = jnp.zeros((HEAD, TOK_DEV), f32)

    dq_ref[0] = o_ref[...].T.astype(bf16)


def attn_bwd(query, keys_p, values_p, key, value, grad, lse):
    own = [pair_spec(TOK_DEV)] * 2
    return pl.pallas_call(
        attn_bwd_kernel,
        grid=(MICRO, HEAD_PAIRS),
        out_shape=(
            jax.ShapeDtypeStruct((MICRO, TOK_DEV, WIDE), bf16),
            jax.ShapeDtypeStruct((MICRO, PROMPT, WIDE), bf16),
            jax.ShapeDtypeStruct((MICRO, PROMPT, WIDE), bf16),
            jax.ShapeDtypeStruct((MICRO, CONT_LEN, WIDE), bf16),
            jax.ShapeDtypeStruct((MICRO, CONT_LEN, WIDE), bf16),
        ),
        in_specs=[pair_spec(TOK_DEV), pair_spec(PROMPT), pair_spec(PROMPT)] + own + [pair_spec(TOK_DEV), LSE_SPEC],
        out_specs=(pair_spec(TOK_DEV), pair_spec(PROMPT), pair_spec(PROMPT), pair_spec(CONT_LEN), pair_spec(CONT_LEN)),
        scratch_shapes=[
            pltpu.VMEM((KEYS, TOK_DEV), f32),
            pltpu.VMEM((KEYS, TOK_DEV), f32),
            pltpu.VMEM((KEYS, TOK_DEV), bf16),
            pltpu.VMEM((2 * HEAD, TOK_DEV), f32),
        ],
        compiler_params=pltpu.CompilerParams(vmem_limit_bytes=32 * 2**20),
        cost_estimate=pl.CostEstimate(
            flops=5 * 7 * MICRO * TOK_DEV * KEYS * 256 * 2, bytes_accessed=32 * 2**20, transcendentals=0
        ),
    )(query, keys_p, values_p, key, value, grad, lse)


def by_block(rows, n_tp):
    cols = rows.shape[-1]
    return rows.reshape(n_tp, MICRO, -1, cols).swapaxes(0, 1).reshape(MICRO, -1, cols)


def by_device(blocks, n_tp):
    cols = blocks.shape[-1]
    return blocks.reshape(MICRO, n_tp, -1, cols).swapaxes(0, 1).reshape(-1, cols)


def widen(value):
    return jnp.pad(value, [(0, 0)] * (value.ndim - 1) + [(0, WIDE - value.shape[-1])])


def forward_layer(x, weights, vecs, fc_bias, member, cols, n_tp):
    w_qkv, w_out, w_fc, w_proj = weights
    rows = x.shape[0]
    width = w_out.shape[0]
    normed = layer_norm(x, vecs[0], vecs[1]).astype(bf16)
    normed_all = tp_gather(normed).reshape(-1, D)
    projected = mm(normed_all, w_qkv)
    query_bias, value_bias = (lax.dynamic_slice_in_dim(vecs[i], cols, width) for i in (2, 3))
    query = (projected[:, :width] + query_bias).astype(bf16) * HEAD ** (-0.5)
    key = projected[:, width : 2 * width].astype(bf16)
    value = (projected[:, 2 * width :] + value_bias).astype(bf16)
    query, key, value = (by_block(part, n_tp) for part in (query, key, value))
    shared = group_gather(jnp.stack([key[:, :PROMPT_DEV], value[:, :PROMPT_DEV]]), member)
    shared = shared.transpose(1, 2, 0, 3, 4).reshape(2, MICRO, PROMPT, width)
    query, key, value, keys_p, values_p = (
        widen(part) for part in (query, key, value, shared[0], shared[1])
    )
    mixed, lse = attn_fwd(query, keys_p, values_p, key, value)
    mixed = by_device(mixed[:, :, :width], n_tp)
    part = mm(mixed, w_out).astype(bf16)
    x_mid = x + (tp_scatter(part.reshape(n_tp, rows, D)) + vecs[4])
    second = layer_norm(x_mid, vecs[5], vecs[6]).astype(bf16)
    second_all = tp_gather(second).reshape(-1, D)
    hidden_pre = mm(second_all, w_fc) + fc_bias
    hidden = gelu_tanh(hidden_pre).astype(bf16)
    part = mm(hidden, w_proj, NT).astype(bf16)
    x_next = x_mid + tp_scatter(part.reshape(n_tp, rows, D)) + vecs[7]
    saved = (x, normed_all, query, keys_p, values_p, key, value, lse, mixed, x_mid, second_all, hidden_pre, hidden)
    return x_next, saved


def fsdp_sum(part):
    return lax.psum_scatter(part.astype(bf16), "fsdp", scatter_dimension=0, tiled=True).astype(f32)


def heads_joined(parts, n_tp):
    step = HEADS // n_tp * HEAD
    return jnp.concatenate([parts[t][..., :step] for t in range(n_tp - 1)] + [parts[n_tp - 1]], axis=-1)


def backward_layer(grad_x, weights, vecs, saved, member, cols, n_tp):
    w_qkv, w_out, w_fc, w_proj = weights
    x, normed_all, query, keys_p, values_p, key, value, lse, mixed, x_mid, second_all, hidden_pre, hidden = saved
    rows = x.shape[0]
    width = w_out.shape[0]
    grad_branch = grad_x.astype(bf16)
    grad_proj_bias = jnp.sum(grad_branch.astype(f32), 0)
    branch_all = tp_gather(grad_branch).reshape(-1, D)
    proj_sum = fsdp_sum(mm(branch_all, hidden, TN))
    grad_hidden = mm(branch_all, w_proj)
    _, gelu_back = jax.vjp(gelu_tanh, hidden_pre)
    grad_pre = gelu_back(grad_hidden)[0].astype(bf16)
    fc_sum = fsdp_sum(mm(second_all, grad_pre, TN))
    grad_fc_bias = jnp.sum(grad_pre.astype(f32), 0)
    part = mm(grad_pre, w_fc, NT).astype(bf16)
    grad_second = tp_scatter(part.reshape(n_tp, rows, D))
    _, norm_back = jax.vjp(layer_norm, x_mid, vecs[5], vecs[6])
    grad_from_norm, grad_gain_two, grad_bias_two = norm_back(grad_second)
    grad_mid = grad_x + grad_from_norm
    grad_attn = grad_mid.astype(bf16)
    grad_out_bias = jnp.sum(grad_attn.astype(f32), 0)
    attn_all = tp_gather(grad_attn).reshape(-1, D)
    mixed_all = heads_joined(lax.all_gather(mixed, "tp"), n_tp)
    out_sum = fsdp_sum(mm(mixed_all, lax.dynamic_slice_in_dim(attn_all, cols, width, 1), TN))
    grad_mixed = widen(by_block(mm(attn_all, w_out, NT).astype(bf16), n_tp))
    dq, dkp, dvp, dkc, dvc = attn_bwd(query, keys_p, values_p, key, value, grad_mixed, lse)
    shared = jnp.stack([dkp[:, :, :width], dvp[:, :, :width]]).reshape(2, MICRO, GROUP, PROMPT_DEV, width)
    own = group_scatter(shared.transpose(2, 0, 1, 3, 4), member).astype(bf16)
    dk = jnp.concatenate([own[0], dkc[:, :, :width]], axis=1)
    dv = jnp.concatenate([own[1], dvc[:, :, :width]], axis=1)
    grad_qkv = by_device(jnp.concatenate([dq[:, :, :width], dk, dv], axis=2), n_tp)
    qkv_sum = fsdp_sum(mm(normed_all, grad_qkv, TN))
    column_sums = jnp.sum(grad_qkv.astype(f32), 0)
    part = mm(grad_qkv, w_qkv, NT).astype(bf16)
    grad_normed = tp_scatter(part.reshape(n_tp, rows, D))
    _, first_back = jax.vjp(layer_norm, x, vecs[0], vecs[1])
    grad_from_first, grad_gain_one, grad_bias_one = first_back(grad_normed)
    grad_in = grad_mid + grad_from_first

    def placed(part):
        return lax.dynamic_update_slice_in_dim(jnp.zeros((D,), f32), part, cols, 0)

    vector_grads = jnp.stack(
        [
            grad_gain_one,
            grad_bias_one,
            placed(column_sums[:width]),
            placed(column_sums[2 * width :]),
            grad_out_bias,
            grad_gain_two,
            grad_bias_two,
            grad_proj_bias,
        ]
    )
    vector_sum = lax.psum(lax.psum_scatter(vector_grads, "fsdp", scatter_dimension=1, tiled=True), "tp")
    fc_bias_sum = lax.psum_scatter(grad_fc_bias, "fsdp", scatter_dimension=0, tiled=True)
    qkv_all = lax.all_gather(qkv_sum.astype(bf16).reshape(-1, 3, width), "tp")
    out_all = lax.all_gather(out_sum.astype(bf16), "tp")
    qkv_grad = heads_joined(qkv_all, n_tp).reshape(-1, 3 * D).astype(f32)
    out_grad = heads_joined(out_all, n_tp).astype(f32)
    return grad_in, (qkv_grad, out_grad, fc_sum, proj_sum.T, fc_bias_sum, vector_sum)


def local(
    tokens,
    qkv_weight,
    query_bias,
    value_bias,
    out_weight,
    out_bias,
    fc_weight,
    fc_bias,
    proj_weight,
    proj_bias,
    first_gain,
    first_bias,
    second_gain,
    second_bias,
    out_grad,
):
    n_tp = lax.axis_size("tp")
    tp = lax.axis_index("tp")
    row_count = tokens.shape[1]
    member = lax.axis_index("fsdp") % GROUP
    step = HEADS // n_tp * HEAD
    width = D - step * (n_tp - 1)
    cols = tp * step
    keep = (lax.iota(jnp.int32, width) < step) | (tp == n_tp - 1)

    def gathered(part):
        return lax.all_gather(part, "fsdp", axis=0, tiled=True)

    vectors = jnp.stack(
        [first_gain, first_bias, query_bias, value_bias, out_bias, second_gain, second_bias, proj_bias, fc_bias[:, 0]]
    )
    vectors = lax.all_gather(vectors, "fsdp", axis=2, tiled=True).astype(f32)

    weights = []
    for layer in range(LAYERS):
        qkv_cols = jnp.concatenate(
            [lax.dynamic_slice_in_dim(qkv_weight[layer], cols + i * D, width, 1) for i in range(3)], axis=1
        )
        w_qkv = gathered(qkv_cols)
        out_cols = gathered(lax.dynamic_slice_in_dim(out_weight[layer], cols, width, 1))
        out_parts = jnp.stack([out_cols[t * step : t * step + width] for t in range(n_tp)])
        w_out = heads_joined(lax.all_to_all(out_parts, "tp", 0, 0), n_tp)
        w_out = jnp.where(keep[:, None], w_out, jnp.zeros_like(w_out))
        w_fc = gathered(fc_weight[layer])
        w_proj = gathered(proj_weight[layer].T)
        weights.append((w_qkv, w_out, w_fc, w_proj))

    state = tokens.astype(f32).reshape(MICRO * row_count, D)
    saves = []
    for layer in range(LAYERS):
        state, saved = forward_layer(
            state, weights[layer], vectors[:8, layer], vectors[8, layer], member, cols, n_tp
        )
        saves.append(saved)
    out_tokens = state.astype(bf16).reshape(tokens.shape)
    grad = out_grad.astype(f32).reshape(MICRO * row_count, D)
    sums = [None] * LAYERS
    for layer in reversed(range(LAYERS)):
        grad, sums[layer] = backward_layer(
            grad, weights[layer], vectors[:8, layer], saves[layer], member, cols, n_tp
        )
    qkv_g, out_g, fc_g, proj_g, fc_bias_g, vec_g = (
        jnp.stack([sums[layer][i] for layer in range(LAYERS)]) for i in range(6)
    )
    return (
        out_tokens,
        grad.reshape(tokens.shape),
        qkv_g,
        vec_g[:, 2],
        vec_g[:, 3],
        out_g,
        vec_g[:, 4],
        fc_g,
        fc_bias_g[:, None],
        proj_g,
        vec_g[:, 7],
        vec_g[:, 0],
        vec_g[:, 1],
        vec_g[:, 5],
        vec_g[:, 6],
    )


def solution(mesh):
    rows = P(None, ("fsdp", "tp"), None)
    weight = P(None, "fsdp", None)
    vector = P(None, "fsdp")
    fc_in = P(None, "fsdp", "tp")
    hidden = P(None, "tp", "fsdp")
    in_specs = (
        rows, weight, vector, vector, weight, vector, fc_in, hidden, hidden,
        vector, vector, vector, vector, vector, rows,
    )
    out_specs = (
        rows, rows, weight, vector, vector, weight, vector, fc_in, hidden, hidden,
        vector, vector, vector, vector, vector,
    )
    return jax.shard_map(local, mesh=mesh, in_specs=in_specs, out_specs=out_specs, check_vma=False)
```

time: 4590 us -> 2230 us (0.49)
  waiting for transfers between devices: 3270 us -> 1100 us
  matrix products: 480 us -> 186 us
  Pallas kernels: 0 us -> 232 us
  blocking collectives: 107 us -> 57.8 us
    ppermute x24 -> x54, waiting for transfers between devices: 1350 us -> 554 us  [swapped(): return lax.ppermute(value, axis, pairs)]
    all_gather x34 -> x12, waiting for transfers between devices: 755 us -> 32.6 us  [the longest x2 32.5 us: backward_layer(): qkv_all = lax.all_gather(qkv_sum.astype(bf16).reshape(-1, 3, width), 'tp')]
    unnamed x52 -> x28, waiting for transfers between devices: 923 us -> 509 us
    dot_general x72 -> x24, matrix products: 480 us -> 186 us  [mm(): return lax.dot_general(left, right, dims, preferred_element_type=f32)]
    reduce_scatter x16 -> x2, waiting for transfers between devices: 235 us -> 0.02 us  [fsdp_sum(): lax.psum_scatter(part.astype(bf16), 'fsdp', scatter_dimension=0, tiled=True)]
    pallas_call x0 -> x4, Pallas kernels: none -> 232 us  [the longest x2 140 us: attn_bwd(): pl.pallas_call(attn_bwd_kernel, grid=(MICRO, HEAD_PAIRS), out_shape=(jax....]
    gather x0 -> x20, local copies, waits for them, and re-layouts: none -> 71.1 us  [by_offset(): return jnp.take(stacked, index ^ jnp.arange(stacked.shape[0]), axis=0)]
    another operation x22 -> x25, local copies, waits for them, and re-layouts: 67.4 us -> 11.5 us  [the longest x2 4.39 us: backward_layer(): qkv_all = lax.all_gather(qkv_sum.astype(bf16).reshape(-1, 3, width), 'tp')]
  transfers between devices with their start and end apart: 83 -> 77, of which waited for: 56 -> 46; matrix products, arithmetic and copies ran while one was open for 18% -> 27% of each run, Pallas kernels for 0% -> 7%
where the time goes in v1:
time: 2230 us; the launch traced here: 2220 us
  waiting for transfers between devices  1100 us (49%)
  local copies, waits for them, and re-layouts  383 us (17%)
  Pallas kernels  232 us (10%)
  matrix products  186 us (8%)
  other arithmetic  161 us (7%)
  starting transfers between devices  83.5 us (4%)
  blocking collectives  57.8 us (3%)
    ppermute x54, waiting for transfers between devices, swapped(): return lax.ppermute(value, axis, pairs)  554 us
    unnamed x28, waiting for transfers between devices  509 us
    dot_general x24, matrix products, mm(): return lax.dot_general(left, right, dims, preferred_element_type=f32)  186 us
    pallas_call x2, Pallas kernels, attn_bwd(): pl.pallas_call(attn_bwd_kernel, grid=(MICRO, HEAD_PAIRS), out_shape=(jax....  140 us
    pallas_call x2, Pallas kernels, attn_fwd(): pl.pallas_call(attn_fwd_kernel, grid=(MICRO, HEAD_PAIRS), out_shape=(jax....  92.9 us
    slice x1, local copies, waits for them, and re-layouts, forward_layer(): x_next = x_mid + tp_scatter(part.reshape(n_tp, rows, D)) + vecs[7]  82.7 us
    ppermute x54, starting transfers between devices, swapped(): return lax.ppermute(value, axis, pairs)  73.7 us
    gather x20, local copies, waits for them, and re-layouts, by_offset(): return jnp.take(stacked, index ^ jnp.arange(stacked.shape[0]), axis=0)  71.1 us
  transfers between devices with their start and end apart: 77, of which 46 were waited for; matrix products, arithmetic and copies ran while one was open for 27% of the time, Pallas kernels for 7%

profile of v1, /device:TPU:9, one launch (start us, length us, event | category | flops | bytes accessed | tf_op | source)
XLA Modules:
  0.0 2218.6 jit_solution(4140381046136342355)
XLA Ops:
  18.5 26.7 %all_gather.51 = bf16[9,2,1600]{0,1,2:T(2,128)(2,1)S(1)} all-gather(bf16[9,2,200]{0,1,2:T(2,128)(2,1)S(1)} %copy.150), channel_id=1, replica_groups=mesh['fsdp'=8,'tp'=4] {'fsdp'}, dimensions={2}, use_global_device_ids=true | all-gather | bytes 64800 | tf_op jit(solution)/shard_map/all_gather | solution.py:444
  48.2 82.7 %slice_reduce_fusion = (f32[1600]{0:T(1024)}, f32[1600]{0:T(1024)}, f32[1600]{0:T(1024)}, f32[1600]{0:T(1024)}, f32[1600]{0:T(1024)}, /*index=5*/f32[1600]{0:T(1...) fusion(f32[9,2,1600]{0,1,2:T(2,128)S(1)} %convert_element_type.380), kind=kLoop, calls=%fused_computation.261 | loop fusion | bytes 179200 | tf_op jit(solution)/shard_map/slice | solution.py:335
  131.4 10.1 collective-permute-done
  203.4 34.0 %collective-permute-done.3 = bf16[2,2,128,448]{3,2,1,0:T(8,128)(2,1)} collective-permute-done((bf16[2,2,128,448]{3,2,1,0:T(8,128)(2,1)}, bf16[2,2,128,448]{3,2,1,0:T(8,128)(2,1)}, u32[]{:S(2)}, u32[]{:S(2)}) %collective-permute-start.3) | collective-permute-done | bytes 458784 | tf_op jit(solution)/shard_map/ppermute | solution.py:37
  242.0 28.6 %collective-permute-done.7 = bf16[2,2,128,448]{3,2,1,0:T(8,128)(2,1)} collective-permute-done((bf16[2,2,128,448]{3,2,1,0:T(8,128)(2,1)}, bf16[2,2,128,448]{3,2,1,0:T(8,128)(2,1)}, u32[]{:S(2)}, u32[]{:S(2)}) %collective-permute-start.7) | collective-permute-done | bytes 458784 | tf_op jit(solution)/shard_map/ppermute | solution.py:37
  298.6 52.3 %shard_map.262 = (bf16[2,384,512]{2,1,0:T(8,128)(2,1)S(1)}, f32[2,4,8,384]{3,2,1,0:T(8,128)S(1)}) custom-call(bf16[2,384,512]{2,1,0:T(8,128)(2,1)S(1)} %pad.38.q_ref, bf16[2,1024,512]{2,1,0:T(8,128)(2,1)S(1)} %pad.39.kp_ref, bf16[2,1024,512]{2,1,0:T(8,128)(2,1)S(1)} %pad.40.vp_ref, bf16[2,384,512]{2,1,0:T(8,128)(2,1)S(1)} %pad.41.k_ref, ...), custom_call_target="tpu_custom_call" | custom-call | flops 7046430720 | bytes 16777216 | tf_op jit(solution)/shard_map/pallas_call | solution.py:182
  373.5 13.1 collective-permute-done.10
  396.3 13.6 collective-permute-done.11
  424.3 10.3 fusion.6
  434.5 10.7 convolution_convert_fusion.11
  464.4 14.5 collective-permute-done.14
  483.1 13.7 collective-permute-done.15
  544.7 30.3 %collective-permute-done.18 = bf16[2,2,128,448]{3,2,1,0:T(8,128)(2,1)} collective-permute-done((bf16[2,2,128,448]{3,2,1,0:T(8,128)(2,1)}, bf16[2,2,128,448]{3,2,1,0:T(8,128)(2,1)}, u32[]{:S(2)}, u32[]{:S(2)}) %collective-permute-start.18) | collective-permute-done | bytes 458784 | tf_op jit(solution)/shard_map/ppermute | solution.py:37
  579.9 29.3 %collective-permute-done.22 = bf16[2,2,128,448]{3,2,1,0:T(8,128)(2,1)} collective-permute-done((bf16[2,2,128,448]{3,2,1,0:T(8,128)(2,1)}, bf16[2,2,128,448]{3,2,1,0:T(8,128)(2,1)}, u32[]{:S(2)}, u32[]{:S(2)}) %collective-permute-start.22) | collective-permute-done | bytes 458784 | tf_op jit(solution)/shard_map/ppermute | solution.py:37
  637.6 40.6 %shard_map.263 = (bf16[2,384,512]{2,1,0:T(8,128)(2,1)S(1)}, f32[2,4,8,384]{3,2,1,0:T(8,128)S(1)}) custom-call(bf16[2,384,512]{2,1,0:T(8,128)(2,1)S(1)} %copy-done.14, bf16[2,1024,512]{2,1,0:T(8,128)(2,1)S(1)} %pad.44.kp_ref, bf16[2,1024,512]{2,1,0:T(8,128)(2,1)S(1)} %pad.45.vp_ref, bf16[2,384,512]{2,1,0:T(8,128)(2,1)S(1)} %copy-done.12, ...), custom_call_target="tpu_custom_call" | custom-call | flops 7046430720 | bytes 16777216 | tf_op jit(solution)/shard_map/pallas_call | solution.py:182
  701.0 13.9 collective-permute-done.25
  717.8 10.8 collective-permute-done.30
  730.9 11.5 collective-permute-done.26
  763.7 10.2 fusion.2
  773.9 14.7 convert_reduce_fusion
  811.5 14.8 collective-permute-done.33
  832.4 13.8 collective-permute-done.34
  868.3 69.7 %shard_map.264 = (bf16[2,384,512]{2,1,0:T(8,128)(2,1)S(1)}, bf16[2,1024,512]{2,1,0:T(8,128)(2,1)S(1)}, bf16[2,1024,512]{2,1,0:T(8,128)(2,1)S(1)}, bf16[2,256,512...) custom-call(bf16[2,384,512]{2,1,0:T(8,128)(2,1)S(1)} %copy-done.15, bf16[2,1024,512]{2,1,0:T(8,128)(2,1)S(1)} %pad.44.kp_ref, ...), custom_call_target="tpu_custom_call" | custom-call | flops 17616076800 | bytes 33554432 | tf_op jit(solution)/shard_map/pallas_call | solution.py:270
  956.5 40.4 %collective-permute-done.36 = bf16[4,2,2,128,448]{3,4,2,1,0:T(8,128)(2,1)} collective-permute-done((bf16[4,2,2,128,448]{3,4,2,1,0:T(8,128)(2,1)}, bf16[4,2,2,128,448]{3,4,2,1,0:T(8,128)(2,1)}, u32[]{:S(2)}, u32[]{:S(2)}) %collective-permute-start.36) | collective-permute-done | bytes 1835040 | tf_op jit(solution)/shard_map/ppermute | solution.py:37
  1008.7 16.7 collective-permute-done.37
  1028.1 24.1 %collective-permute-done.39 = bf16[2,2,128,448]{3,2,1,0:T(8,128)(2,1)} collective-permute-done((bf16[2,2,128,448]{3,2,1,0:T(8,128)(2,1)S(1)}, bf16[2,2,128,448]{3,2,1,0:T(8,128)(2,1)}, u32[]{:S(2)}, u32[]{:S(2)}) %collective-permute-start.39) | collective-permute-done | bytes 458784 | tf_op jit(solution)/shard_map/ppermute | solution.py:37
  1084.5 17.1 collective-permute-done.41
  1109.4 16.5 collective-permute-done.42
  1140.5 13.4 convert_reduce_fusion.1
  1178.8 14.4 collective-permute-done.45
  1204.7 13.8 collective-permute-done.46
  1245.6 69.9 %shard_map.265 = (bf16[2,384,512]{2,1,0:T(8,128)(2,1)S(1)}, bf16[2,1024,512]{2,1,0:T(8,128)(2,1)S(1)}, bf16[2,1024,512]{2,1,0:T(8,128)(2,1)S(1)}, bf16[2,256,512...) custom-call(bf16[2,384,512]{2,1,0:T(8,128)(2,1)S(1)} %copy-done.11, bf16[2,1024,512]{2,1,0:T(8,128)(2,1)S(1)} %copy-done.1, ...), custom_call_target="tpu_custom_call" | custom-call | flops 17616076800 | bytes 33554432 | tf_op jit(solution)/shard_map/pallas_call | solution.py:270
  1338.9 43.9 %collective-permute-done.48 = bf16[4,2,2,128,448]{3,4,2,1,0:T(8,128)(2,1)} collective-permute-done((bf16[4,2,2,128,448]{3,4,2,1,0:T(8,128)(2,1)}, bf16[4,2,2,128,448]{3,4,2,1,0:T(8,128)(2,1)}, u32[]{:S(2)}, u32[]{:S(2)}) %collective-permute-start.48) | collective-permute-done | bytes 1835040 | tf_op jit(solution)/shard_map/ppermute | solution.py:37
  1390.8 24.1 %collective-permute-done.49 = bf16[2,2,128,448]{3,2,1,0:T(8,128)(2,1)S(1)} collective-permute-done((bf16[2,2,128,448]{3,2,1,0:T(8,128)(2,1)S(1)}, bf16[2,2,128,448]{3,2,1,0:T(8,128)(2,1)S(1)}, u32[]{:S(2)}, u32[]{:S(2)}) %collective-permute-start.49) | collective-permute-done | bytes 458784 | tf_op jit(solution)/shard_map/ppermute | solution.py:37
  1417.5 24.9 %collective-permute-done.51 = bf16[2,2,128,448]{3,2,1,0:T(8,128)(2,1)S(1)} collective-permute-done((bf16[2,2,128,448]{3,2,1,0:T(8,128)(2,1)S(1)}, bf16[2,2,128,448]{3,2,1,0:T(8,128)(2,1)S(1)}, u32[]{:S(2)}, u32[]{:S(2)}) %collective-permute-start.51) | collective-permute-done | bytes 458784 | tf_op jit(solution)/shard_map/ppermute | solution.py:37
  1511.6 11.2 collective-permute-done.53
  1526.3 10.2 collective-permute-done.29
  1547.8 11.0 convolution_convert_fusion
  1559.5 11.1 convolution_convert_fusion.1
  1580.7 9.8 convolution_convert_fusion.3
  1592.3 9.9 all-gather.5
  1624.7 12.0 all-reduce.26.cloned.1.call-done
  1640.5 12.0 all-reduce.23
  1672.1 119.3 %reduce-scatter.37.cloned.1.call-done = bf16[200,1600]{1,0:T(8,128)(2,1)} async-done(((bf16[1600,1600]{1,0:T(8,128)(2,1)}), bf16[200,1600]{1,0:T(8,128)(2,1)}) %reduce-scatter.37.cloned.1.call-update) | async-done | bytes 640016
  1791.3 126.5 %reduce-scatter.35.cloned.1.call-done = bf16[200,1600]{1,0:T(8,128)(2,1)} async-done(((bf16[1600,1600]{1,0:T(8,128)(2,1)}), bf16[200,1600]{1,0:T(8,128)(2,1)}) %reduce-scatter.35.cloned.1.call-update) | async-done | bytes 640016
  1920.8 124.4 %reduce-scatter.33.cloned.1.call-done = bf16[200,1600]{1,0:T(8,128)(2,1)} async-done(((bf16[1600,1600]{1,0:T(8,128)(2,1)}), bf16[200,1600]{1,0:T(8,128)(2,1)}) %reduce-scatter.33.cloned.1.call-update) | async-done | bytes 640016
  2045.2 126.5 %reduce-scatter.31.cloned.1.call-done = bf16[200,1600]{1,0:T(8,128)(2,1)} async-done(((bf16[1600,1600]{1,0:T(8,128)(2,1)}), bf16[200,1600]{1,0:T(8,128)(2,1)}) %reduce-scatter.31.cloned.1.call-update) | async-done | bytes 640016
  2174.7 24.2 %all-gather.27.cloned.1.call-done = bf16[4,200,3,448]{3,1,2,0:T(8,128)(2,1)} async-done(((bf16[1,200,3,448]{3,1,2,0:T(8,128)(2,1)}), bf16[4,200,3,448]{3,1,2,0:T(8,128)(2,1)}) %all-gather.27.cloned.1.call-update) | async-done | bytes 2150416 | tf_op jit(solution)/shard_map/all_gather | solution.py:405
  (1001 shorter events, 702.8 us)
Async XLA Ops:
  7.2 157.2 %all-gather.35.cloned.1.call-start = ((), (), s32[]{:S(2)}) async-start(), calls=%async_computation.20 | async-start | bytes 1843200 | tf_op jit(solution)/shard_map/all_gather | solution.py:439
  10.3 160.8 %all-gather.19.cloned.1.call-start = ((), (), s32[]{:S(2)}) async-start(), calls=%async_computation.10 | async-start | bytes 5068800 | tf_op jit(solution)/shard_map/all_gather | solution.py:439
  15.5 408.8 %all-gather.37.cloned.1.call-start = ((), (), s32[]{:S(2)}) async-start(), calls=%async_computation.21 | async-start | bytes 5990400 | tf_op jit(solution)/shard_map/all_gather | solution.py:439
  16.8 417.7 %all-gather.21.cloned.1.call-start = ((), (), s32[]{:S(2)}) async-start(), calls=%async_computation.11 | async-start | bytes 5990400 | tf_op jit(solution)/shard_map/all_gather | solution.py:439
  18.1 484.8 %all-gather.39.cloned.1.call-start = ((), (), s32[]{:S(2)}) async-start(), calls=%async_computation.22 | async-start | bytes 1843200 | tf_op jit(solution)/shard_map/all_gather | solution.py:439
  167.5 28.4 %all-to-all-start = ((bf16[4,448,448]{2,1,0:T(8,128)(2,1)}), bf16[4,448,448]{2,1,0:T(8,128)(2,1)S(1)}, u32[]{:S(2)}, u32[]{:S(2)}) async-start(bf16[4,448,448]{2,1,0:T(8,128)(2,1)} %pad_maximum_fusion.10), calls=%async_computation | async-start | bytes 3670016 | tf_op jit(solution)/shard_map/all_to_all | solution.py:454
  171.0 346.7 %all-gather.23.cloned.1.call-start = ((), (), s32[]{:S(2)}) async-start(), calls=%async_computation.12 | async-start | bytes 5068800 | tf_op jit(solution)/shard_map/all_gather | solution.py:439
  190.8 81.1 %collective-permute-start.2 = (bf16[2,2,128,448]{3,2,1,0:T(8,128)(2,1)}, bf16[2,2,128,448]{3,2,1,0:T(8,128)(2,1)}, u32[]{:S(2)}, u32[]{:S(2)}) collective-permute-start(bf16[2,2,128,448]{3,2,1,0:T(8,128)(2,1)} %pad_maximum_fusion.24), channel_id=1, source_target_pairs={{0,4},{4,0},{8,12},{12,8},{16,20},{20,16},{24,28},{28,24},{1,5},{5... | collective-permute-start | bytes 1376264 | tf_op jit(solution)/shard_map/ppermute | solution.py:37
  191.5 45.8 %collective-permute-start.3 = (bf16[2,2,128,448]{3,2,1,0:T(8,128)(2,1)}, bf16[2,2,128,448]{3,2,1,0:T(8,128)(2,1)}, u32[]{:S(2)}, u32[]{:S(2)}) collective-permute-start(bf16[2,2,128,448]{3,2,1,0:T(8,128)(2,1)} %pad_maximum_fusion.24), channel_id=1, source_target_pairs={{0,8},{4,12},{8,0},{12,4},{16,24},{20,28},{24,16},{28,20},{1,9},{5... | collective-permute-start | bytes 1376264 | tf_op jit(solution)/shard_map/ppermute | solution.py:37
  194.1 47.9 %collective-permute-start.5 = (bf16[2,2,128,448]{3,2,1,0:T(8,128)(2,1)}, bf16[2,2,128,448]{3,2,1,0:T(8,128)(2,1)}, u32[]{:S(2)}, u32[]{:S(2)}) collective-permute-start(bf16[2,2,128,448]{3,2,1,0:T(8,128)(2,1)} %pad_maximum_fusion.24), channel_id=1, source_target_pairs={{0,16},{4,20},{8,24},{12,28},{16,0},{20,4},{24,8},{28,12},{1,17},{... | collective-permute-start | bytes 1376264 | tf_op jit(solution)/shard_map/ppermute | solution.py:37
  195.6 75.0 %collective-permute-start.7 = (bf16[2,2,128,448]{3,2,1,0:T(8,128)(2,1)}, bf16[2,2,128,448]{3,2,1,0:T(8,128)(2,1)}, u32[]{:S(2)}, u32[]{:S(2)}) collective-permute-start(bf16[2,2,128,448]{3,2,1,0:T(8,128)(2,1)} %pad_maximum_fusion.24), channel_id=1, source_target_pairs={{0,24},{4,28},{8,16},{12,20},{16,8},{20,12},{24,0},{28,4},{1,25},{... | collective-permute-start | bytes 1376264 | tf_op jit(solution)/shard_map/ppermute | solution.py:37
  237.3 38.2 %collective-permute-start.4 = (bf16[2,2,128,448]{3,2,1,0:T(8,128)(2,1)}, bf16[2,2,128,448]{3,2,1,0:T(8,128)(2,1)S(1)}, u32[]{:S(2)}, u32[]{:S(2)}) collective-permute-start(bf16[2,2,128,448]{3,2,1,0:T(8,128)(2,1)} %collective-permute-done.3), channel_id=1, source_target_pairs={{0,4},{4,0},{8,12},{12,8},{16,20},{20,16},{24,28},{28,24},{1,5},{5... | collective-permute-start | bytes 1376264 | tf_op jit(solution)/shard_map/ppermute | solution.py:37
  241.9 36.4 %collective-permute-start.6 = (bf16[2,2,128,448]{3,2,1,0:T(8,128)(2,1)}, bf16[2,2,128,448]{3,2,1,0:T(8,128)(2,1)S(1)}, u32[]{:S(2)}, u32[]{:S(2)}) collective-permute-start(bf16[2,2,128,448]{3,2,1,0:T(8,128)(2,1)} %collective-permute-done.5), channel_id=1, source_target_pairs={{0,4},{4,0},{8,12},{12,8},{16,20},{20,16},{24,28},{28,24},{1,5},{5... | collective-permute-start | bytes 1376264 | tf_op jit(solution)/shard_map/ppermute | solution.py:37
  373.5 390.2 %all-gather.41.cloned.1.call-start = ((), (), s32[]{:S(2)}) async-start(), calls=%async_computation.23 | async-start | bytes 5990400 | tf_op jit(solution)/shard_map/all_gather | solution.py:439
  506.0 30.7 %all-to-all-start.1 = ((bf16[4,448,448]{2,1,0:T(8,128)(2,1)}), bf16[4,448,448]{2,1,0:T(8,128)(2,1)}, u32[]{:S(2)}, u32[]{:S(2)}) async-start(bf16[4,448,448]{2,1,0:T(8,128)(2,1)} %pad_maximum_fusion.11), calls=%async_computation.1 | async-start | bytes 3670016 | tf_op jit(solution)/shard_map/all_to_all | solution.py:454
  510.4 263.5 %all-gather.25.cloned.1.call-start = ((), (), s32[]{:S(2)}) async-start(), calls=%async_computation.13 | async-start | bytes 5990400 | tf_op jit(solution)/shard_map/all_gather | solution.py:439
  531.6 43.4 %collective-permute-start.18 = (bf16[2,2,128,448]{3,2,1,0:T(8,128)(2,1)}, bf16[2,2,128,448]{3,2,1,0:T(8,128)(2,1)}, u32[]{:S(2)}, u32[]{:S(2)}) collective-permute-start(bf16[2,2,128,448]{3,2,1,0:T(8,128)(2,1)} %pad_maximum_fusion.25), channel_id=1, source_target_pairs={{0,8},{4,12},{8,0},{12,4},{16,24},{20,28},{24,16},{28,20},{1,9},{5... | collective-permute-start | bytes 1376264 | tf_op jit(solution)/shard_map/ppermute | solution.py:37
  531.6 46.0 %collective-permute-start.20 = (bf16[2,2,128,448]{3,2,1,0:T(8,128)(2,1)}, bf16[2,2,128,448]{3,2,1,0:T(8,128)(2,1)}, u32[]{:S(2)}, u32[]{:S(2)}) collective-permute-start(bf16[2,2,128,448]{3,2,1,0:T(8,128)(2,1)} %pad_maximum_fusion.25), channel_id=1, source_target_pairs={{0,16},{4,20},{8,24},{12,28},{16,0},{20,4},{24,8},{28,12},{1,17},{... | collective-permute-start | bytes 1376264 | tf_op jit(solution)/shard_map/ppermute | solution.py:37
  531.6 77.6 %collective-permute-start.22 = (bf16[2,2,128,448]{3,2,1,0:T(8,128)(2,1)}, bf16[2,2,128,448]{3,2,1,0:T(8,128)(2,1)}, u32[]{:S(2)}, u32[]{:S(2)}) collective-permute-start(bf16[2,2,128,448]{3,2,1,0:T(8,128)(2,1)} %pad_maximum_fusion.25), channel_id=1, source_target_pairs={{0,24},{4,28},{8,16},{12,20},{16,8},{20,12},{24,0},{28,4},{1,25},{... | collective-permute-start | bytes 1376264 | tf_op jit(solution)/shard_map/ppermute | solution.py:37
  534.2 75.9 %collective-permute-start.17 = (bf16[2,2,128,448]{3,2,1,0:T(8,128)(2,1)}, bf16[2,2,128,448]{3,2,1,0:T(8,128)(2,1)}, u32[]{:S(2)}, u32[]{:S(2)}) collective-permute-start(bf16[2,2,128,448]{3,2,1,0:T(8,128)(2,1)} %pad_maximum_fusion.25), channel_id=1, source_target_pairs={{0,4},{4,0},{8,12},{12,8},{16,20},{20,16},{24,28},{28,24},{1,5},{5... | collective-permute-start | bytes 1376264 | tf_op jit(solution)/shard_map/ppermute | solution.py:37
  536.3 685.3 %all-gather.33.cloned.1.call-start = ((), (), s32[]{:S(2)}) async-start(), calls=%async_computation.18 | async-start | bytes 3440640 | tf_op jit(solution)/shard_map/all_gather | solution.py:371
  575.0 38.9 %collective-permute-start.19 = (bf16[2,2,128,448]{3,2,1,0:T(8,128)(2,1)}, bf16[2,2,128,448]{3,2,1,0:T(8,128)(2,1)S(1)}, u32[]{:S(2)}, u32[]{:S(2)}) collective-permute-start(bf16[2,2,128,448]{3,2,1,0:T(8,128)(2,1)} %collective-permute-done.18), channel_id=1, source_target_pairs={{0,4},{4,0},{8,12},{12,8},{16,20},{20,16},{24,28},{28,24},{1,5},{5... | collective-permute-start | bytes 1376264 | tf_op jit(solution)/shard_map/ppermute | solution.py:37
  577.6 39.1 %collective-permute-start.21 = (bf16[2,2,128,448]{3,2,1,0:T(8,128)(2,1)}, bf16[2,2,128,448]{3,2,1,0:T(8,128)(2,1)S(1)}, u32[]{:S(2)}, u32[]{:S(2)}) collective-permute-start(bf16[2,2,128,448]{3,2,1,0:T(8,128)(2,1)} %collective-permute-done.20), channel_id=1, source_target_pairs={{0,4},{4,0},{8,12},{12,8},{16,20},{20,16},{24,28},{28,24},{1,5},{5... | collective-permute-start | bytes 1376264 | tf_op jit(solution)/shard_map/ppermute | solution.py:37
  700.6 28.0 %collective-permute-start.30 = (bf16[1,192,1600]{2,1,0:T(8,128)(2,1)S(1)}, bf16[1,192,1600]{2,1,0:T(8,128)(2,1)S(1)}, u32[]{:S(2)}, u32[]{:S(2)}) collective-permute-start(bf16[1,192,1600]{2,1,0:T(8,128)(2,1)S(1)} %bitcast_convert_fusion), channel_id=1, source_target_pairs={{0,2},{1,3},{2,0},{3,1},{4,6},{5,7},{6,4},{7,5},{8,10},{9,11},{10,... | collective-permute-start | bytes 1843208 | tf_op jit(solution)/shard_map/ppermute | solution.py:37
  716.7 25.6 %collective-permute-start.26 = (bf16[1,192,1600]{2,1,0:T(8,128)(2,1)S(1)}, bf16[1,192,1600]{2,1,0:T(8,128)(2,1)S(1)}, u32[]{:S(2)}, u32[]{:S(2)}) collective-permute-start(bf16[1,192,1600]{2,1,0:T(8,128)(2,1)S(1)} %add_convert_fusion.1), channel_id=1, source_target_pairs={{0,2},{1,3},{2,0},{3,1},{4,6},{5,7},{6,4},{7,5},{8,10},{9,11},{10,... | collective-permute-start | bytes 1843208 | tf_op jit(solution)/shard_map/ppermute | solution.py:37
  954.5 42.3 %collective-permute-start.36 = (bf16[4,2,2,128,448]{3,4,2,1,0:T(8,128)(2,1)}, bf16[4,2,2,128,448]{3,4,2,1,0:T(8,128)(2,1)}, u32[]{:S(2)}, u32[]{:S(2)}) collective-permute-start(bf16[4,2,2,128,448]{3,4,2,1,0:T(8,128)(2,1)} %copy.180), channel_id=1, source_target_pairs={{0,4},{4,0},{8,12},{12,8},{16,20},{20,16},{24,28},{28,24},{1,5},{5... | collective-permute-start | bytes 5505032 | tf_op jit(solution)/shard_map/ppermute | solution.py:37
  1004.9 20.5 collective-permute-start.37
  1004.9 23.2 %collective-permute-start.38 = (bf16[2,2,128,448]{3,2,1,0:T(8,128)(2,1)S(1)}, bf16[2,2,128,448]{3,2,1,0:T(8,128)(2,1)S(1)}, u32[]{:S(2)}, u32[]{:S(2)}) collective-permute-start(bf16[2,2,128,448]{3,2,1,0:T(8,128)(2,1)S(1)} %get-tuple-element.145), channel_id=1, source_target_pairs={{0,16},{4,20},{8,24},{12,28},{16,0},{20,4},{24,8},{28,12},{1,17},{... | collective-permute-start | bytes 1376264 | tf_op jit(solution)/shard_map/ppermute | solution.py:37
  1005.5 46.7 %collective-permute-start.39 = (bf16[2,2,128,448]{3,2,1,0:T(8,128)(2,1)S(1)}, bf16[2,2,128,448]{3,2,1,0:T(8,128)(2,1)}, u32[]{:S(2)}, u32[]{:S(2)}) collective-permute-start(bf16[2,2,128,448]{3,2,1,0:T(8,128)(2,1)S(1)} %get-tuple-element.144), channel_id=1, source_target_pairs={{0,24},{4,28},{8,16},{12,20},{16,8},{20,12},{24,0},{28,4},{1,25},{... | collective-permute-start | bytes 1376264 | tf_op jit(solution)/shard_map/ppermute | solution.py:37
  1008.6 324.2 %all-gather.31.cloned.1.call-start = ((), (), s32[]{:S(2)}) async-start(), calls=%async_computation.16 | async-start | bytes 3440640 | tf_op jit(solution)/shard_map/all_gather | solution.py:371
  1081.9 19.7 collective-permute-start.41
  1084.4 458.8 %reduce-scatter.29.cloned.1.call-start = ((), (), s32[]{:S(2)}) async-start(), calls=%async_computation.25 | async-start | bytes 5068800
  1107.4 18.4 collective-permute-start.42
  1134.3 458.1 %reduce-scatter.25.cloned.1.call-start = ((), (), s32[]{:S(2)}) async-start(), calls=%async_computation.19 | async-start | bytes 1843200 | tf_op jit(solution)/shard_map/reduce_scatter | solution.py:341
  1227.7 375.4 %reduce-scatter.23.cloned.1.call-start = ((), (), s32[]{:S(2)}) async-start(), calls=%async_computation.17 | async-start | bytes 1843200 | tf_op jit(solution)/shard_map/reduce_scatter | solution.py:341
  1332.0 50.8 %collective-permute-start.48 = (bf16[4,2,2,128,448]{3,4,2,1,0:T(8,128)(2,1)}, bf16[4,2,2,128,448]{3,4,2,1,0:T(8,128)(2,1)}, u32[]{:S(2)}, u32[]{:S(2)}) collective-permute-start(bf16[4,2,2,128,448]{3,4,2,1,0:T(8,128)(2,1)} %copy.187), channel_id=1, source_target_pairs={{0,4},{4,0},{8,12},{12,8},{16,20},{20,16},{24,28},{28,24},{1,5},{5... | collective-permute-start | bytes 5505032 | tf_op jit(solution)/shard_map/ppermute | solution.py:37
  1338.9 274.8 %reduce-scatter.27.cloned.1.call-start = ((), (), s32[]{:S(2)}) async-start(), calls=%async_computation.24 | async-start | bytes 5068800
  1388.1 26.8 %collective-permute-start.49 = (bf16[2,2,128,448]{3,2,1,0:T(8,128)(2,1)S(1)}, bf16[2,2,128,448]{3,2,1,0:T(8,128)(2,1)S(1)}, u32[]{:S(2)}, u32[]{:S(2)}) collective-permute-start(bf16[2,2,128,448]{3,2,1,0:T(8,128)(2,1)S(1)} %get-tuple-element.140), channel_id=1, source_target_pairs={{0,8},{4,12},{8,0},{12,4},{16,24},{20,28},{24,16},{28,20},{1,9},{5... | collective-permute-start | bytes 1376264 | tf_op jit(solution)/shard_map/ppermute | solution.py:37
  1388.2 29.3 %collective-permute-start.50 = (bf16[2,2,128,448]{3,2,1,0:T(8,128)(2,1)S(1)}, bf16[2,2,128,448]{3,2,1,0:T(8,128)(2,1)S(1)}, u32[]{:S(2)}, u32[]{:S(2)}) collective-permute-start(bf16[2,2,128,448]{3,2,1,0:T(8,128)(2,1)S(1)} %get-tuple-element.142), channel_id=1, source_target_pairs={{0,16},{4,20},{8,24},{12,28},{16,0},{20,4},{24,8},{28,12},{1,17},{... | collective-permute-start | bytes 1376264 | tf_op jit(solution)/shard_map/ppermute | solution.py:37
  1388.8 53.6 %collective-permute-start.51 = (bf16[2,2,128,448]{3,2,1,0:T(8,128)(2,1)S(1)}, bf16[2,2,128,448]{3,2,1,0:T(8,128)(2,1)S(1)}, u32[]{:S(2)}, u32[]{:S(2)}) collective-permute-start(bf16[2,2,128,448]{3,2,1,0:T(8,128)(2,1)S(1)} %get-tuple-element.141), channel_id=1, source_target_pairs={{0,24},{4,28},{8,16},{12,20},{16,8},{20,12},{24,0},{28,4},{1,25},{... | collective-permute-start | bytes 1376264 | tf_op jit(solution)/shard_map/ppermute | solution.py:37
  1455.9 180.9 %all-reduce.26.cloned.1.call-start = ((), (), s32[]{:S(2)}) async-start(), calls=%async_computation.30 | async-start | bytes 245760
  1511.0 25.5 %collective-permute-start.29 = (bf16[1,192,1600]{2,1,0:T(8,128)(2,1)}, bf16[1,192,1600]{2,1,0:T(8,128)(2,1)}, u32[]{:S(2)}, u32[]{:S(2)}) collective-permute-start(bf16[1,192,1600]{2,1,0:T(8,128)(2,1)} %slice.1190), channel_id=1, source_target_pairs={{0,2},{1,3},{2,0},{3,1},{4,6},{5,7},{6,4},{7,5},{8,10},{9,11},{10,... | collective-permute-start | bytes 1843208 | tf_op jit(solution)/shard_map/ppermute | solution.py:37
  1543.1 122.3 %all-gather.29.cloned.1.call-start = ((), (), s32[]{:S(2)}) async-start(), calls=%async_computation.15 | async-start | bytes 3072000 | tf_op jit(solution)/shard_map/all_gather | solution.py:405
  1547.6 243.7 %reduce-scatter.37.cloned.1.call-start = ((), (), s32[]{:S(2)}) async-start(), calls=%async_computation.29 | async-start | bytes 5990400
  1558.9 359.0 %reduce-scatter.35.cloned.1.call-start = ((), (), s32[]{:S(2)}) async-start(), calls=%async_computation.28 | async-start | bytes 5990400
  1570.6 474.6 %reduce-scatter.33.cloned.1.call-start = ((), (), s32[]{:S(2)}) async-start(), calls=%async_computation.27 | async-start | bytes 5990400
  1580.6 591.1 %reduce-scatter.31.cloned.1.call-start = ((), (), s32[]{:S(2)}) async-start(), calls=%async_computation.26 | async-start | bytes 5990400
  1590.4 608.5 %all-gather.27.cloned.1.call-start = ((), (), s32[]{:S(2)}) async-start(), calls=%async_computation.14 | async-start | bytes 3072000 | tf_op jit(solution)/shard_map/all_gather | solution.py:405
  (262 other events, 7192.5 us)
Sparse Core Ops, SparseCore 0:
  10.4 50.9 all-gather.34
  64.2 75.6 all-gather.18
  142.1 122.0 all-gather.36
  266.3 88.6 all-gather.20
  357.0 44.6 all-gather.38
  403.8 74.4 all-gather.22
  480.5 122.3 all-gather.40
  605.2 88.2 all-gather.24
  1008.8 27.3 all-gather.32
  1084.5 31.7 all-gather.30
  1134.4 107.9 reduce-scatter.28
  1245.7 64.4 reduce-scatter.24
  1339.0 75.6 reduce-scatter.22
  1456.0 108.3 reduce-scatter.26
  1567.9 68.8 all-reduce.25
  1638.8 26.5 all-gather.28
  1669.2 122.0 reduce-scatter.36
  1794.6 123.1 reduce-scatter.34
  1922.3 122.8 reduce-scatter.32
  2048.5 123.1 reduce-scatter.30
  2173.4 25.5 all-gather.26

commit v2 on v1

--- a/solution.py
+++ b/solution.py
@@ -306,6 +306,405 @@
     return jnp.pad(value, [(0, 0)] * (value.ndim - 1) + [(0, WIDE - value.shape[-1])])
 
 
+MESH = pl.DeviceIdType.MESH
+ANY = pl.BlockSpec(memory_space=pl.ANY)
+IN_VMEM = pl.BlockSpec(memory_space=pltpu.VMEM)
+TILE = 512
+ROW_CHUNK = 32
+
+
+class Peers:
+    def __init__(self):
+        self.f = lax.axis_index("fsdp")
+        self.t = lax.axis_index("tp")
+        x, c = self.t // 2, self.t % 2
+        self.x = x
+        self.core = 2 * x + 1 - c
+        self.over = 2 * (1 - x) + c
+        self.diag = 2 * (1 - x) + 1 - c
+
+    def greet(self):
+        barrier = pltpu.get_barrier_semaphore()
+        for t in (self.core, self.over):
+            pl.semaphore_signal(barrier, inc=1, device_id=(self.f, t), device_id_type=MESH)
+        pl.semaphore_wait(barrier, 2)
+
+    def copy(self, source, target, sems, index, t):
+        return pltpu.make_async_remote_copy(
+            src_ref=source,
+            dst_ref=target,
+            send_sem=sems[0].at[index],
+            recv_sem=sems[1].at[index],
+            device_id=(self.f, t),
+            device_id_type=MESH,
+        )
+
+
+class Gather:
+    def __init__(self, peers, buf, sems):
+        self.p, self.buf, self.sems = peers, buf, sems
+
+    def piece(self, slot, index, t):
+        return self.p.copy(self.buf.at[slot], self.buf.at[slot], self.sems, index, t)
+
+    def start(self):
+        p = self.p
+        self.piece(p.t, 1, p.over).start()
+        self.piece(p.t, 0, p.core).start()
+
+    def wait_chip(self):
+        self.piece(self.p.core, 0, self.p.core).wait_recv()
+
+    def relay(self):
+        p = self.p
+        self.piece(p.over, 1, p.over).wait_recv()
+        self.piece(p.over, 2, p.core).start()
+
+    def wait_diag(self):
+        self.piece(self.p.diag, 2, self.p.core).wait_recv()
+
+    def finish(self):
+        p = self.p
+        self.piece(p.t, 1, p.over).wait_send()
+        self.piece(p.t, 0, p.core).wait_send()
+        self.piece(p.over, 2, p.core).wait_send()
+
+
+class Scatter:
+    def __init__(self, peers, part, from_core, over_out, from_over, sems):
+        self.p, self.part, self.sems = peers, part, sems
+        self.from_core, self.over_out, self.from_over = from_core, over_out, from_over
+
+    def far_to_core(self):
+        return self.p.copy(self.part.at[self.p.diag], self.from_core.at[0], self.sems, 3, self.p.core)
+
+    def near_to_core(self):
+        return self.p.copy(self.part.at[self.p.core], self.from_core.at[1], self.sems, 4, self.p.core)
+
+    def to_over(self):
+        return self.p.copy(self.over_out, self.from_over, self.sems, 5, self.p.over)
+
+    def send_over(self):
+        self.far_to_core().wait_recv()
+
+        @pl.loop(0, self.over_out.shape[0] // ROW_CHUNK)
+        def _(i):
+            at = pl.ds(pl.multiple_of(i * ROW_CHUNK, ROW_CHUNK), ROW_CHUNK)
+            total = self.part[self.p.over, at, :].astype(f32) + self.from_core[0, at, :].astype(f32)
+            self.over_out[at, :] = total.astype(bf16)
+
+        self.to_over().start()
+
+    def wait(self):
+        self.near_to_core().wait_recv()
+        self.to_over().wait_recv()
+
+    def rows(self, at):
+        return (
+            self.part[self.p.t, at, :].astype(f32)
+            + self.from_core[1, at, :].astype(f32)
+            + self.from_over[at, :].astype(f32)
+        )
+
+    def finish(self):
+        for copy in (self.far_to_core(), self.near_to_core(), self.to_over()):
+            copy.wait_send()
+
+
+def row_chunks(rows, body):
+    @pl.loop(0, rows // ROW_CHUNK)
+    def _(i):
+        body(pl.ds(pl.multiple_of(i * ROW_CHUNK, ROW_CHUNK), ROW_CHUNK))
+
+
+def tiles(extent, body):
+    whole = extent // TILE
+
+    @pl.loop(0, whole)
+    def _(i):
+        body(pl.ds(pl.multiple_of(i * TILE, TILE), TILE))
+
+    if extent % TILE:
+        body(pl.ds(whole * TILE, extent % TILE))
+
+
+def pair_rows(ref, x):
+    both = ref[pl.ds(2 * x, 2)]
+    return both.reshape(2 * both.shape[1], both.shape[2])
+
+
+def put_pair(ref, x, at, value):
+    ref[pl.ds(2 * x, 2), :, at] = value.reshape(2, value.shape[0] // 2, value.shape[1]).astype(ref.dtype)
+
+
+def norm_stats(x):
+    centred = x - jnp.mean(x, -1, keepdims=True)
+    scale = lax.rsqrt(jnp.mean(centred * centred, -1, keepdims=True) + norm_eps)
+    return centred * scale, scale
+
+
+def ff_fwd_kernel(
+    x_ref, vec_ref, fcb_ref, wfc_hbm, wproj_hbm,
+    out_ref, all_hbm, pre_hbm, hid_hbm,
+    wfc, wproj, buf, pre, hid, part, from_core, over_out, from_over, send, recv, local,
+):
+    p = Peers()
+    rows = x_ref.shape[0]
+    sems = (send, recv)
+    gather = Gather(p, buf, sems)
+    scatter = Scatter(p, part, from_core, over_out, from_over, sems)
+    load_fc = pltpu.make_async_copy(wfc_hbm, wfc, local.at[0])
+    load_proj = pltpu.make_async_copy(wproj_hbm, wproj, local.at[1])
+    load_fc.start()
+    load_proj.start()
+
+    def norm(at):
+        hat, _ = norm_stats(x_ref[at, :])
+        buf[p.t, at, :] = (hat * vec_ref[5:6, :] + vec_ref[6:7, :]).astype(bf16)
+
+    row_chunks(rows, norm)
+    p.greet()
+    gather.start()
+    gather.wait_chip()
+    load_fc.wait()
+
+    def up(x):
+        def tile(at):
+            value = mm(pair_rows(buf, x), wfc[:, at]) + fcb_ref[:, at]
+            put_pair(pre, x, at, value)
+            put_pair(hid, x, at, gelu_tanh(value))
+
+        tiles(wfc.shape[1], tile)
+
+    def down(x):
+        def tile(at):
+            put_pair(part, x, at, mm(pair_rows(hid, x), wproj[at, :], NT))
+
+        tiles(wproj.shape[0], tile)
+
+    up(p.x)
+    gather.relay()
+    gather.wait_diag()
+    keep_all = pltpu.make_async_copy(buf, all_hbm, local.at[2])
+    keep_all.start()
+    up(1 - p.x)
+    keep_pre = pltpu.make_async_copy(pre, pre_hbm, local.at[3])
+    keep_hid = pltpu.make_async_copy(hid, hid_hbm, local.at[4])
+    keep_pre.start()
+    keep_hid.start()
+    load_proj.wait()
+    down(1 - p.x)
+    scatter.far_to_core().start()
+    scatter.send_over()
+    down(p.x)
+    scatter.near_to_core().start()
+    scatter.wait()
+
+    def final(at):
+        out_ref[at, :] = x_ref[at, :] + scatter.rows(at) + vec_ref[7:8, :]
+
+    row_chunks(rows, final)
+    gather.finish()
+    scatter.finish()
+    for copy in (keep_all, keep_pre, keep_hid):
+        copy.wait()
+
+
+def scatter_scratch(n_tp, rows):
+    return [
+        pltpu.VMEM((n_tp, rows, D), bf16),
+        pltpu.VMEM((2, rows, D), bf16),
+        pltpu.VMEM((rows, D), bf16),
+        pltpu.VMEM((rows, D), bf16),
+        pltpu.SemaphoreType.DMA((6,)),
+        pltpu.SemaphoreType.DMA((6,)),
+    ]
+
+
+def params(collective_id):
+    return pltpu.CompilerParams(collective_id=collective_id, has_side_effects=True, vmem_limit_bytes=60 * 2**20)
+
+
+def ff_fwd(x, vecs, fc_bias, w_fc, w_proj, n_tp):
+    rows, width = x.shape[0], w_fc.shape[1]
+    block = (n_tp, rows)
+    return pl.pallas_call(
+        ff_fwd_kernel,
+        out_shape=(
+            jax.ShapeDtypeStruct((rows, D), f32),
+            jax.ShapeDtypeStruct(block + (D,), bf16),
+            jax.ShapeDtypeStruct(block + (width,), f32),
+            jax.ShapeDtypeStruct(block + (width,), bf16),
+        ),
+        in_specs=[IN_VMEM, IN_VMEM, IN_VMEM, ANY, ANY],
+        out_specs=(IN_VMEM, ANY, ANY, ANY),
+        scratch_shapes=[
+            pltpu.VMEM((D, width), bf16),
+            pltpu.VMEM((D, width), bf16),
+            pltpu.VMEM(block + (D,), bf16),
+            pltpu.VMEM(block + (width,), f32),
+            pltpu.VMEM(block + (width,), bf16),
+        ]
+        + scatter_scratch(n_tp, rows)
+        + [pltpu.SemaphoreType.DMA((5,))],
+        compiler_params=params(1),
+        cost_estimate=pl.CostEstimate(
+            flops=4 * n_tp * rows * D * width, bytes_accessed=40 * 2**20, transcendentals=n_tp * rows * width
+        ),
+    )(x, vecs, fc_bias, w_fc, w_proj)
+
+
+def gelu_slope(u):
+    a = 0.7978845608028654
+    square = u * u
+    t = jnp.tanh(a * (u + 0.044715 * u * square))
+    return 0.5 * (1.0 + t) + 0.5 * u * (1.0 - t * t) * (a * (1.0 + 3 * 0.044715 * square))
+
+
+def norm_back(x, dy, gain):
+    hat, scale = norm_stats(x)
+    d_hat = dy * gain
+    inner = d_hat - jnp.mean(d_hat, -1, keepdims=True) - hat * jnp.mean(d_hat * hat, -1, keepdims=True)
+    return scale * inner, dy * hat
+
+
+def add_rows(ref, row, value):
+    ref[row : row + 1, :] += jnp.sum(value, axis=0, keepdims=True)
+
+
+def ff_bwd_kernel(
+    g_ref, x_ref, vec_ref, all_hbm, pre_hbm, hid_hbm, wfc_hbm, wproj_hbm,
+    out_ref, sums_ref, fcb_ref, dfc_hbm, dproj_hbm,
+    wfc, wproj, buf, other, pre, dpre, stage, part, from_core, over_out, from_over, send, recv, local,
+):
+    p = Peers()
+    rows = x_ref.shape[0]
+    n_tp, width = buf.shape[0], wfc.shape[1]
+    sems = (send, recv)
+    gather = Gather(p, buf, sems)
+    scatter = Scatter(p, part, from_core, over_out, from_over, sems)
+    load_proj = pltpu.make_async_copy(wproj_hbm, wproj, local.at[0])
+    load_pre = pltpu.make_async_copy(pre_hbm, pre, local.at[1])
+    load_fc = pltpu.make_async_copy(wfc_hbm, wfc, local.at[2])
+    load_other = pltpu.make_async_copy(hid_hbm, other, local.at[3])
+    for copy in (load_proj, load_pre, load_fc, load_other):
+        copy.start()
+    sums_ref[...] = jnp.zeros_like(sums_ref)
+    fcb_ref[...] = jnp.zeros_like(fcb_ref)
+
+    def lower(at):
+        low = g_ref[at, :].astype(bf16)
+        buf[p.t, at, :] = low
+        add_rows(sums_ref, 7, low.astype(f32))
+
+    row_chunks(rows, lower)
+    p.greet()
+    gather.start()
+    gather.wait_chip()
+    load_proj.wait()
+    load_pre.wait()
+
+    def through(x):
+        def tile(at):
+            d_hidden = mm(pair_rows(buf, x), wproj[:, at])
+            u = pre[pl.ds(2 * x, 2), :, at].reshape(2 * rows, -1)
+            low = (gelu_slope(u) * d_hidden).astype(bf16)
+            put_pair(dpre, x, at, low)
+            fcb_ref[:, at] += jnp.sum(low.astype(f32), axis=0, keepdims=True)
+
+        tiles(width, tile)
+
+    def down(x):
+        def tile(at):
+            put_pair(part, x, at, mm(pair_rows(dpre, x), wfc[at, :], NT))
+
+        tiles(D, tile)
+
+    through(p.x)
+    gather.relay()
+    gather.wait_diag()
+    through(1 - p.x)
+    load_fc.wait()
+    down(1 - p.x)
+    scatter.far_to_core().start()
+    scatter.send_over()
+    down(p.x)
+    scatter.near_to_core().start()
+
+    def outer(left, right, target, sem):
+        whole = D // TILE
+        rest = D - whole * TILE
+        flat = right[...].reshape(n_tp * rows, width)
+
+        def tile(i, size):
+            at = pl.ds(pl.multiple_of(i * TILE, TILE), size)
+            value = mm(left[:, :, at].reshape(n_tp * rows, size), flat, TN)
+            stage[at, :] = value.astype(bf16)
+
+        @pl.loop(0, whole)
+        def _(i):
+            tile(i, TILE)
+
+        if rest:
+            tile(whole, rest)
+        return pltpu.make_async_copy(stage, target, sem)
+
+    load_other.wait()
+    store = outer(buf, other, dproj_hbm, local.at[4])
+    store.start()
+    gather.finish()
+    load_all = pltpu.make_async_copy(all_hbm, buf, local.at[5])
+    load_all.start()
+    scatter.wait()
+
+    def final(at):
+        dy = scatter.rows(at)
+        dx, d_gain = norm_back(x_ref[at, :], dy, vec_ref[5:6, :])
+        add_rows(sums_ref, 5, d_gain)
+        add_rows(sums_ref, 6, dy)
+        out_ref[at, :] = g_ref[at, :] + dx
+
+    row_chunks(rows, final)
+    load_all.wait()
+    store.wait()
+    store = outer(buf, dpre, dfc_hbm, local.at[6])
+    store.start()
+    scatter.finish()
+    store.wait()
+
+
+def ff_bwd(grad, x, vecs, all_rows, pre, hidden, w_fc, w_proj, n_tp):
+    rows, width = x.shape[0], w_fc.shape[1]
+    block = (n_tp, rows)
+    return pl.pallas_call(
+        ff_bwd_kernel,
+        out_shape=(
+            jax.ShapeDtypeStruct((rows, D), f32),
+            jax.ShapeDtypeStruct((8, D), f32),
+            jax.ShapeDtypeStruct((1, width), f32),
+            jax.ShapeDtypeStruct((D, width), bf16),
+            jax.ShapeDtypeStruct((D, width), bf16),
+        ),
+        in_specs=[IN_VMEM, IN_VMEM, IN_VMEM, ANY, ANY, ANY, ANY, ANY],
+        out_specs=(IN_VMEM, IN_VMEM, IN_VMEM, ANY, ANY),
+        scratch_shapes=[
+            pltpu.VMEM((D, width), bf16),
+            pltpu.VMEM((D, width), bf16),
+            pltpu.VMEM(block + (D,), bf16),
+            pltpu.VMEM(block + (width,), bf16),
+            pltpu.VMEM(block + (width,), f32),
+            pltpu.VMEM(block + (width,), bf16),
+            pltpu.VMEM((D, width), bf16),
+        ]
+        + scatter_scratch(n_tp, rows)
+        + [pltpu.SemaphoreType.DMA((7,))],
+        compiler_params=params(2),
+        cost_estimate=pl.CostEstimate(
+            flops=8 * n_tp * rows * D * width, bytes_accessed=50 * 2**20, transcendentals=n_tp * rows * width
+        ),
+    )(grad, x, vecs, all_rows, pre, hidden, w_fc, w_proj)
+
+
 def forward_layer(x, weights, vecs, fc_bias, member, cols, n_tp):
     w_qkv, w_out, w_fc, w_proj = weights
     rows = x.shape[0]
@@ -327,12 +726,7 @@
     mixed = by_device(mixed[:, :, :width], n_tp)
     part = mm(mixed, w_out).astype(bf16)
     x_mid = x + (tp_scatter(part.reshape(n_tp, rows, D)) + vecs[4])
-    second = layer_norm(x_mid, vecs[5], vecs[6]).astype(bf16)
-    second_all = tp_gather(second).reshape(-1, D)
-    hidden_pre = mm(second_all, w_fc) + fc_bias
-    hidden = gelu_tanh(hidden_pre).astype(bf16)
-    part = mm(hidden, w_proj, NT).astype(bf16)
-    x_next = x_mid + tp_scatter(part.reshape(n_tp, rows, D)) + vecs[7]
+    x_next, second_all, hidden_pre, hidden = ff_fwd(x_mid, vecs, fc_bias[None], w_fc, w_proj, n_tp)
     saved = (x, normed_all, query, keys_p, values_p, key, value, lse, mixed, x_mid, second_all, hidden_pre, hidden)
     return x_next, saved
 
@@ -351,20 +745,10 @@
     x, normed_all, query, keys_p, values_p, key, value, lse, mixed, x_mid, second_all, hidden_pre, hidden = saved
     rows = x.shape[0]
     width = w_out.shape[0]
-    grad_branch = grad_x.astype(bf16)
-    grad_proj_bias = jnp.sum(grad_branch.astype(f32), 0)
-    branch_all = tp_gather(grad_branch).reshape(-1, D)
-    proj_sum = fsdp_sum(mm(branch_all, hidden, TN))
-    grad_hidden = mm(branch_all, w_proj)
-    _, gelu_back = jax.vjp(gelu_tanh, hidden_pre)
-    grad_pre = gelu_back(grad_hidden)[0].astype(bf16)
-    fc_sum = fsdp_sum(mm(second_all, grad_pre, TN))
-    grad_fc_bias = jnp.sum(grad_pre.astype(f32), 0)
-    part = mm(grad_pre, w_fc, NT).astype(bf16)
-    grad_second = tp_scatter(part.reshape(n_tp, rows, D))
-    _, norm_back = jax.vjp(layer_norm, x_mid, vecs[5], vecs[6])
-    grad_from_norm, grad_gain_two, grad_bias_two = norm_back(grad_second)
-    grad_mid = grad_x + grad_from_norm
+    grad_mid, ff_sums, grad_fc_bias, grad_fc, grad_proj = ff_bwd(
+        grad_x, x_mid, vecs, second_all, hidden_pre, hidden, w_fc, w_proj, n_tp
+    )
+    proj_sum, fc_sum = fsdp_sum(grad_proj), fsdp_sum(grad_fc)
     grad_attn = grad_mid.astype(bf16)
     grad_out_bias = jnp.sum(grad_attn.astype(f32), 0)
     attn_all = tp_gather(grad_attn).reshape(-1, D)
@@ -395,13 +779,13 @@
             placed(column_sums[:width]),
             placed(column_sums[2 * width :]),
             grad_out_bias,
-            grad_gain_two,
-            grad_bias_two,
-            grad_proj_bias,
+            ff_sums[5],
+            ff_sums[6],
+            ff_sums[7],
         ]
     )
     vector_sum = lax.psum(lax.psum_scatter(vector_grads, "fsdp", scatter_dimension=1, tiled=True), "tp")
-    fc_bias_sum = lax.psum_scatter(grad_fc_bias, "fsdp", scatter_dimension=0, tiled=True)
+    fc_bias_sum = lax.psum_scatter(grad_fc_bias[0], "fsdp", scatter_dimension=0, tiled=True)
     qkv_all = lax.all_gather(qkv_sum.astype(bf16).reshape(-1, 3, width), "tp")
     out_all = lax.all_gather(out_sum.astype(bf16), "tp")
     qkv_grad = heads_joined(qkv_all, n_tp).reshape(-1, 3 * D).astype(f32)

time: 2230 us -> 2230 us (level)
  Pallas kernels: 232 us -> 419 us
  waiting for transfers between devices: 1100 us -> 1250 us
  local copies, waits for them, and re-layouts: 383 us -> 235 us
  matrix products: 186 us -> 60.1 us
  other arithmetic: 161 us -> 116 us
    pallas_call x0 -> x4, Pallas kernels: none -> 197 us  [the longest x2 108 us: ff_bwd(): pl.pallas_call(ff_bwd_kernel, out_shape=(jax.ShapeDtypeStruct((rows, D),...]
    dot_general x24 -> x12, matrix products: 186 us -> 60.1 us  [mm(): return lax.dot_general(left, right, dims, preferred_element_type=f32)]
    ppermute x54 -> x38, waiting for transfers between devices: 554 us -> 432 us  [swapped(): return lax.ppermute(value, axis, pairs)]
    all_gather x8, waiting for transfers between devices: 0.07 us -> 118 us  [gathered(): return lax.all_gather(part, 'fsdp', axis=0, tiled=True)]
    unnamed x28, waiting for transfers between devices: 509 us -> 596 us
    slice x1 -> x3, local copies, waits for them, and re-layouts: 82.7 us -> 0.67 us  [the longest x1 0.65 us: forward_layer(): x_mid = x + (tp_scatter(part.reshape(n_tp, rows, D)) + vecs[4])]
    reduce_scatter x2, waiting for transfers between devices: 0.02 us -> 65.7 us  [fsdp_sum(): lax.psum_scatter(part.astype(bf16), 'fsdp', scatter_dimension=0, tiled=True)]
    gather x20 -> x12, local copies, waits for them, and re-layouts: 71.1 us -> 46.5 us  [by_offset(): return jnp.take(stacked, index ^ jnp.arange(stacked.shape[0]), axis=0)]
  transfers between devices with their start and end apart: 77 -> 61, of which waited for: 46 -> 41; matrix products, arithmetic and copies ran while one was open for 27% -> 16% of each run, Pallas kernels for 7% -> 14%
where the time goes in v2:
time: 2230 us; the launch traced here: 2220 us
  waiting for transfers between devices  1250 us (56%)
  Pallas kernels  419 us (19%)
  local copies, waits for them, and re-layouts  235 us (11%)
  other arithmetic  116 us (5%)
  starting transfers between devices  69.4 us (3%)
  matrix products  60.1 us (3%)
  blocking collectives  58.6 us (3%)
    unnamed x28, waiting for transfers between devices  596 us
    ppermute x38, waiting for transfers between devices, swapped(): return lax.ppermute(value, axis, pairs)  432 us
    pallas_call x2, Pallas kernels, attn_bwd(): pl.pallas_call(attn_bwd_kernel, grid=(MICRO, HEAD_PAIRS), out_shape=(jax....  140 us
    all_gather x8, waiting for transfers between devices, gathered(): return lax.all_gather(part, 'fsdp', axis=0, tiled=True)  118 us
    pallas_call x2, Pallas kernels, ff_bwd(): pl.pallas_call(ff_bwd_kernel, out_shape=(jax.ShapeDtypeStruct((rows, D),...  108 us
    pallas_call x2, Pallas kernels, ff_fwd(): pl.pallas_call(ff_fwd_kernel, out_shape=(jax.ShapeDtypeStruct((rows, D),...  89.3 us
    pallas_call x2, Pallas kernels, attn_fwd(): pl.pallas_call(attn_fwd_kernel, grid=(MICRO, HEAD_PAIRS), out_shape=(jax....  81.8 us
    reduce_scatter x2, waiting for transfers between devices, fsdp_sum(): lax.psum_scatter(part.astype(bf16), 'fsdp', scatter_dimension=0, tiled=True)  65.7 us
  transfers between devices with their start and end apart: 61, of which 41 were waited for; matrix products, arithmetic and copies ran while one was open for 16% of the time, Pallas kernels for 14%

profile of v2, /device:TPU:9, one launch (start us, length us, event | category | flops | bytes accessed | tf_op | source)
XLA Modules:
  0.0 2219.5 jit_solution(8893909436743534221)
XLA Ops:
  22.6 26.6 %all_gather.51 = bf16[9,2,1600]{0,1,2:T(2,128)(2,1)S(1)} all-gather(bf16[9,2,200]{0,1,2:T(2,128)(2,1)S(1)} %copy.83), channel_id=1, replica_groups=mesh['fsdp'=8,'tp'=4] {'fsdp'}, dimensions={2}, use_global_device_ids=true | all-gather | bytes 64800 | tf_op jit(solution)/shard_map/all_gather | solution.py:828
  54.2 8.7 collective-permute-done
  63.0 6.9 collective-permute-start.1
  89.8 51.3 %all-gather.19.cloned.1.call-done = bf16[1600,1344]{1,0:T(8,128)(2,1)} async-done(((bf16[200,1344]{1,0:T(8,128)(2,1)}), bf16[1600,1344]{1,0:T(8,128)(2,1)}) %all-gather.19.cloned.1.call-update) | async-done | bytes 4300816 | tf_op jit(solution)/shard_map/all_gather | solution.py:823
  141.1 7.4 fusion.72
  174.6 21.9 collective-permute-done.3
  200.3 43.8 %collective-permute-done.7 = bf16[2,2,128,448]{3,2,1,0:T(8,128)(2,1)} collective-permute-done((bf16[2,2,128,448]{3,2,1,0:T(8,128)(2,1)}, bf16[2,2,128,448]{3,2,1,0:T(8,128)(2,1)}, u32[]{:S(2)}, u32[]{:S(2)}) %collective-permute-start.7) | collective-permute-done | bytes 458784 | tf_op jit(solution)/shard_map/ppermute | solution.py:37
  270.8 40.8 %shard_map.262 = (bf16[2,384,512]{2,1,0:T(8,128)(2,1)S(1)}, f32[2,4,8,384]{3,2,1,0:T(8,128)S(1)}) custom-call(bf16[2,384,512]{2,1,0:T(8,128)(2,1)S(1)} %pad.38.q_ref, bf16[2,1024,512]{2,1,0:T(8,128)(2,1)S(1)} %pad.39.kp_ref, bf16[2,1024,512]{2,1,0:T(8,128)(2,1)S(1)} %pad.40.vp_ref, bf16[2,384,512]{2,1,0:T(8,128)(2,1)S(1)} %pad.41.k_ref, ...), custom_call_target="tpu_custom_call" | custom-call | flops 7046430720 | bytes 16777216 | tf_op jit(solution)/shard_map/pallas_call | solution.py:182
  332.5 13.9 collective-permute-done.10
  347.7 9.1 all-gather.21.cloned.1.call-done.wproj_hbm
  356.7 44.6 %shard_map.263 = (f32[192,1600]{1,0:T(8,128)}, bf16[4,192,1600]{2,1,0:T(8,128)(2,1)}, f32[4,192,1600]{2,1,0:T(8,128)}, bf16[4,192,1600]{2,1,0:T(8,128)(2,1)}) custom-call(f32[192,1600]{1,0:T(8,128)} %fusion.23.x_ref, f32[8,1600]{1,0:T(8,128)} %get-tuple-element.189.vec_ref, f32[1,1600]{1,0:T(1,128)} %get-tuple-element.190.fcb_ref, ...), custom_call_target="tpu_custom_call" | custom-call | flops 7864320000 | bytes 41943040 | tf_op jit(solution)/shard_map/pallas_call | solution.py:531
  407.6 13.2 collective-permute-done.11
  438.5 41.4 %all-gather.23.cloned.1.call-done = bf16[1600,1344]{1,0:T(8,128)(2,1)} async-done(((bf16[200,1344]{1,0:T(8,128)(2,1)}), bf16[1600,1344]{1,0:T(8,128)(2,1)}) %all-gather.23.cloned.1.call-update) | async-done | bytes 4300816 | tf_op jit(solution)/shard_map/all_gather | solution.py:823
  505.4 29.9 %collective-permute-done.14 = bf16[2,2,128,448]{3,2,1,0:T(8,128)(2,1)} collective-permute-done((bf16[2,2,128,448]{3,2,1,0:T(8,128)(2,1)}, bf16[2,2,128,448]{3,2,1,0:T(8,128)(2,1)}, u32[]{:S(2)}, u32[]{:S(2)}) %collective-permute-start.14) | collective-permute-done | bytes 458784 | tf_op jit(solution)/shard_map/ppermute | solution.py:37
  539.1 42.8 %collective-permute-done.18 = bf16[2,2,128,448]{3,2,1,0:T(8,128)(2,1)} collective-permute-done((bf16[2,2,128,448]{3,2,1,0:T(8,128)(2,1)}, bf16[2,2,128,448]{3,2,1,0:T(8,128)(2,1)}, u32[]{:S(2)}, u32[]{:S(2)}) %collective-permute-start.18) | collective-permute-done | bytes 458784 | tf_op jit(solution)/shard_map/ppermute | solution.py:37
  592.2 7.5 collective-permute-done.19
  610.7 41.0 %shard_map.264 = (bf16[2,384,512]{2,1,0:T(8,128)(2,1)S(1)}, f32[2,4,8,384]{3,2,1,0:T(8,128)S(1)}) custom-call(bf16[2,384,512]{2,1,0:T(8,128)(2,1)S(1)} %copy-done.14, bf16[2,1024,512]{2,1,0:T(8,128)(2,1)S(1)} %pad.44.kp_ref, bf16[2,1024,512]{2,1,0:T(8,128)(2,1)S(1)} %pad.45.vp_ref, bf16[2,384,512]{2,1,0:T(8,128)(2,1)S(1)} %pad.46.k_ref, ...), custom_call_target="tpu_custom_call" | custom-call | flops 7046430720 | bytes 16777216 | tf_op jit(solution)/shard_map/pallas_call | solution.py:182
  673.1 13.3 collective-permute-done.21
  687.7 16.4 all-gather.25.cloned.1.call-done.wproj_hbm
  704.1 44.6 %shard_map.265 = (f32[192,1600]{1,0:T(8,128)}, bf16[4,192,1600]{2,1,0:T(8,128)(2,1)}, f32[4,192,1600]{2,1,0:T(8,128)}, bf16[4,192,1600]{2,1,0:T(8,128)(2,1)}) custom-call(f32[192,1600]{1,0:T(8,128)} %fusion.20.x_ref, f32[8,1600]{1,0:T(8,128)} %get-tuple-element.188.vec_ref, f32[1,1600]{1,0:T(1,128)} %get-tuple-element.187.fcb_ref, ...), custom_call_target="tpu_custom_call" | custom-call | flops 7864320000 | bytes 41943040 | tf_op jit(solution)/shard_map/pallas_call | solution.py:531
  748.7 54.4 %shard_map.266 = (f32[192,1600]{1,0:T(8,128)}, f32[8,1600]{1,0:T(8,128)}, f32[1,1600]{1,0:T(1,128)}, bf16[1600,1600]{1,0:T(8,128)(2,1)}, bf16[1600,1600]{1,0:T(8,128)(2,1)}) custom-call(f32[192,1600]{1,0:T(8,128)} %bitcast_convert_fusion.g_ref, f32[192,1600]{1,0:T(8,128)} %fusion.20.x_ref, f32[8,1600]{1,0:T(8,128)} %get-tuple-element.188.vec_ref, ...), custom_call_target="tpu_custom_call" | custom-call | flops 15728640000 | bytes 52428800 | tf_op jit(solution)/shard_map/pallas_call | solution.py:679
  809.4 13.6 collective-permute-done.22
  847.7 69.9 %shard_map.267 = (bf16[2,384,512]{2,1,0:T(8,128)(2,1)S(1)}, bf16[2,1024,512]{2,1,0:T(8,128)(2,1)S(1)}, bf16[2,1024,512]{2,1,0:T(8,128)(2,1)S(1)}, bf16[2,256,512...) custom-call(bf16[2,384,512]{2,1,0:T(8,128)(2,1)S(1)} %copy-done.15, bf16[2,1024,512]{2,1,0:T(8,128)(2,1)S(1)} %pad.44.kp_ref, ...), custom_call_target="tpu_custom_call" | custom-call | flops 17616076800 | bytes 33554432 | tf_op jit(solution)/shard_map/pallas_call | solution.py:270
  936.3 41.0 %collective-permute-done.24 = bf16[4,2,2,128,448]{3,4,2,1,0:T(8,128)(2,1)} collective-permute-done((bf16[4,2,2,128,448]{3,4,2,1,0:T(8,128)(2,1)}, bf16[4,2,2,128,448]{3,4,2,1,0:T(8,128)(2,1)}, u32[]{:S(2)}, u32[]{:S(2)}) %collective-permute-start.24) | collective-permute-done | bytes 1835040 | tf_op jit(solution)/shard_map/ppermute | solution.py:37
  990.1 30.9 %collective-permute-done.27 = bf16[2,2,128,448]{3,2,1,0:T(8,128)(2,1)S(1)} collective-permute-done((bf16[2,2,128,448]{3,2,1,0:T(8,128)(2,1)}, bf16[2,2,128,448]{3,2,1,0:T(8,128)(2,1)S(1)}, u32[]{:S(2)}, u32[]{:S(2)}) %collective-permute-start.27) | collective-permute-done | bytes 458784 | tf_op jit(solution)/shard_map/ppermute | solution.py:37
  1021.0 11.2 collective-permute-done.26
  1041.5 7.6 convolution_convert_fusion.3
  1070.6 8.0 collective-permute-done.29
  1084.0 53.3 %shard_map.268 = (f32[192,1600]{1,0:T(8,128)}, f32[8,1600]{1,0:T(8,128)}, f32[1,1600]{1,0:T(1,128)}, bf16[1600,1600]{1,0:T(8,128)(2,1)}, bf16[1600,1600]{1,0:T(8,128)(2,1)}) custom-call(f32[192,1600]{1,0:T(8,128)} %get-tuple-element.166.g_ref, f32[192,1600]{1,0:T(8,128)} %fusion.23.x_ref, f32[8,1600]{1,0:T(8,128)} %get-tuple-element.189.vec_ref, ...), custom_call_target="tpu_custom_call" | custom-call | flops 15728640000 | bytes 52428800 | tf_op jit(solution)/shard_map/pallas_call | solution.py:679
  1142.5 13.5 collective-permute-done.30
  1176.1 69.9 %shard_map.269 = (bf16[2,384,512]{2,1,0:T(8,128)(2,1)S(1)}, bf16[2,1024,512]{2,1,0:T(8,128)(2,1)S(1)}, bf16[2,1024,512]{2,1,0:T(8,128)(2,1)S(1)}, bf16[2,256,512...) custom-call(bf16[2,384,512]{2,1,0:T(8,128)(2,1)S(1)} %copy-done.11, bf16[2,1024,512]{2,1,0:T(8,128)(2,1)S(1)} %copy-done.1, ...), custom_call_target="tpu_custom_call" | custom-call | flops 17616076800 | bytes 33554432 | tf_op jit(solution)/shard_map/pallas_call | solution.py:270
  1270.3 42.2 %collective-permute-done.32 = bf16[4,2,2,128,448]{3,4,2,1,0:T(8,128)(2,1)} collective-permute-done((bf16[4,2,2,128,448]{3,4,2,1,0:T(8,128)(2,1)}, bf16[4,2,2,128,448]{3,4,2,1,0:T(8,128)(2,1)}, u32[]{:S(2)}, u32[]{:S(2)}) %collective-permute-start.32) | collective-permute-done | bytes 1835040 | tf_op jit(solution)/shard_map/ppermute | solution.py:37
  1322.2 36.2 %collective-permute-done.35 = bf16[2,2,128,448]{3,2,1,0:T(8,128)(2,1)S(1)} collective-permute-done((bf16[2,2,128,448]{3,2,1,0:T(8,128)(2,1)S(1)}, bf16[2,2,128,448]{3,2,1,0:T(8,128)(2,1)S(1)}, u32[]{:S(2)}, u32[]{:S(2)}) %collective-permute-start.35) | collective-permute-done | bytes 458784 | tf_op jit(solution)/shard_map/ppermute | solution.py:37
  1358.5 9.3 collective-permute-done.34
  1384.8 7.8 convolution_convert_fusion.2
  1425.7 11.3 collective-permute-done.37
  1450.7 9.6 all-gather.5
  1460.3 35.8 %reduce-scatter.27.cloned.1.call-done = bf16[200,1344]{1,0:T(8,128)(2,1)} async-done(((bf16[1600,1344]{1,0:T(8,128)(2,1)}), bf16[200,1344]{1,0:T(8,128)(2,1)}) %reduce-scatter.27.cloned.1.call-update) | async-done | bytes 537616
  1498.6 65.7 %reduce-scatter.23.cloned.1.call-done = bf16[200,448]{1,0:T(8,128)(2,1)} async-done(((bf16[1600,448]{1,0:T(8,128)(2,1)}), bf16[200,448]{1,0:T(8,128)(2,1)}) %reduce-scatter.23.cloned.1.call-update) | async-done | bytes 179216 | tf_op jit(solution)/shard_map/reduce_scatter | solution.py:735
  1564.2 10.7 all-gather.4
  1576.7 60.5 %all-reduce.26.cloned.1.call-done = (f32[8,1600]{1,0:T(8,128)}, f32[8,1600]{1,0:T(8,128)}, f32[1600]{0:T(1024)}, f32[1600]{0:T(1024)}) async-done(((f32[8,1600]{1,0:T(8,128)}, f32[8,1600]{1,0:T(8,128)}, f32[1600]{0:T(1024)}, f32[1600]{0:T(1024)}), (f32[8,1600]{1,0:T(8,128)}, f32[8,1600]{1,0:T(8,128)}, f32[1600]{0:T(1024)}, f32[1600]{0:T(1024)})) %all-reduce.26.cloned.1.call-update) | async-done | bytes 115216
  1638.8 11.6 all-reduce.23
  1657.2 8.6 all-gather.29.cloned.1.call-done
  1672.4 119.5 %reduce-scatter.33.cloned.1.call-done = bf16[200,1600]{1,0:T(8,128)(2,1)} async-done(((bf16[1600,1600]{1,0:T(8,128)(2,1)}), bf16[200,1600]{1,0:T(8,128)(2,1)}) %reduce-scatter.33.cloned.1.call-update) | async-done | bytes 640016
  1791.9 126.6 %reduce-scatter.31.cloned.1.call-done = bf16[200,1600]{1,0:T(8,128)(2,1)} async-done(((bf16[1600,1600]{1,0:T(8,128)(2,1)}), bf16[200,1600]{1,0:T(8,128)(2,1)}) %reduce-scatter.31.cloned.1.call-update) | async-done | bytes 640016
  1921.5 124.1 %reduce-scatter.37.cloned.1.call-done = bf16[200,1600]{1,0:T(8,128)(2,1)} async-done(((bf16[1600,1600]{1,0:T(8,128)(2,1)}), bf16[200,1600]{1,0:T(8,128)(2,1)}) %reduce-scatter.37.cloned.1.call-update) | async-done | bytes 640016
  2045.6 126.6 %reduce-scatter.35.cloned.1.call-done = bf16[200,1600]{1,0:T(8,128)(2,1)} async-done(((bf16[1600,1600]{1,0:T(8,128)(2,1)}), bf16[200,1600]{1,0:T(8,128)(2,1)}) %reduce-scatter.35.cloned.1.call-update) | async-done | bytes 640016
  2175.2 24.9 %all-gather.27.cloned.1.call-done = bf16[4,200,3,448]{3,1,2,0:T(8,128)(2,1)} async-done(((bf16[1,200,3,448]{3,1,2,0:T(8,128)(2,1)}), bf16[4,200,3,448]{3,1,2,0:T(8,128)(2,1)}) %all-gather.27.cloned.1.call-update) | async-done | bytes 2150416 | tf_op jit(solution)/shard_map/all_gather | solution.py:789
  (668 shorter events, 472.7 us)
Async XLA Ops:
  7.2 75.0 %all-gather.35.cloned.1.call-start = ((), (), s32[]{:S(2)}) async-start(), calls=%async_computation.20 | async-start | bytes 1843200 | tf_op jit(solution)/shard_map/all_gather | solution.py:823
  10.3 130.8 %all-gather.19.cloned.1.call-start = ((), (), s32[]{:S(2)}) async-start(), calls=%async_computation.10 | async-start | bytes 5068800 | tf_op jit(solution)/shard_map/all_gather | solution.py:823
  16.2 331.4 %all-gather.37.cloned.1.call-start = ((), (), s32[]{:S(2)}) async-start(), calls=%async_computation.21 | async-start | bytes 5990400 | tf_op jit(solution)/shard_map/all_gather | solution.py:823
  17.6 339.1 %all-gather.21.cloned.1.call-start = ((), (), s32[]{:S(2)}) async-start(), calls=%async_computation.11 | async-start | bytes 5990400 | tf_op jit(solution)/shard_map/all_gather | solution.py:823
  18.8 405.9 %all-gather.39.cloned.1.call-start = ((), (), s32[]{:S(2)}) async-start(), calls=%async_computation.22 | async-start | bytes 1843200 | tf_op jit(solution)/shard_map/all_gather | solution.py:823
  20.8 459.1 %all-gather.23.cloned.1.call-start = ((), (), s32[]{:S(2)}) async-start(), calls=%async_computation.12 | async-start | bytes 5068800 | tf_op jit(solution)/shard_map/all_gather | solution.py:823
  22.2 665.5 %all-gather.41.cloned.1.call-start = ((), (), s32[]{:S(2)}) async-start(), calls=%async_computation.23 | async-start | bytes 5990400 | tf_op jit(solution)/shard_map/all_gather | solution.py:823
  85.3 82.8 %all-to-all-start = ((bf16[4,448,448]{2,1,0:T(8,128)(2,1)}), bf16[4,448,448]{2,1,0:T(8,128)(2,1)S(1)}, u32[]{:S(2)}, u32[]{:S(2)}) async-start(bf16[4,448,448]{2,1,0:T(8,128)(2,1)} %pad_maximum_fusion.6), calls=%async_computation | async-start | bytes 3670016 | tf_op jit(solution)/shard_map/all_to_all | solution.py:838
  89.3 614.8 %all-gather.25.cloned.1.call-start = ((), (), s32[]{:S(2)}) async-start(), calls=%async_computation.13 | async-start | bytes 5990400 | tf_op jit(solution)/shard_map/all_gather | solution.py:823
  164.4 81.6 %collective-permute-start.2 = (bf16[2,2,128,448]{3,2,1,0:T(8,128)(2,1)}, bf16[2,2,128,448]{3,2,1,0:T(8,128)(2,1)}, u32[]{:S(2)}, u32[]{:S(2)}) collective-permute-start(bf16[2,2,128,448]{3,2,1,0:T(8,128)(2,1)} %pad_maximum_fusion.16), channel_id=1, source_target_pairs={{0,4},{4,0},{8,12},{12,8},{16,20},{20,16},{24,28},{28,24},{1,5},{5... | collective-permute-start | bytes 1376264 | tf_op jit(solution)/shard_map/ppermute | solution.py:37
  164.8 31.7 %collective-permute-start.3 = (bf16[2,2,128,448]{3,2,1,0:T(8,128)(2,1)}, bf16[2,2,128,448]{3,2,1,0:T(8,128)(2,1)}, u32[]{:S(2)}, u32[]{:S(2)}) collective-permute-start(bf16[2,2,128,448]{3,2,1,0:T(8,128)(2,1)} %pad_maximum_fusion.16), channel_id=1, source_target_pairs={{0,8},{4,12},{8,0},{12,4},{16,24},{20,28},{24,16},{28,20},{1,9},{5... | collective-permute-start | bytes 1376264 | tf_op jit(solution)/shard_map/ppermute | solution.py:37
  165.5 33.7 %collective-permute-start.5 = (bf16[2,2,128,448]{3,2,1,0:T(8,128)(2,1)}, bf16[2,2,128,448]{3,2,1,0:T(8,128)(2,1)}, u32[]{:S(2)}, u32[]{:S(2)}) collective-permute-start(bf16[2,2,128,448]{3,2,1,0:T(8,128)(2,1)} %pad_maximum_fusion.16), channel_id=1, source_target_pairs={{0,16},{4,20},{8,24},{12,28},{16,0},{20,4},{24,8},{28,12},{1,17},{... | collective-permute-start | bytes 1376264 | tf_op jit(solution)/shard_map/ppermute | solution.py:37
  167.6 76.5 %collective-permute-start.7 = (bf16[2,2,128,448]{3,2,1,0:T(8,128)(2,1)}, bf16[2,2,128,448]{3,2,1,0:T(8,128)(2,1)}, u32[]{:S(2)}, u32[]{:S(2)}) collective-permute-start(bf16[2,2,128,448]{3,2,1,0:T(8,128)(2,1)} %pad_maximum_fusion.16), channel_id=1, source_target_pairs={{0,24},{4,28},{8,16},{12,20},{16,8},{20,12},{24,0},{28,4},{1,25},{... | collective-permute-start | bytes 1376264 | tf_op jit(solution)/shard_map/ppermute | solution.py:37
  196.5 53.3 %collective-permute-start.4 = (bf16[2,2,128,448]{3,2,1,0:T(8,128)(2,1)}, bf16[2,2,128,448]{3,2,1,0:T(8,128)(2,1)S(1)}, u32[]{:S(2)}, u32[]{:S(2)}) collective-permute-start(bf16[2,2,128,448]{3,2,1,0:T(8,128)(2,1)} %collective-permute-done.3), channel_id=1, source_target_pairs={{0,4},{4,0},{8,12},{12,8},{16,20},{20,16},{24,28},{28,24},{1,5},{5... | collective-permute-start | bytes 1376264 | tf_op jit(solution)/shard_map/ppermute | solution.py:37
  199.2 53.3 %collective-permute-start.6 = (bf16[2,2,128,448]{3,2,1,0:T(8,128)(2,1)}, bf16[2,2,128,448]{3,2,1,0:T(8,128)(2,1)S(1)}, u32[]{:S(2)}, u32[]{:S(2)}) collective-permute-start(bf16[2,2,128,448]{3,2,1,0:T(8,128)(2,1)} %collective-permute-done.5), channel_id=1, source_target_pairs={{0,4},{4,0},{8,12},{12,8},{16,20},{20,16},{24,28},{28,24},{1,5},{5... | collective-permute-start | bytes 1376264 | tf_op jit(solution)/shard_map/ppermute | solution.py:37
  244.1 15.8 collective-permute-start.8
  427.9 68.5 %all-to-all-start.1 = ((bf16[4,448,448]{2,1,0:T(8,128)(2,1)}), bf16[4,448,448]{2,1,0:T(8,128)(2,1)}, u32[]{:S(2)}, u32[]{:S(2)}) async-start(bf16[4,448,448]{2,1,0:T(8,128)(2,1)} %pad_maximum_fusion.7), calls=%async_computation.1 | async-start | bytes 3670016 | tf_op jit(solution)/shard_map/all_to_all | solution.py:838
  432.3 832.0 %all-gather.33.cloned.1.call-start = ((), (), s32[]{:S(2)}) async-start(), calls=%async_computation.18 | async-start | bytes 3440640 | tf_op jit(solution)/shard_map/all_gather | solution.py:755
  493.2 42.2 %collective-permute-start.14 = (bf16[2,2,128,448]{3,2,1,0:T(8,128)(2,1)}, bf16[2,2,128,448]{3,2,1,0:T(8,128)(2,1)}, u32[]{:S(2)}, u32[]{:S(2)}) collective-permute-start(bf16[2,2,128,448]{3,2,1,0:T(8,128)(2,1)} %pad_maximum_fusion.17), channel_id=1, source_target_pairs={{0,8},{4,12},{8,0},{12,4},{16,24},{20,28},{24,16},{28,20},{1,9},{5... | collective-permute-start | bytes 1376264 | tf_op jit(solution)/shard_map/ppermute | solution.py:37
  494.0 44.0 %collective-permute-start.16 = (bf16[2,2,128,448]{3,2,1,0:T(8,128)(2,1)}, bf16[2,2,128,448]{3,2,1,0:T(8,128)(2,1)}, u32[]{:S(2)}, u32[]{:S(2)}) collective-permute-start(bf16[2,2,128,448]{3,2,1,0:T(8,128)(2,1)} %pad_maximum_fusion.17), channel_id=1, source_target_pairs={{0,16},{4,20},{8,24},{12,28},{16,0},{20,4},{24,8},{28,12},{1,17},{... | collective-permute-start | bytes 1376264 | tf_op jit(solution)/shard_map/ppermute | solution.py:37
  496.1 85.8 %collective-permute-start.18 = (bf16[2,2,128,448]{3,2,1,0:T(8,128)(2,1)}, bf16[2,2,128,448]{3,2,1,0:T(8,128)(2,1)}, u32[]{:S(2)}, u32[]{:S(2)}) collective-permute-start(bf16[2,2,128,448]{3,2,1,0:T(8,128)(2,1)} %pad_maximum_fusion.17), channel_id=1, source_target_pairs={{0,24},{4,28},{8,16},{12,20},{16,8},{20,12},{24,0},{28,4},{1,25},{... | collective-permute-start | bytes 1376264 | tf_op jit(solution)/shard_map/ppermute | solution.py:37
  496.2 86.9 %collective-permute-start.13 = (bf16[2,2,128,448]{3,2,1,0:T(8,128)(2,1)}, bf16[2,2,128,448]{3,2,1,0:T(8,128)(2,1)}, u32[]{:S(2)}, u32[]{:S(2)}) collective-permute-start(bf16[2,2,128,448]{3,2,1,0:T(8,128)(2,1)} %pad_maximum_fusion.17), channel_id=1, source_target_pairs={{0,4},{4,0},{8,12},{12,8},{16,20},{20,16},{24,28},{28,24},{1,5},{5... | collective-permute-start | bytes 1376264 | tf_op jit(solution)/shard_map/ppermute | solution.py:37
  535.3 51.4 %collective-permute-start.15 = (bf16[2,2,128,448]{3,2,1,0:T(8,128)(2,1)}, bf16[2,2,128,448]{3,2,1,0:T(8,128)(2,1)S(1)}, u32[]{:S(2)}, u32[]{:S(2)}) collective-permute-start(bf16[2,2,128,448]{3,2,1,0:T(8,128)(2,1)} %collective-permute-done.14), channel_id=1, source_target_pairs={{0,4},{4,0},{8,12},{12,8},{16,20},{20,16},{24,28},{28,24},{1,5},{5... | collective-permute-start | bytes 1376264 | tf_op jit(solution)/shard_map/ppermute | solution.py:37
  538.0 51.5 %collective-permute-start.17 = (bf16[2,2,128,448]{3,2,1,0:T(8,128)(2,1)}, bf16[2,2,128,448]{3,2,1,0:T(8,128)(2,1)S(1)}, u32[]{:S(2)}, u32[]{:S(2)}) collective-permute-start(bf16[2,2,128,448]{3,2,1,0:T(8,128)(2,1)} %collective-permute-done.16), channel_id=1, source_target_pairs={{0,4},{4,0},{8,12},{12,8},{16,20},{20,16},{24,28},{28,24},{1,5},{5... | collective-permute-start | bytes 1376264 | tf_op jit(solution)/shard_map/ppermute | solution.py:37
  582.0 17.7 collective-permute-start.19
  804.5 18.4 collective-permute-start.22
  828.2 577.4 %all-gather.31.cloned.1.call-start = ((), (), s32[]{:S(2)}) async-start(), calls=%async_computation.16 | async-start | bytes 3440640 | tf_op jit(solution)/shard_map/all_gather | solution.py:755
  935.7 41.6 %collective-permute-start.24 = (bf16[4,2,2,128,448]{3,4,2,1,0:T(8,128)(2,1)}, bf16[4,2,2,128,448]{3,4,2,1,0:T(8,128)(2,1)}, u32[]{:S(2)}, u32[]{:S(2)}) collective-permute-start(bf16[4,2,2,128,448]{3,4,2,1,0:T(8,128)(2,1)} %copy.111), channel_id=1, source_target_pairs={{0,4},{4,0},{8,12},{12,8},{16,20},{20,16},{24,28},{28,24},{1,5},{5... | collective-permute-start | bytes 5505032 | tf_op jit(solution)/shard_map/ppermute | solution.py:37
  985.5 35.5 %collective-permute-start.27 = (bf16[2,2,128,448]{3,2,1,0:T(8,128)(2,1)}, bf16[2,2,128,448]{3,2,1,0:T(8,128)(2,1)S(1)}, u32[]{:S(2)}, u32[]{:S(2)}) collective-permute-start(bf16[2,2,128,448]{3,2,1,0:T(8,128)(2,1)} %get-tuple-element.133), channel_id=1, source_target_pairs={{0,24},{4,28},{8,16},{12,20},{16,8},{20,12},{24,0},{28,4},{1,25},{... | collective-permute-start | bytes 1376264 | tf_op jit(solution)/shard_map/ppermute | solution.py:37
  986.8 45.4 %collective-permute-start.26 = (bf16[2,2,128,448]{3,2,1,0:T(8,128)(2,1)}, bf16[2,2,128,448]{3,2,1,0:T(8,128)(2,1)S(1)}, u32[]{:S(2)}, u32[]{:S(2)}) collective-permute-start(bf16[2,2,128,448]{3,2,1,0:T(8,128)(2,1)} %get-tuple-element.134), channel_id=1, source_target_pairs={{0,16},{4,20},{8,24},{12,28},{16,0},{20,4},{24,8},{28,12},{1,17},{... | collective-permute-start | bytes 1376264 | tf_op jit(solution)/shard_map/ppermute | solution.py:37
  988.9 43.3 %collective-permute-start.25 = (bf16[2,2,128,448]{3,2,1,0:T(8,128)(2,1)S(1)}, bf16[2,2,128,448]{3,2,1,0:T(8,128)(2,1)}, u32[]{:S(2)}, u32[]{:S(2)}) collective-permute-start(bf16[2,2,128,448]{3,2,1,0:T(8,128)(2,1)S(1)} %get-tuple-element.132), channel_id=1, source_target_pairs={{0,8},{4,12},{8,0},{12,4},{16,24},{20,28},{24,16},{28,20},{1,9},{5... | collective-permute-start | bytes 1376264 | tf_op jit(solution)/shard_map/ppermute | solution.py:37
  990.1 453.4 %reduce-scatter.29.cloned.1.call-start = ((), (), s32[]{:S(2)}) async-start(), calls=%async_computation.25 | async-start | bytes 5068800
  1070.2 380.5 %reduce-scatter.25.cloned.1.call-start = ((), (), s32[]{:S(2)}) async-start(), calls=%async_computation.19 | async-start | bytes 1843200 | tf_op jit(solution)/shard_map/reduce_scatter | solution.py:735
  1138.6 17.3 collective-permute-start.30
  1264.1 48.4 %collective-permute-start.32 = (bf16[4,2,2,128,448]{3,4,2,1,0:T(8,128)(2,1)}, bf16[4,2,2,128,448]{3,4,2,1,0:T(8,128)(2,1)}, u32[]{:S(2)}, u32[]{:S(2)}) collective-permute-start(bf16[4,2,2,128,448]{3,4,2,1,0:T(8,128)(2,1)} %copy.117), channel_id=1, source_target_pairs={{0,4},{4,0},{8,12},{12,8},{16,20},{20,16},{24,28},{28,24},{1,5},{5... | collective-permute-start | bytes 5505032 | tf_op jit(solution)/shard_map/ppermute | solution.py:37
  1270.2 225.9 %reduce-scatter.27.cloned.1.call-start = ((), (), s32[]{:S(2)}) async-start(), calls=%async_computation.24 | async-start | bytes 5068800
  1317.8 40.7 %collective-permute-start.35 = (bf16[2,2,128,448]{3,2,1,0:T(8,128)(2,1)S(1)}, bf16[2,2,128,448]{3,2,1,0:T(8,128)(2,1)S(1)}, u32[]{:S(2)}, u32[]{:S(2)}) collective-permute-start(bf16[2,2,128,448]{3,2,1,0:T(8,128)(2,1)S(1)} %get-tuple-element.130), channel_id=1, source_target_pairs={{0,24},{4,28},{8,16},{12,20},{16,8},{20,12},{24,0},{28,4},{1,25},{... | collective-permute-start | bytes 1376264 | tf_op jit(solution)/shard_map/ppermute | solution.py:37
  1317.9 49.9 %collective-permute-start.34 = (bf16[2,2,128,448]{3,2,1,0:T(8,128)(2,1)S(1)}, bf16[2,2,128,448]{3,2,1,0:T(8,128)(2,1)S(1)}, u32[]{:S(2)}, u32[]{:S(2)}) collective-permute-start(bf16[2,2,128,448]{3,2,1,0:T(8,128)(2,1)S(1)} %get-tuple-element.131), channel_id=1, source_target_pairs={{0,16},{4,20},{8,24},{12,28},{16,0},{20,4},{24,8},{28,12},{1,17},{... | collective-permute-start | bytes 1376264 | tf_op jit(solution)/shard_map/ppermute | solution.py:37
  1321.7 46.0 %collective-permute-start.33 = (bf16[2,2,128,448]{3,2,1,0:T(8,128)(2,1)S(1)}, bf16[2,2,128,448]{3,2,1,0:T(8,128)(2,1)S(1)}, u32[]{:S(2)}, u32[]{:S(2)}) collective-permute-start(bf16[2,2,128,448]{3,2,1,0:T(8,128)(2,1)S(1)} %get-tuple-element.129), channel_id=1, source_target_pairs={{0,8},{4,12},{8,0},{12,4},{16,24},{20,28},{24,16},{28,20},{1,9},{5... | collective-permute-start | bytes 1376264 | tf_op jit(solution)/shard_map/ppermute | solution.py:37
  1383.2 181.1 %reduce-scatter.23.cloned.1.call-start = ((), (), s32[]{:S(2)}) async-start(), calls=%async_computation.17 | async-start | bytes 1843200 | tf_op jit(solution)/shard_map/reduce_scatter | solution.py:735
  1416.0 221.2 %all-reduce.26.cloned.1.call-start = ((), (), s32[]{:S(2)}) async-start(), calls=%async_computation.30 | async-start | bytes 245760
  1420.5 16.5 collective-permute-start.37
  1443.4 222.4 %all-gather.29.cloned.1.call-start = ((), (), s32[]{:S(2)}) async-start(), calls=%async_computation.15 | async-start | bytes 3072000 | tf_op jit(solution)/shard_map/all_gather | solution.py:789
  1445.9 346.0 %reduce-scatter.33.cloned.1.call-start = ((), (), s32[]{:S(2)}) async-start(), calls=%async_computation.27 | async-start | bytes 5990400
  1446.5 472.0 %reduce-scatter.31.cloned.1.call-start = ((), (), s32[]{:S(2)}) async-start(), calls=%async_computation.26 | async-start | bytes 5990400
  1447.1 598.5 %reduce-scatter.37.cloned.1.call-start = ((), (), s32[]{:S(2)}) async-start(), calls=%async_computation.29 | async-start | bytes 5990400
  1447.8 724.4 %reduce-scatter.35.cloned.1.call-start = ((), (), s32[]{:S(2)}) async-start(), calls=%async_computation.28 | async-start | bytes 5990400
  1448.4 751.6 %all-gather.27.cloned.1.call-start = ((), (), s32[]{:S(2)}) async-start(), calls=%async_computation.14 | async-start | bytes 3072000 | tf_op jit(solution)/shard_map/all_gather | solution.py:789
  (140 other events, 1970.8 us)
Sparse Core Ops, SparseCore 0:
  10.8 52.9 all-gather.34
  66.5 74.4 all-gather.18
  143.3 124.6 all-gather.36
  270.1 86.6 all-gather.20
  358.8 44.5 all-gather.38
  405.4 74.4 all-gather.22
  482.0 134.5 all-gather.40
  618.8 85.1 all-gather.24
  828.4 25.7 all-gather.32
  990.2 26.9 all-gather.30
  1070.3 109.6 reduce-scatter.28
  1270.4 87.5 reduce-scatter.24
  1383.3 112.7 reduce-scatter.26
  1499.8 64.3 reduce-scatter.22
  1568.3 68.8 all-reduce.25
  1639.3 26.5 all-gather.28
  1669.5 122.3 reduce-scatter.32
  1795.2 123.2 reduce-scatter.30
  1922.4 123.2 reduce-scatter.36
  2048.9 123.2 reduce-scatter.34
  2174.4 25.5 all-gather.26

commit v3 on v2

v3 whole, which is shorter than its diff:
```python
import functools

import jax
import jax.numpy as jnp
from jax import lax
from jax.experimental import pallas as pl
from jax.experimental.pallas import tpu as pltpu
from jax.sharding import PartitionSpec as P

D = 1600
HEADS = 25
HEAD = 64
GROUP = 8
PROMPT_DEV = 128
CONT_LEN = 256
TOK_DEV = 384
MICRO = 2
LAYERS = 2
PROMPT = 1024
KEYS = PROMPT + CONT_LEN
CHUNK = 128

f32 = jnp.float32
bf16 = jnp.bfloat16
norm_eps = 1e-05
NN = (((1,), (0,)), ((), ()))
NT = (((1,), (1,)), ((), ()))
TN = (((0,), (0,)), ((), ()))


def mm(left, right, dims=NN):
    return lax.dot_general(left, right, dims, preferred_element_type=f32)


def gelu_tanh(value):
    return jax.nn.gelu(value, approximate=True)


MESH = pl.DeviceIdType.MESH
ANY = pl.BlockSpec(memory_space=pl.ANY)
IN_VMEM = pl.BlockSpec(memory_space=pltpu.VMEM)
TILE = 512
ROW_CHUNK = 32


class Peers:
    def __init__(self):
        self.f = lax.axis_index("fsdp")
        self.t = lax.axis_index("tp")
        x, c = self.t // 2, self.t % 2
        self.x = x
        self.core = 2 * x + 1 - c
        self.over = 2 * (1 - x) + c
        self.diag = 2 * (1 - x) + 1 - c

    def greet(self):
        barrier = pltpu.get_barrier_semaphore()
        for t in (self.core, self.over):
            pl.semaphore_signal(barrier, inc=1, device_id=(self.f, t), device_id_type=MESH)
        pl.semaphore_wait(barrier, 2)

    def copy(self, source, target, sems, index, t):
        return pltpu.make_async_remote_copy(
            src_ref=source,
            dst_ref=target,
            send_sem=sems[0].at[index],
            recv_sem=sems[1].at[index],
            device_id=(self.f, t),
            device_id_type=MESH,
        )


class Gather:
    def __init__(self, peers, buf, sems):
        self.p, self.buf, self.sems = peers, buf, sems

    def piece(self, slot, index, t):
        return self.p.copy(self.buf.at[slot], self.buf.at[slot], self.sems, index, t)

    def start(self):
        p = self.p
        self.piece(p.t, 1, p.over).start()
        self.piece(p.t, 0, p.core).start()

    def wait_chip(self):
        self.piece(self.p.core, 0, self.p.core).wait_recv()

    def relay(self):
        p = self.p
        self.piece(p.over, 1, p.over).wait_recv()
        self.piece(p.over, 2, p.core).start()

    def wait_diag(self):
        self.piece(self.p.diag, 2, self.p.core).wait_recv()

    def finish(self):
        p = self.p
        self.piece(p.t, 1, p.over).wait_send()
        self.piece(p.t, 0, p.core).wait_send()
        self.piece(p.over, 2, p.core).wait_send()


class Scatter:
    def __init__(self, peers, part, from_core, over_out, from_over, sems):
        self.p, self.part, self.sems = peers, part, sems
        self.from_core, self.over_out, self.from_over = from_core, over_out, from_over

    def far_to_core(self):
        return self.p.copy(self.part.at[self.p.diag], self.from_core.at[0], self.sems, 3, self.p.core)

    def near_to_core(self):
        return self.p.copy(self.part.at[self.p.core], self.from_core.at[1], self.sems, 4, self.p.core)

    def to_over(self):
        return self.p.copy(self.over_out, self.from_over, self.sems, 5, self.p.over)

    def send_over(self):
        self.far_to_core().wait_recv()

        @pl.loop(0, self.over_out.shape[0] // ROW_CHUNK)
        def _(i):
            at = pl.ds(pl.multiple_of(i * ROW_CHUNK, ROW_CHUNK), ROW_CHUNK)
            total = self.part[self.p.over, at, :].astype(f32) + self.from_core[0, at, :].astype(f32)
            self.over_out[at, :] = total.astype(bf16)

        self.to_over().start()

    def wait(self):
        self.near_to_core().wait_recv()
        self.to_over().wait_recv()

    def rows(self, at):
        return (
            self.part[self.p.t, at, :].astype(f32)
            + self.from_core[1, at, :].astype(f32)
            + self.from_over[at, :].astype(f32)
        )

    def finish(self):
        for copy in (self.far_to_core(), self.near_to_core(), self.to_over()):
            copy.wait_send()


class Group:
    def __init__(self):
        f = lax.axis_index("fsdp")
        self.t = lax.axis_index("tp")
        self.member = f % GROUP
        self.base = f - self.member
        self.z, self.y = self.member // 2, self.member % 2

    def at(self, z, y):
        return z * 2 + y

    def ahead(self, k):
        return (self.z + k) % 4

    def behind(self, k):
        return (self.z + 4 - k) % 4

    def greet(self, peers):
        barrier = pltpu.get_barrier_semaphore()
        others = [self.at(self.z, 1 - self.y)] + [self.at(self.ahead(k), self.y) for k in (1, 2, 3)]
        for member in others:
            pl.semaphore_signal(
                barrier, inc=1, device_id=(self.base + member, self.t), device_id_type=MESH
            )
        for t in (peers.core, peers.over):
            pl.semaphore_signal(barrier, inc=1, device_id=(peers.f, t), device_id_type=MESH)
        pl.semaphore_wait(barrier, 6)

    def copy(self, source, target, sems, index, member):
        return pltpu.make_async_remote_copy(
            src_ref=source,
            dst_ref=target,
            send_sem=sems[0].at[index],
            recv_sem=sems[1].at[index],
            device_id=(self.base + member, self.t),
            device_id_type=MESH,
        )


class Background:
    def __init__(self, group, kinds, sources, targets, sems):
        self.g, self.sems = group, sems
        self.items = list(zip(kinds, sources, targets))

    def copies(self):
        g = self.g
        made = []
        for n, (kind, source, target) in enumerate(self.items):
            if kind == "y":
                made.append(g.copy(source.at[:, 1 - g.y], target, self.sems, 3 * n, g.at(g.z, 1 - g.y)))
            else:
                for k in (1, 2, 3):
                    to = g.ahead(k)
                    made.append(
                        g.copy(source.at[to], target.at[k - 1], self.sems, 3 * n + k - 1, g.at(to, g.y))
                    )
        return made

    def start(self):
        for copy in self.copies():
            copy.start()

    def finish(self):
        for copy in self.copies():
            copy.wait()


def sent_shapes(payload):
    return tuple(
        jax.ShapeDtypeStruct((4 if kind == "y" else 3,) + a.shape[-2:], a.dtype) for kind, a in payload
    )


def sent_scratch(payload):
    return [pltpu.SemaphoreType.DMA((3 * len(payload) + 1,))] * 2


def row_chunks(rows, body):
    @pl.loop(0, rows // ROW_CHUNK)
    def _(i):
        body(pl.ds(pl.multiple_of(i * ROW_CHUNK, ROW_CHUNK), ROW_CHUNK))


def tiles(extent, body):
    whole = extent // TILE

    @pl.loop(0, whole)
    def _(i):
        body(pl.ds(pl.multiple_of(i * TILE, TILE), TILE))

    if extent % TILE:
        body(pl.ds(whole * TILE, extent % TILE))


def pair_rows(ref, x):
    both = ref[pl.ds(2 * x, 2)]
    return both.reshape(2 * both.shape[1], both.shape[2])


def put_pair(ref, x, at, value):
    ref[pl.ds(2 * x, 2), :, at] = value.reshape(2, value.shape[0] // 2, value.shape[1]).astype(ref.dtype)


def norm_stats(x):
    centred = x - jnp.mean(x, -1, keepdims=True)
    scale = lax.rsqrt(jnp.mean(centred * centred, -1, keepdims=True) + norm_eps)
    return centred * scale, scale


def lanes_up(width):
    return -(-width // 128) * 128


def proj_part(w_b, width):
    return w_b.at[:, lanes_up(width) :]


def ff_fwd_kernel(
    x_ref, vec_ref, fcb_ref, wb_hbm,
    out_ref, all_hbm, pre_hbm, hid_hbm,
    wfc, wproj, buf, pre, hid, part, from_core, over_out, from_over, send, recv, local,
):
    p = Peers()
    rows = x_ref.shape[0]
    sems = (send, recv)
    gather = Gather(p, buf, sems)
    scatter = Scatter(p, part, from_core, over_out, from_over, sems)
    width = fcb_ref.shape[1]
    load_fc = pltpu.make_async_copy(wb_hbm.at[:, : wfc.shape[1]], wfc, local.at[0])
    load_proj = pltpu.make_async_copy(proj_part(wb_hbm, width), wproj, local.at[1])
    load_fc.start()
    load_proj.start()

    def norm(at):
        hat, _ = norm_stats(x_ref[at, :])
        buf[p.t, at, :] = (hat * vec_ref[5:6, :] + vec_ref[6:7, :]).astype(bf16)

    row_chunks(rows, norm)
    p.greet()
    gather.start()
    gather.wait_chip()
    load_fc.wait()

    def up(x):
        def tile(at):
            value = mm(pair_rows(buf, x), wfc[:, at]) + fcb_ref[:, at]
            put_pair(pre, x, at, value)
            put_pair(hid, x, at, gelu_tanh(value))

        tiles(width, tile)

    def down(x):
        def tile(at):
            put_pair(part, x, at, mm(pair_rows(hid, x), wproj[at, :width], NT))

        tiles(D, tile)

    up(p.x)
    gather.relay()
    gather.wait_diag()
    keep_all = pltpu.make_async_copy(buf, all_hbm, local.at[2])
    keep_all.start()
    up(1 - p.x)
    keep_pre = pltpu.make_async_copy(pre, pre_hbm, local.at[3])
    keep_hid = pltpu.make_async_copy(hid, hid_hbm, local.at[4])
    keep_pre.start()
    keep_hid.start()
    load_proj.wait()
    down(1 - p.x)
    scatter.far_to_core().start()
    scatter.send_over()
    down(p.x)
    scatter.near_to_core().start()
    scatter.wait()

    def final(at):
        out_ref[at, :] = x_ref[at, :] + scatter.rows(at) + vec_ref[7:8, :]

    row_chunks(rows, final)
    gather.finish()
    scatter.finish()
    for copy in (keep_all, keep_pre, keep_hid):
        copy.wait()


def scatter_scratch(n_tp, rows):
    return [
        pltpu.VMEM((n_tp, rows, D), bf16),
        pltpu.VMEM((2, rows, D), bf16),
        pltpu.VMEM((rows, D), bf16),
        pltpu.VMEM((rows, D), bf16),
        pltpu.SemaphoreType.DMA((6,)),
        pltpu.SemaphoreType.DMA((6,)),
    ]


def params(collective_id):
    return pltpu.CompilerParams(collective_id=collective_id, has_side_effects=True, vmem_limit_bytes=60 * 2**20)


def ff_fwd(x, vecs, fc_bias, w_b, n_tp):
    rows, width = x.shape[0], fc_bias.shape[1]
    block = (n_tp, rows)
    return pl.pallas_call(
        ff_fwd_kernel,
        out_shape=(
            jax.ShapeDtypeStruct((rows, D), f32),
            jax.ShapeDtypeStruct(block + (D,), bf16),
            jax.ShapeDtypeStruct(block + (width,), f32),
            jax.ShapeDtypeStruct(block + (width,), bf16),
        ),
        in_specs=[IN_VMEM, IN_VMEM, IN_VMEM, ANY],
        out_specs=(IN_VMEM, ANY, ANY, ANY),
        scratch_shapes=[
            pltpu.VMEM((D, lanes_up(width)), bf16),
            pltpu.VMEM((D, lanes_up(width)), bf16),
            pltpu.VMEM(block + (D,), bf16),
            pltpu.VMEM(block + (width,), f32),
            pltpu.VMEM(block + (width,), bf16),
        ]
        + scatter_scratch(n_tp, rows)
        + [pltpu.SemaphoreType.DMA((5,))],
        compiler_params=params(1),
        cost_estimate=pl.CostEstimate(
            flops=4 * n_tp * rows * D * width, bytes_accessed=40 * 2**20, transcendentals=n_tp * rows * width
        ),
    )(x, vecs, fc_bias, w_b)


def gelu_slope(u):
    a = 0.7978845608028654
    square = u * u
    t = jnp.tanh(a * (u + 0.044715 * u * square))
    return 0.5 * (1.0 + t) + 0.5 * u * (1.0 - t * t) * (a * (1.0 + 3 * 0.044715 * square))


def norm_back(x, dy, gain):
    hat, scale = norm_stats(x)
    d_hat = dy * gain
    inner = d_hat - jnp.mean(d_hat, -1, keepdims=True) - hat * jnp.mean(d_hat * hat, -1, keepdims=True)
    return scale * inner, dy * hat


def add_rows(ref, row, value):
    ref[row : row + 1, :] += jnp.sum(value, axis=0, keepdims=True)


def ff_bwd_kernel(kinds, *refs):
    n = len(kinds)
    g_ref, x_ref, vec_ref, all_hbm, pre_hbm, hid_hbm, wb_hbm = refs[:7]
    sources, refs = refs[7 : 7 + n], refs[7 + n :]
    out_ref, sums_ref, fcb_ref, dfc_hbm, dproj_hbm = refs[:5]
    targets, refs = refs[5 : 5 + n], refs[5 + n :]
    wfc, wproj, buf, other, pre, dpre, stage, part, from_core, over_out, from_over, send, recv, local = refs[:14]
    p, g = Peers(), Group()
    background = Background(g, kinds, sources, targets, refs[14:])
    rows = x_ref.shape[0]
    n_tp, width = buf.shape[0], fcb_ref.shape[1]
    sems = (send, recv)
    gather = Gather(p, buf, sems)
    scatter = Scatter(p, part, from_core, over_out, from_over, sems)
    load_proj = pltpu.make_async_copy(proj_part(wb_hbm, width), wproj, local.at[0])
    load_pre = pltpu.make_async_copy(pre_hbm, pre, local.at[1])
    load_fc = pltpu.make_async_copy(wb_hbm.at[:, : wfc.shape[1]], wfc, local.at[2])
    load_other = pltpu.make_async_copy(hid_hbm, other, local.at[3])
    for copy in (load_proj, load_pre, load_fc, load_other):
        copy.start()
    sums_ref[...] = jnp.zeros_like(sums_ref)
    fcb_ref[...] = jnp.zeros_like(fcb_ref)

    def lower(at):
        low = g_ref[at, :].astype(bf16)
        buf[p.t, at, :] = low
        add_rows(sums_ref, 7, low.astype(f32))

    row_chunks(rows, lower)
    if n:
        g.greet(p)
    else:
        p.greet()
    gather.start()
    background.start()
    gather.wait_chip()
    load_proj.wait()
    load_pre.wait()

    def through(x):
        def tile(at):
            d_hidden = mm(pair_rows(buf, x), wproj[:, at])
            u = pre[pl.ds(2 * x, 2), :, at].reshape(2 * rows, -1)
            low = (gelu_slope(u) * d_hidden).astype(bf16)
            put_pair(dpre, x, at, low)
            fcb_ref[:, at] += jnp.sum(low.astype(f32), axis=0, keepdims=True)

        tiles(width, tile)

    def down(x):
        def tile(at):
            put_pair(part, x, at, mm(pair_rows(dpre, x), wfc[at, :width], NT))

        tiles(D, tile)

    through(p.x)
    gather.relay()
    gather.wait_diag()
    through(1 - p.x)
    load_fc.wait()
    down(1 - p.x)
    scatter.far_to_core().start()
    scatter.send_over()
    down(p.x)
    scatter.near_to_core().start()

    def outer(left, right, target, sem):
        whole = D // TILE
        rest = D - whole * TILE
        flat = right[...].reshape(n_tp * rows, width)

        def tile(i, size):
            at = pl.ds(pl.multiple_of(i * TILE, TILE), size)
            value = mm(left[:, :, at].reshape(n_tp * rows, size), flat, TN)
            stage[at, :] = value.astype(bf16)

        @pl.loop(0, whole)
        def _(i):
            tile(i, TILE)

        if rest:
            tile(whole, rest)
        return pltpu.make_async_copy(stage, target, sem)

    load_other.wait()
    store = outer(buf, other, dproj_hbm, local.at[4])
    store.start()
    gather.finish()
    load_all = pltpu.make_async_copy(all_hbm, buf, local.at[5])
    load_all.start()
    scatter.wait()

    def final(at):
        dy = scatter.rows(at)
        dx, d_gain = norm_back(x_ref[at, :], dy, vec_ref[5:6, :])
        add_rows(sums_ref, 5, d_gain)
        add_rows(sums_ref, 6, dy)
        out_ref[at, :] = g_ref[at, :] + dx

    row_chunks(rows, final)
    load_all.wait()
    store.wait()
    store = outer(buf, dpre, dfc_hbm, local.at[6])
    store.start()
    scatter.finish()
    store.wait()
    background.finish()


def ff_bwd(grad, x, vecs, all_rows, pre, hidden, w_b, n_tp, payload, collective_id):
    rows, width = x.shape[0], pre.shape[2]
    block = (n_tp, rows)
    return pl.pallas_call(
        functools.partial(ff_bwd_kernel, tuple(kind for kind, _ in payload)),
        out_shape=(
            jax.ShapeDtypeStruct((rows, D), f32),
            jax.ShapeDtypeStruct((8, D), f32),
            jax.ShapeDtypeStruct((1, width), f32),
            jax.ShapeDtypeStruct((D, width), bf16),
            jax.ShapeDtypeStruct((D, width), bf16),
        )
        + sent_shapes(payload),
        in_specs=[IN_VMEM] * 3 + [ANY] * (4 + len(payload)),
        out_specs=(IN_VMEM, IN_VMEM, IN_VMEM) + (ANY,) * (2 + len(payload)),
        scratch_shapes=[
            pltpu.VMEM((D, lanes_up(width)), bf16),
            pltpu.VMEM((D, lanes_up(width)), bf16),
            pltpu.VMEM(block + (D,), bf16),
            pltpu.VMEM(block + (width,), bf16),
            pltpu.VMEM(block + (width,), f32),
            pltpu.VMEM(block + (width,), bf16),
            pltpu.VMEM((D, width), bf16),
        ]
        + scatter_scratch(n_tp, rows)
        + [pltpu.SemaphoreType.DMA((7,))]
        + sent_scratch(payload),
        compiler_params=params(collective_id),
        cost_estimate=pl.CostEstimate(
            flops=8 * n_tp * rows * D * width, bytes_accessed=50 * 2**20, transcendentals=n_tp * rows * width
        ),
    )(grad, x, vecs, all_rows, pre, hidden, w_b, *(a for _, a in payload))


class Share:
    def __init__(self, group, kv, sems):
        self.g, self.kv, self.sems = group, kv, sems
        self.partner = group.at(group.z, 1 - group.y)

    def piece(self, member, micro, index, to):
        ref = self.kv.at[member, micro]
        return self.g.copy(ref, ref, self.sems, micro * 7 + index, to)

    def own(self, micro):
        g = self.g
        return [self.piece(g.member, micro, 0, self.partner)] + [
            self.piece(g.member, micro, k, g.at(g.ahead(k), g.y)) for k in (1, 2, 3)
        ]

    def relayed(self, micro):
        g = self.g
        return [self.piece(g.at(g.behind(k), g.y), micro, 3 + k, self.partner) for k in (1, 2, 3)]

    def start(self, micro):
        for copy in self.own(micro):
            copy.start()

    def relay(self, micro):
        g = self.g
        for k, copy in zip((1, 2, 3), self.relayed(micro)):
            self.piece(g.at(g.behind(k), g.y), micro, k, self.partner).wait_recv()
            copy.start()

    def wait(self, micro):
        g = self.g
        self.piece(self.partner, micro, 0, self.partner).wait_recv()
        for k in (1, 2, 3):
            self.piece(g.at(g.behind(k), 1 - g.y), micro, 3 + k, self.partner).wait_recv()

    def finish(self, micro):
        for copy in self.own(micro) + self.relayed(micro):
            copy.wait_send()


class GroupSum:
    def __init__(self, group, parts, from_y, to_z, from_z, sems):
        self.g, self.parts, self.sems = group, parts, sems
        self.from_y, self.to_z, self.from_z = from_y, to_z, from_z

    def across(self, micro):
        g = self.g
        return g.copy(
            self.parts.at[micro, :, 1 - g.y], self.from_y.at[micro], self.sems, micro * 4, g.at(g.z, 1 - g.y)
        )

    def along(self, micro, k):
        g = self.g
        to = g.ahead(k)
        return g.copy(
            self.to_z.at[micro, to], self.from_z.at[micro, k - 1], self.sems, micro * 4 + k, g.at(to, g.y)
        )

    def start(self, micro):
        self.across(micro).start()

    def turn(self, micro):
        self.across(micro).wait_recv()

        @pl.loop(0, 4)
        def _(z):
            for kv in range(2):
                total = self.parts[micro, z, self.g.y, kv].astype(f32) + self.from_y[micro, z, kv].astype(f32)
                self.to_z[micro, z, kv] = total.astype(bf16)

        for k in (1, 2, 3):
            self.along(micro, k).start()

    def wait(self, micro):
        for k in (1, 2, 3):
            self.along(micro, k).wait_recv()

    def total(self, micro, kv):
        g = self.g
        value = self.parts[micro, g.z, g.y, kv].astype(f32) + self.from_y[micro, g.z, kv].astype(f32)
        for k in range(3):
            value = value + self.from_z[micro, k, kv].astype(f32)
        return value.astype(bf16)

    def finish(self, micro):
        self.across(micro).wait_send()
        for k in (1, 2, 3):
            self.along(micro, k).wait_send()


WIDE = 512
HEAD_PAIRS = WIDE // (2 * HEAD)
PROMPT_CHUNKS = PROMPT // CHUNK
CONT_CHUNKS = CONT_LEN // CHUNK


def chunk_at(c, base=0):
    return pl.ds(pl.multiple_of(base + c * CHUNK, CHUNK), CHUNK)


def key_limit(member):
    row = lax.broadcasted_iota(jnp.int32, (1, TOK_DEV), 1)
    return jnp.where(row < PROMPT_DEV, member * PROMPT_DEV + row, PROMPT - PROMPT_DEV + row)


def half_of(value, half):
    lane = lax.broadcasted_iota(jnp.int32, value.shape, 1)
    return jnp.where((lane >= HEAD * half) & (lane < HEAD * (half + 1)), value, jnp.zeros_like(value))


def fold(value, op):
    return op(value.reshape(value.shape[0] // 8, 8, value.shape[1]), axis=0)


def over_keys(body, prompt, own, carry):
    carry = lax.fori_loop(0, PROMPT_CHUNKS, lambda c, carry: body(c, lambda i: prompt(c, i), carry), carry)
    return lax.fori_loop(
        0, CONT_CHUNKS, lambda c, carry: body(PROMPT_CHUNKS + c, lambda i: own(c, i), carry), carry
    )


def head_pairs(head, finish):
    @pl.loop(0, HEAD_PAIRS)
    def _(pair):
        lanes = pl.ds(pl.multiple_of(pair * 2 * HEAD, 2 * HEAD), 2 * HEAD)
        head(pair, lanes, 0)

        @pl.when(pair < HEAD_PAIRS - 1)
        def _():
            head(pair, lanes, 1)

        finish(pair, lanes)


def to_slots(target, micro, first, value, lanes):
    per = target.shape[1] // MICRO
    row = first
    while row < first + value.shape[0]:
        slot, within = row // per, row % per
        count = min(per - within, first + value.shape[0] - row)
        target[slot, micro * per + within : micro * per + within + count, lanes] = value[
            row - first : row - first + count
        ]
        row += count


def pair_to_blocks(target, x, value):
    per = value.shape[0] // (2 * MICRO)
    for core in range(2):
        for micro in range(MICRO):
            at = pl.ds(pl.multiple_of((2 * x + core) * per, per), per)
            first = (core * MICRO + micro) * per
            target[micro, at, :] = value[first : first + per]


def attn_fwd_kernel(
    x_ref, vec_ref, bias_ref, wqkv_hbm, wout_hbm,
    out_ref, lse_ref, all_hbm, own_hbm, kv_hbm, mix_hbm,
    wqkv, wout, buf, own, kv, mix, s_ref, p_ref, o_ref,
    part, from_core, over_out, from_over, send, recv, gsend, grecv, local,
):
    p, g = Peers(), Group()
    rows = x_ref.shape[0]
    sems = (send, recv)
    gather = Gather(p, buf, sems)
    scatter = Scatter(p, part, from_core, over_out, from_over, sems)
    share = Share(g, kv, (gsend, grecv))
    load_qkv = pltpu.make_async_copy(wqkv_hbm.at[:, : 3 * WIDE], wqkv, local.at[0])
    load_out = pltpu.make_async_copy(wout_hbm, wout, local.at[1])
    load_qkv.start()
    load_out.start()

    def norm(at):
        hat, _ = norm_stats(x_ref[at, :])
        buf[p.t, at, :] = (hat * vec_ref[0:1, :] + vec_ref[1:2, :]).astype(bf16)

    row_chunks(rows, norm)
    g.greet(p)
    gather.start()
    gather.wait_chip()
    load_qkv.wait()

    def project(x):
        for i in range(3):
            value = mm(pair_rows(buf, x), wqkv[:, i * WIDE : (i + 1) * WIDE]) + bias_ref[i : i + 1, :]
            low = value.astype(bf16)
            if i == 0:
                low = low * HEAD ** (-0.5)
            pair_to_blocks(own.at[i], x, low)

    project(p.x)
    gather.relay()
    gather.wait_diag()
    project(1 - p.x)
    for micro in range(MICRO):
        for i in range(2):
            kv[g.member, micro, i] = own[1 + i, micro, :PROMPT_DEV, :]
        share.start(micro)
    keep_all = pltpu.make_async_copy(buf, all_hbm, local.at[2])
    keep_own = pltpu.make_async_copy(own, own_hbm, local.at[3])
    keep_all.start()
    keep_own.start()
    limit = key_limit(g.member)
    sub = lax.broadcasted_iota(jnp.int32, (CHUNK, TOK_DEV), 0)

    for micro in range(MICRO):
        if micro == 0:
            share.relay(0)
        share.wait(micro)
        if micro == 0:
            share.relay(1)

        def head(pair, lanes, half, micro=micro):
            qh = half_of(own[0, micro, :, lanes], half)

            def first(c, load, top):
                s = jnp.where(sub + c * CHUNK <= limit, mm(load(0), qh, NT), -1e30)
                s_ref[chunk_at(c), :] = s
                return jnp.maximum(top, fold(s, jnp.max))

            top = over_keys(
                first,
                lambda c, i: kv[c, micro, i, :, lanes],
                lambda c, i: own[1 + i, micro, chunk_at(c, PROMPT_DEV), lanes],
                jnp.full((8, TOK_DEV), -1e30, f32),
            )
            top = jnp.max(top, axis=0, keepdims=True)

            def second(c, total):
                e = jnp.exp(s_ref[chunk_at(c), :] - top)
                p_ref[chunk_at(c), :] = e.astype(bf16)
                return total + fold(e, jnp.sum)

            total = lax.fori_loop(0, KEYS // CHUNK, second, jnp.zeros((8, TOK_DEV), f32))
            total = jnp.sum(total, axis=0, keepdims=True)
            values = kv[:, micro, 1, :, lanes].reshape(PROMPT, 2 * HEAD)
            out = mm(values, p_ref[:PROMPT, :], TN) + mm(own[2, micro, PROMPT_DEV:, lanes], p_ref[PROMPT:, :], TN)
            at = slice(HEAD * half, HEAD * (half + 1))
            o_ref[at, :] = out[at, :] / total
            lse_ref[micro, pair, half : half + 1, :] = top + jnp.log(total)

        def finish(pair, lanes, micro=micro):
            @pl.when(pair == HEAD_PAIRS - 1)
            def _():
                o_ref[HEAD:, :] = jnp.zeros((HEAD, TOK_DEV), f32)

            to_slots(mix, micro, 0, o_ref[...].T.astype(bf16), lanes)

        head_pairs(head, finish)

    keep_kv = pltpu.make_async_copy(kv, kv_hbm, local.at[4])
    keep_mix = pltpu.make_async_copy(mix, mix_hbm, local.at[5])
    keep_kv.start()
    keep_mix.start()
    load_out.wait()

    def down(x):
        def tile(at):
            put_pair(part, x, at, mm(pair_rows(mix, x), wout[:, at]))

        tiles(D, tile)

    down(1 - p.x)
    scatter.far_to_core().start()
    scatter.send_over()
    down(p.x)
    scatter.near_to_core().start()
    scatter.wait()

    def final(at):
        out_ref[at, :] = x_ref[at, :] + (scatter.rows(at) + vec_ref[4:5, :])

    row_chunks(rows, final)
    gather.finish()
    scatter.finish()
    for micro in range(MICRO):
        share.finish(micro)
    for copy in (keep_all, keep_own, keep_kv, keep_mix):
        copy.wait()


def attn_shapes(n_tp, rows):
    return (
        ((n_tp, rows, D), bf16),
        ((3, MICRO, TOK_DEV, WIDE), bf16),
        ((GROUP, MICRO, 2, PROMPT_DEV, WIDE), bf16),
        ((n_tp, rows, WIDE), bf16),
    )


def attn_fwd(x, vecs, biases, w_qkv, w_out, n_tp, collective_id):
    rows = x.shape[0]
    saved = attn_shapes(n_tp, rows)
    return pl.pallas_call(
        attn_fwd_kernel,
        out_shape=(
            jax.ShapeDtypeStruct((rows, D), f32),
            jax.ShapeDtypeStruct((MICRO, HEAD_PAIRS, 8, TOK_DEV), f32),
        )
        + tuple(jax.ShapeDtypeStruct(*s) for s in saved),
        in_specs=[IN_VMEM, IN_VMEM, IN_VMEM, ANY, ANY],
        out_specs=(IN_VMEM, IN_VMEM, ANY, ANY, ANY, ANY),
        scratch_shapes=[pltpu.VMEM((D, 3 * WIDE), bf16), pltpu.VMEM((WIDE, D), bf16)]
        + [pltpu.VMEM(*s) for s in saved]
        + [
            pltpu.VMEM((KEYS, TOK_DEV), f32),
            pltpu.VMEM((KEYS, TOK_DEV), bf16),
            pltpu.VMEM((2 * HEAD, TOK_DEV), f32),
        ]
        + scatter_scratch(n_tp, rows)
        + [
            pltpu.SemaphoreType.DMA((7 * MICRO,)),
            pltpu.SemaphoreType.DMA((7 * MICRO,)),
            pltpu.SemaphoreType.DMA((6,)),
        ],
        compiler_params=params(collective_id),
        cost_estimate=pl.CostEstimate(flops=10**11, bytes_accessed=30 * 2**20, transcendentals=0),
    )(x, vecs, biases, w_qkv, w_out)


def attn_bwd_kernel(kinds, *refs):
    n = len(kinds)
    g_ref, x_ref, vec_ref, lse_ref, all_hbm, own_hbm, kv_hbm, mix_hbm, wqkv_hbm, wout_hbm = refs[:10]
    sources, refs = refs[10 : 10 + n], refs[10 + n :]
    out_ref, sums_ref, cols_ref, dqkv_hbm, dout_hbm = refs[:5]
    targets, refs = refs[5 : 5 + n], refs[5 + n :]
    wqkv, wout, buf, other, own, kv, gm, dkv, from_y, to_z, from_z, dkc, dqkv, stage, stage_out = refs[:15]
    p_ref, dp_ref, ds_ref, o_ref = refs[15:19]
    part, from_core, over_out, from_over, send, recv, gsend, grecv, local = refs[19:28]
    p, g = Peers(), Group()
    background = Background(g, kinds, sources, targets, refs[28:])
    rows = x_ref.shape[0]
    n_tp = buf.shape[0]
    out_width = stage_out.shape[1]
    out_step = (D - out_width) // (n_tp - 1)
    sems = (send, recv)
    gather = Gather(p, buf, sems)
    scatter = Scatter(p, part, from_core, over_out, from_over, sems)
    reduce = GroupSum(g, dkv, from_y, to_z, from_z, (gsend, grecv))
    load_out = pltpu.make_async_copy(wout_hbm, wout, local.at[0])
    load_own = pltpu.make_async_copy(own_hbm, own, local.at[1])
    load_kv = pltpu.make_async_copy(kv_hbm, kv, local.at[2])
    load_qkv = pltpu.make_async_copy(wqkv_hbm.at[:, : 3 * WIDE], wqkv, local.at[3])
    load_mix = pltpu.make_async_copy(mix_hbm, other, local.at[4])
    for copy in (load_out, load_own, load_kv, load_qkv, load_mix):
        copy.start()
    sums_ref[...] = jnp.zeros_like(sums_ref)

    def lower(at):
        low = g_ref[at, :].astype(bf16)
        buf[p.t, at, :] = low
        add_rows(sums_ref, 4, low.astype(f32))

    row_chunks(rows, lower)
    g.greet(p)
    gather.start()
    background.start()
    gather.wait_chip()
    load_out.wait()

    def mixed_back(x):
        pair_to_blocks(gm, x, mm(pair_rows(buf, x), wout[...], NT).astype(bf16))

    mixed_back(p.x)
    gather.relay()
    gather.wait_diag()
    mixed_back(1 - p.x)
    load_own.wait()
    load_kv.wait()
    limit = key_limit(g.member)
    sub = lax.broadcasted_iota(jnp.int32, (CHUNK, TOK_DEV), 0)

    for micro in range(MICRO):

        def head(pair, lanes, half, micro=micro):
            if micro == 1 and half == 0:

                @pl.when(pair == HEAD_PAIRS - 1)
                def _():
                    reduce.turn(0)

            qh = half_of(own[0, micro, :, lanes], half)
            gh = half_of(gm[micro, :, lanes], half)
            lse = lse_ref[micro, pair, half : half + 1, :]

            def first(c, load, inner):
                s = jnp.where(sub + c * CHUNK <= limit, mm(load(0), qh, NT), -1e30)
                e = jnp.exp(s - lse)
                dp = mm(load(1), gh, NT)
                p_ref[chunk_at(c), :] = e
                dp_ref[chunk_at(c), :] = dp
                return inner + fold(e * dp, jnp.sum)

            inner = over_keys(
                first,
                lambda c, i: kv[c, micro, i, :, lanes],
                lambda c, i: own[1 + i, micro, chunk_at(c, PROMPT_DEV), lanes],
                jnp.zeros((8, TOK_DEV), f32),
            )
            inner = jnp.sum(inner, axis=0, keepdims=True)

            def second(c, put):
                e = p_ref[chunk_at(c), :]
                ds = (e * (dp_ref[chunk_at(c), :] - inner)).astype(bf16)
                ds_ref[chunk_at(c), :] = ds
                put(0, mm(ds, qh))
                put(1, mm(e.astype(bf16), gh))

            @pl.loop(0, PROMPT_CHUNKS)
            def _(c):
                def put(i, value):
                    at = (micro, c // 2, c % 2, i, slice(None), lanes)
                    if half:
                        value = value + dkv[at].astype(f32)
                    dkv[at] = value.astype(bf16)

                second(c, put)

            @pl.loop(0, CONT_CHUNKS)
            def _(c):
                def put(i, value):
                    at = (i, chunk_at(c), lanes)
                    if half:
                        value = value + dkc[at].astype(f32)
                    dkc[at] = value.astype(bf16)

                second(PROMPT_CHUNKS + c, put)

            keys = kv[:, micro, 0, :, lanes].reshape(PROMPT, 2 * HEAD)
            dq = mm(keys, ds_ref[:PROMPT, :], TN) + mm(own[1, micro, PROMPT_DEV:, lanes], ds_ref[PROMPT:, :], TN)
            at = slice(HEAD * half, HEAD * (half + 1))
            o_ref[at, :] = dq[at, :] * HEAD ** (-0.5)

        def finish(pair, lanes, micro=micro):
            @pl.when(pair == HEAD_PAIRS - 1)
            def _():
                o_ref[HEAD:, :] = jnp.zeros((HEAD, TOK_DEV), f32)

            to_slots(dqkv, micro, 0, o_ref[...].T.astype(bf16), lanes)

        head_pairs(head, finish)
        reduce.start(micro)
        for i in range(2):
            to_slots(dqkv, micro, PROMPT_DEV, dkc[i], slice((1 + i) * WIDE, (2 + i) * WIDE))

    load_mix.wait()
    columns = pl.ds(pl.multiple_of(p.t * out_step, 128), out_width)

    def outer(source, target, right, body):
        flat = right.reshape(n_tp * rows, right.shape[-1])

        def tile(at):
            left = source[:, :, at].reshape(n_tp * rows, -1)
            target[at, :] = mm(left, flat, TN).astype(bf16)

        body(D, tile)

    outer(other, stage_out, buf[:, :, columns], tiles)
    keep_out = pltpu.make_async_copy(stage_out, dout_hbm, local.at[5])
    keep_out.start()
    load_all = pltpu.make_async_copy(all_hbm, other, local.at[6])
    load_all.start()
    reduce.turn(1)
    for micro in range(MICRO):
        reduce.wait(micro)
        for i in range(2):
            to_slots(dqkv, micro, 0, reduce.total(micro, i), slice((1 + i) * WIDE, (2 + i) * WIDE))
    load_qkv.wait()

    def down(x):
        def tile(at):
            put_pair(part, x, at, mm(pair_rows(dqkv, x), wqkv[at, :], NT))

        tiles(D, tile)

    down(1 - p.x)
    scatter.far_to_core().start()
    scatter.send_over()
    down(p.x)
    scatter.near_to_core().start()
    load_all.wait()
    outer(other, stage, dqkv[...], tiles)
    keep_qkv = pltpu.make_async_copy(stage, dqkv_hbm, local.at[7])
    keep_qkv.start()
    cols_ref[...] = jnp.zeros_like(cols_ref)

    @pl.loop(0, n_tp * rows // ROW_CHUNK)
    def _(i):
        per = rows // ROW_CHUNK
        at = pl.ds(pl.multiple_of((i % per) * ROW_CHUNK, ROW_CHUNK), ROW_CHUNK)
        add_rows(cols_ref, 0, dqkv[i // per, at, :].astype(f32))

    scatter.wait()

    def final(at):
        dy = scatter.rows(at)
        dx, d_gain = norm_back(x_ref[at, :], dy, vec_ref[0:1, :])
        add_rows(sums_ref, 0, d_gain)
        add_rows(sums_ref, 1, dy)
        out_ref[at, :] = g_ref[at, :] + dx

    row_chunks(rows, final)
    gather.finish()
    scatter.finish()
    for micro in range(MICRO):
        reduce.finish(micro)
    keep_out.wait()
    keep_qkv.wait()
    background.finish()


def attn_bwd(grad, x, vecs, lse, all_rows, own, kv, mixed_all, w_a, w_out, out_width, n_tp, payload, collective_id):
    rows = x.shape[0]
    pieces = (MICRO, 4, 2, 2, PROMPT_DEV, WIDE)
    return pl.pallas_call(
        functools.partial(attn_bwd_kernel, tuple(kind for kind, _ in payload)),
        out_shape=(
            jax.ShapeDtypeStruct((rows, D), f32),
            jax.ShapeDtypeStruct((8, D), f32),
            jax.ShapeDtypeStruct((1, 3 * WIDE), f32),
            jax.ShapeDtypeStruct((D, 3 * WIDE), bf16),
            jax.ShapeDtypeStruct((D, out_width), bf16),
        )
        + sent_shapes(payload),
        in_specs=[IN_VMEM] * 4 + [ANY] * (6 + len(payload)),
        out_specs=(IN_VMEM, IN_VMEM, IN_VMEM) + (ANY,) * (2 + len(payload)),
        scratch_shapes=[
            pltpu.VMEM((D, 3 * WIDE), bf16),
            pltpu.VMEM((WIDE, D), bf16),
            pltpu.VMEM((n_tp, rows, D), bf16),
            pltpu.VMEM((n_tp, rows, D), bf16),
            pltpu.VMEM((3, MICRO, TOK_DEV, WIDE), bf16),
            pltpu.VMEM((GROUP, MICRO, 2, PROMPT_DEV, WIDE), bf16),
            pltpu.VMEM((MICRO, TOK_DEV, WIDE), bf16),
            pltpu.VMEM(pieces, bf16),
            pltpu.VMEM((MICRO, 4, 2, PROMPT_DEV, WIDE), bf16),
            pltpu.VMEM((MICRO, 4, 2, PROMPT_DEV, WIDE), bf16),
            pltpu.VMEM((MICRO, 3, 2, PROMPT_DEV, WIDE), bf16),
            pltpu.VMEM((2, CONT_LEN, WIDE), bf16),
            pltpu.VMEM((n_tp, rows, 3 * WIDE), bf16),
            pltpu.VMEM((D, 3 * WIDE), bf16),
            pltpu.VMEM((D, out_width), bf16),
            pltpu.VMEM((KEYS, TOK_DEV), f32),
            pltpu.VMEM((KEYS, TOK_DEV), f32),
            pltpu.VMEM((KEYS, TOK_DEV), bf16),
            pltpu.VMEM((2 * HEAD, TOK_DEV), f32),
        ]
        + scatter_scratch(n_tp, rows)
        + [
            pltpu.SemaphoreType.DMA((4 * MICRO,)),
            pltpu.SemaphoreType.DMA((4 * MICRO,)),
            pltpu.SemaphoreType.DMA((8,)),
        ]
        + sent_scratch(payload),
        compiler_params=params(collective_id),
        cost_estimate=pl.CostEstimate(flops=2 * 10**11, bytes_accessed=50 * 2**20, transcendentals=0),
    )(grad, x, vecs, lse, all_rows, own, kv, mixed_all, w_a, w_out, *(a for _, a in payload))


def send_kernel(kinds, *refs):
    n = len(kinds)
    g = Group()
    background = Background(g, kinds, refs[:n], refs[n : 2 * n], refs[2 * n :])
    barrier = pltpu.get_barrier_semaphore()
    others = []
    if "y" in kinds:
        others += [g.at(g.z, 1 - g.y)]
    if "z" in kinds:
        others += [g.at(g.ahead(k), g.y) for k in (1, 2, 3)]
    for member in others:
        pl.semaphore_signal(barrier, inc=1, device_id=(g.base + member, g.t), device_id_type=MESH)
    pl.semaphore_wait(barrier, len(others))
    background.start()
    background.finish()


def send_only(payload, collective_id):
    return pl.pallas_call(
        functools.partial(send_kernel, tuple(kind for kind, _ in payload)),
        out_shape=sent_shapes(payload),
        in_specs=[ANY] * len(payload),
        out_specs=(ANY,) * len(payload),
        scratch_shapes=sent_scratch(payload),
        compiler_params=params(collective_id),
    )(*(a for _, a in payload))


def forward_layer(x, layer, weights, vecs, fc_bias, cols, n_tp):
    w_a, w_out, w_b = weights
    width = D - HEADS // n_tp * HEAD * (n_tp - 1)
    query_bias, value_bias = (lax.dynamic_slice_in_dim(vecs[i], cols, width) for i in (2, 3))
    biases = widen(jnp.stack([query_bias, jnp.zeros_like(query_bias), value_bias]))
    x_mid, lse, all_rows, own, kv, mixed = attn_fwd(x, vecs, biases, w_a, w_out, n_tp, 5 + layer)
    x_next, second_all, hidden_pre, hidden = ff_fwd(x_mid, vecs, fc_bias[None], w_b, n_tp)
    mixed_all = heads_joined(lax.all_gather(mixed[:, :, :width], "tp"), n_tp)
    return x_next, (x, lse, all_rows, own, kv, mixed_all, x_mid, second_all, hidden_pre, hidden)


def fsdp_sum(part):
    return lax.psum_scatter(part, "fsdp", scatter_dimension=0, tiled=True).astype(f32)


def heads_joined(parts, n_tp):
    step = HEADS // n_tp * HEAD
    return jnp.concatenate([parts[t][..., :step] for t in range(n_tp - 1)] + [parts[n_tp - 1]], axis=-1)


def widen(value, axis=-1):
    pads = [(0, 0)] * value.ndim
    pads[axis] = (0, WIDE - value.shape[axis])
    return jnp.pad(value, pads)


def to_y(part):
    return ("y", part.reshape(4, 2, -1, part.shape[1]))


def to_z(part, arrived):
    own = lax.dynamic_index_in_dim(part.reshape(4, 2, -1, part.shape[1]), lax.axis_index("fsdp") % 2, 1, False)
    return ("z", (own.astype(f32) + arrived.astype(f32)).astype(bf16))


def owned(summed, arrived):
    own = lax.dynamic_index_in_dim(summed[1], lax.axis_index("fsdp") // 2, 0, False)
    return own.astype(f32) + jnp.sum(arrived.astype(f32), 0)


def vector_sums(ff_sums, attn_sums, col_sums, fc_bias_sums, cols, width):
    def placed(part):
        return lax.dynamic_update_slice_in_dim(jnp.zeros((D,), f32), part, cols, 0)

    vector_grads = jnp.stack(
        [
            attn_sums[0],
            attn_sums[1],
            placed(col_sums[0, :width]),
            placed(col_sums[0, 2 * WIDE : 2 * WIDE + width]),
            attn_sums[4],
            ff_sums[5],
            ff_sums[6],
            ff_sums[7],
        ]
    )
    vector_sum = lax.psum(lax.psum_scatter(vector_grads, "fsdp", scatter_dimension=1, tiled=True), "tp")
    return vector_sum, lax.psum_scatter(fc_bias_sums[0], "fsdp", scatter_dimension=0, tiled=True)


def backward(grad, weights, vecs, saves, cols, n_tp):
    width = D - HEADS // n_tp * HEAD * (n_tp - 1)
    staged = lax.axis_size("fsdp") == GROUP
    sums = [None] * LAYERS
    parts = [None] * LAYERS
    waiting_y, waiting_z, done = [], [], {}

    def load(limit_z, limit_y):
        chosen_z = [waiting_z.pop(0) for _ in range(min(limit_z, len(waiting_z)))]
        chosen_y = [waiting_y.pop(0) for _ in range(min(limit_y, len(waiting_y)))]
        return chosen_z, chosen_y, [item for _, item in chosen_z] + [to_y(part) for _, part in chosen_y]

    def unload(chosen_z, chosen_y, arrived):
        for (name, item), got in zip(chosen_z, arrived):
            done[name] = owned(item, got)
        for (name, part), got in zip(chosen_y, arrived[len(chosen_z) :]):
            waiting_z.append((name, to_z(part, got)))

    def produced(layer, names, values):
        for name, value in zip(names, values):
            if staged:
                waiting_y.append(((layer, name), value))
            else:
                done[layer, name] = fsdp_sum(value)

    plan = {(1, 0): (0, 0), (1, 1): (0, 2), (0, 0): (1, 2), (0, 1): (3, 2)}
    for layer in reversed(range(LAYERS)):
        w_a, w_out, w_b = weights[layer]
        x, lse, all_rows, own, kv, mixed_all, x_mid, second_all, hidden_pre, hidden = saves[layer]
        chosen_z, chosen_y, payload = load(*plan[layer, 0])
        grad, ff_sums, fc_bias_sums, grad_fc, grad_proj, *arrived = ff_bwd(
            grad, x_mid, vecs[layer], second_all, hidden_pre, hidden, w_b, n_tp, payload, 10 + layer
        )
        unload(chosen_z, chosen_y, arrived)
        produced(layer, ("proj", "fc"), (grad_proj, grad_fc))
        chosen_z, chosen_y, payload = load(*plan[layer, 1])
        grad, attn_sums, col_sums, grad_qkv, grad_out, *arrived = attn_bwd(
            grad, x, vecs[layer], lse, all_rows, own, kv, mixed_all, w_a, w_out, width, n_tp, payload, 20 + layer
        )
        unload(chosen_z, chosen_y, arrived)
        produced(layer, ("qkv", "out"), (grad_qkv, grad_out))
        parts[layer] = (ff_sums, attn_sums, col_sums, fc_bias_sums)
    number = 30
    while waiting_y or waiting_z:
        chosen_z, chosen_y, payload = load(9, 9)
        unload(chosen_z, chosen_y, send_only(payload, number))
        number += 1
    for layer in range(LAYERS):
        vector_sum, fc_bias_sum = vector_sums(*parts[layer], cols, width)
        qkv_all = lax.all_gather(done[layer, "qkv"].astype(bf16).reshape(-1, 3, WIDE)[:, :, :width], "tp")
        out_all = lax.all_gather(done[layer, "out"].astype(bf16), "tp")
        qkv_grad = heads_joined(qkv_all, n_tp).reshape(-1, 3 * D).astype(f32)
        out_grad = heads_joined(out_all, n_tp).astype(f32)
        sums[layer] = (qkv_grad, out_grad, done[layer, "fc"], done[layer, "proj"].T, fc_bias_sum, vector_sum)
    return grad, sums


def local(
    tokens,
    qkv_weight,
    query_bias,
    value_bias,
    out_weight,
    out_bias,
    fc_weight,
    fc_bias,
    proj_weight,
    proj_bias,
    first_gain,
    first_bias,
    second_gain,
    second_bias,
    out_grad,
):
    n_tp = lax.axis_size("tp")
    tp = lax.axis_index("tp")
    row_count = tokens.shape[1]
    step = HEADS // n_tp * HEAD
    width = D - step * (n_tp - 1)
    cols = tp * step
    keep = (lax.iota(jnp.int32, width) < step) | (tp == n_tp - 1)

    def gathered(part):
        return lax.all_gather(part, "fsdp", axis=0, tiled=True)

    vectors = jnp.stack(
        [first_gain, first_bias, query_bias, value_bias, out_bias, second_gain, second_bias, proj_bias, fc_bias[:, 0]]
    ).reshape(9 * LAYERS, -1)

    weights = []
    for layer in range(LAYERS):
        sides = [widen(lax.dynamic_slice_in_dim(qkv_weight[layer], cols + i * D, width, 1)) for i in range(3)]
        sides.append(widen(lax.dynamic_slice_in_dim(out_weight[layer], cols, width, 1)))
        if layer == 0:
            sides.append(jnp.pad(vectors.T, ((0, 0), (0, 128 - 9 * LAYERS))))
        w_a = gathered(jnp.concatenate(sides, axis=1))
        if layer == 0:
            vectors = w_a[:, 4 * WIDE : 4 * WIDE + 9 * LAYERS].T.astype(f32).reshape(9, LAYERS, D)
        out_cols = w_a[:, 3 * WIDE : 3 * WIDE + width]
        out_parts = jnp.stack([out_cols[t * step : t * step + width] for t in range(n_tp)])
        w_out = heads_joined(lax.all_to_all(out_parts, "tp", 0, 0), n_tp)
        w_out = widen(jnp.where(keep[:, None], w_out, jnp.zeros_like(w_out)), 0)
        fc, proj = fc_weight[layer], proj_weight[layer].T
        more = ((0, 0), (0, lanes_up(fc.shape[1]) - fc.shape[1]))
        w_b = gathered(jnp.concatenate([jnp.pad(fc, more), jnp.pad(proj, more)], axis=1))
        weights.append((w_a, w_out, w_b))

    state = tokens.astype(f32).reshape(MICRO * row_count, D)
    saves = []
    for layer in range(LAYERS):
        state, saved = forward_layer(
            state, layer, weights[layer], vectors[:8, layer], vectors[8, layer], cols, n_tp
        )
        saves.append(saved)
    out_tokens = state.astype(bf16).reshape(tokens.shape)
    grad = out_grad.astype(f32).reshape(MICRO * row_count, D)
    grad, sums = backward(
        grad, weights, [vectors[:8, layer] for layer in range(LAYERS)], saves, cols, n_tp
    )
    qkv_g, out_g, fc_g, proj_g, fc_bias_g, vec_g = (
        jnp.stack([sums[layer][i] for layer in range(LAYERS)]) for i in range(6)
    )
    return (
        out_tokens,
        grad.reshape(tokens.shape),
        qkv_g,
        vec_g[:, 2],
        vec_g[:, 3],
        out_g,
        vec_g[:, 4],
        fc_g,
        fc_bias_g[:, None],
        proj_g,
        vec_g[:, 7],
        vec_g[:, 0],
        vec_g[:, 1],
        vec_g[:, 5],
        vec_g[:, 6],
    )


def solution(mesh):
    rows = P(None, ("fsdp", "tp"), None)
    weight = P(None, "fsdp", None)
    vector = P(None, "fsdp")
    fc_in = P(None, "fsdp", "tp")
    hidden = P(None, "tp", "fsdp")
    in_specs = (
        rows, weight, vector, vector, weight, vector, fc_in, hidden, hidden,
        vector, vector, vector, vector, vector, rows,
    )
    out_specs = (
        rows, rows, weight, vector, vector, weight, vector, fc_in, hidden, hidden,
        vector, vector, vector, vector, vector,
    )
    return jax.shard_map(local, mesh=mesh, in_specs=in_specs, out_specs=out_specs, check_vma=False)
```

time: 2230 us -> 1750 us (0.78)
  waiting for transfers between devices: 1250 us -> 280 us
  Pallas kernels: 419 us -> 1240 us
  local copies, waits for them, and re-layouts: 235 us -> 84.7 us
  matrix products: 60.1 us -> 0 us
  starting transfers between devices: 69.4 us -> 11.2 us
  other arithmetic: 116 us -> 78.7 us
  blocking collectives: 58.6 us -> 29.5 us
    pallas_call x6 -> x8, Pallas kernels: 329 us -> 1120 us  [the longest x2 434 us: attn_bwd(): pl.pallas_call(functools.partial(attn_bwd_kernel, tuple((kind for kind, _...]
    unnamed x28 -> x10, waiting for transfers between devices: 596 us -> 37.7 us
    ppermute x38 -> x0, waiting for transfers between devices: 432 us -> none  [swapped(): return lax.ppermute(value, axis, pairs)]
    all_gather x8 -> x4, waiting for transfers between devices: 118 us -> 194 us  [gathered(): return lax.all_gather(part, 'fsdp', axis=0, tiled=True)]
    reduce_scatter x2 -> x0, waiting for transfers between devices: 65.7 us -> none  [fsdp_sum(): lax.psum_scatter(part.astype(bf16), 'fsdp', scatter_dimension=0, tiled=True)]
    dot_general x12 -> x0, matrix products: 60.1 us -> none  [mm(): return lax.dot_general(left, right, dims, preferred_element_type=f32)]
    ppermute x38 -> x0, starting transfers between devices: 59.1 us -> none  [swapped(): return lax.ppermute(value, axis, pairs)]
    gather x12 -> x0, local copies, waits for them, and re-layouts: 46.5 us -> none  [by_offset(): return jnp.take(stacked, index ^ jnp.arange(stacked.shape[0]), axis=0)]
  transfers between devices with their start and end apart: 61 -> 11, of which waited for: 41 -> 6; matrix products, arithmetic and copies ran while one was open for 16% -> 4% of each run, Pallas kernels for 14% -> 31%
where the time goes in v3:
time: 1750 us; the launch traced here: 1740 us
  Pallas kernels  1240 us (71%)
  waiting for transfers between devices  280 us (16%)
  local copies, waits for them, and re-layouts  84.7 us (5%)
  other arithmetic  78.7 us (4%)
  blocking collectives  29.5 us (2%)
    pallas_call x2, Pallas kernels, attn_bwd(): pl.pallas_call(functools.partial(attn_bwd_kernel, tuple((kind for kind, _...  434 us
    pallas_call x2, Pallas kernels, attn_fwd(): pl.pallas_call(attn_fwd_kernel, out_shape=(jax.ShapeDtypeStruct((rows, D)...  359 us
    all_gather x4, waiting for transfers between devices, gathered(): return lax.all_gather(part, 'fsdp', axis=0, tiled=True)  194 us
    pallas_call x2, Pallas kernels, send_only(): pl.pallas_call(functools.partial(send_kernel, tuple((kind for kind, _ in...  190 us
    pallas_call x2, Pallas kernels, ff_bwd(): pl.pallas_call(functools.partial(ff_bwd_kernel, tuple((kind for kind, _ i...  134 us
    pallas_call x2, Pallas kernels, ff_fwd(): pl.pallas_call(ff_fwd_kernel, out_shape=(jax.ShapeDtypeStruct((rows, D),...  123 us
    unnamed x10, waiting for transfers between devices  37.7 us
  transfers between devices with their start and end apart: 11, of which 6 were waited for; matrix products, arithmetic and copies ran while one was open for 4% of the time, Pallas kernels for 31%

profile of v3, /device:TPU:9, one launch (start us, length us, event | category | flops | bytes accessed | tf_op | source)
XLA Modules:
  0.0 1739.5 jit_solution(12365139121833032525)
XLA Ops:
  7.2 3.7 fusion.34
  13.3 1.8 dynamic-slice_bitcast_fusion.3
  18.9 2.2 slice_bitcast_fusion.1
  23.6 93.8 %all-gather.17.cloned.1.call-done.wqkv_hbm.refs_8_ = bf16[1600,2048]{1,0:T(8,128)(2,1)} async-done(((bf16[200,2048]{1,0:T(8,128)(2,1)}), bf16[1600,2048]{1,0:T(8,128)(2,1)}) %all-gather.17.cloned.1.call-update) | async-done | bytes 6553616 | tf_op jit(solution)/shard_map/all_gather | solution.py:1264
  120.5 5.0 all-to-all-start.1
  125.5 100.3 %all-gather.13.cloned.1.call-done.wqkv_hbm.refs_8_ = bf16[1600,2176]{1,0:T(8,128)(2,1)} async-done(((bf16[200,2176]{1,0:T(8,128)(2,1)}), bf16[1600,2176]{1,0:T(8,128)(2,1)}) %all-gather.13.cloned.1.call-update) | async-done | bytes 6963216 | tf_op jit(solution)/shard_map/all_gather | solution.py:1264
  231.1 5.6 all-to-all-start
  239.3 19.5 %all-to-all-done = bf16[4,448,448]{2,1,0:T(8,128)(2,1)} async-done(((bf16[4,448,448]{2,1,0:T(8,128)(2,1)}), bf16[4,448,448]{2,1,0:T(8,128)(2,1)}, u32[]{:S(2)}, u32[]{:S(2)}) %all-to-all-start) | async-done | bytes 1605664 | tf_op jit(solution)/shard_map/all_to_all | solution.py:1281
  258.8 1.6 slice_bitcast_fusion.15
  262.8 181.4 %shard_map.262 = (f32[192,1600]{1,0:T(8,128)}, f32[2,4,8,384]{3,2,1,0:T(8,128)}, bf16[4,192,1600]{2,1,0:T(8,128)(2,1)}, bf16[3,2,384,512]{3,2,1,0:T(8,128)(2,1)}...) custom-call(f32[192,1600]{1,0:T(8,128)} %bitcast_convert_fusion.1.x_ref.refs_1_, ...), custom_call_target="tpu_custom_call" | custom-call | flops 99999997952 | bytes 31457280 | tf_op jit(solution)/shard_map/pallas_call | solution.py:827
  448.3 62.0 %shard_map.263 = (f32[192,1600]{1,0:T(8,128)}, bf16[4,192,1600]{2,1,0:T(8,128)(2,1)}, f32[4,192,1600]{2,1,0:T(8,128)}, bf16[4,192,1600]{2,1,0:T(8,128)(2,1)}) custom-call(f32[192,1600]{1,0:T(8,128)} %get-tuple-element.71.x_ref.refs_1_, f32[8,1600]{1,0:T(8,128)} %bitcast.265, f32[1,1600]{1,0:T(1,128)} %get-tuple-element.186.fcb_ref, ...), custom_call_target="tpu_custom_call" | custom-call | flops 7864320000 | bytes 41943040 | tf_op jit(solution)/shard_map/pallas_call | solution.py:347
  510.3 177.7 %shard_map.264 = (f32[192,1600]{1,0:T(8,128)}, f32[2,4,8,384]{3,2,1,0:T(8,128)}, bf16[4,192,1600]{2,1,0:T(8,128)(2,1)}, bf16[3,2,384,512]{3,2,1,0:T(8,128)(2,1)}...) custom-call(f32[192,1600]{1,0:T(8,128)} %get-tuple-element.72.x_ref.refs_1_, f32[8,1600]{1,0:T(8,128)} %bitcast.268, ...), custom_call_target="tpu_custom_call" | custom-call | flops 99999997952 | bytes 31457280 | tf_op jit(solution)/shard_map/pallas_call | solution.py:827
  690.5 1.7 fusion.35
  692.2 2.0 pad_maximum_fusion.3.refs_7_
  694.2 60.6 %shard_map.265 = (f32[192,1600]{1,0:T(8,128)}, bf16[4,192,1600]{2,1,0:T(8,128)(2,1)}, f32[4,192,1600]{2,1,0:T(8,128)}, bf16[4,192,1600]{2,1,0:T(8,128)(2,1)}) custom-call(f32[192,1600]{1,0:T(8,128)} %get-tuple-element.73.x_ref.refs_1_, f32[8,1600]{1,0:T(8,128)} %bitcast.269, f32[1,1600]{1,0:T(1,128)} %get-tuple-element.183.fcb_ref, ...), custom_call_target="tpu_custom_call" | custom-call | flops 7864320000 | bytes 41943040 | tf_op jit(solution)/shard_map/pallas_call | solution.py:347
  754.8 2.2 convert_element_type.248
  757.0 54.9 %shard_map.266 = (f32[192,1600]{1,0:T(8,128)}, f32[8,1600]{1,0:T(8,128)}, f32[1,1600]{1,0:T(1,128)}, bf16[1600,1600]{1,0:T(8,128)(2,1)}, bf16[1600,1600]{1,0:T(8,128)(2,1)}) custom-call(f32[192,1600]{1,0:T(8,128)} %bitcast_convert_fusion.refs_0_, f32[192,1600]{1,0:T(8,128)} %get-tuple-element.73.x_ref.refs_1_, f32[8,1600]{1,0:T(8,128)} %bitcast.270, ...), custom_call_target="tpu_custom_call" | custom-call | flops 15728640000 | bytes 52428800 | tf_op jit(solution)/shard_map/pallas_call | solution.py:503
  814.6 1.7 fusion.36
  816.3 1.6 pad_maximum_fusion.2.refs_7_
  817.9 215.3 %shard_map.267 = (f32[192,1600]{1,0:T(8,128)}, f32[8,1600]{1,0:T(8,128)}, f32[1,1536]{1,0:T(1,128)}, bf16[1600,1536]{1,0:T(8,128)(2,1)}, bf16[1600,448]{1,0:T(8,...) custom-call(f32[192,1600]{1,0:T(8,128)} %get-tuple-element.78.refs_0_, ...), custom_call_target="tpu_custom_call" | custom-call | flops 199999995904 | bytes 52428800 | tf_op jit(solution)/shard_map/pallas_call | solution.py:1048
  1033.3 4.9 fusion.3.refs_7_
  1039.1 2.3 fusion.2.refs_10_
  1041.4 79.1 %shard_map.268 = (f32[192,1600]{1,0:T(8,128)}, f32[8,1600]{1,0:T(8,128)}, f32[1,1600]{1,0:T(1,128)}, bf16[1600,1600]{1,0:T(8,128)(2,1)}, bf16[1600,1600]{1,0:T(8...) custom-call(f32[192,1600]{1,0:T(8,128)} %get-tuple-element.86.refs_0_, ...), custom_call_target="tpu_custom_call" | custom-call | flops 15728640000 | bytes 52428800 | tf_op jit(solution)/shard_map/pallas_call | solution.py:503
  1120.5 4.7 fusion.5.refs_11_
  1126.3 218.8 %shard_map.269 = (f32[192,1600]{1,0:T(8,128)}, f32[8,1600]{1,0:T(8,128)}, f32[1,1536]{1,0:T(1,128)}, bf16[1600,1536]{1,0:T(8,128)(2,1)}, bf16[1600,448]{1,0:T(8,...) custom-call(f32[192,1600]{1,0:T(8,128)} %get-tuple-element.93.refs_0, ...), custom_call_target="tpu_custom_call" | custom-call | flops 199999995904 | bytes 52428800 | tf_op jit(solution)/shard_map/pallas_call | solution.py:1048
  1350.2 1.9 convert_reduce_fusion.4
  1353.0 2.2 dynamic-slice_convert_fusion
  1355.3 2.5 reshape.326
  1359.2 4.8 fusion.1.refs_0_
  1364.1 3.9 fusion.refs_1_
  1368.0 117.1 %shard_map.270 = (bf16[3,200,1600]{2,1,0:T(8,128)(2,1)}, bf16[3,200,1600]{2,1,0:T(8,128)(2,1)}, bf16[4,200,1536]{2,1,0:T(8,128)(2,1)}, bf16[4,200,448]{2,1,0:T(8,128)(2,1)}) custom-call(bf16[4,200,1600]{2,1,0:T(8,128)(2,1)} %fusion.1.refs_0_, bf16[4,200,1600]{2,1,0:T(8,128)(2,1)} %fusion.refs_1_, bf16[4,2,200,1536]{3,2,1,0:T(8,128)(2,1)} %bitcast.243, ...), custom_call_target="tpu_custom_call" | custom-call | tf_op jit(solution)/shard_map/pallas_call | solution.py:1111
  1485.2 3.2 fusion.4.refs_0_
  1491.0 72.4 %shard_map.271 = (bf16[3,200,1536]{2,1,0:T(8,128)(2,1)}, bf16[3,200,448]{2,1,0:T(8,128)(2,1)}) custom-call(bf16[4,200,1536]{2,1,0:T(8,128)(2,1)} %copy-done, bf16[4,200,448]{2,1,0:T(8,128)(2,1)} %fusion.12.refs_1_), custom_call_target="tpu_custom_call" | custom-call | tf_op jit(solution)/shard_map/pallas_call | solution.py:1111
  1563.5 1.9 convert_reduce_fusion.5
  1566.3 2.4 reshape.324
  1572.9 9.0 all_gather.57
  1596.1 3.0 convert_reduce_fusion
  1604.4 8.9 all_gather.56
  1617.9 1.7 pad_maximum_fusion
  1623.6 1.7 pad_maximum_fusion.1
  1625.3 1.7 maximum_convert_fusion.1
  1627.0 37.6 %all-reduce.25.cloned.1.call-done = (f32[8,1600]{1,0:T(8,128)}, f32[8,1600]{1,0:T(8,128)}, f32[1600]{0:T(1024)}, f32[1600]{0:T(1024)}) async-done(((f32[8,1600]{1,0:T(8,128)}, f32[8,1600]{1,0:T(8,128)}, f32[1600]{0:T(1024)}, f32[1600]{0:T(1024)}), (f32[8,1600]{1,0:T(8,128)}, f32[8,1600]{1,0:T(8,128)}, f32[1600]{0:T(1024)}, f32[1600]{0:T(1024)})) %all-reduce.25.cloned.1.call-update) | async-done | bytes 115216
  1666.1 11.6 all-reduce.22
  1684.5 8.3 all-gather.27.cloned.1.call-done
  1695.5 3.3 convert_element_type.290
  1698.9 20.8 %all-gather.25.cloned.1.call-done = bf16[800,3,448]{2,0,1:T(8,128)(2,1)} async-done(((bf16[200,3,448]{2,0,1:T(8,128)(2,1)}), bf16[800,3,448]{2,0,1:T(8,128)(2,1)}) %all-gather.25.cloned.1.call-update) | async-done | bytes 2150416 | tf_op jit(solution)/shard_map/all_gather | solution.py:1230
  1722.4 3.4 convert_element_type.285
  1725.8 5.9 maximum_convert_fusion
  (253 shorter events, 90.0 us)
Async XLA Ops:
  7.2 110.2 %all-gather.17.cloned.1.call-start = ((), (), s32[]{:S(2)}) async-start(), calls=%async_computation.4 | async-start | bytes 7372800 | tf_op jit(solution)/shard_map/all_gather | solution.py:1264
  7.2 3.8 copy-start.13
  13.2 3.0 copy-start.37
  13.2 3.0 copy-start.38
  13.2 3.0 copy-start.39
  13.3 3.0 copy-start.40
  13.3 3.0 copy-start.41
  13.3 3.0 copy-start.42
  13.3 3.0 copy-start.43
  13.3 3.1 copy-start.44
  13.3 3.1 copy-start.45
  15.1 3.7 copy-start.14
  16.1 209.7 %all-gather.13.cloned.1.call-start = ((), (), s32[]{:S(2)}) async-start(), calls=%async_computation.2 | async-start | bytes 7833600 | tf_op jit(solution)/shard_map/all_gather | solution.py:1264
  18.7 429.5 %all-gather.15.cloned.1.call-start = ((), (), s32[]{:S(2)}) async-start(), calls=%async_computation.3 | async-start | bytes 11980800 | tf_op jit(solution)/shard_map/all_gather | solution.py:1264
  120.5 110.6 %all-to-all-start.1 = ((bf16[4,448,448]{2,1,0:T(8,128)(2,1)}), bf16[4,448,448]{2,1,0:T(8,128)(2,1)S(1)}, u32[]{:S(2)}, u32[]{:S(2)}) async-start(bf16[4,448,448]{2,1,0:T(8,128)(2,1)} %pad_maximum_fusion.7), calls=%async_computation.1 | async-start | bytes 3670016 | tf_op jit(solution)/shard_map/all_to_all | solution.py:1281
  231.1 27.8 %all-to-all-start = ((bf16[4,448,448]{2,1,0:T(8,128)(2,1)}), bf16[4,448,448]{2,1,0:T(8,128)(2,1)}, u32[]{:S(2)}, u32[]{:S(2)}) async-start(bf16[4,448,448]{2,1,0:T(8,128)(2,1)} %pad_maximum_fusion.6), calls=%async_computation | async-start | bytes 3670016 | tf_op jit(solution)/shard_map/all_to_all | solution.py:1281
  236.7 453.8 %all-gather.23.cloned.1.call-start = ((), (), s32[]{:S(2)}) async-start(), calls=%async_computation.7 | async-start | bytes 3932160 | tf_op jit(solution)/shard_map/all_gather | solution.py:1128
  258.8 1.8 copy-start.11
  262.8 181.4 %copy-start.7 = (bf16[200,1600]{1,0:T(8,128)(2,1)S(1)}, bf16[200,1600]{1,0:T(8,128)(2,1)}, u32[]{:S(2)}) copy-start(bf16[200,1600]{1,0:T(8,128)(2,1)} %get-tuple-element.169) | copy-start | bytes 1920004
  444.2 250.0 %all-gather.19.cloned.1.call-start = ((), (), s32[]{:S(2)}) async-start(), calls=%async_computation.5 | async-start | bytes 11980800 | tf_op jit(solution)/shard_map/all_gather | solution.py:1264
  445.5 369.1 %all-gather.21.cloned.1.call-start = ((), (), s32[]{:S(2)}) async-start(), calls=%async_computation.6 | async-start | bytes 3932160 | tf_op jit(solution)/shard_map/all_gather | solution.py:1128
  510.3 177.8 %copy-start.46 = (u32[32]{0:T(128)S(1)}, u32[32]{0:T(128)}, u32[]{:S(2)}) copy-start(u32[32]{0:T(128)} %constant.183) | copy-start | bytes 388
  510.3 179.1 %copy-start.20 = (bf16[2,96,1600]{2,1,0:T(8,128)(2,1)S(1)}, bf16[2,96,1600]{2,1,0:T(8,128)(2,1)}, u32[]{:S(2)}) copy-start(bf16[2,96,1600]{2,1,0:T(8,128)(2,1)} %param.29) | copy-start | bytes 1843204
  688.0 976.6 %all-reduce.25.cloned.1.call-start = ((), (), s32[]{:S(2)}) async-start(), calls=%async_computation.10 | async-start | bytes 245760
  1033.2 4.9 copy-start.6
  1033.3 5.9 copy-start.12
  1120.5 4.7 copy-start.17
  1120.5 4.7 copy-start.31
  1359.2 4.9 copy-start.5
  1485.2 3.3 copy-start.4
  1485.2 3.3 copy-start.18
  1488.4 2.6 copy-start
  1565.4 3.3 copy-start.36
  1565.4 3.9 copy-start.33
  1565.4 3.9 copy-start.35
  1565.4 4.5 copy-start.34
  1570.6 12.2 copy-start.9
  1581.9 2.2 copy-start.10
  1584.1 10.5 copy-start.32
  1596.1 96.7 %all-gather.27.cloned.1.call-start = ((), (), s32[]{:S(2)}) async-start(), calls=%async_computation.9 | async-start | bytes 3072000 | tf_op jit(solution)/shard_map/all_gather | solution.py:1230
  1599.2 120.5 %all-gather.25.cloned.1.call-start = ((), (), s32[]{:S(2)}) async-start(), calls=%async_computation.8 | async-start | bytes 3072000 | tf_op jit(solution)/shard_map/all_gather | solution.py:1230
  1599.7 2.4 copy-start.22
  1599.7 3.0 copy-start.21
  1602.0 13.3 copy-start.2
  1613.3 3.3 copy-start.1
  1617.9 2.5 copy-start.8
  1623.5 1.7 copy-start.24
  1725.8 5.9 copy-start.16
  (14 other events, 21.4 us)
Sparse Core Ops, SparseCore 0:
  16.3 101.0 all-gather.16
  120.2 105.5 all-gather.12
  228.5 192.4 all-gather.14
  444.3 42.0 all-gather.22
  489.0 191.6 all-gather.18
  688.1 42.3 all-gather.20
  1596.2 68.3 all-reduce.24
  1666.2 26.5 all-gather.26
  1695.0 24.6 all-gather.24

commit v4 on v3

--- a/solution.py
+++ b/solution.py
@@ -158,16 +158,17 @@
     def behind(self, k):
         return (self.z + 4 - k) % 4
 
-    def greet(self, peers):
+    def greet(self, peers, with_diag=False):
         barrier = pltpu.get_barrier_semaphore()
         others = [self.at(self.z, 1 - self.y)] + [self.at(self.ahead(k), self.y) for k in (1, 2, 3)]
         for member in others:
             pl.semaphore_signal(
                 barrier, inc=1, device_id=(self.base + member, self.t), device_id_type=MESH
             )
-        for t in (peers.core, peers.over):
+        near = [peers.core, peers.over] + [peers.diag] * with_diag
+        for t in near:
             pl.semaphore_signal(barrier, inc=1, device_id=(peers.f, t), device_id_type=MESH)
-        pl.semaphore_wait(barrier, 6)
+        pl.semaphore_wait(barrier, 4 + len(near))
 
     def copy(self, source, target, sems, index, member):
         return pltpu.make_async_remote_copy(
@@ -181,41 +182,69 @@
 
 
 class Background:
-    def __init__(self, group, kinds, sources, targets, sems):
-        self.g, self.sems = group, sems
+    def __init__(self, group, peers, kinds, sources, targets, sems):
+        self.g, self.p, self.sems = group, peers, sems
         self.items = list(zip(kinds, sources, targets))
+
+    def block_copies(self, n, source, target):
+        p, sems = self.p, self.sems
+        return (
+            p.copy(source, target.at[p.t], sems, 4 * n, p.core),
+            p.copy(source, target.at[p.t], sems, 4 * n + 1, p.over),
+            p.copy(target.at[p.over], target.at[p.over], sems, 4 * n + 2, p.core),
+            pltpu.make_async_copy(source, target.at[p.t], sems[0].at[4 * n + 3]),
+        )
 
     def copies(self):
         g = self.g
         made = []
         for n, (kind, source, target) in enumerate(self.items):
             if kind == "y":
-                made.append(g.copy(source.at[:, 1 - g.y], target, self.sems, 3 * n, g.at(g.z, 1 - g.y)))
-            else:
+                made.append(g.copy(source.at[:, 1 - g.y], target, self.sems, 4 * n, g.at(g.z, 1 - g.y)))
+            elif kind == "z":
                 for k in (1, 2, 3):
                     to = g.ahead(k)
                     made.append(
-                        g.copy(source.at[to], target.at[k - 1], self.sems, 3 * n + k - 1, g.at(to, g.y))
+                        g.copy(source.at[to], target.at[k - 1], self.sems, 4 * n + k - 1, g.at(to, g.y))
                     )
         return made
 
     def start(self):
         for copy in self.copies():
             copy.start()
+        for n, (kind, source, target) in enumerate(self.items):
+            if kind == "t":
+                to_core, to_over, _, local = self.block_copies(n, source, target)
+                to_over.start()
+                to_core.start()
+                local.start()
 
     def finish(self):
+        p = self.p
+        for n, (kind, source, target) in enumerate(self.items):
+            if kind == "t":
+                p.copy(source, target.at[p.over], self.sems, 4 * n + 1, p.over).wait_recv()
+                self.block_copies(n, source, target)[2].start()
         for copy in self.copies():
             copy.wait()
+        for n, (kind, source, target) in enumerate(self.items):
+            if kind == "t":
+                p.copy(source, target.at[p.core], self.sems, 4 * n, p.core).wait_recv()
+                p.copy(source, target.at[p.diag], self.sems, 4 * n + 2, p.core).wait_recv()
+                to_core, to_over, relay, local = self.block_copies(n, source, target)
+                for copy in (to_core, to_over, relay):
+                    copy.wait_send()
+                local.wait()
 
 
 def sent_shapes(payload):
     return tuple(
-        jax.ShapeDtypeStruct((4 if kind == "y" else 3,) + a.shape[-2:], a.dtype) for kind, a in payload
+        jax.ShapeDtypeStruct((3 if kind == "z" else 4,) + a.shape[-2:], a.dtype) for kind, a in payload
     )
 
 
 def sent_scratch(payload):
-    return [pltpu.SemaphoreType.DMA((3 * len(payload) + 1,))] * 2
+    return [pltpu.SemaphoreType.DMA((4 * len(payload) + 1,))] * 2
 
 
 def row_chunks(rows, body):
@@ -396,7 +425,7 @@
     targets, refs = refs[5 : 5 + n], refs[5 + n :]
     wfc, wproj, buf, other, pre, dpre, stage, part, from_core, over_out, from_over, send, recv, local = refs[:14]
     p, g = Peers(), Group()
-    background = Background(g, kinds, sources, targets, refs[14:])
+    background = Background(g, p, kinds, sources, targets, refs[14:])
     rows = x_ref.shape[0]
     n_tp, width = buf.shape[0], fcb_ref.shape[1]
     sems = (send, recv)
@@ -687,29 +716,41 @@
 
 
 def attn_fwd_kernel(
-    x_ref, vec_ref, bias_ref, wqkv_hbm, wout_hbm,
-    out_ref, lse_ref, all_hbm, own_hbm, kv_hbm, mix_hbm,
-    wqkv, wout, buf, own, kv, mix, s_ref, p_ref, o_ref,
-    part, from_core, over_out, from_over, send, recv, gsend, grecv, local,
+    x_ref, vec_ref, bias_ref, wqkv_hbm,
+    out_ref, lse_ref, all_hbm, own_hbm, kv_hbm, mix_hbm, wout_hbm,
+    wqkv, wout, wparts, buf, own, kv, mix, s_ref, p_ref, o_ref,
+    part, from_core, over_out, from_over, send, recv, gsend, grecv, wsend, wrecv, local,
 ):
     p, g = Peers(), Group()
     rows = x_ref.shape[0]
+    n_tp = buf.shape[0]
+    step = HEADS // n_tp * HEAD
+    width = wparts.shape[1]
     sems = (send, recv)
     gather = Gather(p, buf, sems)
     scatter = Scatter(p, part, from_core, over_out, from_over, sems)
     share = Share(g, kv, (gsend, grecv))
     load_qkv = pltpu.make_async_copy(wqkv_hbm.at[:, : 3 * WIDE], wqkv, local.at[0])
-    load_out = pltpu.make_async_copy(wout_hbm, wout, local.at[1])
     load_qkv.start()
-    load_out.start()
+
+    def rows_for(t):
+        return wqkv_hbm.at[pl.ds(pl.multiple_of(t * step, 128), width), 3 * WIDE : 4 * WIDE]
+
+    keep_part = pltpu.make_async_copy(rows_for(p.t), wparts.at[p.t], local.at[1])
+    keep_part.start()
+    give_parts = [
+        p.copy(rows_for(t), wparts.at[p.t], (wsend, wrecv), i, t) for i, t in enumerate((p.core, p.over, p.diag))
+    ]
 
     def norm(at):
         hat, _ = norm_stats(x_ref[at, :])
         buf[p.t, at, :] = (hat * vec_ref[0:1, :] + vec_ref[1:2, :]).astype(bf16)
 
     row_chunks(rows, norm)
-    g.greet(p)
+    g.greet(p, True)
     gather.start()
+    for copy in give_parts:
+        copy.start()
     gather.wait_chip()
     load_qkv.wait()
 
@@ -785,7 +826,20 @@
     keep_mix = pltpu.make_async_copy(mix, mix_hbm, local.at[5])
     keep_kv.start()
     keep_mix.start()
-    load_out.wait()
+    keep_part.wait()
+    for i, t in enumerate((p.core, p.over, p.diag)):
+        p.copy(rows_for(t), wparts.at[t], (wsend, wrecv), i, t).wait_recv()
+    for t in range(n_tp):
+        count = min(WIDE, D - t * step)
+        wout[:width, t * step : t * step + count] = wparts[t, :, :count]
+    wout[width:, :] = jnp.zeros((WIDE - width, D), bf16)
+
+    @pl.when(p.t < n_tp - 1)
+    def _():
+        wout[step:width, :] = jnp.zeros((width - step, D), bf16)
+
+    keep_out = pltpu.make_async_copy(wout, wout_hbm, local.at[6])
+    keep_out.start()
 
     def down(x):
         def tile(at):
@@ -808,7 +862,9 @@
     scatter.finish()
     for micro in range(MICRO):
         share.finish(micro)
-    for copy in (keep_all, keep_own, keep_kv, keep_mix):
+    for copy in give_parts:
+        copy.wait_send()
+    for copy in (keep_all, keep_own, keep_kv, keep_mix, keep_out):
         copy.wait()
 
 
@@ -821,8 +877,9 @@
     )
 
 
-def attn_fwd(x, vecs, biases, w_qkv, w_out, n_tp, collective_id):
+def attn_fwd(x, vecs, biases, w_a, n_tp, collective_id):
     rows = x.shape[0]
+    width = D - HEADS // n_tp * HEAD * (n_tp - 1)
     saved = attn_shapes(n_tp, rows)
     return pl.pallas_call(
         attn_fwd_kernel,
@@ -830,10 +887,10 @@
             jax.ShapeDtypeStruct((rows, D), f32),
             jax.ShapeDtypeStruct((MICRO, HEAD_PAIRS, 8, TOK_DEV), f32),
         )
-        + tuple(jax.ShapeDtypeStruct(*s) for s in saved),
-        in_specs=[IN_VMEM, IN_VMEM, IN_VMEM, ANY, ANY],
-        out_specs=(IN_VMEM, IN_VMEM, ANY, ANY, ANY, ANY),
-        scratch_shapes=[pltpu.VMEM((D, 3 * WIDE), bf16), pltpu.VMEM((WIDE, D), bf16)]
+        + tuple(jax.ShapeDtypeStruct(*s) for s in saved + (((WIDE, D), bf16),)),
+        in_specs=[IN_VMEM, IN_VMEM, IN_VMEM, ANY],
+        out_specs=(IN_VMEM, IN_VMEM, ANY, ANY, ANY, ANY, ANY),
+        scratch_shapes=[pltpu.VMEM((D, 3 * WIDE), bf16), pltpu.VMEM((WIDE, D), bf16), pltpu.VMEM((n_tp, width, WIDE), bf16)]
         + [pltpu.VMEM(*s) for s in saved]
         + [
             pltpu.VMEM((KEYS, TOK_DEV), f32),
@@ -844,11 +901,13 @@
         + [
             pltpu.SemaphoreType.DMA((7 * MICRO,)),
             pltpu.SemaphoreType.DMA((7 * MICRO,)),
-            pltpu.SemaphoreType.DMA((6,)),
+            pltpu.SemaphoreType.DMA((3,)),
+            pltpu.SemaphoreType.DMA((3,)),
+            pltpu.SemaphoreType.DMA((7,)),
         ],
         compiler_params=params(collective_id),
         cost_estimate=pl.CostEstimate(flops=10**11, bytes_accessed=30 * 2**20, transcendentals=0),
-    )(x, vecs, biases, w_qkv, w_out)
+    )(x, vecs, biases, w_a)
 
 
 def attn_bwd_kernel(kinds, *refs):
@@ -861,7 +920,7 @@
     p_ref, dp_ref, ds_ref, o_ref = refs[15:19]
     part, from_core, over_out, from_over, send, recv, gsend, grecv, local = refs[19:28]
     p, g = Peers(), Group()
-    background = Background(g, kinds, sources, targets, refs[28:])
+    background = Background(g, p, kinds, sources, targets, refs[28:])
     rows = x_ref.shape[0]
     n_tp = buf.shape[0]
     out_width = stage_out.shape[1]
@@ -1092,8 +1151,8 @@
 
 def send_kernel(kinds, *refs):
     n = len(kinds)
-    g = Group()
-    background = Background(g, kinds, refs[:n], refs[n : 2 * n], refs[2 * n :])
+    p, g = Peers(), Group()
+    background = Background(g, p, kinds, refs[:n], refs[n : 2 * n], refs[2 * n :])
     barrier = pltpu.get_barrier_semaphore()
     others = []
     if "y" in kinds:
@@ -1102,7 +1161,10 @@
         others += [g.at(g.ahead(k), g.y) for k in (1, 2, 3)]
     for member in others:
         pl.semaphore_signal(barrier, inc=1, device_id=(g.base + member, g.t), device_id_type=MESH)
-    pl.semaphore_wait(barrier, len(others))
+    near = [p.core, p.over] if "t" in kinds else []
+    for t in near:
+        pl.semaphore_signal(barrier, inc=1, device_id=(p.f, t), device_id_type=MESH)
+    pl.semaphore_wait(barrier, len(others) + len(near))
     background.start()
     background.finish()
 
@@ -1119,14 +1181,14 @@
 
 
 def forward_layer(x, layer, weights, vecs, fc_bias, cols, n_tp):
-    w_a, w_out, w_b = weights
+    w_a, w_b = weights
     width = D - HEADS // n_tp * HEAD * (n_tp - 1)
     query_bias, value_bias = (lax.dynamic_slice_in_dim(vecs[i], cols, width) for i in (2, 3))
     biases = widen(jnp.stack([query_bias, jnp.zeros_like(query_bias), value_bias]))
-    x_mid, lse, all_rows, own, kv, mixed = attn_fwd(x, vecs, biases, w_a, w_out, n_tp, 5 + layer)
+    x_mid, lse, all_rows, own, kv, mixed, w_out = attn_fwd(x, vecs, biases, w_a, n_tp, 5 + layer)
     x_next, second_all, hidden_pre, hidden = ff_fwd(x_mid, vecs, fc_bias[None], w_b, n_tp)
     mixed_all = heads_joined(lax.all_gather(mixed[:, :, :width], "tp"), n_tp)
-    return x_next, (x, lse, all_rows, own, kv, mixed_all, x_mid, second_all, hidden_pre, hidden)
+    return x_next, (x, w_out, lse, all_rows, own, kv, mixed_all, x_mid, second_all, hidden_pre, hidden)
 
 
 def fsdp_sum(part):
@@ -1158,32 +1220,31 @@
     return own.astype(f32) + jnp.sum(arrived.astype(f32), 0)
 
 
-def vector_sums(ff_sums, attn_sums, col_sums, fc_bias_sums, cols, width):
+def with_vectors(grad_out, ff_sums, attn_sums, col_sums, fc_bias_sums, cols):
+    width = grad_out.shape[1]
+
     def placed(part):
-        return lax.dynamic_update_slice_in_dim(jnp.zeros((D,), f32), part, cols, 0)
-
-    vector_grads = jnp.stack(
+        return lax.dynamic_update_slice_in_dim(jnp.zeros((1, D), f32), part, cols, 1)
+
+    vector_grads = jnp.concatenate(
         [
-            attn_sums[0],
-            attn_sums[1],
-            placed(col_sums[0, :width]),
-            placed(col_sums[0, 2 * WIDE : 2 * WIDE + width]),
-            attn_sums[4],
-            ff_sums[5],
-            ff_sums[6],
-            ff_sums[7],
+            attn_sums[:2],
+            placed(col_sums[:, :width]),
+            placed(col_sums[:, 2 * WIDE : 2 * WIDE + width]),
+            attn_sums[4:5],
+            ff_sums[5:],
+            fc_bias_sums,
         ]
     )
-    vector_sum = lax.psum(lax.psum_scatter(vector_grads, "fsdp", scatter_dimension=1, tiled=True), "tp")
-    return vector_sum, lax.psum_scatter(fc_bias_sums[0], "fsdp", scatter_dimension=0, tiled=True)
+    return widen(jnp.concatenate([grad_out, vector_grads.astype(bf16).T], axis=1))
 
 
 def backward(grad, weights, vecs, saves, cols, n_tp):
     width = D - HEADS // n_tp * HEAD * (n_tp - 1)
     staged = lax.axis_size("fsdp") == GROUP
     sums = [None] * LAYERS
-    parts = [None] * LAYERS
-    waiting_y, waiting_z, done = [], [], {}
+    joined = [None] * LAYERS
+    waiting_y, waiting_z, waiting_t, done = [], [], [], {}
 
     def load(limit_z, limit_y):
         chosen_z = [waiting_z.pop(0) for _ in range(min(limit_z, len(waiting_z)))]
@@ -1205,8 +1266,8 @@
 
     plan = {(1, 0): (0, 0), (1, 1): (0, 2), (0, 0): (1, 2), (0, 1): (3, 2)}
     for layer in reversed(range(LAYERS)):
-        w_a, w_out, w_b = weights[layer]
-        x, lse, all_rows, own, kv, mixed_all, x_mid, second_all, hidden_pre, hidden = saves[layer]
+        w_a, w_b = weights[layer]
+        x, w_out, lse, all_rows, own, kv, mixed_all, x_mid, second_all, hidden_pre, hidden = saves[layer]
         chosen_z, chosen_y, payload = load(*plan[layer, 0])
         grad, ff_sums, fc_bias_sums, grad_fc, grad_proj, *arrived = ff_bwd(
             grad, x_mid, vecs[layer], second_all, hidden_pre, hidden, w_b, n_tp, payload, 10 + layer
@@ -1218,19 +1279,33 @@
             grad, x, vecs[layer], lse, all_rows, own, kv, mixed_all, w_a, w_out, width, n_tp, payload, 20 + layer
         )
         unload(chosen_z, chosen_y, arrived)
+        grad_out = with_vectors(grad_out, ff_sums, attn_sums, col_sums, fc_bias_sums, cols)
         produced(layer, ("qkv", "out"), (grad_qkv, grad_out))
-        parts[layer] = (ff_sums, attn_sums, col_sums, fc_bias_sums)
     number = 30
-    while waiting_y or waiting_z:
+    asked = set()
+    while len(asked) < LAYERS or waiting_t:
         chosen_z, chosen_y, payload = load(9, 9)
-        unload(chosen_z, chosen_y, send_only(payload, number))
-        number += 1
+        chosen_t, waiting_t = waiting_t, []
+        arrived = []
+        if payload or chosen_t:
+            arrived = list(send_only(payload + [("t", part) for _, part in chosen_t], number))
+            number += 1
+        unload(chosen_z, chosen_y, arrived)
+        for (layer, _), got in zip(chosen_t, arrived[len(payload) :]):
+            joined[layer] = got
+        for layer in range(LAYERS):
+            if layer not in asked and (layer, "qkv") in done and (layer, "out") in done:
+                asked.add(layer)
+                both = jnp.concatenate([done[layer, "qkv"], done[layer, "out"]], axis=1).astype(bf16)
+                waiting_t.append((layer, both))
     for layer in range(LAYERS):
-        vector_sum, fc_bias_sum = vector_sums(*parts[layer], cols, width)
-        qkv_all = lax.all_gather(done[layer, "qkv"].astype(bf16).reshape(-1, 3, WIDE)[:, :, :width], "tp")
-        out_all = lax.all_gather(done[layer, "out"].astype(bf16), "tp")
-        qkv_grad = heads_joined(qkv_all, n_tp).reshape(-1, 3 * D).astype(f32)
-        out_grad = heads_joined(out_all, n_tp).astype(f32)
+        got = joined[layer]
+        qkv_grad = jnp.concatenate(
+            [heads_joined(got[:, :, i * WIDE : i * WIDE + width], n_tp) for i in range(3)], axis=1
+        ).astype(f32)
+        out_grad = heads_joined(got[:, :, 3 * WIDE : 3 * WIDE + width], n_tp).astype(f32)
+        vector_sum = jnp.sum(got[:, :, 3 * WIDE + width : 3 * WIDE + width + 8].astype(f32), 0).T
+        fc_bias_sum = done[layer, "out"][:, width + 8]
         sums[layer] = (qkv_grad, out_grad, done[layer, "fc"], done[layer, "proj"].T, fc_bias_sum, vector_sum)
     return grad, sums
 
@@ -1258,10 +1333,15 @@
     step = HEADS // n_tp * HEAD
     width = D - step * (n_tp - 1)
     cols = tp * step
-    keep = (lax.iota(jnp.int32, width) < step) | (tp == n_tp - 1)
+
+    last = []
 
     def gathered(part):
-        return lax.all_gather(part, "fsdp", axis=0, tiled=True)
+        if last:
+            part, _ = lax.optimization_barrier((part, last.pop()))
+        whole = lax.all_gather(part, "fsdp", axis=0, tiled=True)
+        last.append(whole[:8, :128])
+        return whole
 
     vectors = jnp.stack(
         [first_gain, first_bias, query_bias, value_bias, out_bias, second_gain, second_bias, proj_bias, fc_bias[:, 0]]
@@ -1276,14 +1356,10 @@
         w_a = gathered(jnp.concatenate(sides, axis=1))
         if layer == 0:
             vectors = w_a[:, 4 * WIDE : 4 * WIDE + 9 * LAYERS].T.astype(f32).reshape(9, LAYERS, D)
-        out_cols = w_a[:, 3 * WIDE : 3 * WIDE + width]
-        out_parts = jnp.stack([out_cols[t * step : t * step + width] for t in range(n_tp)])
-        w_out = heads_joined(lax.all_to_all(out_parts, "tp", 0, 0), n_tp)
-        w_out = widen(jnp.where(keep[:, None], w_out, jnp.zeros_like(w_out)), 0)
         fc, proj = fc_weight[layer], proj_weight[layer].T
         more = ((0, 0), (0, lanes_up(fc.shape[1]) - fc.shape[1]))
         w_b = gathered(jnp.concatenate([jnp.pad(fc, more), jnp.pad(proj, more)], axis=1))
-        weights.append((w_a, w_out, w_b))
+        weights.append((w_a, w_b))
 
     state = tokens.astype(f32).reshape(MICRO * row_count, D)
     saves = []

time: 1750 us -> 1630 us (0.931)
  waiting for transfers between devices: 280 us -> 231 us
  blocking collectives: 29.5 us -> 0 us
    unnamed x10 -> x6, waiting for transfers between devices: 37.7 us -> 0.1 us
    pallas_call x2 -> x3, Pallas kernels: 190 us -> 219 us  [send_only(): pl.pallas_call(functools.partial(send_kernel, tuple((kind for kind, _ in...]
    pallas_call x2, Pallas kernels: 123 us -> 96.9 us  [ff_fwd(): pl.pallas_call(ff_fwd_kernel, out_shape=(jax.ShapeDtypeStruct((rows, D),...]
    concatenate x0 -> x24, local copies, waits for them, and re-layouts: none -> 20.8 us  [the longest x20 20.1 us: backward(): jnp.concatenate([heads_joined(got[:, :, i * WIDE:i * WIDE + width], n_tp)...]
    all_to_all x2 -> x0, waiting for transfers between devices: 19.5 us -> none  [local(): w_out = heads_joined(lax.all_to_all(out_parts, 'tp', 0, 0), n_tp)]
    pallas_call x2, Pallas kernels: 359 us -> 340 us  [attn_fwd(): pl.pallas_call(attn_fwd_kernel, out_shape=(jax.ShapeDtypeStruct((rows, D)...]
    all_gather x2 -> x0, blocking collectives: 17.9 us -> none  [backward(): out_all = lax.all_gather(done[layer, 'out'].astype(bf16), 'tp')]
    all_gather x6 -> x4, waiting for transfers between devices: 223 us -> 231 us  [gathered(): whole = lax.all_gather(part, 'fsdp', axis=0, tiled=True)]
  transfers between devices with their start and end apart: 11 -> 6, of which waited for: 6 -> 4; matrix products, arithmetic and copies ran while one was open for 4% -> 1% of each run, Pallas kernels for 31% -> 31%
where the time goes in v4:
time: 1630 us; the launch traced here: 1620 us
  Pallas kernels  1230 us (75%)
  waiting for transfers between devices  231 us (14%)
  other arithmetic  75 us (5%)
  local copies, waits for them, and re-layouts  70.7 us (4%)
    pallas_call x2, Pallas kernels, attn_bwd(): pl.pallas_call(functools.partial(attn_bwd_kernel, tuple((kind for kind, _...  434 us
    pallas_call x2, Pallas kernels, attn_fwd(): pl.pallas_call(attn_fwd_kernel, out_shape=(jax.ShapeDtypeStruct((rows, D)...  340 us
    all_gather x4, waiting for transfers between devices, gathered(): whole = lax.all_gather(part, 'fsdp', axis=0, tiled=True)  231 us
    pallas_call x3, Pallas kernels, send_only(): pl.pallas_call(functools.partial(send_kernel, tuple((kind for kind, _ in...  219 us
    pallas_call x2, Pallas kernels, ff_bwd(): pl.pallas_call(functools.partial(ff_bwd_kernel, tuple((kind for kind, _ i...  135 us
    pallas_call x2, Pallas kernels, ff_fwd(): pl.pallas_call(ff_fwd_kernel, out_shape=(jax.ShapeDtypeStruct((rows, D),...  96.9 us
  transfers between devices with their start and end apart: 6, of which 4 were waited for; matrix products, arithmetic and copies ran while one was open for 1% of the time, Pallas kernels for 31%

profile of v4, /device:TPU:9, one launch (start us, length us, event | category | flops | bytes accessed | tf_op | source)
XLA Modules:
  0.0 1617.9 jit_solution(17978703170813345299)
XLA Ops:
  7.2 3.6 fusion.46
  11.0 2.7 dynamic-slice_bitcast_fusion.3
  22.7 101.3 %all-gather.9.cloned.1.call-done.wqkv_hbm.refs_8_ = bf16[1600,2176]{1,0:T(8,128)(2,1)} async-done(((bf16[200,2176]{1,0:T(8,128)(2,1)}), bf16[1600,2176]{1,0:T(8,128)(2,1)}) %all-gather.9.cloned.1.call-update) | async-done | bytes 6963216 | tf_op jit(solution)/shard_map/all_gather | solution.py:1342
  127.8 166.2 %shard_map.262 = (f32[192,1600]{1,0:T(8,128)}, f32[2,4,8,384]{3,2,1,0:T(8,128)}, bf16[4,192,1600]{2,1,0:T(8,128)(2,1)}, bf16[3,2,384,512]{3,2,1,0:T(8,128)(2,1)}...) custom-call(f32[192,1600]{1,0:T(8,128)} %bitcast_convert_fusion.1.x_ref.refs_1_, ...), custom_call_target="tpu_custom_call" | custom-call | flops 99999997952 | bytes 31457280 | tf_op jit(solution)/shard_map/pallas_call | solution.py:884
  296.7 27.6 %all-gather.11.cloned.1.call-done.wb_hbm.refs_6_ = bf16[1600,3328]{1,0:T(8,128)(2,1)} async-done(((bf16[200,3328]{1,0:T(8,128)(2,1)}), bf16[1600,3328]{1,0:T(8,128)(2,1)}) %all-gather.11.cloned.1.call-update) | async-done | bytes 10649616 | tf_op jit(solution)/shard_map/all_gather | solution.py:1342
  324.3 44.3 %shard_map.263 = (f32[192,1600]{1,0:T(8,128)}, bf16[4,192,1600]{2,1,0:T(8,128)(2,1)}, f32[4,192,1600]{2,1,0:T(8,128)}, bf16[4,192,1600]{2,1,0:T(8,128)(2,1)}) custom-call(f32[192,1600]{1,0:T(8,128)} %get-tuple-element.74.x_ref.refs_1_, f32[8,1600]{1,0:T(8,128)} %bitcast.316, f32[1,1600]{1,0:T(1,128)} %get-tuple-element.252.fcb_ref, ...), custom_call_target="tpu_custom_call" | custom-call | flops 7864320000 | bytes 41943040 | tf_op jit(solution)/shard_map/pallas_call | solution.py:376
  368.7 61.8 %all-gather.13.cloned.1.call-done.wqkv_hbm.refs_8_ = bf16[1600,2048]{1,0:T(8,128)(2,1)} async-done(((bf16[200,2048]{1,0:T(8,128)(2,1)}), bf16[1600,2048]{1,0:T(8,128)(2,1)}) %all-gather.13.cloned.1.call-update) | async-done | bytes 6553616 | tf_op jit(solution)/shard_map/all_gather | solution.py:1342
  430.5 174.2 %shard_map.264 = (f32[192,1600]{1,0:T(8,128)}, f32[2,4,8,384]{3,2,1,0:T(8,128)}, bf16[4,192,1600]{2,1,0:T(8,128)(2,1)}, bf16[3,2,384,512]{3,2,1,0:T(8,128)(2,1)}...) custom-call(f32[192,1600]{1,0:T(8,128)} %get-tuple-element.75.x_ref.refs_1_, ...), custom_call_target="tpu_custom_call" | custom-call | flops 99999997952 | bytes 31457280 | tf_op jit(solution)/shard_map/pallas_call | solution.py:884
  605.9 1.7 fusion.47
  607.6 1.6 pad_maximum_fusion.3.refs_7_
  609.2 40.2 %all-gather.15.cloned.1.call-done.wb_hbm.refs_6_ = bf16[1600,3328]{1,0:T(8,128)(2,1)} async-done(((bf16[200,3328]{1,0:T(8,128)(2,1)}), bf16[1600,3328]{1,0:T(8,128)(2,1)}) %all-gather.15.cloned.1.call-update) | async-done | bytes 10649616 | tf_op jit(solution)/shard_map/all_gather | solution.py:1342
  649.4 52.6 %shard_map.265 = (f32[192,1600]{1,0:T(8,128)}, bf16[4,192,1600]{2,1,0:T(8,128)(2,1)}, f32[4,192,1600]{2,1,0:T(8,128)}, bf16[4,192,1600]{2,1,0:T(8,128)(2,1)}) custom-call(f32[192,1600]{1,0:T(8,128)} %get-tuple-element.76.x_ref.refs_1_, f32[8,1600]{1,0:T(8,128)} %bitcast.320, f32[1,1600]{1,0:T(1,128)} %get-tuple-element.249.fcb_ref, ...), custom_call_target="tpu_custom_call" | custom-call | flops 7864320000 | bytes 41943040 | tf_op jit(solution)/shard_map/pallas_call | solution.py:376
  702.0 2.2 convert_element_type.238
  704.2 57.5 %shard_map.266 = (f32[192,1600]{1,0:T(8,128)}, f32[8,1600]{1,0:T(8,128)}, f32[1,1600]{1,0:T(1,128)}, bf16[1600,1600]{1,0:T(8,128)(2,1)}, bf16[1600,1600]{1,0:T(8,128)(2,1)}) custom-call(f32[192,1600]{1,0:T(8,128)} %bitcast_convert_fusion.refs_0_, f32[192,1600]{1,0:T(8,128)} %get-tuple-element.76.x_ref.refs_1_, f32[8,1600]{1,0:T(8,128)} %bitcast.321, ...), custom_call_target="tpu_custom_call" | custom-call | flops 15728640000 | bytes 52428800 | tf_op jit(solution)/shard_map/pallas_call | solution.py:532
  761.8 1.4 slice.688
  764.5 1.7 fusion.48
  766.2 1.6 pad_maximum_fusion.2.refs_7_
  767.8 216.6 %shard_map.267 = (f32[192,1600]{1,0:T(8,128)}, f32[8,1600]{1,0:T(8,128)}, f32[1,1536]{1,0:T(1,128)}, bf16[1600,1536]{1,0:T(8,128)(2,1)}, bf16[1600,448]{1,0:T(8,...) custom-call(f32[192,1600]{1,0:T(8,128)} %get-tuple-element.81.refs_0_, ...), custom_call_target="tpu_custom_call" | custom-call | flops 199999995904 | bytes 52428800 | tf_op jit(solution)/shard_map/pallas_call | solution.py:1107
  986.8 4.9 fusion.3.refs_7_
  992.6 2.3 fusion.2.refs_10_
  994.9 1.5 fusion.14
  996.4 77.6 %shard_map.268 = (f32[192,1600]{1,0:T(8,128)}, f32[8,1600]{1,0:T(8,128)}, f32[1,1600]{1,0:T(1,128)}, bf16[1600,1600]{1,0:T(8,128)(2,1)}, bf16[1600,1600]{1,0:T(8...) custom-call(f32[192,1600]{1,0:T(8,128)} %get-tuple-element.90.refs_0_, ...), custom_call_target="tpu_custom_call" | custom-call | flops 15728640000 | bytes 52428800 | tf_op jit(solution)/shard_map/pallas_call | solution.py:532
  1074.0 4.7 fusion.5.refs_11_
  1079.9 217.9 %shard_map.269 = (f32[192,1600]{1,0:T(8,128)}, f32[8,1600]{1,0:T(8,128)}, f32[1,1536]{1,0:T(1,128)}, bf16[1600,1536]{1,0:T(8,128)(2,1)}, bf16[1600,448]{1,0:T(8,...) custom-call(f32[192,1600]{1,0:T(8,128)} %get-tuple-element.101.refs_, ...), custom_call_target="tpu_custom_call" | custom-call | flops 199999995904 | bytes 52428800 | tf_op jit(solution)/shard_map/pallas_call | solution.py:1107
  1298.6 4.9 fusion.1.refs_0_
  1304.5 2.3 fusion.refs_1_
  1308.7 1.5 fusion.15
  1310.2 117.8 %shard_map.270 = (bf16[3,200,1600]{2,1,0:T(8,128)(2,1)}, bf16[3,200,1600]{2,1,0:T(8,128)(2,1)}, bf16[4,200,1536]{2,1,0:T(8,128)(2,1)}, bf16[4,200,512]{2,1,0:T(8,128)(2,1)}) custom-call(bf16[4,200,1600]{2,1,0:T(8,128)(2,1)} %fusion.1.refs_0_, bf16[4,200,1600]{2,1,0:T(8,128)(2,1)} %fusion.refs_1_, bf16[4,2,200,1536]{3,2,1,0:T(8,128)(2,1)} %bitcast.290, ...), custom_call_target="tpu_custom_call" | custom-call | tf_op jit(solution)/shard_map/pallas_call | solution.py:1173
  1428.1 4.7 fusion.4.refs_0_
  1438.3 73.7 %shard_map.271 = (bf16[3,200,1536]{2,1,0:T(8,128)(2,1)}, bf16[3,200,512]{2,1,0:T(8,128)(2,1)}, bf16[4,200,2048]{2,1,0:T(8,128)(2,1)}) custom-call(bf16[4,200,1536]{2,1,0:T(8,128)(2,1)} %fusion.4.refs_0_, bf16[4,200,512]{2,1,0:T(8,128)(2,1)} %fusion.16.refs_1_, bf16[200,2048]{1,0:T(8,128)(2,1)} %pad_maximum_fusion.4.refs_2_), custom_call_target="tpu_custom_call" | custom-call | tf_op jit(solution)/shard_map/pallas_call | solution.py:1173
  1512.0 3.2 slice_bitcast_fusion.6
  1515.2 1.8 convert_reduce_fusion.8
  1520.7 26.9 %shard_map.272 = bf16[4,200,2048]{2,1,0:T(8,128)(2,1)} custom-call(bf16[200,2048]{1,0:T(8,128)(2,1)} %pad_maximum_fusion.5.refs_0_), custom_call_target="tpu_custom_call" | custom-call | tf_op jit(solution)/shard_map/pallas_call | solution.py:1173
  1547.6 3.1 slice_bitcast_fusion.9
  1550.7 1.7 convert_reduce_fusion.9
  1567.7 1.6 slice_bitcast_fusion.28
  1570.6 1.6 slice_bitcast_fusion.31
  1572.2 1.6 slice_bitcast_fusion.32
  1573.8 1.6 slice_bitcast_fusion.33
  1578.3 2.4 bitcast_add_fusion.1
  1582.1 2.5 fusion.26
  1584.8 2.3 fusion.27
  1590.0 3.4 concatenate.159
  1593.4 4.5 concatenate.149
  1598.0 5.3 maximum_convert_fusion
  1603.3 1.7 pad_maximum_fusion
  1606.0 1.7 pad_maximum_fusion.1
  1607.9 1.7 maximum_convert_fusion.1
  (239 shorter events, 61.2 us)
Async XLA Ops:
  7.2 116.8 %all-gather.9.cloned.1.call-start = ((), (), s32[]{:S(2)}) async-start(), calls=%async_computation | async-start | bytes 7833600 | tf_op jit(solution)/shard_map/all_gather | solution.py:1342
  10.9 2.9 copy-start.17
  10.9 4.0 copy-start.43
  10.9 4.0 copy-start.44
  10.9 4.0 copy-start.45
  10.9 4.1 copy-start.46
  10.9 4.1 copy-start.47
  10.9 4.1 copy-start.48
  10.9 4.1 copy-start.49
  10.9 4.1 copy-start.50
  10.9 4.1 copy-start.51
  14.9 2.7 copy-start.18
  17.6 306.8 %all-gather.11.cloned.1.call-start = ((), (), s32[]{:S(2)}) async-start(), calls=%async_computation.1 | async-start | bytes 11980800 | tf_op jit(solution)/shard_map/all_gather | solution.py:1342
  20.4 410.1 %all-gather.13.cloned.1.call-start = ((), (), s32[]{:S(2)}) async-start(), calls=%async_computation.2 | async-start | bytes 7372800 | tf_op jit(solution)/shard_map/all_gather | solution.py:1342
  21.4 584.5 %all-gather.19.cloned.1.call-start = ((), (), s32[]{:S(2)}) async-start(), calls=%async_computation.5 | async-start | bytes 3932160 | tf_op jit(solution)/shard_map/all_gather | solution.py:1190
  294.0 355.4 %all-gather.15.cloned.1.call-start = ((), (), s32[]{:S(2)}) async-start(), calls=%async_computation.3 | async-start | bytes 11980800 | tf_op jit(solution)/shard_map/all_gather | solution.py:1342
  295.3 469.2 %all-gather.17.cloned.1.call-start = ((), (), s32[]{:S(2)}) async-start(), calls=%async_computation.4 | async-start | bytes 3932160 | tf_op jit(solution)/shard_map/all_gather | solution.py:1190
  430.4 174.3 %copy-start.29 = (bf16[2,96,1600]{2,1,0:T(8,128)(2,1)S(1)}, bf16[2,96,1600]{2,1,0:T(8,128)(2,1)}, u32[]{:S(2)}) copy-start(bf16[2,96,1600]{2,1,0:T(8,128)(2,1)} %param.29) | copy-start | bytes 1843204
  767.8 218.6 %copy-start.39 = (bf16[3,1600]{1,0:T(4,128)(2,1)S(1)}, bf16[3,1600]{1,0:T(4,128)(2,1)}, u32[]{:S(2)}) copy-start(bf16[3,1600]{1,0:T(4,128)(2,1)} %slice.688) | copy-start | bytes 28804
  767.8 218.6 %copy-start.40 = (bf16[1,1600]{1,0:T(2,128)(2,1)S(1)}, bf16[1,1600]{1,0:T(2,128)(2,1)}, u32[]{:S(2)}) copy-start(bf16[1,1600]{1,0:T(2,128)(2,1)} %convert.74) | copy-start | bytes 9604
  986.8 4.9 copy-start.5
  986.8 5.9 copy-start.15
  992.6 2.3 copy-start.14
  1074.0 4.7 copy-start.4
  1074.0 4.7 copy-start.25
  1298.6 4.9 copy-start.38
  1298.6 4.9 copy-start.6
  1298.6 5.9 copy-start.16
  1304.5 2.3 copy-start.42
  1304.5 3.1 copy-start.41
  1304.5 3.8 slice-start.2
  1304.5 4.2 copy-start.13
  1428.1 4.7 copy-start
  1428.1 4.7 copy-start.26
  1432.8 2.0 copy-start.11
  1512.0 5.0 copy-start.37
  1515.2 2.9 copy-start.12
  1558.5 17.5 %copy-start.8 = (bf16[3,200,1600]{2,1,0:T(8,128)(2,1)S(1)}, bf16[3,200,1600]{2,1,0:T(8,128)(2,1)}, u32[]{:S(2)}) copy-start(bf16[3,200,1600]{2,1,0:T(8,128)(2,1)} %get-tuple-element.130) | copy-start | bytes 5760004
  1576.3 1.8 copy-start.10
  1578.3 3.4 copy-start.7
  1582.0 2.5 copy-start.9
  1597.9 5.4 copy-start.1
  1603.3 1.8 copy-start.2
  1603.3 2.7 copy-start.3
  1606.0 1.7 copy-start.33
  1606.0 1.7 copy-start.34
  1606.0 1.9 copy-start.35
  1607.7 1.9 copy-start.20
  (13 other events, 19.2 us)
Sparse Core Ops, SparseCore 0:
  17.7 106.2 all-gather.8
  126.8 197.5 all-gather.10
  327.1 103.2 all-gather.12
  431.9 46.3 all-gather.18
  480.9 168.4 all-gather.14
  650.8 37.3 all-gather.16

commit v5 on v4

--- a/solution.py
+++ b/solution.py
@@ -237,6 +237,91 @@
                 local.wait()
 
 
+class Spread:
+    def __init__(self, group, source, target, sems, chunks):
+        self.g, self.source, self.target, self.sems = group, source, target, sems
+        count = source.shape[1] // 128
+        ends = [128 * (count * (c + 1) // chunks) for c in range(chunks)]
+        self.columns = [slice(a, b) for a, b in zip([0] + ends, ends)]
+        self.partner = group.at(group.z, 1 - group.y)
+
+    def piece(self, member, c, index, to, own=False):
+        target = self.target.at[member, :, self.columns[c]]
+        source = self.source.at[:, self.columns[c]] if own else target
+        return self.g.copy(source, target, self.sems, 7 * c + index, to)
+
+    def own(self, c):
+        g = self.g
+        return [self.piece(g.member, c, k, g.at(g.ahead(k), g.y), True) for k in (1, 2, 3)] + [
+            self.piece(g.member, c, 0, self.partner, True)
+        ]
+
+    def relayed(self, c):
+        g = self.g
+        return [self.piece(g.at(g.behind(k), g.y), c, 3 + k, self.partner) for k in (1, 2, 3)]
+
+    def keep(self):
+        return pltpu.make_async_copy(
+            self.source, self.target.at[self.g.member], self.sems[0].at[7 * len(self.columns)]
+        )
+
+    def start(self, first=0, last=None):
+        if first == 0:
+            self.keep().start()
+        for c in range(len(self.columns))[first:last]:
+            for copy in self.own(c):
+                copy.start()
+
+    def relay(self, c):
+        g = self.g
+        for k, copy in zip((1, 2, 3), self.relayed(c)):
+            self.piece(g.at(g.behind(k), g.y), c, k, self.partner).wait_recv()
+            copy.start()
+
+    def finish(self):
+        g = self.g
+        for c in range(len(self.columns)):
+            self.piece(self.partner, c, 0, self.partner).wait_recv()
+            for k in (1, 2, 3):
+                self.piece(g.at(g.behind(k), 1 - g.y), c, 3 + k, self.partner).wait_recv()
+            for copy in self.own(c) + self.relayed(c):
+                copy.wait_send()
+        self.keep().wait()
+
+
+def spread_parts(shard, chunks):
+    if shard is None:
+        return (), (), []
+    whole = jax.ShapeDtypeStruct((GROUP,) + shard.shape, shard.dtype)
+    return (shard,), (whole,), [pltpu.SemaphoreType.DMA((7 * chunks + 1,))] * 2
+
+
+def spread_kernel(chunks, source, target, send, recv):
+    g = Group()
+    barrier = pltpu.get_barrier_semaphore()
+    others = [g.at(g.z, 1 - g.y)] + [g.at(g.ahead(k), g.y) for k in (1, 2, 3)]
+    for member in others:
+        pl.semaphore_signal(barrier, inc=1, device_id=(g.base + member, g.t), device_id_type=MESH)
+    pl.semaphore_wait(barrier, len(others))
+    spread = Spread(g, source, target, (send, recv), chunks)
+    spread.start()
+    for c in range(chunks):
+        spread.relay(c)
+    spread.finish()
+
+
+def spread_only(shard, chunks, collective_id):
+    operands, results, scratch = spread_parts(shard, chunks)
+    return pl.pallas_call(
+        functools.partial(spread_kernel, chunks),
+        out_shape=results[0],
+        in_specs=[ANY],
+        out_specs=ANY,
+        scratch_shapes=scratch,
+        compiler_params=params(collective_id),
+    )(shard)
+
+
 def sent_shapes(payload):
     return tuple(
         jax.ShapeDtypeStruct((3 if kind == "z" else 4,) + a.shape[-2:], a.dtype) for kind, a in payload
@@ -287,12 +372,18 @@
     return w_b.at[:, lanes_up(width) :]
 
 
-def ff_fwd_kernel(
-    x_ref, vec_ref, fcb_ref, wb_hbm,
-    out_ref, all_hbm, pre_hbm, hid_hbm,
-    wfc, wproj, buf, pre, hid, part, from_core, over_out, from_over, send, recv, local,
-):
-    p = Peers()
+FF_CHUNKS = 3
+ATTN_CHUNKS = 5
+
+
+def ff_fwd_kernel(n, *refs):
+    x_ref, vec_ref, fcb_ref, wb_hbm = refs[:4]
+    shard, refs = refs[4 : 4 + n], refs[4 + n :]
+    out_ref, all_hbm, pre_hbm, hid_hbm = refs[:4]
+    whole, refs = refs[4 : 4 + n], refs[4 + n :]
+    wfc, wproj, buf, pre, hid, part, from_core, over_out, from_over, send, recv, local = refs[:12]
+    p, g = Peers(), Group()
+    spread = Spread(g, shard[0], whole[0], refs[12:], FF_CHUNKS) if n else None
     rows = x_ref.shape[0]
     sems = (send, recv)
     gather = Gather(p, buf, sems)
@@ -308,8 +399,13 @@
         buf[p.t, at, :] = (hat * vec_ref[5:6, :] + vec_ref[6:7, :]).astype(bf16)
 
     row_chunks(rows, norm)
-    p.greet()
+    if n:
+        g.greet(p)
+    else:
+        p.greet()
     gather.start()
+    if n:
+        spread.start()
     gather.wait_chip()
     load_fc.wait()
 
@@ -328,6 +424,8 @@
         tiles(D, tile)
 
     up(p.x)
+    if n:
+        spread.relay(0)
     gather.relay()
     gather.wait_diag()
     keep_all = pltpu.make_async_copy(buf, all_hbm, local.at[2])
@@ -341,8 +439,12 @@
     down(1 - p.x)
     scatter.far_to_core().start()
     scatter.send_over()
+    if n:
+        spread.relay(1)
     down(p.x)
     scatter.near_to_core().start()
+    if n:
+        spread.relay(2)
     scatter.wait()
 
     def final(at):
@@ -353,6 +455,8 @@
     scatter.finish()
     for copy in (keep_all, keep_pre, keep_hid):
         copy.wait()
+    if n:
+        spread.finish()
 
 
 def scatter_scratch(n_tp, rows):
@@ -370,19 +474,21 @@
     return pltpu.CompilerParams(collective_id=collective_id, has_side_effects=True, vmem_limit_bytes=60 * 2**20)
 
 
-def ff_fwd(x, vecs, fc_bias, w_b, n_tp):
+def ff_fwd(x, vecs, fc_bias, w_b, n_tp, shard, collective_id):
     rows, width = x.shape[0], fc_bias.shape[1]
     block = (n_tp, rows)
+    operands, results, sems = spread_parts(shard, FF_CHUNKS)
     return pl.pallas_call(
-        ff_fwd_kernel,
+        functools.partial(ff_fwd_kernel, len(operands)),
         out_shape=(
             jax.ShapeDtypeStruct((rows, D), f32),
             jax.ShapeDtypeStruct(block + (D,), bf16),
             jax.ShapeDtypeStruct(block + (width,), f32),
             jax.ShapeDtypeStruct(block + (width,), bf16),
-        ),
-        in_specs=[IN_VMEM, IN_VMEM, IN_VMEM, ANY],
-        out_specs=(IN_VMEM, ANY, ANY, ANY),
+        )
+        + results,
+        in_specs=[IN_VMEM, IN_VMEM, IN_VMEM, ANY] + [ANY] * len(operands),
+        out_specs=(IN_VMEM, ANY, ANY, ANY) + (ANY,) * len(operands),
         scratch_shapes=[
             pltpu.VMEM((D, lanes_up(width)), bf16),
             pltpu.VMEM((D, lanes_up(width)), bf16),
@@ -391,12 +497,13 @@
             pltpu.VMEM(block + (width,), bf16),
         ]
         + scatter_scratch(n_tp, rows)
-        + [pltpu.SemaphoreType.DMA((5,))],
-        compiler_params=params(1),
+        + [pltpu.SemaphoreType.DMA((5,))]
+        + sems,
+        compiler_params=params(collective_id),
         cost_estimate=pl.CostEstimate(
             flops=4 * n_tp * rows * D * width, bytes_accessed=40 * 2**20, transcendentals=n_tp * rows * width
         ),
-    )(x, vecs, fc_bias, w_b)
+    )(x, vecs, fc_bias, w_b, *operands)
 
 
 def gelu_slope(u):
@@ -715,13 +822,15 @@
             target[micro, at, :] = value[first : first + per]
 
 
-def attn_fwd_kernel(
-    x_ref, vec_ref, bias_ref, wqkv_hbm,
-    out_ref, lse_ref, all_hbm, own_hbm, kv_hbm, mix_hbm, wout_hbm,
-    wqkv, wout, wparts, buf, own, kv, mix, s_ref, p_ref, o_ref,
-    part, from_core, over_out, from_over, send, recv, gsend, grecv, wsend, wrecv, local,
-):
+def attn_fwd_kernel(n, *refs):
+    x_ref, vec_ref, bias_ref, wqkv_hbm = refs[:4]
+    shard, refs = refs[4 : 4 + n], refs[4 + n :]
+    out_ref, lse_ref, all_hbm, own_hbm, kv_hbm, mix_hbm, wout_hbm = refs[:7]
+    whole, refs = refs[7 : 7 + n], refs[7 + n :]
+    wqkv, wout, wparts, buf, own, kv, mix, s_ref, p_ref, o_ref = refs[:10]
+    part, from_core, over_out, from_over, send, recv, gsend, grecv, wsend, wrecv, local = refs[10:21]
     p, g = Peers(), Group()
+    spread = Spread(g, shard[0], whole[0], refs[21:], ATTN_CHUNKS) if n else None
     rows = x_ref.shape[0]
     n_tp = buf.shape[0]
     step = HEADS // n_tp * HEAD
@@ -751,6 +860,8 @@
     gather.start()
     for copy in give_parts:
         copy.start()
+    if n:
+        spread.start(0, 1)
     gather.wait_chip()
     load_qkv.wait()
 
@@ -770,6 +881,9 @@
         for i in range(2):
             kv[g.member, micro, i] = own[1 + i, micro, :PROMPT_DEV, :]
         share.start(micro)
+    if n:
+        spread.start(1)
+        spread.relay(0)
     keep_all = pltpu.make_async_copy(buf, all_hbm, local.at[2])
     keep_own = pltpu.make_async_copy(own, own_hbm, local.at[3])
     keep_all.start()
@@ -781,10 +895,22 @@
         if micro == 0:
             share.relay(0)
         share.wait(micro)
-        if micro == 0:
-            share.relay(1)
 
         def head(pair, lanes, half, micro=micro):
+            if half == 0:
+
+                @pl.when(pair == 1)
+                def _():
+                    if micro == 0:
+                        share.relay(1)
+                    elif n:
+                        spread.relay(2)
+
+                @pl.when(pair == HEAD_PAIRS - 1)
+                def _():
+                    if n:
+                        spread.relay(1 + 2 * micro)
+
             qh = half_of(own[0, micro, :, lanes], half)
 
             def first(c, load, top):
@@ -852,6 +978,8 @@
     scatter.send_over()
     down(p.x)
     scatter.near_to_core().start()
+    if n:
+        spread.relay(4)
     scatter.wait()
 
     def final(at):
@@ -866,6 +994,8 @@
         copy.wait_send()
     for copy in (keep_all, keep_own, keep_kv, keep_mix, keep_out):
         copy.wait()
+    if n:
+        spread.finish()
 
 
 def attn_shapes(n_tp, rows):
@@ -877,19 +1007,21 @@
     )
 
 
-def attn_fwd(x, vecs, biases, w_a, n_tp, collective_id):
+def attn_fwd(x, vecs, biases, w_a, n_tp, shard, collective_id):
     rows = x.shape[0]
     width = D - HEADS // n_tp * HEAD * (n_tp - 1)
     saved = attn_shapes(n_tp, rows)
+    operands, results, sems = spread_parts(shard, ATTN_CHUNKS)
     return pl.pallas_call(
-        attn_fwd_kernel,
+        functools.partial(attn_fwd_kernel, len(operands)),
         out_shape=(
             jax.ShapeDtypeStruct((rows, D), f32),
             jax.ShapeDtypeStruct((MICRO, HEAD_PAIRS, 8, TOK_DEV), f32),
         )
-        + tuple(jax.ShapeDtypeStruct(*s) for s in saved + (((WIDE, D), bf16),)),
-        in_specs=[IN_VMEM, IN_VMEM, IN_VMEM, ANY],
-        out_specs=(IN_VMEM, IN_VMEM, ANY, ANY, ANY, ANY, ANY),
+        + tuple(jax.ShapeDtypeStruct(*s) for s in saved + (((WIDE, D), bf16),))
+        + results,
+        in_specs=[IN_VMEM, IN_VMEM, IN_VMEM, ANY] + [ANY] * len(operands),
+        out_specs=(IN_VMEM, IN_VMEM) + (ANY,) * (5 + len(operands)),
         scratch_shapes=[pltpu.VMEM((D, 3 * WIDE), bf16), pltpu.VMEM((WIDE, D), bf16), pltpu.VMEM((n_tp, width, WIDE), bf16)]
         + [pltpu.VMEM(*s) for s in saved]
         + [
@@ -904,10 +1036,11 @@
             pltpu.SemaphoreType.DMA((3,)),
             pltpu.SemaphoreType.DMA((3,)),
             pltpu.SemaphoreType.DMA((7,)),
-        ],
+        ]
+        + sems,
         compiler_params=params(collective_id),
         cost_estimate=pl.CostEstimate(flops=10**11, bytes_accessed=30 * 2**20, transcendentals=0),
-    )(x, vecs, biases, w_a)
+    )(x, vecs, biases, w_a, *operands)
 
 
 def attn_bwd_kernel(kinds, *refs):
@@ -1180,15 +1313,45 @@
     )(*(a for _, a in payload))
 
 
-def forward_layer(x, layer, weights, vecs, fc_bias, cols, n_tp):
-    w_a, w_b = weights
+def forward_layer(x, layer, fetch, vecs, fc_bias, cols, n_tp):
     width = D - HEADS // n_tp * HEAD * (n_tp - 1)
     query_bias, value_bias = (lax.dynamic_slice_in_dim(vecs[i], cols, width) for i in (2, 3))
     biases = widen(jnp.stack([query_bias, jnp.zeros_like(query_bias), value_bias]))
-    x_mid, lse, all_rows, own, kv, mixed, w_out = attn_fwd(x, vecs, biases, w_a, n_tp, 5 + layer)
-    x_next, second_all, hidden_pre, hidden = ff_fwd(x_mid, vecs, fc_bias[None], w_b, n_tp)
+    w_a = fetch.weights[layer, "a"]
+    x_mid, lse, all_rows, own, kv, mixed, w_out = fetch.during(
+        (layer, "b"), lambda shard: attn_fwd(x, vecs, biases, w_a, n_tp, shard, 5 + layer)
+    )
+    w_b = fetch.weights[layer, "b"]
+    x_next, second_all, hidden_pre, hidden = fetch.during(
+        (layer + 1, "a"), lambda shard: ff_fwd(x_mid, vecs, fc_bias[None], w_b, n_tp, shard, 1 + layer)
+    )
     mixed_all = heads_joined(lax.all_gather(mixed[:, :, :width], "tp"), n_tp)
     return x_next, (x, w_out, lse, all_rows, own, kv, mixed_all, x_mid, second_all, hidden_pre, hidden)
+
+
+class Fetch:
+    def __init__(self, shards):
+        self.staged = lax.axis_size("fsdp") == GROUP
+        self.shards, self.weights = shards, {}
+        last = None
+        for key, shard in shards.items():
+            if self.staged:
+                if last is None:
+                    last = spread_only(shard, 8, 9)
+                    self.weights[key] = last.reshape(-1, shard.shape[1])
+                continue
+            if last is not None:
+                shard, _ = lax.optimization_barrier((shard, last))
+            whole = lax.all_gather(shard, "fsdp", axis=0, tiled=True)
+            self.weights[key] = whole
+            last = whole[:8, :128]
+
+    def during(self, key, kernel):
+        if not self.staged or key not in self.shards:
+            return kernel(None)
+        *results, whole = kernel(self.shards[key])
+        self.weights[key] = whole.reshape(-1, whole.shape[2])
+        return results
 
 
 def fsdp_sum(part):
@@ -1266,7 +1429,7 @@
 
     plan = {(1, 0): (0, 0), (1, 1): (0, 2), (0, 0): (1, 2), (0, 1): (3, 2)}
     for layer in reversed(range(LAYERS)):
-        w_a, w_b = weights[layer]
+        w_a, w_b = weights[layer, "a"], weights[layer, "b"]
         x, w_out, lse, all_rows, own, kv, mixed_all, x_mid, second_all, hidden_pre, hidden = saves[layer]
         chosen_z, chosen_y, payload = load(*plan[layer, 0])
         grad, ff_sums, fc_bias_sums, grad_fc, grad_proj, *arrived = ff_bwd(
@@ -1334,44 +1497,32 @@
     width = D - step * (n_tp - 1)
     cols = tp * step
 
-    last = []
-
-    def gathered(part):
-        if last:
-            part, _ = lax.optimization_barrier((part, last.pop()))
-        whole = lax.all_gather(part, "fsdp", axis=0, tiled=True)
-        last.append(whole[:8, :128])
-        return whole
-
     vectors = jnp.stack(
         [first_gain, first_bias, query_bias, value_bias, out_bias, second_gain, second_bias, proj_bias, fc_bias[:, 0]]
     ).reshape(9 * LAYERS, -1)
 
-    weights = []
+    shards = {}
     for layer in range(LAYERS):
         sides = [widen(lax.dynamic_slice_in_dim(qkv_weight[layer], cols + i * D, width, 1)) for i in range(3)]
         sides.append(widen(lax.dynamic_slice_in_dim(out_weight[layer], cols, width, 1)))
         if layer == 0:
             sides.append(jnp.pad(vectors.T, ((0, 0), (0, 128 - 9 * LAYERS))))
-        w_a = gathered(jnp.concatenate(sides, axis=1))
-        if layer == 0:
-            vectors = w_a[:, 4 * WIDE : 4 * WIDE + 9 * LAYERS].T.astype(f32).reshape(9, LAYERS, D)
+        shards[layer, "a"] = jnp.concatenate(sides, axis=1)
         fc, proj = fc_weight[layer], proj_weight[layer].T
         more = ((0, 0), (0, lanes_up(fc.shape[1]) - fc.shape[1]))
-        w_b = gathered(jnp.concatenate([jnp.pad(fc, more), jnp.pad(proj, more)], axis=1))
-        weights.append((w_a, w_b))
+        shards[layer, "b"] = jnp.concatenate([jnp.pad(fc, more), jnp.pad(proj, more)], axis=1)
+    fetch = Fetch(shards)
+    vectors = fetch.weights[0, "a"][:, 4 * WIDE : 4 * WIDE + 9 * LAYERS].T.astype(f32).reshape(9, LAYERS, D)
 
     state = tokens.astype(f32).reshape(MICRO * row_count, D)
     saves = []
     for layer in range(LAYERS):
-        state, saved = forward_layer(
-            state, layer, weights[layer], vectors[:8, layer], vectors[8, layer], cols, n_tp
-        )
+        state, saved = forward_layer(state, layer, fetch, vectors[:8, layer], vectors[8, layer], cols, n_tp)
         saves.append(saved)
     out_tokens = state.astype(bf16).reshape(tokens.shape)
     grad = out_grad.astype(f32).reshape(MICRO * row_count, D)
     grad, sums = backward(
-        grad, weights, [vectors[:8, layer] for layer in range(LAYERS)], saves, cols, n_tp
+        grad, fetch.weights, [vectors[:8, layer] for layer in range(LAYERS)], saves, cols, n_tp
     )
     qkv_g, out_g, fc_g, proj_g, fc_bias_g, vec_g = (
         jnp.stack([sums[layer][i] for layer in range(LAYERS)]) for i in range(6)

time: 1630 us -> 1610 us (0.988)
  waiting for transfers between devices: 231 us -> 0.5 us
  Pallas kernels: 1230 us -> 1440 us
    all_gather x4 -> x0, waiting for transfers between devices: 231 us -> none  [gathered(): whole = lax.all_gather(part, 'fsdp', axis=0, tiled=True)]
    pallas_call x4 -> x5, Pallas kernels: 437 us -> 639 us  [the longest x2 386 us: attn_fwd(): pl.pallas_call(functools.partial(attn_fwd_kernel, len(operands)), out_sha...]
  transfers between devices with their start and end apart: 6 -> 2, of which waited for: 4 -> 0; matrix products, arithmetic and copies ran while one was open for 1% -> 2% of each run, Pallas kernels for 31% -> 26%
where the time goes in v5:
time: 1610 us; the launch traced here: 1600 us
  Pallas kernels  1440 us (89%)
  other arithmetic  79.7 us (5%)
  local copies, waits for them, and re-layouts  66.7 us (4%)
    pallas_call x2, Pallas kernels, attn_bwd(): pl.pallas_call(functools.partial(attn_bwd_kernel, tuple((kind for kind, _...  439 us
    pallas_call x2, Pallas kernels, attn_fwd(): pl.pallas_call(functools.partial(attn_fwd_kernel, len(operands)), out_sha...  386 us
    pallas_call x3, Pallas kernels, send_only(): pl.pallas_call(functools.partial(send_kernel, tuple((kind for kind, _ in...  217 us
    pallas_call x2, Pallas kernels, ff_fwd(): pl.pallas_call(functools.partial(ff_fwd_kernel, len(operands)), out_shape...  160 us
    pallas_call x2, Pallas kernels, ff_bwd(): pl.pallas_call(functools.partial(ff_bwd_kernel, tuple((kind for kind, _ i...  142 us
    pallas_call x1, Pallas kernels, spread_only(): pl.pallas_call(functools.partial(spread_kernel, chunks), out_shape=result...  93.8 us
  transfers between devices with their start and end apart: 2, of which 0 were waited for; matrix products, arithmetic and copies ran while one was open for 2% of the time, Pallas kernels for 26%

profile of v5, /device:TPU:9, one launch (start us, length us, event | category | flops | bytes accessed | tf_op | source)
XLA Modules:
  0.0 1600.1 jit_solution(13431572772713226533)
XLA Ops:
  7.2 3.6 fusion.46
  11.0 2.7 dynamic-slice_bitcast_fusion.3
  18.1 93.8 %shard_map.262 = bf16[8,200,2176]{2,1,0:T(8,128)(2,1)} custom-call(bf16[200,2176]{1,0:T(8,128)(2,1)} %copy-done.19), custom_call_target="tpu_custom_call" | custom-call | tf_op jit(solution)/shard_map/pallas_call | solution.py:315
  118.5 1.7 fusion.24
  120.2 193.2 %shard_map.263 = (f32[192,1600]{1,0:T(8,128)}, f32[2,4,8,384]{3,2,1,0:T(8,128)}, bf16[4,192,1600]{2,1,0:T(8,128)(2,1)}, bf16[3,2,384,512]{3,2,1,0:T(8,128)(2,1)}...) custom-call(f32[192,1600]{1,0:T(8,128)} %bitcast_convert_fusion.1.re, ...), custom_call_target="tpu_custom_call" | custom-call | flops 99999997952 | bytes 31457280 | tf_op jit(solution)/shard_map/pallas_call | solution.py:1015
  314.5 105.2 %shard_map.264 = (f32[192,1600]{1,0:T(8,128)}, bf16[4,192,1600]{2,1,0:T(8,128)(2,1)}, f32[4,192,1600]{2,1,0:T(8,128)}, bf16[4,192,1600]{2,1,0:T(8,128)(2,1)}, bf16[8,200,2048]{2,1,0:T(8,128)(2,1)}) custom-call(f32[192,1600]{1,0:T(8,128)} %get-tuple-element.77.refs_0_.refs_1_, f32[8,1600]{1,0:T(8,128)} %bitcast.323, f32[1,1600]{1,0:T(1,128)} %get-tuple-element.258.refs_2_, ...), custom_call_target="tpu_custom_call" | custom-call | flops 7864320000 | bytes 41943040 | tf_op jit(solution)/shard_map/pallas_call | solution.py:481
  419.6 193.0 %shard_map.265 = (f32[192,1600]{1,0:T(8,128)}, f32[2,4,8,384]{3,2,1,0:T(8,128)}, bf16[4,192,1600]{2,1,0:T(8,128)(2,1)}, bf16[3,2,384,512]{3,2,1,0:T(8,128)(2,1)}...) custom-call(f32[192,1600]{1,0:T(8,128)} %get-tuple-element.79.refs_0, ...), custom_call_target="tpu_custom_call" | custom-call | flops 99999997952 | bytes 31457280 | tf_op jit(solution)/shard_map/pallas_call | solution.py:1015
  613.4 54.3 %shard_map.266 = (f32[192,1600]{1,0:T(8,128)}, bf16[4,192,1600]{2,1,0:T(8,128)(2,1)}, f32[4,192,1600]{2,1,0:T(8,128)}, bf16[4,192,1600]{2,1,0:T(8,128)(2,1)}) custom-call(f32[192,1600]{1,0:T(8,128)} %get-tuple-element.81.refs_0_.refs_1_, f32[8,1600]{1,0:T(8,128)} %bitcast.327, f32[1,1600]{1,0:T(1,128)} %get-tuple-element.255.refs_2_, ...), custom_call_target="tpu_custom_call" | custom-call | flops 7864320000 | bytes 41943040 | tf_op jit(solution)/shard_map/pallas_call | solution.py:481
  667.8 2.2 convert_element_type.238
  671.2 65.1 %shard_map.267 = (f32[192,1600]{1,0:T(8,128)}, f32[8,1600]{1,0:T(8,128)}, f32[1,1600]{1,0:T(1,128)}, bf16[1600,1600]{1,0:T(8,128)(2,1)}, bf16[1600,1600]{1,0:T(8,128)(2,1)}) custom-call(f32[192,1600]{1,0:T(8,128)} %bitcast_convert_fusion.refs_0_, f32[192,1600]{1,0:T(8,128)} %get-tuple-element.81.refs_0_.refs_1_, f32[8,1600]{1,0:T(8,128)} %bitcast.328, ...), custom_call_target="tpu_custom_call" | custom-call | flops 15728640000 | bytes 52428800 | tf_op jit(solution)/shard_map/pallas_call | solution.py:639
  736.3 1.4 slice.685
  737.7 1.3 convert.74
  739.0 1.7 fusion.48
  740.7 1.6 pad_maximum_fusion.2.refs_7_
  742.3 219.5 %shard_map.268 = (f32[192,1600]{1,0:T(8,128)}, f32[8,1600]{1,0:T(8,128)}, f32[1,1536]{1,0:T(1,128)}, bf16[1600,1536]{1,0:T(8,128)(2,1)}, bf16[1600,448]{1,0:T(8,...) custom-call(f32[192,1600]{1,0:T(8,128)} %get-tuple-element.87.refs_0_, ...), custom_call_target="tpu_custom_call" | custom-call | flops 199999995904 | bytes 52428800 | tf_op jit(solution)/shard_map/pallas_call | solution.py:1240
  964.3 2.9 fusion.14
  967.2 3.9 fusion.3.refs_7_
  971.1 77.1 %shard_map.269 = (f32[192,1600]{1,0:T(8,128)}, f32[8,1600]{1,0:T(8,128)}, f32[1,1600]{1,0:T(1,128)}, bf16[1600,1600]{1,0:T(8,128)(2,1)}, bf16[1600,1600]{1,0:T(8...) custom-call(f32[192,1600]{1,0:T(8,128)} %get-tuple-element.96.refs_0_, ...), custom_call_target="tpu_custom_call" | custom-call | flops 15728640000 | bytes 52428800 | tf_op jit(solution)/shard_map/pallas_call | solution.py:639
  1048.2 2.3 fusion.17.refs_12_
  1050.5 4.8 fusion.2.refs_10_
  1055.4 3.8 fusion.5.refs_11_
  1059.2 1.7 fusion.47
  1060.9 1.6 pad_maximum_fusion.3.refs_7_
  1062.5 219.2 %shard_map.270 = (f32[192,1600]{1,0:T(8,128)}, f32[8,1600]{1,0:T(8,128)}, f32[1,1536]{1,0:T(1,128)}, bf16[1600,1536]{1,0:T(8,128)(2,1)}, bf16[1600,448]{1,0:T(8,...) custom-call(f32[192,1600]{1,0:T(8,128)} %get-tuple-element.107.refs_, ...), custom_call_target="tpu_custom_call" | custom-call | flops 199999995904 | bytes 52428800 | tf_op jit(solution)/shard_map/pallas_call | solution.py:1240
  1282.6 4.9 fusion.1.refs_0_
  1288.5 2.3 fusion.refs_1_
  1292.6 1.5 fusion.15
  1294.1 117.2 %shard_map.271 = (bf16[3,200,1600]{2,1,0:T(8,128)(2,1)}, bf16[3,200,1600]{2,1,0:T(8,128)(2,1)}, bf16[4,200,1536]{2,1,0:T(8,128)(2,1)}, bf16[4,200,512]{2,1,0:T(8,128)(2,1)}) custom-call(bf16[4,200,1600]{2,1,0:T(8,128)(2,1)} %fusion.1.refs_0_, bf16[4,200,1600]{2,1,0:T(8,128)(2,1)} %fusion.refs_1_, bf16[4,2,200,1536]{3,2,1,0:T(8,128)(2,1)} %bitcast.294, ...), custom_call_target="tpu_custom_call" | custom-call | tf_op jit(solution)/shard_map/pallas_call | solution.py:1306
  1411.4 4.7 fusion.4.refs_0_
  1418.3 1.8 fusion.45
  1422.3 72.6 %shard_map.272 = (bf16[3,200,1536]{2,1,0:T(8,128)(2,1)}, bf16[3,200,512]{2,1,0:T(8,128)(2,1)}, bf16[4,200,2048]{2,1,0:T(8,128)(2,1)}) custom-call(bf16[4,200,1536]{2,1,0:T(8,128)(2,1)} %fusion.4.refs_0_, bf16[4,200,512]{2,1,0:T(8,128)(2,1)} %fusion.16.refs_1_, bf16[200,2048]{1,0:T(8,128)(2,1)} %pad_maximum_fusion.4.refs_2_), custom_call_target="tpu_custom_call" | custom-call | tf_op jit(solution)/shard_map/pallas_call | solution.py:1306
  1494.9 3.1 slice_bitcast_fusion.6
  1498.0 1.8 convert_reduce_fusion.8
  1499.9 1.8 fusion.44
  1502.0 1.2 fusion.29
  1504.2 27.4 %shard_map.273 = bf16[4,200,2048]{2,1,0:T(8,128)(2,1)} custom-call(bf16[200,2048]{1,0:T(8,128)(2,1)} %pad_maximum_fusion.5.refs_0_), custom_call_target="tpu_custom_call" | custom-call | tf_op jit(solution)/shard_map/pallas_call | solution.py:1306
  1531.6 3.0 slice_bitcast_fusion.9
  1534.6 1.7 convert_reduce_fusion.9
  1556.6 1.4 bitcast_add_fusion
  1558.7 2.4 bitcast_add_fusion.1
  1564.2 2.5 fusion.26
  1567.0 2.3 fusion.27
  1572.2 3.4 concatenate.159
  1575.5 4.5 concatenate.149
  1580.1 5.3 maximum_convert_fusion
  1585.4 1.8 pad_maximum_fusion
  1588.2 1.7 pad_maximum_fusion.1
  1590.0 1.7 maximum_convert_fusion.1
  (223 shorter events, 54.9 us)
Async XLA Ops:
  7.2 731.8 %all-gather.5.cloned.1.call-start = ((), (), s32[]{:S(2)}) async-start(), calls=%async_computation | async-start | bytes 3932160 | tf_op jit(solution)/shard_map/all_gather | solution.py:1328
  10.9 2.8 copy-start.16
  10.9 3.8 copy-start.41
  10.9 3.8 copy-start.42
  10.9 3.8 copy-start.43
  10.9 3.8 copy-start.44
  10.9 3.8 copy-start.45
  10.9 3.9 copy-start.46
  10.9 3.9 copy-start.47
  10.9 3.9 copy-start.48
  10.9 3.9 copy-start.49
  13.7 2.3 copy-start.23
  111.9 2.3 copy-start.26
  111.9 4.4 copy-start.17
  113.5 2.9 copy-start.18
  120.2 193.2 %copy-start.21 = (bf16[200,448]{1,0:T(8,128)(2,1)S(1)}, bf16[200,448]{1,0:T(8,128)(2,1)}, u32[]{:S(2)}) copy-start(bf16[200,448]{1,0:T(8,128)(2,1)} %get-tuple-element.244) | copy-start | bytes 537604
  120.2 193.2 %copy-start.22 = (bf16[200,448]{1,0:T(8,128)(2,1)S(1)}, bf16[200,448]{1,0:T(8,128)(2,1)}, u32[]{:S(2)}) copy-start(bf16[200,448]{1,0:T(8,128)(2,1)} %get-tuple-element.245) | copy-start | bytes 537604
  612.7 446.6 %all-gather.7.cloned.1.call-start = ((), (), s32[]{:S(2)}) async-start(), calls=%async_computation.1 | async-start | bytes 3932160 | tf_op jit(solution)/shard_map/all_gather | solution.py:1328
  613.4 56.6 %copy-start.27 = (bf16[2,96,1600]{2,1,0:T(8,128)(2,1)S(1)}, bf16[2,96,1600]{2,1,0:T(8,128)(2,1)}, u32[]{:S(2)}) copy-start(bf16[2,96,1600]{2,1,0:T(8,128)(2,1)} %param.29) | copy-start | bytes 1843204
  742.3 221.6 %copy-start.37 = (bf16[3,1600]{1,0:T(4,128)(2,1)S(1)}, bf16[3,1600]{1,0:T(4,128)(2,1)}, u32[]{:S(2)}) copy-start(bf16[3,1600]{1,0:T(4,128)(2,1)} %slice.685) | copy-start | bytes 28804
  742.3 221.6 %copy-start.38 = (bf16[1,1600]{1,0:T(2,128)(2,1)S(1)}, bf16[1,1600]{1,0:T(2,128)(2,1)}, u32[]{:S(2)}) copy-start(bf16[1,1600]{1,0:T(2,128)(2,1)} %convert.74) | copy-start | bytes 9604
  961.8 5.4 copy-start.5
  971.1 77.1 %copy-start.4 = (bf16[1600,512]{1,0:T(8,128)(2,1)S(1)}, bf16[1600,512]{1,0:T(8,128)(2,1)}, u32[]{:S(2)}) copy-start(bf16[1600,512]{1,0:T(8,128)(2,1)} %fusion.14) | copy-start | bytes 4915204
  1050.5 4.9 copy-start.7
  1282.6 4.9 copy-start.36
  1282.6 4.9 copy-start.6
  1282.6 5.9 copy-start.15
  1288.4 2.3 copy-start.40
  1288.4 3.1 copy-start.39
  1288.5 3.8 slice-start.2
  1288.5 4.2 copy-start.14
  1411.4 4.7 copy-start
  1411.4 4.7 copy-start.24
  1416.1 2.0 copy-start.12
  1494.9 5.0 copy-start.35
  1498.0 3.7 copy-start.13
  1542.5 13.8 copy-start.9
  1556.6 1.8 copy-start.11
  1558.6 5.2 copy-start.8
  1564.2 2.5 copy-start.10
  1580.1 5.3 copy-start.1
  1585.4 1.9 copy-start.2
  1585.4 2.7 copy-start.3
  1588.1 1.7 copy-start.30
  1588.1 1.7 copy-start.31
  1588.1 1.7 copy-start.32
  1588.2 1.9 copy-start.33
  1589.8 1.9 copy-start.20
  (7 other events, 10.6 us)
Sparse Core Ops, SparseCore 0:
  612.8 38.3 all-gather.4
  652.7 43.2 all-gather.6

commit v6 on v5

--- a/solution.py
+++ b/solution.py
@@ -158,6 +158,15 @@
     def behind(self, k):
         return (self.z + 4 - k) % 4
 
+    def greet_group(self):
+        barrier = pltpu.get_barrier_semaphore()
+        others = [self.at(self.z, 1 - self.y)] + [self.at(self.ahead(k), self.y) for k in (1, 2, 3)]
+        for member in others:
+            pl.semaphore_signal(
+                barrier, inc=1, device_id=(self.base + member, self.t), device_id_type=MESH
+            )
+        pl.semaphore_wait(barrier, 4)
+
     def greet(self, peers, with_diag=False):
         barrier = pltpu.get_barrier_semaphore()
         others = [self.at(self.z, 1 - self.y)] + [self.at(self.ahead(k), self.y) for k in (1, 2, 3)]
@@ -181,60 +190,127 @@
         )
 
 
-class Background:
-    def __init__(self, group, peers, kinds, sources, targets, sems):
-        self.g, self.p, self.sems = group, peers, sems
-        self.items = list(zip(kinds, sources, targets))
-
-    def block_copies(self, n, source, target):
-        p, sems = self.p, self.sems
-        return (
-            p.copy(source, target.at[p.t], sems, 4 * n, p.core),
-            p.copy(source, target.at[p.t], sems, 4 * n + 1, p.over),
-            p.copy(target.at[p.over], target.at[p.over], sems, 4 * n + 2, p.core),
-            pltpu.make_async_copy(source, target.at[p.t], sems[0].at[4 * n + 3]),
+class Reduce:
+    def __init__(self, group, source, from_y, from_z, sems, tiles):
+        self.g, self.source, self.from_y, self.from_z, self.sems = group, source, from_y, from_z, sems
+        self.own, self.got, self.gone, self.local = tiles
+
+    def across(self, j):
+        g = self.g
+        z = g.ahead(j)
+        return g.copy(
+            self.source.at[z, 1 - g.y], self.from_y.at[z], self.sems, j, g.at(g.z, 1 - g.y)
         )
 
-    def copies(self):
+    def along(self, j):
         g = self.g
-        made = []
-        for n, (kind, source, target) in enumerate(self.items):
-            if kind == "y":
-                made.append(g.copy(source.at[:, 1 - g.y], target, self.sems, 4 * n, g.at(g.z, 1 - g.y)))
-            elif kind == "z":
-                for k in (1, 2, 3):
-                    to = g.ahead(k)
-                    made.append(
-                        g.copy(source.at[to], target.at[k - 1], self.sems, 4 * n + k - 1, g.at(to, g.y))
-                    )
-        return made
+        return g.copy(self.gone.at[j - 1], self.from_z.at[j - 1], self.sems, 3 + j, g.at(g.ahead(j), g.y))
 
     def start(self):
-        for copy in self.copies():
-            copy.start()
-        for n, (kind, source, target) in enumerate(self.items):
-            if kind == "t":
-                to_core, to_over, _, local = self.block_copies(n, source, target)
-                to_over.start()
-                to_core.start()
-                local.start()
-
-    def finish(self):
-        p = self.p
-        for n, (kind, source, target) in enumerate(self.items):
-            if kind == "t":
-                p.copy(source, target.at[p.over], self.sems, 4 * n + 1, p.over).wait_recv()
-                self.block_copies(n, source, target)[2].start()
-        for copy in self.copies():
-            copy.wait()
-        for n, (kind, source, target) in enumerate(self.items):
-            if kind == "t":
-                p.copy(source, target.at[p.core], self.sems, 4 * n, p.core).wait_recv()
-                p.copy(source, target.at[p.diag], self.sems, 4 * n + 2, p.core).wait_recv()
-                to_core, to_over, relay, local = self.block_copies(n, source, target)
-                for copy in (to_core, to_over, relay):
-                    copy.wait_send()
-                local.wait()
+        for j in (1, 2, 3, 0):
+            self.across(j).start()
+
+    def pump(self, j, before=None):
+        g = self.g
+        load_own = pltpu.make_async_copy(self.source.at[g.ahead(j), g.y], self.own, self.local.at[0])
+        load_own.start()
+        self.across(j).wait_recv()
+        load_got = pltpu.make_async_copy(self.from_y.at[g.ahead(j)], self.got, self.local.at[1])
+        load_got.start()
+        load_own.wait()
+        load_got.wait()
+        if before is not None:
+            before.along(j).wait_send()
+        self.gone[j - 1] = self.own[...] + self.got[...]
+        self.along(j).start()
+
+    def finish(self, reused=False):
+        self.across(0).wait_recv()
+        for j in range(4):
+            self.across(j).wait_send()
+        for j in (1, 2, 3):
+            self.along(j).wait_recv()
+            if not reused:
+                self.along(j).wait_send()
+
+
+def reduce_parts(payload):
+    results, scratch = (), []
+    for part in payload:
+        rows = part.shape[2:]
+        results += (jax.ShapeDtypeStruct((4,) + rows, bf16), jax.ShapeDtypeStruct((3,) + rows, bf16))
+        scratch += [pltpu.SemaphoreType.DMA((7,))] * 2
+    if payload:
+        scratch += [pltpu.VMEM(rows, bf16), pltpu.VMEM(rows, bf16), pltpu.VMEM((3,) + rows, bf16)]
+        scratch += [pltpu.SemaphoreType.DMA((2,))]
+    return tuple(payload), results, scratch
+
+
+def reduces(group, sources, results, scratch):
+    tiles = scratch[2 * len(sources) :]
+    return [
+        Reduce(group, source, results[2 * n], results[2 * n + 1], scratch[2 * n : 2 * n + 2], tiles)
+        for n, source in enumerate(sources)
+    ]
+
+
+def reduce_kernel(source, from_y, from_z, *scratch):
+    g = Group()
+    g.greet_group()
+    item = reduces(g, [source], [from_y, from_z], scratch)[0]
+    item.start()
+    for j in (1, 2, 3):
+        item.pump(j)
+    item.finish()
+
+
+def reduce_only(part, collective_id):
+    operands, results, scratch = reduce_parts([part])
+    return pl.pallas_call(
+        reduce_kernel,
+        out_shape=results,
+        in_specs=[ANY],
+        out_specs=(ANY, ANY),
+        scratch_shapes=scratch,
+        compiler_params=params(collective_id),
+    )(part)
+
+
+def block_gather_kernel(n, *refs):
+    p = Peers()
+    p.greet()
+    sources, targets, (send, recv, local) = refs[:n], refs[n : 2 * n], refs[2 * n :]
+    keeps = []
+    for i in range(n):
+        keeps.append(pltpu.make_async_copy(sources[i], targets[i].at[p.t], local.at[i]))
+        keeps[-1].start()
+        p.copy(sources[i], targets[i].at[p.t], (send, recv), 3 * i + 1, p.over).start()
+        p.copy(sources[i], targets[i].at[p.t], (send, recv), 3 * i, p.core).start()
+
+    def relay(i):
+        return p.copy(targets[i].at[p.over], targets[i].at[p.over], (send, recv), 3 * i + 2, p.core)
+
+    for i in range(n):
+        p.copy(sources[i], targets[i].at[p.over], (send, recv), 3 * i + 1, p.over).wait_recv()
+        relay(i).start()
+    for i in range(n):
+        p.copy(sources[i], targets[i].at[p.core], (send, recv), 3 * i, p.core).wait()
+        p.copy(sources[i], targets[i].at[p.diag], (send, recv), 3 * i + 2, p.core).wait_recv()
+        p.copy(sources[i], targets[i].at[p.over], (send, recv), 3 * i + 1, p.over).wait_send()
+        relay(i).wait_send()
+        keeps[i].wait()
+
+
+def block_gather(parts, n_tp, collective_id):
+    n = len(parts)
+    return pl.pallas_call(
+        functools.partial(block_gather_kernel, n),
+        out_shape=tuple(jax.ShapeDtypeStruct((n_tp,) + part.shape, part.dtype) for part in parts),
+        in_specs=[ANY] * n,
+        out_specs=(ANY,) * n,
+        scratch_shapes=[pltpu.SemaphoreType.DMA((3 * n,))] * 2 + [pltpu.SemaphoreType.DMA((n,))],
+        compiler_params=params(collective_id),
+    )(*parts)
 
 
 class Spread:
@@ -298,11 +374,7 @@
 
 def spread_kernel(chunks, source, target, send, recv):
     g = Group()
-    barrier = pltpu.get_barrier_semaphore()
-    others = [g.at(g.z, 1 - g.y)] + [g.at(g.ahead(k), g.y) for k in (1, 2, 3)]
-    for member in others:
-        pl.semaphore_signal(barrier, inc=1, device_id=(g.base + member, g.t), device_id_type=MESH)
-    pl.semaphore_wait(barrier, len(others))
+    g.greet_group()
     spread = Spread(g, source, target, (send, recv), chunks)
     spread.start()
     for c in range(chunks):
@@ -320,16 +392,6 @@
         scratch_shapes=scratch,
         compiler_params=params(collective_id),
     )(shard)
-
-
-def sent_shapes(payload):
-    return tuple(
-        jax.ShapeDtypeStruct((3 if kind == "z" else 4,) + a.shape[-2:], a.dtype) for kind, a in payload
-    )
-
-
-def sent_scratch(payload):
-    return [pltpu.SemaphoreType.DMA((4 * len(payload) + 1,))] * 2
 
 
 def row_chunks(rows, body):
@@ -524,15 +586,14 @@
     ref[row : row + 1, :] += jnp.sum(value, axis=0, keepdims=True)
 
 
-def ff_bwd_kernel(kinds, *refs):
-    n = len(kinds)
+def ff_bwd_kernel(n, *refs):
     g_ref, x_ref, vec_ref, all_hbm, pre_hbm, hid_hbm, wb_hbm = refs[:7]
     sources, refs = refs[7 : 7 + n], refs[7 + n :]
     out_ref, sums_ref, fcb_ref, dfc_hbm, dproj_hbm = refs[:5]
-    targets, refs = refs[5 : 5 + n], refs[5 + n :]
+    results, refs = refs[5 : 5 + 2 * n], refs[5 + 2 * n :]
     wfc, wproj, buf, other, pre, dpre, stage, part, from_core, over_out, from_over, send, recv, local = refs[:14]
     p, g = Peers(), Group()
-    background = Background(g, p, kinds, sources, targets, refs[14:])
+    sums = reduces(g, sources, results, refs[14:])
     rows = x_ref.shape[0]
     n_tp, width = buf.shape[0], fcb_ref.shape[1]
     sems = (send, recv)
@@ -558,7 +619,13 @@
     else:
         p.greet()
     gather.start()
-    background.start()
+    for item in sums:
+        item.start()
+
+    def pump(j):
+        for item in sums:
+            item.pump(j)
+
     gather.wait_chip()
     load_proj.wait()
     load_pre.wait()
@@ -583,6 +650,7 @@
     gather.relay()
     gather.wait_diag()
     through(1 - p.x)
+    pump(1)
     load_fc.wait()
     down(1 - p.x)
     scatter.far_to_core().start()
@@ -609,6 +677,7 @@
         return pltpu.make_async_copy(stage, target, sem)
 
     load_other.wait()
+    pump(2)
     store = outer(buf, other, dproj_hbm, local.at[4])
     store.start()
     gather.finish()
@@ -628,16 +697,19 @@
     store.wait()
     store = outer(buf, dpre, dfc_hbm, local.at[6])
     store.start()
+    pump(3)
     scatter.finish()
     store.wait()
-    background.finish()
+    for item in sums:
+        item.finish()
 
 
 def ff_bwd(grad, x, vecs, all_rows, pre, hidden, w_b, n_tp, payload, collective_id):
     rows, width = x.shape[0], pre.shape[2]
     block = (n_tp, rows)
+    operands, results, more = reduce_parts(payload)
     return pl.pallas_call(
-        functools.partial(ff_bwd_kernel, tuple(kind for kind, _ in payload)),
+        functools.partial(ff_bwd_kernel, len(payload)),
         out_shape=(
             jax.ShapeDtypeStruct((rows, D), f32),
             jax.ShapeDtypeStruct((8, D), f32),
@@ -645,9 +717,9 @@
             jax.ShapeDtypeStruct((D, width), bf16),
             jax.ShapeDtypeStruct((D, width), bf16),
         )
-        + sent_shapes(payload),
+        + results,
         in_specs=[IN_VMEM] * 3 + [ANY] * (4 + len(payload)),
-        out_specs=(IN_VMEM, IN_VMEM, IN_VMEM) + (ANY,) * (2 + len(payload)),
+        out_specs=(IN_VMEM, IN_VMEM, IN_VMEM) + (ANY,) * (2 + 2 * len(payload)),
         scratch_shapes=[
             pltpu.VMEM((D, lanes_up(width)), bf16),
             pltpu.VMEM((D, lanes_up(width)), bf16),
@@ -659,12 +731,12 @@
         ]
         + scatter_scratch(n_tp, rows)
         + [pltpu.SemaphoreType.DMA((7,))]
-        + sent_scratch(payload),
+        + more,
         compiler_params=params(collective_id),
         cost_estimate=pl.CostEstimate(
             flops=8 * n_tp * rows * D * width, bytes_accessed=50 * 2**20, transcendentals=n_tp * rows * width
         ),
-    )(grad, x, vecs, all_rows, pre, hidden, w_b, *(a for _, a in payload))
+    )(grad, x, vecs, all_rows, pre, hidden, w_b, *operands)
 
 
 class Share:
@@ -712,37 +784,50 @@
         self.g, self.parts, self.sems = group, parts, sems
         self.from_y, self.to_z, self.from_z = from_y, to_z, from_z
 
-    def across(self, micro):
-        g = self.g
+    def lanes(self, half):
+        return slice(half * WIDE // 2, (half + 1) * WIDE // 2)
+
+    def across(self, micro, half):
+        g, lanes = self.g, self.lanes(half)
         return g.copy(
-            self.parts.at[micro, :, 1 - g.y], self.from_y.at[micro], self.sems, micro * 4, g.at(g.z, 1 - g.y)
+            self.parts.at[micro, :, 1 - g.y, :, :, lanes],
+            self.from_y.at[micro, :, :, :, lanes],
+            self.sems,
+            (2 * micro + half) * 4,
+            g.at(g.z, 1 - g.y),
         )
 
-    def along(self, micro, k):
-        g = self.g
+    def along(self, micro, half, k):
+        g, lanes = self.g, self.lanes(half)
         to = g.ahead(k)
         return g.copy(
-            self.to_z.at[micro, to], self.from_z.at[micro, k - 1], self.sems, micro * 4 + k, g.at(to, g.y)
+            self.to_z.at[micro, to, :, :, lanes],
+            self.from_z.at[micro, k - 1, :, :, lanes],
+            self.sems,
+            (2 * micro + half) * 4 + k,
+            g.at(to, g.y),
         )
 
-    def start(self, micro):
-        self.across(micro).start()
-
-    def turn(self, micro):
-        self.across(micro).wait_recv()
+    def start(self, micro, half):
+        self.across(micro, half).start()
+
+    def turn(self, micro, half):
+        lanes = self.lanes(half)
+        self.across(micro, half).wait_recv()
 
         @pl.loop(0, 4)
         def _(z):
             for kv in range(2):
-                total = self.parts[micro, z, self.g.y, kv].astype(f32) + self.from_y[micro, z, kv].astype(f32)
-                self.to_z[micro, z, kv] = total.astype(bf16)
+                total = self.parts[micro, z, self.g.y, kv, :, lanes] + self.from_y[micro, z, kv, :, lanes]
+                self.to_z[micro, z, kv, :, lanes] = total
 
         for k in (1, 2, 3):
-            self.along(micro, k).start()
+            self.along(micro, half, k).start()
 
     def wait(self, micro):
-        for k in (1, 2, 3):
-            self.along(micro, k).wait_recv()
+        for half in range(2):
+            for k in (1, 2, 3):
+                self.along(micro, half, k).wait_recv()
 
     def total(self, micro, kv):
         g = self.g
@@ -752,9 +837,10 @@
         return value.astype(bf16)
 
     def finish(self, micro):
-        self.across(micro).wait_send()
-        for k in (1, 2, 3):
-            self.along(micro, k).wait_send()
+        for half in range(2):
+            self.across(micro, half).wait_send()
+            for k in (1, 2, 3):
+                self.along(micro, half, k).wait_send()
 
 
 WIDE = 512
@@ -1043,21 +1129,20 @@
     )(x, vecs, biases, w_a, *operands)
 
 
-def attn_bwd_kernel(kinds, *refs):
-    n = len(kinds)
+def attn_bwd_kernel(n, *refs):
     g_ref, x_ref, vec_ref, lse_ref, all_hbm, own_hbm, kv_hbm, mix_hbm, wqkv_hbm, wout_hbm = refs[:10]
     sources, refs = refs[10 : 10 + n], refs[10 + n :]
-    out_ref, sums_ref, cols_ref, dqkv_hbm, dout_hbm = refs[:5]
-    targets, refs = refs[5 : 5 + n], refs[5 + n :]
+    out_ref, sums_ref, cols_ref, dqo_hbm = refs[:4]
+    results, refs = refs[4 : 4 + 2 * n], refs[4 + 2 * n :]
     wqkv, wout, buf, other, own, kv, gm, dkv, from_y, to_z, from_z, dkc, dqkv, stage, stage_out = refs[:15]
     p_ref, dp_ref, ds_ref, o_ref = refs[15:19]
     part, from_core, over_out, from_over, send, recv, gsend, grecv, local = refs[19:28]
     p, g = Peers(), Group()
-    background = Background(g, p, kinds, sources, targets, refs[28:])
+    sums = reduces(g, sources, results, refs[28:])
     rows = x_ref.shape[0]
     n_tp = buf.shape[0]
-    out_width = stage_out.shape[1]
-    out_step = (D - out_width) // (n_tp - 1)
+    out_step = HEADS // n_tp * HEAD
+    out_width = D - out_step * (n_tp - 1)
     sems = (send, recv)
     gather = Gather(p, buf, sems)
     scatter = Scatter(p, part, from_core, over_out, from_over, sems)
@@ -1079,7 +1164,14 @@
     row_chunks(rows, lower)
     g.greet(p)
     gather.start()
-    background.start()
+    hooks = {(1, 0): [lambda: reduce.turn(0, 0)], (1, 1): [lambda: reduce.turn(0, 1)]}
+    if n:
+        first_sum, second_sum = sums
+        first_sum.start()
+        hooks[0, 1] = [lambda: first_sum.pump(2)]
+        hooks[0, 2] = [lambda: first_sum.pump(3), second_sum.start]
+        for k in range(3):
+            hooks.setdefault((1, k), []).append(lambda k=k: second_sum.pump(k + 1, first_sum))
     gather.wait_chip()
     load_out.wait()
 
@@ -1095,14 +1187,19 @@
     limit = key_limit(g.member)
     sub = lax.broadcasted_iota(jnp.int32, (CHUNK, TOK_DEV), 0)
 
+    if n:
+        first_sum.pump(1)
+
     for micro in range(MICRO):
 
         def head(pair, lanes, half, micro=micro):
-            if micro == 1 and half == 0:
-
-                @pl.when(pair == HEAD_PAIRS - 1)
-                def _():
-                    reduce.turn(0)
+            for at in range(HEAD_PAIRS):
+                if half == 0 and (micro, at) in hooks:
+
+                    @pl.when(pair == at)
+                    def _(at=at):
+                        for hook in hooks[micro, at]:
+                            hook()
 
             qh = half_of(own[0, micro, :, lanes], half)
             gh = half_of(gm[micro, :, lanes], half)
@@ -1163,8 +1260,12 @@
 
             to_slots(dqkv, micro, 0, o_ref[...].T.astype(bf16), lanes)
 
+            @pl.when(pair == HEAD_PAIRS // 2 - 1)
+            def _():
+                reduce.start(micro, 0)
+
         head_pairs(head, finish)
-        reduce.start(micro)
+        reduce.start(micro, 1)
         for i in range(2):
             to_slots(dqkv, micro, PROMPT_DEV, dkc[i], slice((1 + i) * WIDE, (2 + i) * WIDE))
 
@@ -1176,16 +1277,18 @@
 
         def tile(at):
             left = source[:, :, at].reshape(n_tp * rows, -1)
-            target[at, :] = mm(left, flat, TN).astype(bf16)
+            target[at, : flat.shape[1]] = mm(left, flat, TN).astype(bf16)
 
         body(D, tile)
 
+    reduce.turn(1, 0)
+    stage_out[:, out_width:] = jnp.zeros((D, WIDE - out_width), bf16)
     outer(other, stage_out, buf[:, :, columns], tiles)
-    keep_out = pltpu.make_async_copy(stage_out, dout_hbm, local.at[5])
+    keep_out = pltpu.make_async_copy(stage_out, dqo_hbm.at[:, 3 * WIDE :], local.at[5])
     keep_out.start()
     load_all = pltpu.make_async_copy(all_hbm, other, local.at[6])
     load_all.start()
-    reduce.turn(1)
+    reduce.turn(1, 1)
     for micro in range(MICRO):
         reduce.wait(micro)
         for i in range(2):
@@ -1205,7 +1308,7 @@
     scatter.near_to_core().start()
     load_all.wait()
     outer(other, stage, dqkv[...], tiles)
-    keep_qkv = pltpu.make_async_copy(stage, dqkv_hbm, local.at[7])
+    keep_qkv = pltpu.make_async_copy(stage, dqo_hbm.at[:, : 3 * WIDE], local.at[7])
     keep_qkv.start()
     cols_ref[...] = jnp.zeros_like(cols_ref)
 
@@ -1231,24 +1334,25 @@
         reduce.finish(micro)
     keep_out.wait()
     keep_qkv.wait()
-    background.finish()
-
-
-def attn_bwd(grad, x, vecs, lse, all_rows, own, kv, mixed_all, w_a, w_out, out_width, n_tp, payload, collective_id):
+    for i, item in enumerate(sums):
+        item.finish(i < n - 1)
+
+
+def attn_bwd(grad, x, vecs, lse, all_rows, own, kv, mixed_all, w_a, w_out, n_tp, payload, collective_id):
     rows = x.shape[0]
+    operands, results, more = reduce_parts(payload)
     pieces = (MICRO, 4, 2, 2, PROMPT_DEV, WIDE)
     return pl.pallas_call(
-        functools.partial(attn_bwd_kernel, tuple(kind for kind, _ in payload)),
+        functools.partial(attn_bwd_kernel, len(payload)),
         out_shape=(
             jax.ShapeDtypeStruct((rows, D), f32),
             jax.ShapeDtypeStruct((8, D), f32),
             jax.ShapeDtypeStruct((1, 3 * WIDE), f32),
-            jax.ShapeDtypeStruct((D, 3 * WIDE), bf16),
-            jax.ShapeDtypeStruct((D, out_width), bf16),
+            jax.ShapeDtypeStruct((D, 4 * WIDE), bf16),
         )
-        + sent_shapes(payload),
+        + results,
         in_specs=[IN_VMEM] * 4 + [ANY] * (6 + len(payload)),
-        out_specs=(IN_VMEM, IN_VMEM, IN_VMEM) + (ANY,) * (2 + len(payload)),
+        out_specs=(IN_VMEM, IN_VMEM, IN_VMEM) + (ANY,) * (1 + 2 * len(payload)),
         scratch_shapes=[
             pltpu.VMEM((D, 3 * WIDE), bf16),
             pltpu.VMEM((WIDE, D), bf16),
@@ -1264,7 +1368,7 @@
             pltpu.VMEM((2, CONT_LEN, WIDE), bf16),
             pltpu.VMEM((n_tp, rows, 3 * WIDE), bf16),
             pltpu.VMEM((D, 3 * WIDE), bf16),
-            pltpu.VMEM((D, out_width), bf16),
+            pltpu.VMEM((D, WIDE), bf16),
             pltpu.VMEM((KEYS, TOK_DEV), f32),
             pltpu.VMEM((KEYS, TOK_DEV), f32),
             pltpu.VMEM((KEYS, TOK_DEV), bf16),
@@ -1272,45 +1376,14 @@
         ]
         + scatter_scratch(n_tp, rows)
         + [
-            pltpu.SemaphoreType.DMA((4 * MICRO,)),
-            pltpu.SemaphoreType.DMA((4 * MICRO,)),
+            pltpu.SemaphoreType.DMA((8 * MICRO,)),
+            pltpu.SemaphoreType.DMA((8 * MICRO,)),
             pltpu.SemaphoreType.DMA((8,)),
         ]
-        + sent_scratch(payload),
+        + more,
         compiler_params=params(collective_id),
         cost_estimate=pl.CostEstimate(flops=2 * 10**11, bytes_accessed=50 * 2**20, transcendentals=0),
-    )(grad, x, vecs, lse, all_rows, own, kv, mixed_all, w_a, w_out, *(a for _, a in payload))
-
-
-def send_kernel(kinds, *refs):
-    n = len(kinds)
-    p, g = Peers(), Group()
-    background = Background(g, p, kinds, refs[:n], refs[n : 2 * n], refs[2 * n :])
-    barrier = pltpu.get_barrier_semaphore()
-    others = []
-    if "y" in kinds:
-        others += [g.at(g.z, 1 - g.y)]
-    if "z" in kinds:
-        others += [g.at(g.ahead(k), g.y) for k in (1, 2, 3)]
-    for member in others:
-        pl.semaphore_signal(barrier, inc=1, device_id=(g.base + member, g.t), device_id_type=MESH)
-    near = [p.core, p.over] if "t" in kinds else []
-    for t in near:
-        pl.semaphore_signal(barrier, inc=1, device_id=(p.f, t), device_id_type=MESH)
-    pl.semaphore_wait(barrier, len(others) + len(near))
-    background.start()
-    background.finish()
-
-
-def send_only(payload, collective_id):
-    return pl.pallas_call(
-        functools.partial(send_kernel, tuple(kind for kind, _ in payload)),
-        out_shape=sent_shapes(payload),
-        in_specs=[ANY] * len(payload),
-        out_specs=(ANY,) * len(payload),
-        scratch_shapes=sent_scratch(payload),
-        compiler_params=params(collective_id),
-    )(*(a for _, a in payload))
+    )(grad, x, vecs, lse, all_rows, own, kv, mixed_all, w_a, w_out, *operands)
 
 
 def forward_layer(x, layer, fetch, vecs, fc_bias, cols, n_tp):
@@ -1369,23 +1442,18 @@
     return jnp.pad(value, pads)
 
 
-def to_y(part):
-    return ("y", part.reshape(4, 2, -1, part.shape[1]))
-
-
-def to_z(part, arrived):
-    own = lax.dynamic_index_in_dim(part.reshape(4, 2, -1, part.shape[1]), lax.axis_index("fsdp") % 2, 1, False)
-    return ("z", (own.astype(f32) + arrived.astype(f32)).astype(bf16))
-
-
-def owned(summed, arrived):
-    own = lax.dynamic_index_in_dim(summed[1], lax.axis_index("fsdp") // 2, 0, False)
-    return own.astype(f32) + jnp.sum(arrived.astype(f32), 0)
-
-
-def with_vectors(grad_out, ff_sums, attn_sums, col_sums, fc_bias_sums, cols):
-    width = grad_out.shape[1]
-
+def by_owner(part):
+    return part.reshape(4, 2, -1, part.shape[1])
+
+
+def owned(part, from_y, from_z):
+    z, y = lax.axis_index("fsdp") // 2, lax.axis_index("fsdp") % 2
+    own = lax.dynamic_index_in_dim(lax.dynamic_index_in_dim(part, z, 0, False), y, 0, False)
+    near = lax.dynamic_index_in_dim(from_y, z, 0, False)
+    return own.astype(f32) + near.astype(f32) + jnp.sum(from_z.astype(f32), 0)
+
+
+def with_vectors(grad_qo, ff_sums, attn_sums, col_sums, fc_bias_sums, cols, width):
     def placed(part):
         return lax.dynamic_update_slice_in_dim(jnp.zeros((1, D), f32), part, cols, 1)
 
@@ -1399,77 +1467,59 @@
             fc_bias_sums,
         ]
     )
-    return widen(jnp.concatenate([grad_out, vector_grads.astype(bf16).T], axis=1))
+    return lax.dynamic_update_slice(grad_qo, vector_grads.astype(bf16).T, (0, 3 * WIDE + width))
 
 
 def backward(grad, weights, vecs, saves, cols, n_tp):
     width = D - HEADS // n_tp * HEAD * (n_tp - 1)
     staged = lax.axis_size("fsdp") == GROUP
-    sums = [None] * LAYERS
-    joined = [None] * LAYERS
-    waiting_y, waiting_z, waiting_t, done = [], [], [], {}
-
-    def load(limit_z, limit_y):
-        chosen_z = [waiting_z.pop(0) for _ in range(min(limit_z, len(waiting_z)))]
-        chosen_y = [waiting_y.pop(0) for _ in range(min(limit_y, len(waiting_y)))]
-        return chosen_z, chosen_y, [item for _, item in chosen_z] + [to_y(part) for _, part in chosen_y]
-
-    def unload(chosen_z, chosen_y, arrived):
-        for (name, item), got in zip(chosen_z, arrived):
-            done[name] = owned(item, got)
-        for (name, part), got in zip(chosen_y, arrived[len(chosen_z) :]):
-            waiting_z.append((name, to_z(part, got)))
-
-    def produced(layer, names, values):
-        for name, value in zip(names, values):
-            if staged:
-                waiting_y.append(((layer, name), value))
-            else:
-                done[layer, name] = fsdp_sum(value)
-
-    plan = {(1, 0): (0, 0), (1, 1): (0, 2), (0, 0): (1, 2), (0, 1): (3, 2)}
+    done, joined, waiting = {}, {}, {}
+
+    def during(keys, kernel):
+        payload = [waiting.pop(key) for key in keys if key in waiting]
+        results = list(kernel(payload))
+        if payload:
+            arrived = results[-2 * len(payload) :]
+            results = results[: -2 * len(payload)]
+            for i, key in enumerate(keys):
+                done[key] = owned(payload[i], arrived[2 * i], arrived[2 * i + 1])
+        return results
+
+    def produced(key, value):
+        if staged:
+            waiting[key] = by_owner(value)
+        else:
+            done[key] = fsdp_sum(value)
+
     for layer in reversed(range(LAYERS)):
         w_a, w_b = weights[layer, "a"], weights[layer, "b"]
         x, w_out, lse, all_rows, own, kv, mixed_all, x_mid, second_all, hidden_pre, hidden = saves[layer]
-        chosen_z, chosen_y, payload = load(*plan[layer, 0])
-        grad, ff_sums, fc_bias_sums, grad_fc, grad_proj, *arrived = ff_bwd(
-            grad, x_mid, vecs[layer], second_all, hidden_pre, hidden, w_b, n_tp, payload, 10 + layer
+        grad, ff_sums, fc_bias_sums, grad_fc, grad_proj = during(
+            [(layer + 1, "qo")],
+            lambda payload: ff_bwd(
+                grad, x_mid, vecs[layer], second_all, hidden_pre, hidden, w_b, n_tp, payload, 10 + layer
+            ),
         )
-        unload(chosen_z, chosen_y, arrived)
-        produced(layer, ("proj", "fc"), (grad_proj, grad_fc))
-        chosen_z, chosen_y, payload = load(*plan[layer, 1])
-        grad, attn_sums, col_sums, grad_qkv, grad_out, *arrived = attn_bwd(
-            grad, x, vecs[layer], lse, all_rows, own, kv, mixed_all, w_a, w_out, width, n_tp, payload, 20 + layer
+        produced((layer, "proj"), grad_proj)
+        produced((layer, "fc"), grad_fc)
+        grad, attn_sums, col_sums, grad_qo = during(
+            [(layer, "proj"), (layer, "fc")],
+            lambda payload: attn_bwd(
+                grad, x, vecs[layer], lse, all_rows, own, kv, mixed_all, w_a, w_out, n_tp, payload, 20 + layer
+            ),
         )
-        unload(chosen_z, chosen_y, arrived)
-        grad_out = with_vectors(grad_out, ff_sums, attn_sums, col_sums, fc_bias_sums, cols)
-        produced(layer, ("qkv", "out"), (grad_qkv, grad_out))
-    number = 30
-    asked = set()
-    while len(asked) < LAYERS or waiting_t:
-        chosen_z, chosen_y, payload = load(9, 9)
-        chosen_t, waiting_t = waiting_t, []
-        arrived = []
-        if payload or chosen_t:
-            arrived = list(send_only(payload + [("t", part) for _, part in chosen_t], number))
-            number += 1
-        unload(chosen_z, chosen_y, arrived)
-        for (layer, _), got in zip(chosen_t, arrived[len(payload) :]):
-            joined[layer] = got
-        for layer in range(LAYERS):
-            if layer not in asked and (layer, "qkv") in done and (layer, "out") in done:
-                asked.add(layer)
-                both = jnp.concatenate([done[layer, "qkv"], done[layer, "out"]], axis=1).astype(bf16)
-                waiting_t.append((layer, both))
-    for layer in range(LAYERS):
-        got = joined[layer]
+        produced((layer, "qo"), with_vectors(grad_qo, ff_sums, attn_sums, col_sums, fc_bias_sums, cols, width))
+    during([(0, "qo")] if staged else [], lambda payload: reduce_only(payload[0], 30) if payload else ())
+    sums = []
+    both = block_gather([done[layer, "qo"].astype(bf16) for layer in range(LAYERS)], n_tp, 31)
+    for layer, got in enumerate(both):
         qkv_grad = jnp.concatenate(
             [heads_joined(got[:, :, i * WIDE : i * WIDE + width], n_tp) for i in range(3)], axis=1
         ).astype(f32)
         out_grad = heads_joined(got[:, :, 3 * WIDE : 3 * WIDE + width], n_tp).astype(f32)
         vector_sum = jnp.sum(got[:, :, 3 * WIDE + width : 3 * WIDE + width + 8].astype(f32), 0).T
-        fc_bias_sum = done[layer, "out"][:, width + 8]
-        sums[layer] = (qkv_grad, out_grad, done[layer, "fc"], done[layer, "proj"].T, fc_bias_sum, vector_sum)
+        fc_bias_sum = done[layer, "qo"][:, 3 * WIDE + width + 8]
+        sums.append((qkv_grad, out_grad, done[layer, "fc"], done[layer, "proj"].T, fc_bias_sum, vector_sum))
     return grad, sums
 
 

time: 1610 us -> 1590 us (0.988)
  other arithmetic: 79.7 us -> 47.5 us
    convert_element_type x8 -> x2, other arithmetic: 27.9 us -> 6.46 us  [backward(): done[layer, 'qo'].astype(bf16)]
    pallas_call x7 -> x6, Pallas kernels: 798 us -> 802 us  [the longest x2 490 us: attn_bwd(): pl.pallas_call(functools.partial(attn_bwd_kernel, len(payload)), out_shap...]
  transfers between devices with their start and end apart: 2 -> 2, of which waited for: 0 -> 0; matrix products, arithmetic and copies ran while one was open for 2% -> 1% of each run, Pallas kernels for 26% -> 23%
where the time goes in v6:
time: 1590 us; the launch traced here: 1580 us
  Pallas kernels  1440 us (91%)
  local copies, waits for them, and re-layouts  73.8 us (5%)
  other arithmetic  47.5 us (3%)
    pallas_call x2, Pallas kernels, attn_bwd(): pl.pallas_call(functools.partial(attn_bwd_kernel, len(payload)), out_shap...  490 us
    pallas_call x2, Pallas kernels, attn_fwd(): pl.pallas_call(functools.partial(attn_fwd_kernel, len(operands)), out_sha...  386 us
    pallas_call x2, Pallas kernels, ff_bwd(): pl.pallas_call(functools.partial(ff_bwd_kernel, len(payload)), out_shape=...  165 us
    pallas_call x2, Pallas kernels, ff_fwd(): pl.pallas_call(functools.partial(ff_fwd_kernel, len(operands)), out_shape...  160 us
    pallas_call x1, Pallas kernels, reduce_only(): pl.pallas_call(reduce_kernel, out_shape=results, in_specs=[ANY], out_spec...  94.5 us
    pallas_call x1, Pallas kernels, spread_only(): pl.pallas_call(functools.partial(spread_kernel, chunks), out_shape=result...  93.8 us
    pallas_call x1, Pallas kernels, block_gather(): pl.pallas_call(functools.partial(block_gather_kernel, n), out_shape=tuple...  52 us
  transfers between devices with their start and end apart: 2, of which 0 were waited for; matrix products, arithmetic and copies ran while one was open for 1% of the time, Pallas kernels for 23%

profile of v6, /device:TPU:9, one launch (start us, length us, event | category | flops | bytes accessed | tf_op | source)
XLA Modules:
  0.0 1578.9 jit_solution(4843039561638465621)
XLA Ops:
  7.2 3.6 fusion.38
  11.0 2.7 dynamic-slice_bitcast_fusion.3
  16.0 1.1 dynamic-slice_bitcast_fusion
  18.1 93.8 %shard_map.262 = bf16[8,200,2176]{2,1,0:T(8,128)(2,1)} custom-call(bf16[200,2176]{1,0:T(8,128)(2,1)} %copy-done.12), custom_call_target="tpu_custom_call" | custom-call | tf_op jit(solution)/shard_map/pallas_call | solution.py:387
  111.9 1.2 convert_bitcast_fusion
  114.2 1.2 bitcast_convert_fusion.1.refs_0_.refs_1_
  118.5 1.7 fusion.12
  120.3 193.2 %shard_map.263 = (f32[192,1600]{1,0:T(8,128)}, f32[2,4,8,384]{3,2,1,0:T(8,128)}, bf16[4,192,1600]{2,1,0:T(8,128)(2,1)}, bf16[3,2,384,512]{3,2,1,0:T(8,128)(2,1)}...) custom-call(f32[192,1600]{1,0:T(8,128)} %bitcast_convert_fusion.1.re, ...), custom_call_target="tpu_custom_call" | custom-call | flops 99999997952 | bytes 31457280 | tf_op jit(solution)/shard_map/pallas_call | solution.py:1101
  314.5 105.1 %shard_map.264 = (f32[192,1600]{1,0:T(8,128)}, bf16[4,192,1600]{2,1,0:T(8,128)(2,1)}, f32[4,192,1600]{2,1,0:T(8,128)}, bf16[4,192,1600]{2,1,0:T(8,128)(2,1)}, bf16[8,200,2048]{2,1,0:T(8,128)(2,1)}) custom-call(f32[192,1600]{1,0:T(8,128)} %get-tuple-element.72.refs_0_.refs_1_, f32[8,1600]{1,0:T(8,128)} %bitcast.291, f32[1,1600]{1,0:T(1,128)} %get-tuple-element.248.refs_2_, ...), custom_call_target="tpu_custom_call" | custom-call | flops 7864320000 | bytes 41943040 | tf_op jit(solution)/shard_map/pallas_call | solution.py:543
  419.6 193.0 %shard_map.265 = (f32[192,1600]{1,0:T(8,128)}, f32[2,4,8,384]{3,2,1,0:T(8,128)}, bf16[4,192,1600]{2,1,0:T(8,128)(2,1)}, bf16[3,2,384,512]{3,2,1,0:T(8,128)(2,1)}...) custom-call(f32[192,1600]{1,0:T(8,128)} %get-tuple-element.74.refs_0, ...), custom_call_target="tpu_custom_call" | custom-call | flops 99999997952 | bytes 31457280 | tf_op jit(solution)/shard_map/pallas_call | solution.py:1101
  613.4 54.4 %shard_map.266 = (f32[192,1600]{1,0:T(8,128)}, bf16[4,192,1600]{2,1,0:T(8,128)(2,1)}, f32[4,192,1600]{2,1,0:T(8,128)}, bf16[4,192,1600]{2,1,0:T(8,128)(2,1)}) custom-call(f32[192,1600]{1,0:T(8,128)} %get-tuple-element.76.refs_0_.refs_1_, f32[8,1600]{1,0:T(8,128)} %bitcast.295, f32[1,1600]{1,0:T(1,128)} %get-tuple-element.245.refs_2_, ...), custom_call_target="tpu_custom_call" | custom-call | flops 7864320000 | bytes 41943040 | tf_op jit(solution)/shard_map/pallas_call | solution.py:543
  667.9 2.2 convert_element_type.175
  670.1 1.2 bitcast_convert_fusion.refs_0_
  671.2 65.0 %shard_map.267 = (f32[192,1600]{1,0:T(8,128)}, f32[8,1600]{1,0:T(8,128)}, f32[1,1600]{1,0:T(1,128)}, bf16[1600,1600]{1,0:T(8,128)(2,1)}, bf16[1600,1600]{1,0:T(8,128)(2,1)}) custom-call(f32[192,1600]{1,0:T(8,128)} %bitcast_convert_fusion.refs_0_, f32[192,1600]{1,0:T(8,128)} %get-tuple-element.76.refs_0_.refs_1_, f32[8,1600]{1,0:T(8,128)} %bitcast.296, ...), custom_call_target="tpu_custom_call" | custom-call | flops 15728640000 | bytes 52428800 | tf_op jit(solution)/shard_map/pallas_call | solution.py:711
  736.3 1.4 slice.685
  737.7 1.3 convert.58
  739.0 1.7 fusion.40
  740.7 1.6 pad_maximum_fusion.2.refs_7_
  742.3 247.7 %shard_map.268 = (f32[192,1600]{1,0:T(8,128)}, f32[8,1600]{1,0:T(8,128)}, f32[1,1536]{1,0:T(1,128)}, bf16[1600,2048]{1,0:T(8,128)(2,1)}, bf16[4,200,1600]{2,1,0:...) custom-call(f32[192,1600]{1,0:T(8,128)} %get-tuple-element.82.refs_0_, ...), custom_call_target="tpu_custom_call" | custom-call | flops 199999995904 | bytes 52428800 | tf_op jit(solution)/shard_map/pallas_call | solution.py:1345
  992.2 5.6 dynamic_update_slice.20
  997.8 1.7 fusion.39
  999.5 1.6 pad_maximum_fusion.3.refs_7_
  1001.1 100.3 %shard_map.269 = (f32[192,1600]{1,0:T(8,128)}, f32[8,1600]{1,0:T(8,128)}, f32[1,1600]{1,0:T(1,128)}, bf16[1600,1600]{1,0:T(8,128)(2,1)}, bf16[1600,1600]{1,0:T(8...) custom-call(f32[192,1600]{1,0:T(8,128)} %get-tuple-element.91.refs_0_, ...), custom_call_target="tpu_custom_call" | custom-call | flops 15728640000 | bytes 52428800 | tf_op jit(solution)/shard_map/pallas_call | solution.py:711
  1101.4 242.7 %shard_map.270 = (f32[192,1600]{1,0:T(8,128)}, f32[8,1600]{1,0:T(8,128)}, f32[1,1536]{1,0:T(1,128)}, bf16[1600,2048]{1,0:T(8,128)(2,1)}, bf16[4,200,1600]{2,1,0:...) custom-call(f32[192,1600]{1,0:T(8,128)} %get-tuple-element.100.refs_0_, ...), custom_call_target="tpu_custom_call" | custom-call | flops 199999995904 | bytes 52428800 | tf_op jit(solution)/shard_map/pallas_call | solution.py:1345
  1347.2 5.8 dynamic_update_slice.23
  1353.1 94.5 %shard_map.271 = (bf16[4,200,2048]{2,1,0:T(8,128)(2,1)}, bf16[3,200,2048]{2,1,0:T(8,128)(2,1)}) custom-call(bf16[4,2,200,2048]{3,2,1,0:T(8,128)(2,1)} %bitcast.266), custom_call_target="tpu_custom_call" | custom-call | tf_op jit(solution)/shard_map/pallas_call | solution.py:269
  1447.6 2.5 convert_reduce_fusion.1
  1450.6 3.2 fusion.36
  1453.9 3.2 fusion.34
  1457.1 52.0 %shard_map.272 = (bf16[4,200,2048]{2,1,0:T(8,128)(2,1)}, bf16[4,200,2048]{2,1,0:T(8,128)(2,1)}) custom-call(bf16[200,2048]{1,0:T(8,128)(2,1)} %get-tuple-element.191.refs_0_, bf16[200,2048]{1,0:T(8,128)(2,1)} %get-tuple-element.189.refs_1_), custom_call_target="tpu_custom_call" | custom-call | tf_op jit(solution)/shard_map/pallas_call | solution.py:306
  1509.1 3.1 slice_bitcast_fusion.6
  1512.2 1.7 convert_reduce_fusion.6
  1513.9 1.1 slice_bitcast_fusion.9
  1535.7 1.3 convert_reduce_fusion.4
  1537.0 1.4 convert_reduce_fusion.5
  1538.4 1.2 slice_reduce_fusion
  1539.6 1.1 slice_reduce_fusion.1
  1541.3 1.4 convert_reduce_fusion.2
  1545.9 3.4 concatenate.141
  1549.2 4.5 concatenate.131
  1553.8 5.3 maximum_convert_fusion
  1559.1 1.6 fusion.18
  1560.9 1.5 fusion.19
  1562.4 1.7 pad_maximum_fusion
  1564.2 1.5 fusion.15
  1565.7 1.5 fusion.17
  1567.2 1.7 pad_maximum_fusion.1
  1569.0 1.7 maximum_convert_fusion.1
  (183 shorter events, 40.7 us)
Async XLA Ops:
  7.2 731.8 %all-gather.5.cloned.1.call-start = ((), (), s32[]{:S(2)}) async-start(), calls=%async_computation | async-start | bytes 3932160 | tf_op jit(solution)/shard_map/all_gather | solution.py:1401
  10.9 2.8 copy-start.9
  10.9 3.8 copy-start.29
  10.9 3.8 copy-start.30
  10.9 3.8 copy-start.31
  10.9 3.8 copy-start.32
  10.9 3.8 copy-start.33
  10.9 3.9 copy-start.34
  10.9 3.9 copy-start.35
  10.9 3.9 copy-start.36
  10.9 3.9 copy-start.37
  13.7 2.3 copy-start.16
  17.2 0.9 copy-start.12
  111.9 2.3 copy-start.18
  111.9 4.4 copy-start.10
  114.2 2.2 copy-start.11
  120.3 193.2 %copy-start.14 = (bf16[200,448]{1,0:T(8,128)(2,1)S(1)}, bf16[200,448]{1,0:T(8,128)(2,1)}, u32[]{:S(2)}) copy-start(bf16[200,448]{1,0:T(8,128)(2,1)} %get-tuple-element.234) | copy-start | bytes 537604
  120.3 193.2 %copy-start.15 = (bf16[200,448]{1,0:T(8,128)(2,1)S(1)}, bf16[200,448]{1,0:T(8,128)(2,1)}, u32[]{:S(2)}) copy-start(bf16[200,448]{1,0:T(8,128)(2,1)} %get-tuple-element.235) | copy-start | bytes 537604
  612.6 385.2 %all-gather.7.cloned.1.call-start = ((), (), s32[]{:S(2)}) async-start(), calls=%async_computation.1 | async-start | bytes 3932160 | tf_op jit(solution)/shard_map/all_gather | solution.py:1401
  613.4 56.6 %copy-start.19 = (bf16[2,96,1600]{2,1,0:T(8,128)(2,1)S(1)}, bf16[2,96,1600]{2,1,0:T(8,128)(2,1)}, u32[]{:S(2)}) copy-start(bf16[2,96,1600]{2,1,0:T(8,128)(2,1)} %param.29) | copy-start | bytes 1843204
  739.0 1.7 slice-start
  742.3 249.6 %copy-start.26 = (bf16[3,1600]{1,0:T(4,128)(2,1)S(1)}, bf16[3,1600]{1,0:T(4,128)(2,1)}, u32[]{:S(2)}) copy-start(bf16[3,1600]{1,0:T(4,128)(2,1)} %slice.685) | copy-start | bytes 28804
  742.3 249.6 %copy-start.27 = (bf16[1,1600]{1,0:T(2,128)(2,1)S(1)}, bf16[1,1600]{1,0:T(2,128)(2,1)}, u32[]{:S(2)}) copy-start(bf16[1,1600]{1,0:T(2,128)(2,1)} %convert.58) | copy-start | bytes 9604
  997.8 1.7 slice-start.1
  1101.4 245.1 %copy-start.28 = (f32[1,1600]{1,0:T(1,128)S(1)}, f32[1,1600]{1,0:T(1,128)}, u32[]{:S(2)}) copy-start(f32[1,1600]{1,0:T(1,128)} %get-tuple-element.114) | copy-start | bytes 19204
  1447.6 2.5 copy-start.4
  1509.0 4.8 copy-start.3
  1522.5 13.1 copy-start.6
  1532.4 4.6 copy-start.8
  1537.0 4.3 copy-start.5
  1538.4 4.3 copy-start.7
  1553.8 5.4 copy-start.1
  1559.1 1.7 copy-start
  1562.4 1.8 copy-start.2
  1567.2 1.8 copy-start.17
  1567.2 1.7 copy-start.20
  1567.2 1.7 copy-start.21
  1567.2 1.7 copy-start.22
  1567.2 1.7 copy-start.23
  1567.2 1.7 copy-start.24
  1567.2 1.8 copy-start.25
  1568.9 1.8 copy-start.13
Sparse Core Ops, SparseCore 0:
  612.8 38.3 all-gather.4
  652.7 43.2 all-gather.6

commit v7 on v6

--- a/solution.py
+++ b/solution.py
@@ -206,8 +206,8 @@
         g = self.g
         return g.copy(self.gone.at[j - 1], self.from_z.at[j - 1], self.sems, 3 + j, g.at(g.ahead(j), g.y))
 
-    def start(self):
-        for j in (1, 2, 3, 0):
+    def start(self, *pieces):
+        for j in pieces:
             self.across(j).start()
 
     def pump(self, j, before=None):
@@ -254,63 +254,165 @@
     ]
 
 
-def reduce_kernel(source, from_y, from_z, *scratch):
-    g = Group()
-    g.greet_group()
+class BlockGather:
+    def __init__(self, peers, source, target, sems, first, local):
+        self.p, self.source, self.target, self.sems, self.first = peers, source, target, sems, first
+        self.local = local
+
+    def piece(self, slot, index, to, own=False):
+        target = self.target.at[slot]
+        return self.p.copy(self.source if own else target, target, self.sems, self.first + index, to)
+
+    def keep(self):
+        return pltpu.make_async_copy(self.source, self.target.at[self.p.t], self.local)
+
+    def start(self):
+        p = self.p
+        self.piece(p.t, 1, p.over, True).start()
+        self.piece(p.t, 0, p.core, True).start()
+        self.keep().start()
+
+    def relay(self):
+        p = self.p
+        self.piece(p.over, 1, p.over).wait_recv()
+        self.piece(p.over, 2, p.core).start()
+
+    def finish(self):
+        p = self.p
+        self.piece(p.core, 0, p.core).wait_recv()
+        self.piece(p.diag, 2, p.core).wait_recv()
+        self.piece(p.t, 1, p.over, True).wait_send()
+        self.piece(p.t, 0, p.core, True).wait_send()
+        self.piece(p.over, 2, p.core).wait_send()
+        self.keep().wait()
+
+
+def add_up(own, others, target):
+    rows = own.shape[0]
+    for first in range(0, rows, 40):
+        at = slice(first, min(first + 40, rows))
+        total = own[at, :].astype(f32)
+        for other in others:
+            total = total + other[at, :].astype(f32)
+        target[at, :] = total.astype(target.dtype)
+
+
+def last_sum_kernel(source, earlier, from_y, from_z, got, got_earlier, *scratch):
+    p, g = Peers(), Group()
+    scratch, (bsend, brecv, blocal, mine) = scratch[:-4], scratch[-4:]
+    own, near, gone, local = scratch[2:]
+    before = BlockGather(p, earlier, got_earlier, (bsend, brecv), 0, blocal.at[0])
+    after = BlockGather(p, mine, got, (bsend, brecv), 3, blocal.at[1])
     item = reduces(g, [source], [from_y, from_z], scratch)[0]
-    item.start()
-    for j in (1, 2, 3):
-        item.pump(j)
+    g.greet(p)
+    item.start(1, 2)
+    before.start()
+    item.pump(1)
+    item.start(3)
+    before.relay()
+    item.pump(2)
+    item.start(0)
+    item.pump(3)
     item.finish()
-
-
-def reduce_only(part, collective_id):
+    loads = [
+        pltpu.make_async_copy(source.at[g.z, g.y], own, local.at[0]),
+        pltpu.make_async_copy(from_y.at[g.z], near, local.at[1]),
+        pltpu.make_async_copy(from_z, gone, blocal.at[2]),
+    ]
+    for load in loads:
+        load.start()
+    for load in loads:
+        load.wait()
+    add_up(own, [near] + [gone.at[k] for k in range(3)], mine)
+    after.start()
+    before.finish()
+    after.relay()
+    after.finish()
+
+
+def last_sum(part, earlier, n_tp, collective_id):
     operands, results, scratch = reduce_parts([part])
+    whole = jax.ShapeDtypeStruct((n_tp,) + earlier.shape, bf16)
+    _, _, got, got_earlier = pl.pallas_call(
+        last_sum_kernel,
+        out_shape=results + (whole, whole),
+        in_specs=[ANY, ANY],
+        out_specs=(ANY,) * 4,
+        scratch_shapes=scratch
+        + [pltpu.SemaphoreType.DMA((6,))] * 2
+        + [pltpu.SemaphoreType.DMA((3,)), pltpu.VMEM(earlier.shape, bf16)],
+        compiler_params=params(collective_id),
+    )(part, earlier)
+    return got, got_earlier
+
+
+def assemble_kernel(*refs):
+    inputs, refs = refs[: 7 * LAYERS], refs[7 * LAYERS :]
+    qkv_ref, out_ref, fc_ref, proj_ref = refs[:4]
+    vector_refs, (tiles, sems) = refs[4:13], refs[13:]
+    t, f = lax.axis_index("tp"), lax.axis_index("fsdp")
+    z, y = f // 2, f % 2
+    loads = []
+    for layer in range(LAYERS):
+        for w in range(2):
+            part, near, far = inputs[7 * layer + 1 + 3 * w : 7 * layer + 4 + 3 * w]
+            n = 2 * layer + w
+            loads.append(
+                [
+                    pltpu.make_async_copy(part.at[z, y], tiles.at[n, 0], sems.at[n, 0]),
+                    pltpu.make_async_copy(near.at[z], tiles.at[n, 1], sems.at[n, 1]),
+                    pltpu.make_async_copy(far, tiles.at[n, 2:5], sems.at[n, 2]),
+                ]
+            )
+    for load in sum(loads, []):
+        load.start()
+    n_tp = inputs[0].shape[0]
+    step = HEADS // n_tp * HEAD
+    width = D - step * (n_tp - 1)
+    counts = [step] * (n_tp - 1) + [width]
+    for layer in range(LAYERS):
+        got = inputs[7 * layer]
+        for i in range(3):
+            for k, count in enumerate(counts):
+                value = got[k, :, i * WIDE : i * WIDE + count].astype(f32)
+                qkv_ref[layer, :, i * D + k * step : i * D + k * step + count] = value
+        for k, count in enumerate(counts):
+            out_ref[layer, :, k * step : k * step + count] = got[k, :, 3 * WIDE : 3 * WIDE + count].astype(f32)
+        extra = got[:, :, 3 * WIDE + step : 4 * WIDE].astype(f32)
+        total = jnp.sum(extra, axis=0).T
+        own = got[t, :, 3 * WIDE + step : 4 * WIDE].astype(f32).T
+        skip = width - step
+        for v in range(8):
+            vector_refs[v][layer : layer + 1, :] = total[skip + v : skip + v + 1, :]
+        vector_refs[8][layer : layer + 1, :] = own[skip + 8 : skip + 9, :]
+        for w in range(2):
+            n = 2 * layer + w
+            for load in loads[n]:
+                load.wait()
+            total = tiles[n, 0].astype(f32)
+            for k in range(1, 5):
+                total = total + tiles[n, k].astype(f32)
+            if w:
+                fc_ref[layer] = total
+            else:
+                proj_ref[layer] = total.T
+
+
+def assemble(layers):
+    rows, width = layers[0][1].shape[2:]
+    outs = [(LAYERS, rows, 3 * D), (LAYERS, rows, D), (LAYERS, rows, width), (LAYERS, width, rows)]
+    outs += [(LAYERS, rows)] * 9
     return pl.pallas_call(
-        reduce_kernel,
-        out_shape=results,
-        in_specs=[ANY],
-        out_specs=(ANY, ANY),
-        scratch_shapes=scratch,
-        compiler_params=params(collective_id),
-    )(part)
-
-
-def block_gather_kernel(n, *refs):
-    p = Peers()
-    p.greet()
-    sources, targets, (send, recv, local) = refs[:n], refs[n : 2 * n], refs[2 * n :]
-    keeps = []
-    for i in range(n):
-        keeps.append(pltpu.make_async_copy(sources[i], targets[i].at[p.t], local.at[i]))
-        keeps[-1].start()
-        p.copy(sources[i], targets[i].at[p.t], (send, recv), 3 * i + 1, p.over).start()
-        p.copy(sources[i], targets[i].at[p.t], (send, recv), 3 * i, p.core).start()
-
-    def relay(i):
-        return p.copy(targets[i].at[p.over], targets[i].at[p.over], (send, recv), 3 * i + 2, p.core)
-
-    for i in range(n):
-        p.copy(sources[i], targets[i].at[p.over], (send, recv), 3 * i + 1, p.over).wait_recv()
-        relay(i).start()
-    for i in range(n):
-        p.copy(sources[i], targets[i].at[p.core], (send, recv), 3 * i, p.core).wait()
-        p.copy(sources[i], targets[i].at[p.diag], (send, recv), 3 * i + 2, p.core).wait_recv()
-        p.copy(sources[i], targets[i].at[p.over], (send, recv), 3 * i + 1, p.over).wait_send()
-        relay(i).wait_send()
-        keeps[i].wait()
-
-
-def block_gather(parts, n_tp, collective_id):
-    n = len(parts)
-    return pl.pallas_call(
-        functools.partial(block_gather_kernel, n),
-        out_shape=tuple(jax.ShapeDtypeStruct((n_tp,) + part.shape, part.dtype) for part in parts),
-        in_specs=[ANY] * n,
-        out_specs=(ANY,) * n,
-        scratch_shapes=[pltpu.SemaphoreType.DMA((3 * n,))] * 2 + [pltpu.SemaphoreType.DMA((n,))],
-        compiler_params=params(collective_id),
-    )(*parts)
+        assemble_kernel,
+        out_shape=tuple(jax.ShapeDtypeStruct(o, f32) for o in outs),
+        in_specs=([IN_VMEM] + [ANY] * 6) * LAYERS,
+        out_specs=(IN_VMEM,) * len(outs),
+        scratch_shapes=[
+            pltpu.VMEM((2 * LAYERS, 5, rows, width), bf16),
+            pltpu.SemaphoreType.DMA((2 * LAYERS, 3)),
+        ],
+        compiler_params=pltpu.CompilerParams(vmem_limit_bytes=60 * 2**20),
+    )(*sum((list(layer) for layer in layers), []))
 
 
 class Spread:
@@ -620,11 +722,13 @@
         p.greet()
     gather.start()
     for item in sums:
-        item.start()
+        item.start(1)
 
     def pump(j):
         for item in sums:
             item.pump(j)
+            if j == 2:
+                item.start(0)
 
     gather.wait_chip()
     load_proj.wait()
@@ -647,6 +751,8 @@
         tiles(D, tile)
 
     through(p.x)
+    for item in sums:
+        item.start(2)
     gather.relay()
     gather.wait_diag()
     through(1 - p.x)
@@ -655,6 +761,8 @@
     down(1 - p.x)
     scatter.far_to_core().start()
     scatter.send_over()
+    for item in sums:
+        item.start(3)
     down(p.x)
     scatter.near_to_core().start()
 
@@ -739,44 +847,53 @@
     )(grad, x, vecs, all_rows, pre, hidden, w_b, *operands)
 
 
+HALVES = [(micro, half) for micro in range(MICRO) for half in range(2)]
+
+
+def half_lanes(half):
+    return slice(half * WIDE // 2, (half + 1) * WIDE // 2)
+
+
 class Share:
     def __init__(self, group, kv, sems):
         self.g, self.kv, self.sems = group, kv, sems
         self.partner = group.at(group.z, 1 - group.y)
 
-    def piece(self, member, micro, index, to):
-        ref = self.kv.at[member, micro]
-        return self.g.copy(ref, ref, self.sems, micro * 7 + index, to)
-
-    def own(self, micro):
+    def piece(self, member, part, index, to):
+        micro, half = part
+        ref = self.kv.at[member, micro, :, :, half_lanes(half)]
+        return self.g.copy(ref, ref, self.sems, (2 * micro + half) * 7 + index, to)
+
+    def own(self, part):
         g = self.g
-        return [self.piece(g.member, micro, 0, self.partner)] + [
-            self.piece(g.member, micro, k, g.at(g.ahead(k), g.y)) for k in (1, 2, 3)
+        return [self.piece(g.member, part, 0, self.partner)] + [
+            self.piece(g.member, part, k, g.at(g.ahead(k), g.y)) for k in (1, 2, 3)
         ]
 
-    def relayed(self, micro):
+    def relayed(self, part):
         g = self.g
-        return [self.piece(g.at(g.behind(k), g.y), micro, 3 + k, self.partner) for k in (1, 2, 3)]
-
-    def start(self, micro):
-        for copy in self.own(micro):
+        return [self.piece(g.at(g.behind(k), g.y), part, 3 + k, self.partner) for k in (1, 2, 3)]
+
+    def start(self, *part):
+        for copy in self.own(part):
             copy.start()
 
-    def relay(self, micro):
+    def relay(self, *part):
         g = self.g
-        for k, copy in zip((1, 2, 3), self.relayed(micro)):
-            self.piece(g.at(g.behind(k), g.y), micro, k, self.partner).wait_recv()
+        for k, copy in zip((1, 2, 3), self.relayed(part)):
+            self.piece(g.at(g.behind(k), g.y), part, k, self.partner).wait_recv()
             copy.start()
 
-    def wait(self, micro):
+    def wait(self, *part):
         g = self.g
-        self.piece(self.partner, micro, 0, self.partner).wait_recv()
+        self.piece(self.partner, part, 0, self.partner).wait_recv()
         for k in (1, 2, 3):
-            self.piece(g.at(g.behind(k), 1 - g.y), micro, 3 + k, self.partner).wait_recv()
-
-    def finish(self, micro):
-        for copy in self.own(micro) + self.relayed(micro):
-            copy.wait_send()
+            self.piece(g.at(g.behind(k), 1 - g.y), part, 3 + k, self.partner).wait_recv()
+
+    def finish(self):
+        for part in HALVES:
+            for copy in self.own(part) + self.relayed(part):
+                copy.wait_send()
 
 
 class GroupSum:
@@ -784,11 +901,8 @@
         self.g, self.parts, self.sems = group, parts, sems
         self.from_y, self.to_z, self.from_z = from_y, to_z, from_z
 
-    def lanes(self, half):
-        return slice(half * WIDE // 2, (half + 1) * WIDE // 2)
-
     def across(self, micro, half):
-        g, lanes = self.g, self.lanes(half)
+        g, lanes = self.g, half_lanes(half)
         return g.copy(
             self.parts.at[micro, :, 1 - g.y, :, :, lanes],
             self.from_y.at[micro, :, :, :, lanes],
@@ -798,7 +912,7 @@
         )
 
     def along(self, micro, half, k):
-        g, lanes = self.g, self.lanes(half)
+        g, lanes = self.g, half_lanes(half)
         to = g.ahead(k)
         return g.copy(
             self.to_z.at[micro, to, :, :, lanes],
@@ -812,7 +926,7 @@
         self.across(micro, half).start()
 
     def turn(self, micro, half):
-        lanes = self.lanes(half)
+        lanes = half_lanes(half)
         self.across(micro, half).wait_recv()
 
         @pl.loop(0, 4)
@@ -885,6 +999,16 @@
             head(pair, lanes, 1)
 
         finish(pair, lanes)
+
+
+def run_hooks(hooks, micro, pair, half):
+    for at in range(HEAD_PAIRS):
+        if half == 0 and (micro, at) in hooks:
+
+            @pl.when(pair == at)
+            def _(at=at):
+                for hook in hooks[micro, at]:
+                    hook()
 
 
 def to_slots(target, micro, first, value, lanes):
@@ -966,10 +1090,19 @@
     for micro in range(MICRO):
         for i in range(2):
             kv[g.member, micro, i] = own[1 + i, micro, :PROMPT_DEV, :]
-        share.start(micro)
-    if n:
-        spread.start(1)
+    share.start(0, 0)
+    if n:
         spread.relay(0)
+    hooks = {
+        (0, 1): [lambda: share.relay(0, 1), lambda: share.start(1, 0)],
+        (0, 2): [lambda: share.wait(0, 1)],
+        (0, 3): [lambda: share.relay(1, 0), lambda: share.start(1, 1)],
+        (1, 0): [lambda: share.wait(1, 0)],
+        (1, 1): [lambda: share.relay(1, 1)],
+        (1, 2): [lambda: share.wait(1, 1)],
+    }
+    if n:
+        hooks[1, 1].append(lambda: spread.start(1, 2))
     keep_all = pltpu.make_async_copy(buf, all_hbm, local.at[2])
     keep_own = pltpu.make_async_copy(own, own_hbm, local.at[3])
     keep_all.start()
@@ -977,26 +1110,14 @@
     limit = key_limit(g.member)
     sub = lax.broadcasted_iota(jnp.int32, (CHUNK, TOK_DEV), 0)
 
+    share.relay(0, 0)
+    share.start(0, 1)
+    share.wait(0, 0)
+
     for micro in range(MICRO):
-        if micro == 0:
-            share.relay(0)
-        share.wait(micro)
 
         def head(pair, lanes, half, micro=micro):
-            if half == 0:
-
-                @pl.when(pair == 1)
-                def _():
-                    if micro == 0:
-                        share.relay(1)
-                    elif n:
-                        spread.relay(2)
-
-                @pl.when(pair == HEAD_PAIRS - 1)
-                def _():
-                    if n:
-                        spread.relay(1 + 2 * micro)
-
+            run_hooks(hooks, micro, pair, half)
             qh = half_of(own[0, micro, :, lanes], half)
 
             def first(c, load, top):
@@ -1059,23 +1180,30 @@
 
         tiles(D, tile)
 
+    if n:
+        spread.start(2, 3)
     down(1 - p.x)
     scatter.far_to_core().start()
     scatter.send_over()
     down(p.x)
     scatter.near_to_core().start()
     if n:
-        spread.relay(4)
+        spread.relay(1)
+        spread.start(3, 4)
     scatter.wait()
 
     def final(at):
         out_ref[at, :] = x_ref[at, :] + (scatter.rows(at) + vec_ref[4:5, :])
 
     row_chunks(rows, final)
+    if n:
+        spread.relay(2)
+        spread.start(4)
+        spread.relay(3)
+        spread.relay(4)
     gather.finish()
     scatter.finish()
-    for micro in range(MICRO):
-        share.finish(micro)
+    share.finish()
     for copy in give_parts:
         copy.wait_send()
     for copy in (keep_all, keep_own, keep_kv, keep_mix, keep_out):
@@ -1117,8 +1245,8 @@
         ]
         + scatter_scratch(n_tp, rows)
         + [
-            pltpu.SemaphoreType.DMA((7 * MICRO,)),
-            pltpu.SemaphoreType.DMA((7 * MICRO,)),
+            pltpu.SemaphoreType.DMA((14 * MICRO,)),
+            pltpu.SemaphoreType.DMA((14 * MICRO,)),
             pltpu.SemaphoreType.DMA((3,)),
             pltpu.SemaphoreType.DMA((3,)),
             pltpu.SemaphoreType.DMA((7,)),
@@ -1167,11 +1295,11 @@
     hooks = {(1, 0): [lambda: reduce.turn(0, 0)], (1, 1): [lambda: reduce.turn(0, 1)]}
     if n:
         first_sum, second_sum = sums
-        first_sum.start()
-        hooks[0, 1] = [lambda: first_sum.pump(2)]
-        hooks[0, 2] = [lambda: first_sum.pump(3), second_sum.start]
-        for k in range(3):
-            hooks.setdefault((1, k), []).append(lambda k=k: second_sum.pump(k + 1, first_sum))
+        first_sum.start(1)
+        hooks[0, 1] = [lambda: first_sum.start(0), lambda: first_sum.pump(2)]
+        hooks[0, 2] = [lambda: second_sum.start(1), lambda: first_sum.pump(3)]
+        hooks[0, 3] = [lambda: second_sum.start(2)]
+        hooks[1, 1] += [lambda: second_sum.pump(1, first_sum), lambda: second_sum.start(3)]
     gather.wait_chip()
     load_out.wait()
 
@@ -1179,6 +1307,8 @@
         pair_to_blocks(gm, x, mm(pair_rows(buf, x), wout[...], NT).astype(bf16))
 
     mixed_back(p.x)
+    if n:
+        first_sum.start(2)
     gather.relay()
     gather.wait_diag()
     mixed_back(1 - p.x)
@@ -1188,19 +1318,13 @@
     sub = lax.broadcasted_iota(jnp.int32, (CHUNK, TOK_DEV), 0)
 
     if n:
+        first_sum.start(3)
         first_sum.pump(1)
 
     for micro in range(MICRO):
 
         def head(pair, lanes, half, micro=micro):
-            for at in range(HEAD_PAIRS):
-                if half == 0 and (micro, at) in hooks:
-
-                    @pl.when(pair == at)
-                    def _(at=at):
-                        for hook in hooks[micro, at]:
-                            hook()
-
+            run_hooks(hooks, micro, pair, half)
             qh = half_of(own[0, micro, :, lanes], half)
             gh = half_of(gm[micro, :, lanes], half)
             lse = lse_ref[micro, pair, half : half + 1, :]
@@ -1289,10 +1413,15 @@
     load_all = pltpu.make_async_copy(all_hbm, other, local.at[6])
     load_all.start()
     reduce.turn(1, 1)
+    if n:
+        second_sum.start(0)
     for micro in range(MICRO):
         reduce.wait(micro)
         for i in range(2):
             to_slots(dqkv, micro, 0, reduce.total(micro, i), slice((1 + i) * WIDE, (2 + i) * WIDE))
+    if n:
+        second_sum.pump(2, first_sum)
+        second_sum.pump(3, first_sum)
     load_qkv.wait()
 
     def down(x):
@@ -1473,16 +1602,17 @@
 def backward(grad, weights, vecs, saves, cols, n_tp):
     width = D - HEADS // n_tp * HEAD * (n_tp - 1)
     staged = lax.axis_size("fsdp") == GROUP
-    done, joined, waiting = {}, {}, {}
+    done, waiting = {}, {}
 
     def during(keys, kernel):
-        payload = [waiting.pop(key) for key in keys if key in waiting]
+        keys = [key for key in keys if key in waiting]
+        payload = [waiting.pop(key) for key in keys]
         results = list(kernel(payload))
         if payload:
             arrived = results[-2 * len(payload) :]
             results = results[: -2 * len(payload)]
             for i, key in enumerate(keys):
-                done[key] = owned(payload[i], arrived[2 * i], arrived[2 * i + 1])
+                done[key] = (payload[i], arrived[2 * i], arrived[2 * i + 1])
         return results
 
     def produced(key, value):
@@ -1509,18 +1639,21 @@
             ),
         )
         produced((layer, "qo"), with_vectors(grad_qo, ff_sums, attn_sums, col_sums, fc_bias_sums, cols, width))
-    during([(0, "qo")] if staged else [], lambda payload: reduce_only(payload[0], 30) if payload else ())
-    sums = []
-    both = block_gather([done[layer, "qo"].astype(bf16) for layer in range(LAYERS)], n_tp, 31)
-    for layer, got in enumerate(both):
+    if staged:
+        got = last_sum(waiting[0, "qo"], owned(*done[1, "qo"]).astype(bf16), n_tp, 30)
+        return grad, assemble([(got[k],) + done[k, "proj"] + done[k, "fc"] for k in range(LAYERS)])
+    outs = []
+    for layer in range(LAYERS):
+        qo = done[layer, "qo"]
+        got = lax.all_gather(qo.astype(bf16), "tp")
         qkv_grad = jnp.concatenate(
             [heads_joined(got[:, :, i * WIDE : i * WIDE + width], n_tp) for i in range(3)], axis=1
-        ).astype(f32)
-        out_grad = heads_joined(got[:, :, 3 * WIDE : 3 * WIDE + width], n_tp).astype(f32)
+        )
+        out_grad = heads_joined(got[:, :, 3 * WIDE : 3 * WIDE + width], n_tp)
         vector_sum = jnp.sum(got[:, :, 3 * WIDE + width : 3 * WIDE + width + 8].astype(f32), 0).T
-        fc_bias_sum = done[layer, "qo"][:, 3 * WIDE + width + 8]
-        sums.append((qkv_grad, out_grad, done[layer, "fc"], done[layer, "proj"].T, fc_bias_sum, vector_sum))
-    return grad, sums
+        rest = (vector_sum[v] for v in range(8))
+        outs.append((qkv_grad, out_grad, done[layer, "fc"], done[layer, "proj"].T, *rest, qo[:, 3 * WIDE + width + 8]))
+    return grad, tuple(jnp.stack(pair).astype(f32) for pair in zip(*outs))
 
 
 def local(
@@ -1571,28 +1704,25 @@
         saves.append(saved)
     out_tokens = state.astype(bf16).reshape(tokens.shape)
     grad = out_grad.astype(f32).reshape(MICRO * row_count, D)
-    grad, sums = backward(
+    grad, (qkv_g, out_g, fc_g, proj_g, *vec_g) = backward(
         grad, fetch.weights, [vectors[:8, layer] for layer in range(LAYERS)], saves, cols, n_tp
-    )
-    qkv_g, out_g, fc_g, proj_g, fc_bias_g, vec_g = (
-        jnp.stack([sums[layer][i] for layer in range(LAYERS)]) for i in range(6)
     )
     return (
         out_tokens,
         grad.reshape(tokens.shape),
         qkv_g,
-        vec_g[:, 2],
-        vec_g[:, 3],
+        vec_g[2],
+        vec_g[3],
         out_g,
-        vec_g[:, 4],
+        vec_g[4],
         fc_g,
-        fc_bias_g[:, None],
+        vec_g[8][:, None],
         proj_g,
-        vec_g[:, 7],
-        vec_g[:, 0],
-        vec_g[:, 1],
-        vec_g[:, 5],
-        vec_g[:, 6],
+        vec_g[7],
+        vec_g[0],
+        vec_g[1],
+        vec_g[5],
+        vec_g[6],
     )
 
 

time: 1590 us -> 1490 us (0.937)
  Pallas kernels: 1440 us -> 1400 us
  local copies, waits for them, and re-layouts: 73.8 us -> 40.5 us
  other arithmetic: 47.5 us -> 19.6 us
    pallas_call x2, Pallas kernels: 490 us -> 417 us  [attn_bwd(): pl.pallas_call(functools.partial(attn_bwd_kernel, len(payload)), out_shap...]
    pallas_call x2, Pallas kernels: 386 us -> 422 us  [attn_fwd(): pl.pallas_call(functools.partial(attn_fwd_kernel, len(operands)), out_sha...]
    concatenate x26 -> x0, local copies, waits for them, and re-layouts: 24.1 us -> none  [the longest x20 20.1 us: backward(): jnp.concatenate([heads_joined(got[:, :, i * WIDE:i * WIDE + width], n_tp)...]
  transfers between devices with their start and end apart: 2 -> 2, of which waited for: 0 -> 0; matrix products, arithmetic and copies ran while one was open for 1% -> 1% of each run, Pallas kernels for 23% -> 22%
where the time goes in v7:
time: 1490 us; the launch traced here: 1480 us
  Pallas kernels  1400 us (94%)
  local copies, waits for them, and re-layouts  40.5 us (3%)
  other arithmetic  19.6 us (1%)
    pallas_call x2, Pallas kernels, attn_fwd(): pl.pallas_call(functools.partial(attn_fwd_kernel, len(operands)), out_sha...  422 us
    pallas_call x2, Pallas kernels, attn_bwd(): pl.pallas_call(functools.partial(attn_bwd_kernel, len(payload)), out_shap...  417 us
    pallas_call x2, Pallas kernels, ff_bwd(): pl.pallas_call(functools.partial(ff_bwd_kernel, len(payload)), out_shape=...  180 us
    pallas_call x2, Pallas kernels, ff_fwd(): pl.pallas_call(functools.partial(ff_fwd_kernel, len(operands)), out_shape...  144 us
    pallas_call x1, Pallas kernels, last_sum(): pl.pallas_call(last_sum_kernel, out_shape=results + (whole, whole), in_sp...  131 us
    pallas_call x1, Pallas kernels, spread_only(): pl.pallas_call(functools.partial(spread_kernel, chunks), out_shape=result...  93.8 us
  transfers between devices with their start and end apart: 2, of which 0 were waited for; matrix products, arithmetic and copies ran while one was open for 1% of the time, Pallas kernels for 22%

profile of v7, /device:TPU:9, one launch (start us, length us, event | category | flops | bytes accessed | tf_op | source)
XLA Modules:
  0.0 1477.9 jit_solution(5643650377805881899)
XLA Ops:
  7.2 3.6 fusion.21
  11.0 2.7 dynamic-slice_bitcast_fusion.3
  13.7 0.9 fusion.24
  15.0 1.0 pad_dynamic-update-slice_fusion.2
  16.0 1.1 dynamic-slice_bitcast_fusion
  17.2 0.9 copy-done.3
  18.1 93.8 %shard_map.262 = bf16[8,200,2176]{2,1,0:T(8,128)(2,1)} custom-call(bf16[200,2176]{1,0:T(8,128)(2,1)} %copy-done.3), custom_call_target="tpu_custom_call" | custom-call | tf_op jit(solution)/shard_map/pallas_call | solution.py:489
  111.9 1.2 convert_bitcast_fusion
  113.1 0.3 copy.66
  113.6 0.6 slice_bitcast_fusion.4
  114.2 1.2 bitcast_convert_fusion.1.refs_0_.refs_1_
  115.4 0.6 copy.78
  116.6 0.6 copy.77
  117.3 0.6 pad.54.refs_2_
  117.9 0.6 pad.61.refs_2_
  118.5 1.7 fusion.12
  120.2 197.4 %shard_map.263 = (f32[192,1600]{1,0:T(8,128)}, f32[2,4,8,384]{3,2,1,0:T(8,128)}, bf16[4,192,1600]{2,1,0:T(8,128)(2,1)}, bf16[3,2,384,512]{3,2,1,0:T(8,128)(2,1)}...) custom-call(f32[192,1600]{1,0:T(8,128)} %bitcast_convert_fusion.1.re, ...), custom_call_target="tpu_custom_call" | custom-call | flops 99999997952 | bytes 31457280 | tf_op jit(solution)/shard_map/pallas_call | solution.py:1229
  317.7 1.0 fusion.15.refs_4_
  318.7 95.7 %shard_map.264 = (f32[192,1600]{1,0:T(8,128)}, bf16[4,192,1600]{2,1,0:T(8,128)(2,1)}, f32[4,192,1600]{2,1,0:T(8,128)}, bf16[4,192,1600]{2,1,0:T(8,128)(2,1)}, bf16[8,200,2048]{2,1,0:T(8,128)(2,1)}) custom-call(f32[192,1600]{1,0:T(8,128)} %get-tuple-element.83.refs_0_.refs_1_, f32[8,1600]{1,0:T(8,128)} %bitcast.119, f32[1,1600]{1,0:T(1,128)} %get-tuple-element.219.refs_2_, ...), custom_call_target="tpu_custom_call" | custom-call | flops 7864320000 | bytes 41943040 | tf_op jit(solution)/shard_map/pallas_call | solution.py:645
  414.3 224.9 %shard_map.265 = (f32[192,1600]{1,0:T(8,128)}, f32[2,4,8,384]{3,2,1,0:T(8,128)}, bf16[4,192,1600]{2,1,0:T(8,128)(2,1)}, bf16[3,2,384,512]{3,2,1,0:T(8,128)(2,1)}...) custom-call(f32[192,1600]{1,0:T(8,128)} %get-tuple-element.85.refs_0, ...), custom_call_target="tpu_custom_call" | custom-call | flops 99999997952 | bytes 31457280 | tf_op jit(solution)/shard_map/pallas_call | solution.py:1229
  639.5 0.5 all-gather.7.cloned.1.call-update
  640.1 48.8 %shard_map.266 = (f32[192,1600]{1,0:T(8,128)}, bf16[4,192,1600]{2,1,0:T(8,128)(2,1)}, f32[4,192,1600]{2,1,0:T(8,128)}, bf16[4,192,1600]{2,1,0:T(8,128)(2,1)}) custom-call(f32[192,1600]{1,0:T(8,128)} %get-tuple-element.87.refs_0_.refs_1_, f32[8,1600]{1,0:T(8,128)} %bitcast.123, f32[1,1600]{1,0:T(1,128)} %get-tuple-element.216.refs_2_, ...), custom_call_target="tpu_custom_call" | custom-call | flops 7864320000 | bytes 41943040 | tf_op jit(solution)/shard_map/pallas_call | solution.py:645
  688.9 2.2 convert_element_type.49
  691.1 1.2 bitcast_convert_fusion.refs_0_
  692.2 70.6 %shard_map.267 = (f32[192,1600]{1,0:T(8,128)}, f32[8,1600]{1,0:T(8,128)}, f32[1,1600]{1,0:T(1,128)}, bf16[1600,1600]{1,0:T(8,128)(2,1)}, bf16[1600,1600]{1,0:T(8,128)(2,1)}) custom-call(f32[192,1600]{1,0:T(8,128)} %bitcast_convert_fusion.refs_0_, f32[192,1600]{1,0:T(8,128)} %get-tuple-element.87.refs_0_.refs_1_, f32[8,1600]{1,0:T(8,128)} %bitcast.124, ...), custom_call_target="tpu_custom_call" | custom-call | flops 15728640000 | bytes 52428800 | tf_op jit(solution)/shard_map/pallas_call | solution.py:819
  762.9 1.4 slice.239
  764.3 1.3 convert.48
  765.6 1.7 fusion.23
  767.3 1.6 pad_maximum_fusion.refs_7_
  768.9 208.7 %shard_map.268 = (f32[192,1600]{1,0:T(8,128)}, f32[8,1600]{1,0:T(8,128)}, f32[1,1536]{1,0:T(1,128)}, bf16[1600,2048]{1,0:T(8,128)(2,1)}, bf16[4,200,1600]{2,1,0:...) custom-call(f32[192,1600]{1,0:T(8,128)} %get-tuple-element.93.refs_0_, ...), custom_call_target="tpu_custom_call" | custom-call | flops 199999995904 | bytes 52428800 | tf_op jit(solution)/shard_map/pallas_call | solution.py:1474
  977.6 0.8 convert.44
  978.5 0.7 fusion.27
  979.9 5.6 dynamic_update_slice.20
  985.5 1.7 fusion.22
  987.2 1.6 pad_maximum_fusion.1.refs_7_
  988.8 108.9 %shard_map.269 = (f32[192,1600]{1,0:T(8,128)}, f32[8,1600]{1,0:T(8,128)}, f32[1,1600]{1,0:T(1,128)}, bf16[1600,1600]{1,0:T(8,128)(2,1)}, bf16[1600,1600]{1,0:T(8...) custom-call(f32[192,1600]{1,0:T(8,128)} %get-tuple-element.102.refs_0_, ...), custom_call_target="tpu_custom_call" | custom-call | flops 15728640000 | bytes 52428800 | tf_op jit(solution)/shard_map/pallas_call | solution.py:819
  1097.7 208.3 %shard_map.270 = (f32[192,1600]{1,0:T(8,128)}, f32[8,1600]{1,0:T(8,128)}, f32[1,1536]{1,0:T(1,128)}, bf16[1600,2048]{1,0:T(8,128)(2,1)}, bf16[4,200,1600]{2,1,0:...) custom-call(f32[192,1600]{1,0:T(8,128)} %get-tuple-element.111.refs_0_, ...), custom_call_target="tpu_custom_call" | custom-call | flops 199999995904 | bytes 52428800 | tf_op jit(solution)/shard_map/pallas_call | solution.py:1474
  1306.1 0.8 convert.49
  1306.9 0.7 fusion.26
  1307.6 0.8 slice.238
  1309.2 2.3 convert_reduce_fusion
  1311.5 5.8 dynamic_update_slice.23
  1317.3 2.6 fusion.5.earlier
  1319.9 130.6 %shard_map.271 = (bf16[4,200,2048]{2,1,0:T(8,128)(2,1)}, bf16[3,200,2048]{2,1,0:T(8,128)(2,1)}, bf16[4,200,2048]{2,1,0:T(8,128)(2,1)}, bf16[4,200,2048]{2,1,0:T(8,128)(2,1)}) custom-call(bf16[4,2,200,2048]{3,2,1,0:T(8,128)(2,1)} %bitcast.100, bf16[200,2048]{1,0:T(8,128)(2,1)} %fusion.5.earlier), custom_call_target="tpu_custom_call" | custom-call | tf_op jit(solution)/shard_map/pallas_call | solution.py:336
  1450.5 14.4 shard_map.272
  1464.9 1.3 copy.71
  1466.2 3.6 copy.72
  1469.8 1.0 copy.101
  (94 shorter events, 3.0 us)
Async XLA Ops:
  7.2 758.4 %all-gather.5.cloned.1.call-start = ((), (), s32[]{:S(2)}) async-start(), calls=%async_computation | async-start | bytes 3932160 | tf_op jit(solution)/shard_map/all_gather | solution.py:1530
  10.9 2.8 copy-start
  10.9 3.8 copy-start.13
  10.9 3.8 copy-start.14
  10.9 3.8 copy-start.15
  10.9 3.8 copy-start.16
  10.9 3.8 copy-start.17
  10.9 3.9 copy-start.18
  10.9 3.9 copy-start.19
  10.9 3.9 copy-start.20
  10.9 3.9 copy-start.21
  13.7 2.3 copy-start.7
  17.2 0.9 copy-start.3
  111.9 2.3 copy-start.8
  111.9 4.4 copy-start.1
  113.5 2.9 copy-start.2
  120.2 197.4 %copy-start.5 = (bf16[200,448]{1,0:T(8,128)(2,1)S(1)}, bf16[200,448]{1,0:T(8,128)(2,1)}, u32[]{:S(2)}) copy-start(bf16[200,448]{1,0:T(8,128)(2,1)} %get-tuple-element.205) | copy-start | bytes 537604
  120.2 197.4 %copy-start.6 = (bf16[200,448]{1,0:T(8,128)(2,1)S(1)}, bf16[200,448]{1,0:T(8,128)(2,1)}, u32[]{:S(2)}) copy-start(bf16[200,448]{1,0:T(8,128)(2,1)} %get-tuple-element.206) | copy-start | bytes 537604
  639.3 346.2 %all-gather.7.cloned.1.call-start = ((), (), s32[]{:S(2)}) async-start(), calls=%async_computation.1 | async-start | bytes 3932160 | tf_op jit(solution)/shard_map/all_gather | solution.py:1530
  640.1 51.0 %copy-start.9 = (bf16[2,96,1600]{2,1,0:T(8,128)(2,1)S(1)}, bf16[2,96,1600]{2,1,0:T(8,128)(2,1)}, u32[]{:S(2)}) copy-start(bf16[2,96,1600]{2,1,0:T(8,128)(2,1)} %param.29) | copy-start | bytes 1843204
  765.6 1.7 slice-start
  768.9 210.7 %copy-start.10 = (bf16[3,1600]{1,0:T(4,128)(2,1)S(1)}, bf16[3,1600]{1,0:T(4,128)(2,1)}, u32[]{:S(2)}) copy-start(bf16[3,1600]{1,0:T(4,128)(2,1)} %slice.239) | copy-start | bytes 28804
  768.9 210.7 %copy-start.11 = (bf16[1,1600]{1,0:T(2,128)(2,1)S(1)}, bf16[1,1600]{1,0:T(2,128)(2,1)}, u32[]{:S(2)}) copy-start(bf16[1,1600]{1,0:T(2,128)(2,1)} %convert.48) | copy-start | bytes 9604
  985.5 1.7 slice-start.1
  1097.7 210.7 %copy-start.12 = (f32[1,1600]{1,0:T(1,128)S(1)}, f32[1,1600]{1,0:T(1,128)}, u32[]{:S(2)}) copy-start(f32[1,1600]{1,0:T(1,128)} %get-tuple-element.125) | copy-start | bytes 19204
  1466.2 3.6 copy-start.4
Sparse Core Ops, SparseCore 0:
  639.4 39.2 all-gather.4
  680.3 47.7 all-gather.6

commit v8 on v7

--- a/solution.py
+++ b/solution.py
@@ -191,37 +191,48 @@
 
 
 class Reduce:
-    def __init__(self, group, source, from_y, from_z, sems, tiles):
-        self.g, self.source, self.from_y, self.from_z, self.sems = group, source, from_y, from_z, sems
+    def __init__(self, group, source, from_y, from_z, sems, tiles, columns=None):
+        self.g, self.sems, self.columns = group, sems, columns
+        self.source, self.from_y, self.from_z = source, from_y, from_z
         self.own, self.got, self.gone, self.local = tiles
+
+    def cut(self, ref, *index):
+        if self.columns is None:
+            return ref.at[index]
+        return ref.at[index + (slice(None), self.columns)]
 
     def across(self, j):
         g = self.g
         z = g.ahead(j)
         return g.copy(
-            self.source.at[z, 1 - g.y], self.from_y.at[z], self.sems, j, g.at(g.z, 1 - g.y)
+            self.cut(self.source, z, 1 - g.y), self.cut(self.from_y, z), self.sems, j, g.at(g.z, 1 - g.y)
         )
 
     def along(self, j):
         g = self.g
-        return g.copy(self.gone.at[j - 1], self.from_z.at[j - 1], self.sems, 3 + j, g.at(g.ahead(j), g.y))
+        source, target = self.cut(self.gone, j - 1), self.cut(self.from_z, j - 1)
+        return g.copy(source, target, self.sems, 3 + j, g.at(g.ahead(j), g.y))
 
     def start(self, *pieces):
         for j in pieces:
             self.across(j).start()
 
-    def pump(self, j, before=None):
+    def pump(self, j, before=None, then=None):
         g = self.g
-        load_own = pltpu.make_async_copy(self.source.at[g.ahead(j), g.y], self.own, self.local.at[0])
+        own, got = (self.own, self.got) if self.columns is None else (self.cut(self.own), self.cut(self.got))
+        load_own = pltpu.make_async_copy(self.cut(self.source, g.ahead(j), g.y), own, self.local.at[0])
         load_own.start()
         self.across(j).wait_recv()
-        load_got = pltpu.make_async_copy(self.from_y.at[g.ahead(j)], self.got, self.local.at[1])
+        if then is not None:
+            then()
+        load_got = pltpu.make_async_copy(self.cut(self.from_y, g.ahead(j)), got, self.local.at[1])
         load_got.start()
         load_own.wait()
         load_got.wait()
         if before is not None:
             before.along(j).wait_send()
-        self.gone[j - 1] = self.own[...] + self.got[...]
+        columns = slice(None) if self.columns is None else self.columns
+        self.gone[j - 1, :, columns] = self.own[:, columns] + self.got[:, columns]
         self.along(j).start()
 
     def finish(self, reused=False):
@@ -239,7 +250,7 @@
     for part in payload:
         rows = part.shape[2:]
         results += (jax.ShapeDtypeStruct((4,) + rows, bf16), jax.ShapeDtypeStruct((3,) + rows, bf16))
-        scratch += [pltpu.SemaphoreType.DMA((7,))] * 2
+    scratch += [pltpu.SemaphoreType.DMA((7,))] * (2 * max(2, len(payload)) if payload else 0)
     if payload:
         scratch += [pltpu.VMEM(rows, bf16), pltpu.VMEM(rows, bf16), pltpu.VMEM((3,) + rows, bf16)]
         scratch += [pltpu.SemaphoreType.DMA((2,))]
@@ -247,11 +258,29 @@
 
 
 def reduces(group, sources, results, scratch):
-    tiles = scratch[2 * len(sources) :]
+    tiles = scratch[4:]
+    if len(sources) == 1:
+        middle, end = sources[0].shape[3] // 2, sources[0].shape[3]
+        halves = (slice(0, middle), slice(middle, end))
+        return [
+            Reduce(group, sources[0], *results, scratch[2 * n : 2 * n + 2], tiles, columns)
+            for n, columns in enumerate(halves)
+        ]
     return [
         Reduce(group, source, results[2 * n], results[2 * n + 1], scratch[2 * n : 2 * n + 2], tiles)
         for n, source in enumerate(sources)
     ]
+
+
+def in_turn(items):
+    order = [(item, j) for item in items for j in (1, 2, 3)] + [(item, 0) for item in items]
+
+    def step(n):
+        item, j = order[n]
+        item.pump(j, then=lambda: order[n + 1][0].start(order[n + 1][1]))
+
+    steps = [functools.partial(step, n) for n in range(3 * len(items))]
+    return [lambda: items[0].start(1)] + steps + [lambda item=item: item.start(0) for item in items[1:]]
 
 
 class BlockGather:
@@ -300,20 +329,20 @@
 def last_sum_kernel(source, earlier, from_y, from_z, got, got_earlier, *scratch):
     p, g = Peers(), Group()
     scratch, (bsend, brecv, blocal, mine) = scratch[:-4], scratch[-4:]
-    own, near, gone, local = scratch[2:]
+    own, near, gone, local = scratch[4:]
     before = BlockGather(p, earlier, got_earlier, (bsend, brecv), 0, blocal.at[0])
     after = BlockGather(p, mine, got, (bsend, brecv), 3, blocal.at[1])
-    item = reduces(g, [source], [from_y, from_z], scratch)[0]
+    items = reduces(g, [source], [from_y, from_z], scratch)
+    steps = in_turn(items)
     g.greet(p)
-    item.start(1, 2)
+    steps[0]()
     before.start()
-    item.pump(1)
-    item.start(3)
-    before.relay()
-    item.pump(2)
-    item.start(0)
-    item.pump(3)
-    item.finish()
+    for n, step in enumerate(steps[1:]):
+        if n == 3:
+            before.relay()
+        step()
+    for item in items:
+        item.finish()
     loads = [
         pltpu.make_async_copy(source.at[g.z, g.y], own, local.at[0]),
         pltpu.make_async_copy(from_y.at[g.z], near, local.at[1]),
@@ -419,7 +448,7 @@
     def __init__(self, group, source, target, sems, chunks):
         self.g, self.source, self.target, self.sems = group, source, target, sems
         count = source.shape[1] // 128
-        ends = [128 * (count * (c + 1) // chunks) for c in range(chunks)]
+        ends = [128 * (count * sum(chunks[: c + 1]) // sum(chunks)) for c in range(len(chunks))]
         self.columns = [slice(a, b) for a, b in zip([0] + ends, ends)]
         self.partner = group.at(group.z, 1 - group.y)
 
@@ -471,16 +500,17 @@
     if shard is None:
         return (), (), []
     whole = jax.ShapeDtypeStruct((GROUP,) + shard.shape, shard.dtype)
-    return (shard,), (whole,), [pltpu.SemaphoreType.DMA((7 * chunks + 1,))] * 2
+    return (shard,), (whole,), [pltpu.SemaphoreType.DMA((7 * len(chunks) + 1,))] * 2
 
 
 def spread_kernel(chunks, source, target, send, recv):
     g = Group()
     g.greet_group()
     spread = Spread(g, source, target, (send, recv), chunks)
-    spread.start()
-    for c in range(chunks):
+    spread.start(0, 2)
+    for c in range(len(chunks)):
         spread.relay(c)
+        spread.start(c + 2, c + 3)
     spread.finish()
 
 
@@ -536,8 +566,9 @@
     return w_b.at[:, lanes_up(width) :]
 
 
-FF_CHUNKS = 3
-ATTN_CHUNKS = 5
+FIRST_CHUNKS = (3, 3, 3, 3, 3, 2)
+FF_CHUNKS = (5, 5, 4, 2)
+ATTN_CHUNKS = (5, 6, 6, 5, 4)
 
 
 def ff_fwd_kernel(n, *refs):
@@ -569,7 +600,7 @@
         p.greet()
     gather.start()
     if n:
-        spread.start()
+        spread.start(0, 1)
     gather.wait_chip()
     load_fc.wait()
 
@@ -589,9 +620,11 @@
 
     up(p.x)
     if n:
-        spread.relay(0)
+        spread.start(1, 2)
     gather.relay()
     gather.wait_diag()
+    if n:
+        spread.relay(0)
     keep_all = pltpu.make_async_copy(buf, all_hbm, local.at[2])
     keep_all.start()
     up(1 - p.x)
@@ -604,17 +637,21 @@
     scatter.far_to_core().start()
     scatter.send_over()
     if n:
-        spread.relay(1)
+        spread.start(2, 3)
     down(p.x)
     scatter.near_to_core().start()
     if n:
-        spread.relay(2)
+        spread.relay(1)
+        spread.start(3)
     scatter.wait()
 
     def final(at):
         out_ref[at, :] = x_ref[at, :] + scatter.rows(at) + vec_ref[7:8, :]
 
     row_chunks(rows, final)
+    if n:
+        spread.relay(2)
+        spread.relay(3)
     gather.finish()
     scatter.finish()
     for copy in (keep_all, keep_pre, keep_hid):
@@ -721,15 +758,13 @@
     else:
         p.greet()
     gather.start()
-    for item in sums:
-        item.start(1)
-
-    def pump(j):
-        for item in sums:
-            item.pump(j)
-            if j == 2:
-                item.start(0)
-
+    steps = in_turn(sums) if n else []
+
+    def advance():
+        if steps:
+            steps.pop(0)()
+
+    advance()
     gather.wait_chip()
     load_proj.wait()
     load_pre.wait()
@@ -751,20 +786,19 @@
         tiles(D, tile)
 
     through(p.x)
-    for item in sums:
-        item.start(2)
     gather.relay()
+    advance()
     gather.wait_diag()
     through(1 - p.x)
-    pump(1)
+    advance()
     load_fc.wait()
     down(1 - p.x)
     scatter.far_to_core().start()
     scatter.send_over()
-    for item in sums:
-        item.start(3)
+    advance()
     down(p.x)
     scatter.near_to_core().start()
+    advance()
 
     def outer(left, right, target, sem):
         whole = D // TILE
@@ -785,12 +819,12 @@
         return pltpu.make_async_copy(stage, target, sem)
 
     load_other.wait()
-    pump(2)
     store = outer(buf, other, dproj_hbm, local.at[4])
     store.start()
     gather.finish()
     load_all = pltpu.make_async_copy(all_hbm, buf, local.at[5])
     load_all.start()
+    advance()
     scatter.wait()
 
     def final(at):
@@ -805,7 +839,8 @@
     store.wait()
     store = outer(buf, dpre, dfc_hbm, local.at[6])
     store.start()
-    pump(3)
+    while steps:
+        advance()
     scatter.finish()
     store.wait()
     for item in sums:
@@ -1039,8 +1074,10 @@
     whole, refs = refs[7 : 7 + n], refs[7 + n :]
     wqkv, wout, wparts, buf, own, kv, mix, s_ref, p_ref, o_ref = refs[:10]
     part, from_core, over_out, from_over, send, recv, gsend, grecv, wsend, wrecv, local = refs[10:21]
+    msend, mrecv = refs[21:23]
     p, g = Peers(), Group()
-    spread = Spread(g, shard[0], whole[0], refs[21:], ATTN_CHUNKS) if n else None
+    spread = Spread(g, shard[0], whole[0], refs[23:], ATTN_CHUNKS) if n else None
+    mixes = BlockGather(p, mix, mix_hbm, (msend, mrecv), 0, local.at[5])
     rows = x_ref.shape[0]
     n_tp = buf.shape[0]
     step = HEADS // n_tp * HEAD
@@ -1093,6 +1130,7 @@
     share.start(0, 0)
     if n:
         spread.relay(0)
+        spread.start(1, 2)
     hooks = {
         (0, 1): [lambda: share.relay(0, 1), lambda: share.start(1, 0)],
         (0, 2): [lambda: share.wait(0, 1)],
@@ -1102,7 +1140,9 @@
         (1, 2): [lambda: share.wait(1, 1)],
     }
     if n:
-        hooks[1, 1].append(lambda: spread.start(1, 2))
+        hooks[0, 1] += [lambda: spread.start(2, 3), lambda: spread.relay(1)]
+        hooks[1, 1] += [lambda: spread.start(3, 4), lambda: spread.relay(2)]
+        hooks[1, 3] = [lambda: spread.start(4)]
     keep_all = pltpu.make_async_copy(buf, all_hbm, local.at[2])
     keep_own = pltpu.make_async_copy(own, own_hbm, local.at[3])
     keep_all.start()
@@ -1156,9 +1196,7 @@
         head_pairs(head, finish)
 
     keep_kv = pltpu.make_async_copy(kv, kv_hbm, local.at[4])
-    keep_mix = pltpu.make_async_copy(mix, mix_hbm, local.at[5])
     keep_kv.start()
-    keep_mix.start()
     keep_part.wait()
     for i, t in enumerate((p.core, p.over, p.diag)):
         p.copy(rows_for(t), wparts.at[t], (wsend, wrecv), i, t).wait_recv()
@@ -1180,34 +1218,31 @@
 
         tiles(D, tile)
 
-    if n:
-        spread.start(2, 3)
     down(1 - p.x)
     scatter.far_to_core().start()
     scatter.send_over()
     down(p.x)
     scatter.near_to_core().start()
     if n:
-        spread.relay(1)
-        spread.start(3, 4)
+        spread.relay(3)
     scatter.wait()
+    mixes.start()
 
     def final(at):
         out_ref[at, :] = x_ref[at, :] + (scatter.rows(at) + vec_ref[4:5, :])
 
     row_chunks(rows, final)
-    if n:
-        spread.relay(2)
-        spread.start(4)
-        spread.relay(3)
+    mixes.relay()
+    if n:
         spread.relay(4)
     gather.finish()
     scatter.finish()
     share.finish()
     for copy in give_parts:
         copy.wait_send()
-    for copy in (keep_all, keep_own, keep_kv, keep_mix, keep_out):
+    for copy in (keep_all, keep_own, keep_kv, keep_out):
         copy.wait()
+    mixes.finish()
     if n:
         spread.finish()
 
@@ -1232,7 +1267,8 @@
             jax.ShapeDtypeStruct((rows, D), f32),
             jax.ShapeDtypeStruct((MICRO, HEAD_PAIRS, 8, TOK_DEV), f32),
         )
-        + tuple(jax.ShapeDtypeStruct(*s) for s in saved + (((WIDE, D), bf16),))
+        + tuple(jax.ShapeDtypeStruct(*s) for s in saved[:3])
+        + (jax.ShapeDtypeStruct((n_tp,) + saved[3][0], bf16), jax.ShapeDtypeStruct((WIDE, D), bf16))
         + results,
         in_specs=[IN_VMEM, IN_VMEM, IN_VMEM, ANY] + [ANY] * len(operands),
         out_specs=(IN_VMEM, IN_VMEM) + (ANY,) * (5 + len(operands)),
@@ -1250,6 +1286,8 @@
             pltpu.SemaphoreType.DMA((3,)),
             pltpu.SemaphoreType.DMA((3,)),
             pltpu.SemaphoreType.DMA((7,)),
+            pltpu.SemaphoreType.DMA((3,)),
+            pltpu.SemaphoreType.DMA((3,)),
         ]
         + sems,
         compiler_params=params(collective_id),
@@ -1262,11 +1300,11 @@
     sources, refs = refs[10 : 10 + n], refs[10 + n :]
     out_ref, sums_ref, cols_ref, dqo_hbm = refs[:4]
     results, refs = refs[4 : 4 + 2 * n], refs[4 + 2 * n :]
-    wqkv, wout, buf, other, own, kv, gm, dkv, from_y, to_z, from_z, dkc, dqkv, stage, stage_out = refs[:15]
-    p_ref, dp_ref, ds_ref, o_ref = refs[15:19]
-    part, from_core, over_out, from_over, send, recv, gsend, grecv, local = refs[19:28]
+    wqkv, wout, buf, other, mixed, own, kv, gm, dkv, from_y, to_z, from_z, dkc, dqkv, stage, stage_out = refs[:16]
+    p_ref, dp_ref, ds_ref, o_ref = refs[16:20]
+    part, from_core, over_out, from_over, send, recv, gsend, grecv, local = refs[20:29]
     p, g = Peers(), Group()
-    sums = reduces(g, sources, results, refs[28:])
+    sums = reduces(g, sources, results, refs[29:])
     rows = x_ref.shape[0]
     n_tp = buf.shape[0]
     out_step = HEADS // n_tp * HEAD
@@ -1279,8 +1317,9 @@
     load_own = pltpu.make_async_copy(own_hbm, own, local.at[1])
     load_kv = pltpu.make_async_copy(kv_hbm, kv, local.at[2])
     load_qkv = pltpu.make_async_copy(wqkv_hbm.at[:, : 3 * WIDE], wqkv, local.at[3])
-    load_mix = pltpu.make_async_copy(mix_hbm, other, local.at[4])
-    for copy in (load_out, load_own, load_kv, load_qkv, load_mix):
+    load_mix = pltpu.make_async_copy(mix_hbm, mixed, local.at[4])
+    load_all = pltpu.make_async_copy(all_hbm, other, local.at[6])
+    for copy in (load_out, load_own, load_kv, load_qkv, load_mix, load_all):
         copy.start()
     sums_ref[...] = jnp.zeros_like(sums_ref)
 
@@ -1407,11 +1446,13 @@
 
     reduce.turn(1, 0)
     stage_out[:, out_width:] = jnp.zeros((D, WIDE - out_width), bf16)
-    outer(other, stage_out, buf[:, :, columns], tiles)
+    low = buf[:, :, columns].reshape(n_tp * rows, out_width)
+    for t in range(n_tp):
+        count = out_step if t < n_tp - 1 else out_width
+        value = mm(mixed[t].reshape(n_tp * rows, WIDE), low, TN).astype(bf16)
+        stage_out[t * out_step : t * out_step + count, :out_width] = value[:count, :]
     keep_out = pltpu.make_async_copy(stage_out, dqo_hbm.at[:, 3 * WIDE :], local.at[5])
     keep_out.start()
-    load_all = pltpu.make_async_copy(all_hbm, other, local.at[6])
-    load_all.start()
     reduce.turn(1, 1)
     if n:
         second_sum.start(0)
@@ -1487,6 +1528,7 @@
             pltpu.VMEM((WIDE, D), bf16),
             pltpu.VMEM((n_tp, rows, D), bf16),
             pltpu.VMEM((n_tp, rows, D), bf16),
+            pltpu.VMEM((n_tp, n_tp, rows, WIDE), bf16),
             pltpu.VMEM((3, MICRO, TOK_DEV, WIDE), bf16),
             pltpu.VMEM((GROUP, MICRO, 2, PROMPT_DEV, WIDE), bf16),
             pltpu.VMEM((MICRO, TOK_DEV, WIDE), bf16),
@@ -1527,8 +1569,7 @@
     x_next, second_all, hidden_pre, hidden = fetch.during(
         (layer + 1, "a"), lambda shard: ff_fwd(x_mid, vecs, fc_bias[None], w_b, n_tp, shard, 1 + layer)
     )
-    mixed_all = heads_joined(lax.all_gather(mixed[:, :, :width], "tp"), n_tp)
-    return x_next, (x, w_out, lse, all_rows, own, kv, mixed_all, x_mid, second_all, hidden_pre, hidden)
+    return x_next, (x, w_out, lse, all_rows, own, kv, mixed, x_mid, second_all, hidden_pre, hidden)
 
 
 class Fetch:
@@ -1539,7 +1580,7 @@
         for key, shard in shards.items():
             if self.staged:
                 if last is None:
-                    last = spread_only(shard, 8, 9)
+                    last = spread_only(shard, FIRST_CHUNKS, 9)
                     self.weights[key] = last.reshape(-1, shard.shape[1])
                 continue
             if last is not None:

time: 1490 us -> 1420 us (0.953)
  Pallas kernels: 1400 us -> 1360 us
    pallas_call x2, Pallas kernels: 422 us -> 401 us  [attn_fwd(): pl.pallas_call(functools.partial(attn_fwd_kernel, len(operands)), out_sha...]
    pallas_call x2, Pallas kernels: 180 us -> 162 us  [ff_bwd(): pl.pallas_call(functools.partial(ff_bwd_kernel, len(payload)), out_shape=...]
  transfers between devices with their start and end apart: 2 -> 0, of which waited for: 0 -> 0; matrix products, arithmetic and copies ran while one was open for 1% -> 0% of each run, Pallas kernels for 22% -> 0%
where the time goes in v8:
time: 1420 us; the launch traced here: 1410 us
  Pallas kernels  1360 us (96%)
  local copies, waits for them, and re-layouts  38.1 us (3%)
  other arithmetic  16.2 us (1%)
    pallas_call x2, Pallas kernels, attn_bwd(): pl.pallas_call(functools.partial(attn_bwd_kernel, len(payload)), out_shap...  421 us
    pallas_call x2, Pallas kernels, attn_fwd(): pl.pallas_call(functools.partial(attn_fwd_kernel, len(operands)), out_sha...  401 us
    pallas_call x2, Pallas kernels, ff_bwd(): pl.pallas_call(functools.partial(ff_bwd_kernel, len(payload)), out_shape=...  162 us
    pallas_call x2, Pallas kernels, ff_fwd(): pl.pallas_call(functools.partial(ff_fwd_kernel, len(operands)), out_shape...  145 us
    pallas_call x1, Pallas kernels, last_sum(): pl.pallas_call(last_sum_kernel, out_shape=results + (whole, whole), in_sp...  125 us
    pallas_call x1, Pallas kernels, spread_only(): pl.pallas_call(functools.partial(spread_kernel, chunks), out_shape=result...  89 us

profile of v8, /device:TPU:9, one launch (start us, length us, event | category | flops | bytes accessed | tf_op | source)
XLA Modules:
  0.0 1412.6 jit_solution(10271185722718116334)
XLA Ops:
  0.6 2.2 bitcast_convert_fusion.1.refs_0_.refs_1_
  2.9 3.6 fusion.21
  6.5 2.7 dynamic-slice_bitcast_fusion.3
  9.4 0.9 fusion.22
  10.3 1.8 dynamic-slice_bitcast_fusion
  12.6 0.9 copy-done.3
  13.5 89.0 %shard_map.262 = bf16[8,200,2176]{2,1,0:T(8,128)(2,1)} custom-call(bf16[200,2176]{1,0:T(8,128)(2,1)} %copy-done.3), custom_call_target="tpu_custom_call" | custom-call | tf_op jit(solution)/shard_map/pallas_call | solution.py:519
  102.5 1.2 convert_bitcast_fusion
  103.7 1.0 copy.66
  104.6 1.1 reshape.137
  105.8 0.6 copy.78
  106.4 0.6 slice_bitcast_fusion.4
  107.5 0.6 pad.54.refs_2_
  108.3 1.7 fusion.12
  110.1 202.0 %shard_map.263 = (f32[192,1600]{1,0:T(8,128)}, f32[2,4,8,384]{3,2,1,0:T(8,128)}, bf16[4,192,1600]{2,1,0:T(8,128)(2,1)}, bf16[3,2,384,512]{3,2,1,0:T(8,128)(2,1)}...) custom-call(f32[192,1600]{1,0:T(8,128)} %bitcast_convert_fusion.1.re, ...), custom_call_target="tpu_custom_call" | custom-call | flops 99999997952 | bytes 31457280 | tf_op jit(solution)/shard_map/pallas_call | solution.py:1264
  312.1 1.0 fusion.15.refs_4_
  313.1 98.3 %shard_map.264 = (f32[192,1600]{1,0:T(8,128)}, bf16[4,192,1600]{2,1,0:T(8,128)(2,1)}, f32[4,192,1600]{2,1,0:T(8,128)}, bf16[4,192,1600]{2,1,0:T(8,128)(2,1)}, bf16[8,200,2048]{2,1,0:T(8,128)(2,1)}) custom-call(f32[192,1600]{1,0:T(8,128)} %get-tuple-element.83.refs_0_.refs_1_, f32[8,1600]{1,0:T(8,128)} %bitcast.115, f32[1,1600]{1,0:T(1,128)} %get-tuple-element.213.refs_2_, ...), custom_call_target="tpu_custom_call" | custom-call | flops 7864320000 | bytes 41943040 | tf_op jit(solution)/shard_map/pallas_call | solution.py:682
  411.3 0.6 copy.77
  412.0 0.6 pad.61.refs_2_
  412.6 198.6 %shard_map.265 = (f32[192,1600]{1,0:T(8,128)}, f32[2,4,8,384]{3,2,1,0:T(8,128)}, bf16[4,192,1600]{2,1,0:T(8,128)(2,1)}, bf16[3,2,384,512]{3,2,1,0:T(8,128)(2,1)}...) custom-call(f32[192,1600]{1,0:T(8,128)} %get-tuple-element.85.refs_0, ...), custom_call_target="tpu_custom_call" | custom-call | flops 99999997952 | bytes 31457280 | tf_op jit(solution)/shard_map/pallas_call | solution.py:1264
  611.2 46.9 %shard_map.266 = (f32[192,1600]{1,0:T(8,128)}, bf16[4,192,1600]{2,1,0:T(8,128)(2,1)}, f32[4,192,1600]{2,1,0:T(8,128)}, bf16[4,192,1600]{2,1,0:T(8,128)(2,1)}) custom-call(f32[192,1600]{1,0:T(8,128)} %get-tuple-element.87.refs_0_.refs_1_, f32[8,1600]{1,0:T(8,128)} %bitcast.119, f32[1,1600]{1,0:T(1,128)} %get-tuple-element.210.refs_2_, ...), custom_call_target="tpu_custom_call" | custom-call | flops 7864320000 | bytes 41943040 | tf_op jit(solution)/shard_map/pallas_call | solution.py:682
  658.1 2.3 convert_element_type.49
  660.3 1.2 bitcast_convert_fusion.refs_0_
  661.5 54.4 %shard_map.267 = (f32[192,1600]{1,0:T(8,128)}, f32[8,1600]{1,0:T(8,128)}, f32[1,1600]{1,0:T(1,128)}, bf16[1600,1600]{1,0:T(8,128)(2,1)}, bf16[1600,1600]{1,0:T(8,128)(2,1)}) custom-call(f32[192,1600]{1,0:T(8,128)} %bitcast_convert_fusion.refs_0_, f32[192,1600]{1,0:T(8,128)} %get-tuple-element.87.refs_0_.refs_1_, f32[8,1600]{1,0:T(8,128)} %bitcast.120, ...), custom_call_target="tpu_custom_call" | custom-call | flops 15728640000 | bytes 52428800 | tf_op jit(solution)/shard_map/pallas_call | solution.py:854
  715.9 211.3 %shard_map.268 = (f32[192,1600]{1,0:T(8,128)}, f32[8,1600]{1,0:T(8,128)}, f32[1,1536]{1,0:T(1,128)}, bf16[1600,2048]{1,0:T(8,128)(2,1)}, bf16[4,200,1600]{2,1,0:...) custom-call(f32[192,1600]{1,0:T(8,128)} %get-tuple-element.93.refs_0_, ...), custom_call_target="tpu_custom_call" | custom-call | flops 199999995904 | bytes 52428800 | tf_op jit(solution)/shard_map/pallas_call | solution.py:1515
  927.2 0.8 convert.44
  928.1 0.6 fusion.25
  928.7 0.3 dynamic_update_slice.18
  929.1 0.2 dynamic_update_slice.19
  929.3 0.8 slice.153
  930.2 0.3 copy.69
  930.5 5.6 dynamic_update_slice.20
  936.0 107.3 %shard_map.269 = (f32[192,1600]{1,0:T(8,128)}, f32[8,1600]{1,0:T(8,128)}, f32[1,1600]{1,0:T(1,128)}, bf16[1600,1600]{1,0:T(8,128)(2,1)}, bf16[1600,1600]{1,0:T(8...) custom-call(f32[192,1600]{1,0:T(8,128)} %get-tuple-element.102.refs_0_, ...), custom_call_target="tpu_custom_call" | custom-call | flops 15728640000 | bytes 52428800 | tf_op jit(solution)/shard_map/pallas_call | solution.py:854
  1043.3 209.4 %shard_map.270 = (f32[192,1600]{1,0:T(8,128)}, f32[8,1600]{1,0:T(8,128)}, f32[1,1536]{1,0:T(1,128)}, bf16[1600,2048]{1,0:T(8,128)(2,1)}, bf16[4,200,1600]{2,1,0:...) custom-call(f32[192,1600]{1,0:T(8,128)} %get-tuple-element.111.refs_0_, ...), custom_call_target="tpu_custom_call" | custom-call | flops 199999995904 | bytes 52428800 | tf_op jit(solution)/shard_map/pallas_call | solution.py:1515
  1252.8 0.8 convert.49
  1253.6 0.7 fusion.24
  1254.3 0.2 dynamic_update_slice.21
  1254.5 0.2 dynamic_update_slice.22
  1254.7 0.8 slice.152
  1255.6 0.3 copy.70
  1255.9 5.8 dynamic_update_slice.23
  1261.7 2.3 convert_reduce_fusion
  1264.1 2.6 fusion.5.earlier
  1266.7 125.1 %shard_map.271 = (bf16[4,200,2048]{2,1,0:T(8,128)(2,1)}, bf16[3,200,2048]{2,1,0:T(8,128)(2,1)}, bf16[4,200,2048]{2,1,0:T(8,128)(2,1)}, bf16[4,200,2048]{2,1,0:T(8,128)(2,1)}) custom-call(bf16[4,2,200,2048]{3,2,1,0:T(8,128)(2,1)} %bitcast.98, bf16[200,2048]{1,0:T(8,128)(2,1)} %fusion.5.earlier), custom_call_target="tpu_custom_call" | custom-call | tf_op jit(solution)/shard_map/pallas_call | solution.py:365
  1391.8 14.4 %shard_map.272 = (f32[2,200,4800]{2,1,0:T(8,128)}, f32[2,200,1600]{2,1,0:T(8,128)}, f32[2,200,1600]{2,1,0:T(8,128)}, f32[2,1600,200]{2,1,0:T(8,128)}, f32[2,200]...) custom-call(bf16[4,200,2048]{2,1,0:T(8,128)(2,1)} %get-tuple-element, ...), custom_call_target="tpu_custom_call" | custom-call | tf_op jit(solution)/shard_map/pallas_call | solution.py:434
  1406.2 1.3 copy.71
  1407.5 3.6 copy.72
  1411.1 1.0 copy.101
  (78 shorter events, 1.5 us)
Async XLA Ops:
  6.5 2.8 copy-start
  9.3 2.9 copy-start.12
  9.3 2.9 copy-start.13
  9.3 2.9 copy-start.14
  9.3 2.9 copy-start.15
  9.3 2.9 copy-start.16
  9.3 2.9 copy-start.17
  9.3 3.0 copy-start.18
  9.3 3.0 copy-start.19
  9.4 3.0 copy-start.20
  12.5 0.9 copy-start.3
  102.5 5.6 copy-start.1
  104.6 3.6 copy-start.2
  110.0 202.0 %copy-start.5 = (bf16[200,448]{1,0:T(8,128)(2,1)S(1)}, bf16[200,448]{1,0:T(8,128)(2,1)}, u32[]{:S(2)}) copy-start(bf16[200,448]{1,0:T(8,128)(2,1)} %get-tuple-element.198) | copy-start | bytes 537604
  110.0 202.0 %copy-start.6 = (bf16[200,448]{1,0:T(8,128)(2,1)S(1)}, bf16[200,448]{1,0:T(8,128)(2,1)}, u32[]{:S(2)}) copy-start(bf16[200,448]{1,0:T(8,128)(2,1)} %get-tuple-element.199) | copy-start | bytes 537604
  110.1 202.0 %copy-start.7 = (bf16[200,448]{1,0:T(8,128)(2,1)S(1)}, bf16[200,448]{1,0:T(8,128)(2,1)}, u32[]{:S(2)}) copy-start(bf16[200,448]{1,0:T(8,128)(2,1)} %get-tuple-element.200) | copy-start | bytes 537604
  110.1 202.0 %copy-start.8 = (bf16[200,448]{1,0:T(8,128)(2,1)S(1)}, bf16[200,448]{1,0:T(8,128)(2,1)}, u32[]{:S(2)}) copy-start(bf16[200,448]{1,0:T(8,128)(2,1)} %get-tuple-element.227) | copy-start | bytes 537604
  658.1 2.3 copy-start.9
  715.9 214.2 %copy-start.11 = (f32[1,1600]{1,0:T(1,128)S(1)}, f32[1,1600]{1,0:T(1,128)}, u32[]{:S(2)}) copy-start(f32[1,1600]{1,0:T(1,128)} %get-tuple-element.110) | copy-start | bytes 19204
  1043.3 212.2 %copy-start.10 = (f32[1,1600]{1,0:T(1,128)S(1)}, f32[1,1600]{1,0:T(1,128)}, u32[]{:S(2)}) copy-start(f32[1,1600]{1,0:T(1,128)} %get-tuple-element.125) | copy-start | bytes 19204
  1407.5 3.6 copy-start.4

commit v9 on v8

--- a/solution.py
+++ b/solution.py
@@ -149,6 +149,11 @@
         self.base = f - self.member
         self.z, self.y = self.member // 2, self.member % 2
 
+        half = self.z // 2
+        self.inner = (self.z + half) % 2 == 1
+        self.mate = 2 * half + 1 - self.z % 2
+        self.far_inner, self.far_end = 2 - half, 3 - 3 * half
+
     def at(self, z, y):
         return z * 2 + y
 
@@ -179,11 +184,11 @@
             pl.semaphore_signal(barrier, inc=1, device_id=(peers.f, t), device_id_type=MESH)
         pl.semaphore_wait(barrier, 4 + len(near))
 
-    def copy(self, source, target, sems, index, member):
+    def copy(self, source, target, sems, index, member, send_index=None):
         return pltpu.make_async_remote_copy(
             src_ref=source,
             dst_ref=target,
-            send_sem=sems[0].at[index],
+            send_sem=sems[0].at[index if send_index is None else send_index],
             recv_sem=sems[1].at[index],
             device_id=(self.base + member, self.t),
             device_id_type=MESH,
@@ -235,8 +240,9 @@
         self.gone[j - 1, :, columns] = self.own[:, columns] + self.got[:, columns]
         self.along(j).start()
 
-    def finish(self, reused=False):
-        self.across(0).wait_recv()
+    def finish(self, reused=False, arrived=False):
+        if not arrived:
+            self.across(0).wait_recv()
         for j in range(4):
             self.across(j).wait_send()
         for j in (1, 2, 3):
@@ -273,27 +279,35 @@
 
 
 def in_turn(items):
-    order = [(item, j) for item in items for j in (1, 2, 3)] + [(item, 0) for item in items]
+    order = [(item, j) for item in items for j in (1, 2, 3, 0)]
 
     def step(n):
+        def following():
+            item, j = order[n + 1]
+            item.start(j)
+
         item, j = order[n]
-        item.pump(j, then=lambda: order[n + 1][0].start(order[n + 1][1]))
-
-    steps = [functools.partial(step, n) for n in range(3 * len(items))]
-    return [lambda: items[0].start(1)] + steps + [lambda item=item: item.start(0) for item in items[1:]]
+        if j:
+            item.pump(j, then=following)
+        else:
+            item.across(0).wait_recv()
+            following()
+
+    return [lambda: items[0].start(1)] + [functools.partial(step, n) for n in range(len(order) - 1)]
 
 
 class BlockGather:
-    def __init__(self, peers, source, target, sems, first, local):
-        self.p, self.source, self.target, self.sems, self.first = peers, source, target, sems, first
-        self.local = local
+    def __init__(self, peers, source, target, sems, first, local, columns=None):
+        self.p, self.sems, self.first, self.local = peers, sems, first, local
+        self.source = source if columns is None else source.at[:, columns]
+        self.slot = lambda t: target.at[t] if columns is None else target.at[t, :, columns]
 
     def piece(self, slot, index, to, own=False):
-        target = self.target.at[slot]
+        target = self.slot(slot)
         return self.p.copy(self.source if own else target, target, self.sems, self.first + index, to)
 
     def keep(self):
-        return pltpu.make_async_copy(self.source, self.target.at[self.p.t], self.local)
+        return pltpu.make_async_copy(self.source, self.slot(self.p.t), self.local)
 
     def start(self):
         p = self.p
@@ -316,47 +330,57 @@
         self.keep().wait()
 
 
-def add_up(own, others, target):
+def add_up(own, others, target, columns):
     rows = own.shape[0]
     for first in range(0, rows, 40):
-        at = slice(first, min(first + 40, rows))
-        total = own[at, :].astype(f32)
+        at = (slice(first, min(first + 40, rows)), columns)
+        total = own[at].astype(f32)
         for other in others:
-            total = total + other[at, :].astype(f32)
-        target[at, :] = total.astype(target.dtype)
+            total = total + other[at].astype(f32)
+        target[at] = total.astype(target.dtype)
 
 
 def last_sum_kernel(source, earlier, from_y, from_z, got, got_earlier, *scratch):
     p, g = Peers(), Group()
-    scratch, (bsend, brecv, blocal, mine) = scratch[:-4], scratch[-4:]
-    own, near, gone, local = scratch[4:]
+    scratch, (bsend, brecv, blocal, terms, mine) = scratch[:-5], scratch[-5:]
     before = BlockGather(p, earlier, got_earlier, (bsend, brecv), 0, blocal.at[0])
-    after = BlockGather(p, mine, got, (bsend, brecv), 3, blocal.at[1])
     items = reduces(g, [source], [from_y, from_z], scratch)
+    after = [
+        BlockGather(p, mine, got, (bsend, brecv), 3 + 3 * n, blocal.at[1 + n], item.columns)
+        for n, item in enumerate(items)
+    ]
     steps = in_turn(items)
     g.greet(p)
     steps[0]()
     before.start()
+
+    def total(n):
+        item = items[n]
+        item.finish(arrived=n == 0)
+        loads = [
+            pltpu.make_async_copy(item.cut(source, g.z, g.y), item.cut(terms, 0), blocal.at[3]),
+            pltpu.make_async_copy(item.cut(from_y, g.z), item.cut(terms, 1), blocal.at[4]),
+        ]
+        for k in range(3):
+            loads.append(pltpu.make_async_copy(item.cut(from_z, k), item.cut(terms, 2 + k), blocal.at[5 + k]))
+        for load in loads:
+            load.start()
+        for load in loads:
+            load.wait()
+        add_up(terms.at[0], [terms.at[k] for k in range(1, 5)], mine, item.columns)
+        after[n].start()
+
     for n, step in enumerate(steps[1:]):
         if n == 3:
             before.relay()
         step()
-    for item in items:
-        item.finish()
-    loads = [
-        pltpu.make_async_copy(source.at[g.z, g.y], own, local.at[0]),
-        pltpu.make_async_copy(from_y.at[g.z], near, local.at[1]),
-        pltpu.make_async_copy(from_z, gone, blocal.at[2]),
-    ]
-    for load in loads:
-        load.start()
-    for load in loads:
-        load.wait()
-    add_up(own, [near] + [gone.at[k] for k in range(3)], mine)
-    after.start()
+    total(0)
+    after[0].relay()
+    total(1)
     before.finish()
-    after.relay()
-    after.finish()
+    after[0].finish()
+    after[1].relay()
+    after[1].finish()
 
 
 def last_sum(part, earlier, n_tp, collective_id):
@@ -368,8 +392,8 @@
         in_specs=[ANY, ANY],
         out_specs=(ANY,) * 4,
         scratch_shapes=scratch
-        + [pltpu.SemaphoreType.DMA((6,))] * 2
-        + [pltpu.SemaphoreType.DMA((3,)), pltpu.VMEM(earlier.shape, bf16)],
+        + [pltpu.SemaphoreType.DMA((9,))] * 2
+        + [pltpu.SemaphoreType.DMA((8,)), pltpu.VMEM((5,) + earlier.shape, bf16), pltpu.VMEM(earlier.shape, bf16)],
         compiler_params=params(collective_id),
     )(part, earlier)
     return got, got_earlier
@@ -451,25 +475,34 @@
         ends = [128 * (count * sum(chunks[: c + 1]) // sum(chunks)) for c in range(len(chunks))]
         self.columns = [slice(a, b) for a, b in zip([0] + ends, ends)]
         self.partner = group.at(group.z, 1 - group.y)
-
-    def piece(self, member, c, index, to, own=False):
+        self.origins = (group.mate, group.far_inner, group.far_end)
+
+    def piece(self, member, c, index, to, own=False, send_index=None):
         target = self.target.at[member, :, self.columns[c]]
         source = self.source.at[:, self.columns[c]] if own else target
-        return self.g.copy(source, target, self.sems, 7 * c + index, to)
+        send = None if send_index is None else 9 * c + send_index
+        return self.g.copy(source, target, self.sems, 9 * c + index, to, send)
 
     def own(self, c):
         g = self.g
-        return [self.piece(g.member, c, k, g.at(g.ahead(k), g.y), True) for k in (1, 2, 3)] + [
-            self.piece(g.member, c, 0, self.partner, True)
+        arrives = jnp.where(g.inner, 2, 3)
+        return [
+            self.piece(g.member, c, arrives, g.at(g.far_inner, g.y), True, 2),
+            self.piece(g.member, c, 1, g.at(g.mate, g.y), True),
+            self.piece(g.member, c, 0, self.partner, True),
         ]
 
-    def relayed(self, c):
+    def relayed(self, c, k):
         g = self.g
-        return [self.piece(g.at(g.behind(k), g.y), c, 3 + k, self.partner) for k in (1, 2, 3)]
+        return self.piece(g.at(self.origins[k - 1], g.y), c, 3 + k, self.partner)
+
+    def passed(self, c, k):
+        g = self.g
+        return self.piece(g.at(self.origins[k - 1], g.y), c, k, g.at(g.mate, g.y), send_index=5 + k)
 
     def keep(self):
         return pltpu.make_async_copy(
-            self.source, self.target.at[self.g.member], self.sems[0].at[7 * len(self.columns)]
+            self.source, self.target.at[self.g.member], self.sems[0].at[9 * len(self.columns)]
         )
 
     def start(self, first=0, last=None):
@@ -481,18 +514,31 @@
 
     def relay(self, c):
         g = self.g
-        for k, copy in zip((1, 2, 3), self.relayed(c)):
-            self.piece(g.at(g.behind(k), g.y), c, k, self.partner).wait_recv()
-            copy.start()
+        for k in (1, 2, 3):
+            self.piece(g.at(self.origins[k - 1], g.y), c, k, self.partner).wait_recv()
+            if k > 1:
+
+                @pl.when(g.inner)
+                def _(k=k):
+                    self.passed(c, k).start()
+
+            self.relayed(c, k).start()
 
     def finish(self):
         g = self.g
         for c in range(len(self.columns)):
             self.piece(self.partner, c, 0, self.partner).wait_recv()
             for k in (1, 2, 3):
-                self.piece(g.at(g.behind(k), 1 - g.y), c, 3 + k, self.partner).wait_recv()
-            for copy in self.own(c) + self.relayed(c):
+                self.piece(g.at(self.origins[k - 1], 1 - g.y), c, 3 + k, self.partner).wait_recv()
+                self.relayed(c, k).wait_send()
+            for copy in self.own(c):
                 copy.wait_send()
+
+            @pl.when(g.inner)
+            def _(c=c):
+                self.passed(c, 2).wait_send()
+                self.passed(c, 3).wait_send()
+
         self.keep().wait()
 
 
@@ -500,7 +546,7 @@
     if shard is None:
         return (), (), []
     whole = jax.ShapeDtypeStruct((GROUP,) + shard.shape, shard.dtype)
-    return (shard,), (whole,), [pltpu.SemaphoreType.DMA((7 * len(chunks) + 1,))] * 2
+    return (shard,), (whole,), [pltpu.SemaphoreType.DMA((9 * len(chunks) + 1,))] * 2
 
 
 def spread_kernel(chunks, source, target, send, recv):
@@ -843,8 +889,8 @@
         advance()
     scatter.finish()
     store.wait()
-    for item in sums:
-        item.finish()
+    for i, item in enumerate(sums):
+        item.finish(arrived=i == 0)
 
 
 def ff_bwd(grad, x, vecs, all_rows, pre, hidden, w_b, n_tp, payload, collective_id):
@@ -1129,7 +1175,6 @@
             kv[g.member, micro, i] = own[1 + i, micro, :PROMPT_DEV, :]
     share.start(0, 0)
     if n:
-        spread.relay(0)
         spread.start(1, 2)
     hooks = {
         (0, 1): [lambda: share.relay(0, 1), lambda: share.start(1, 0)],
@@ -1140,9 +1185,10 @@
         (1, 2): [lambda: share.wait(1, 1)],
     }
     if n:
-        hooks[0, 1] += [lambda: spread.start(2, 3), lambda: spread.relay(1)]
-        hooks[1, 1] += [lambda: spread.start(3, 4), lambda: spread.relay(2)]
-        hooks[1, 3] = [lambda: spread.start(4)]
+        hooks[0, 0] = [lambda: spread.start(2, 3)]
+        hooks[0, 2] += [lambda: spread.relay(1)]
+        hooks[0, 3] += [lambda: spread.start(3, 4)]
+        hooks[1, 1] += [lambda: spread.relay(2), lambda: spread.start(4)]
     keep_all = pltpu.make_async_copy(buf, all_hbm, local.at[2])
     keep_own = pltpu.make_async_copy(own, own_hbm, local.at[3])
     keep_all.start()
@@ -1152,6 +1198,8 @@
 
     share.relay(0, 0)
     share.start(0, 1)
+    if n:
+        spread.relay(0)
     share.wait(0, 0)
 
     for micro in range(MICRO):
@@ -1331,14 +1379,14 @@
     row_chunks(rows, lower)
     g.greet(p)
     gather.start()
-    hooks = {(1, 0): [lambda: reduce.turn(0, 0)], (1, 1): [lambda: reduce.turn(0, 1)]}
+    hooks = {(1, 1): [lambda: reduce.turn(0, 0)], (1, 2): [lambda: reduce.turn(0, 1)]}
     if n:
         first_sum, second_sum = sums
         first_sum.start(1)
-        hooks[0, 1] = [lambda: first_sum.start(0), lambda: first_sum.pump(2)]
-        hooks[0, 2] = [lambda: second_sum.start(1), lambda: first_sum.pump(3)]
-        hooks[0, 3] = [lambda: second_sum.start(2)]
-        hooks[1, 1] += [lambda: second_sum.pump(1, first_sum), lambda: second_sum.start(3)]
+        hooks[0, 1] = [lambda: first_sum.pump(2)]
+        hooks[0, 2] = [lambda: first_sum.pump(3)]
+        hooks[1, 1] += [lambda: second_sum.start(1)]
+        hooks[1, 3] = [lambda: second_sum.pump(1, first_sum)]
     gather.wait_chip()
     load_out.wait()
 
@@ -1357,8 +1405,7 @@
     sub = lax.broadcasted_iota(jnp.int32, (CHUNK, TOK_DEV), 0)
 
     if n:
-        first_sum.start(3)
-        first_sum.pump(1)
+        first_sum.pump(1, then=lambda: first_sum.start(3))
 
     for micro in range(MICRO):
 
@@ -1455,14 +1502,13 @@
     keep_out.start()
     reduce.turn(1, 1)
     if n:
-        second_sum.start(0)
+        second_sum.start(2)
     for micro in range(MICRO):
         reduce.wait(micro)
         for i in range(2):
             to_slots(dqkv, micro, 0, reduce.total(micro, i), slice((1 + i) * WIDE, (2 + i) * WIDE))
     if n:
-        second_sum.pump(2, first_sum)
-        second_sum.pump(3, first_sum)
+        second_sum.pump(2, first_sum, lambda: second_sum.start(3))
     load_qkv.wait()
 
     def down(x):
@@ -1476,6 +1522,9 @@
     scatter.send_over()
     down(p.x)
     scatter.near_to_core().start()
+    if n:
+        second_sum.pump(3, first_sum, lambda: second_sum.start(0))
+        first_sum.start(0)
     load_all.wait()
     outer(other, stage, dqkv[...], tiles)
     keep_qkv = pltpu.make_async_copy(stage, dqo_hbm.at[:, : 3 * WIDE], local.at[7])

time: 1420 us -> 1350 us (0.951)
  Pallas kernels: 1360 us -> 1280 us
    pallas_call x1, Pallas kernels: 125 us -> 95.4 us  [last_sum(): pl.pallas_call(last_sum_kernel, out_shape=results + (whole, whole), in_sp...]
    pallas_call x2, Pallas kernels: 421 us -> 404 us  [attn_bwd(): pl.pallas_call(functools.partial(attn_bwd_kernel, len(payload)), out_shap...]
where the time goes in v9:
time: 1350 us; the launch traced here: 1340 us
  Pallas kernels  1280 us (95%)
  local copies, waits for them, and re-layouts  38.1 us (3%)
  other arithmetic  16.2 us (1%)
    pallas_call x2, Pallas kernels, attn_bwd(): pl.pallas_call(functools.partial(attn_bwd_kernel, len(payload)), out_shap...  404 us
    pallas_call x2, Pallas kernels, attn_fwd(): pl.pallas_call(functools.partial(attn_fwd_kernel, len(operands)), out_sha...  390 us
    pallas_call x2, Pallas kernels, ff_bwd(): pl.pallas_call(functools.partial(ff_bwd_kernel, len(payload)), out_shape=...  158 us
    pallas_call x2, Pallas kernels, ff_fwd(): pl.pallas_call(functools.partial(ff_fwd_kernel, len(operands)), out_shape...  141 us
    pallas_call x1, Pallas kernels, last_sum(): pl.pallas_call(last_sum_kernel, out_shape=results + (whole, whole), in_sp...  95.4 us
    pallas_call x1, Pallas kernels, spread_only(): pl.pallas_call(functools.partial(spread_kernel, chunks), out_shape=result...  79.5 us

profile of v9, /device:TPU:9, one launch (start us, length us, event | category | flops | bytes accessed | tf_op | source)
XLA Modules:
  0.0 1338.7 jit_solution(1154075413105981270)
XLA Ops:
  0.6 2.2 bitcast_convert_fusion.1.refs_0_.refs_1_
  2.9 3.6 fusion.21
  6.5 2.7 dynamic-slice_bitcast_fusion.3
  9.4 0.9 fusion.22
  10.3 1.8 dynamic-slice_bitcast_fusion
  12.6 0.9 copy-done.3
  13.5 79.5 %shard_map.262 = bf16[8,200,2176]{2,1,0:T(8,128)(2,1)} custom-call(bf16[200,2176]{1,0:T(8,128)(2,1)} %copy-done.3), custom_call_target="tpu_custom_call" | custom-call | tf_op jit(solution)/shard_map/pallas_call | solution.py:565
  93.0 1.2 convert_bitcast_fusion
  94.2 1.0 copy.66
  95.1 1.1 reshape.137
  96.3 0.6 copy.78
  96.9 0.6 slice_bitcast_fusion.4
  98.0 0.6 pad.54.refs_2_
  98.8 1.7 fusion.12
  100.5 191.0 %shard_map.263 = (f32[192,1600]{1,0:T(8,128)}, f32[2,4,8,384]{3,2,1,0:T(8,128)}, bf16[4,192,1600]{2,1,0:T(8,128)(2,1)}, bf16[3,2,384,512]{3,2,1,0:T(8,128)(2,1)}...) custom-call(f32[192,1600]{1,0:T(8,128)} %bitcast_convert_fusion.1.re, ...), custom_call_target="tpu_custom_call" | custom-call | flops 99999997952 | bytes 31457280 | tf_op jit(solution)/shard_map/pallas_call | solution.py:1312
  291.6 1.0 fusion.15.refs_4_
  292.6 95.8 %shard_map.264 = (f32[192,1600]{1,0:T(8,128)}, bf16[4,192,1600]{2,1,0:T(8,128)(2,1)}, f32[4,192,1600]{2,1,0:T(8,128)}, bf16[4,192,1600]{2,1,0:T(8,128)(2,1)}, bf16[8,200,2048]{2,1,0:T(8,128)(2,1)}) custom-call(f32[192,1600]{1,0:T(8,128)} %get-tuple-element.83.refs_0_.refs_1_, f32[8,1600]{1,0:T(8,128)} %bitcast.115, f32[1,1600]{1,0:T(1,128)} %get-tuple-element.213.refs_2_, ...), custom_call_target="tpu_custom_call" | custom-call | flops 7864320000 | bytes 41943040 | tf_op jit(solution)/shard_map/pallas_call | solution.py:728
  388.4 0.6 copy.77
  389.0 0.6 pad.61.refs_2_
  389.6 199.0 %shard_map.265 = (f32[192,1600]{1,0:T(8,128)}, f32[2,4,8,384]{3,2,1,0:T(8,128)}, bf16[4,192,1600]{2,1,0:T(8,128)(2,1)}, bf16[3,2,384,512]{3,2,1,0:T(8,128)(2,1)}...) custom-call(f32[192,1600]{1,0:T(8,128)} %get-tuple-element.85.refs_0, ...), custom_call_target="tpu_custom_call" | custom-call | flops 99999997952 | bytes 31457280 | tf_op jit(solution)/shard_map/pallas_call | solution.py:1312
  588.6 45.6 %shard_map.266 = (f32[192,1600]{1,0:T(8,128)}, bf16[4,192,1600]{2,1,0:T(8,128)(2,1)}, f32[4,192,1600]{2,1,0:T(8,128)}, bf16[4,192,1600]{2,1,0:T(8,128)(2,1)}) custom-call(f32[192,1600]{1,0:T(8,128)} %get-tuple-element.87.refs_0_.refs_1_, f32[8,1600]{1,0:T(8,128)} %bitcast.119, f32[1,1600]{1,0:T(1,128)} %get-tuple-element.210.refs_2_, ...), custom_call_target="tpu_custom_call" | custom-call | flops 7864320000 | bytes 41943040 | tf_op jit(solution)/shard_map/pallas_call | solution.py:728
  634.3 2.3 convert_element_type.49
  636.5 1.2 bitcast_convert_fusion.refs_0_
  637.7 54.6 %shard_map.267 = (f32[192,1600]{1,0:T(8,128)}, f32[8,1600]{1,0:T(8,128)}, f32[1,1600]{1,0:T(1,128)}, bf16[1600,1600]{1,0:T(8,128)(2,1)}, bf16[1600,1600]{1,0:T(8,128)(2,1)}) custom-call(f32[192,1600]{1,0:T(8,128)} %bitcast_convert_fusion.refs_0_, f32[192,1600]{1,0:T(8,128)} %get-tuple-element.87.refs_0_.refs_1_, f32[8,1600]{1,0:T(8,128)} %bitcast.120, ...), custom_call_target="tpu_custom_call" | custom-call | flops 15728640000 | bytes 52428800 | tf_op jit(solution)/shard_map/pallas_call | solution.py:900
  692.4 199.4 %shard_map.268 = (f32[192,1600]{1,0:T(8,128)}, f32[8,1600]{1,0:T(8,128)}, f32[1,1536]{1,0:T(1,128)}, bf16[1600,2048]{1,0:T(8,128)(2,1)}, bf16[4,200,1600]{2,1,0:...) custom-call(f32[192,1600]{1,0:T(8,128)} %get-tuple-element.93.refs_0_, ...), custom_call_target="tpu_custom_call" | custom-call | flops 199999995904 | bytes 52428800 | tf_op jit(solution)/shard_map/pallas_call | solution.py:1564
  891.8 0.8 convert.44
  892.6 0.6 fusion.25
  893.3 0.3 dynamic_update_slice.18
  893.6 0.2 dynamic_update_slice.19
  893.8 0.8 slice.153
  894.8 0.3 copy.69
  895.0 5.6 dynamic_update_slice.20
  900.6 103.2 %shard_map.269 = (f32[192,1600]{1,0:T(8,128)}, f32[8,1600]{1,0:T(8,128)}, f32[1,1600]{1,0:T(1,128)}, bf16[1600,1600]{1,0:T(8,128)(2,1)}, bf16[1600,1600]{1,0:T(8...) custom-call(f32[192,1600]{1,0:T(8,128)} %get-tuple-element.102.refs_0_, ...), custom_call_target="tpu_custom_call" | custom-call | flops 15728640000 | bytes 52428800 | tf_op jit(solution)/shard_map/pallas_call | solution.py:900
  1003.8 204.8 %shard_map.270 = (f32[192,1600]{1,0:T(8,128)}, f32[8,1600]{1,0:T(8,128)}, f32[1,1536]{1,0:T(1,128)}, bf16[1600,2048]{1,0:T(8,128)(2,1)}, bf16[4,200,1600]{2,1,0:...) custom-call(f32[192,1600]{1,0:T(8,128)} %get-tuple-element.111.refs_0_, ...), custom_call_target="tpu_custom_call" | custom-call | flops 199999995904 | bytes 52428800 | tf_op jit(solution)/shard_map/pallas_call | solution.py:1564
  1208.6 0.8 convert.49
  1209.5 0.7 fusion.24
  1210.2 0.2 dynamic_update_slice.21
  1210.3 0.2 dynamic_update_slice.22
  1210.5 0.8 slice.152
  1211.5 0.3 copy.70
  1211.7 5.8 dynamic_update_slice.23
  1217.6 2.3 convert_reduce_fusion
  1219.9 2.6 fusion.5.earlier
  1222.6 95.4 %shard_map.271 = (bf16[4,200,2048]{2,1,0:T(8,128)(2,1)}, bf16[3,200,2048]{2,1,0:T(8,128)(2,1)}, bf16[4,200,2048]{2,1,0:T(8,128)(2,1)}, bf16[4,200,2048]{2,1,0:T(8,128)(2,1)}) custom-call(bf16[4,2,200,2048]{3,2,1,0:T(8,128)(2,1)} %bitcast.98, bf16[200,2048]{1,0:T(8,128)(2,1)} %fusion.5.earlier), custom_call_target="tpu_custom_call" | custom-call | tf_op jit(solution)/shard_map/pallas_call | solution.py:389
  1318.0 14.4 %shard_map.272 = (f32[2,200,4800]{2,1,0:T(8,128)}, f32[2,200,1600]{2,1,0:T(8,128)}, f32[2,200,1600]{2,1,0:T(8,128)}, f32[2,1600,200]{2,1,0:T(8,128)}, f32[2,200]...) custom-call(bf16[4,200,2048]{2,1,0:T(8,128)(2,1)} %get-tuple-element, ...), custom_call_target="tpu_custom_call" | custom-call | tf_op jit(solution)/shard_map/pallas_call | solution.py:458
  1332.3 1.3 copy.71
  1333.6 3.6 copy.72
  1337.2 1.0 copy.101
  (78 shorter events, 1.5 us)
Async XLA Ops:
  6.5 2.8 copy-start
  9.3 2.9 copy-start.12
  9.3 2.9 copy-start.13
  9.3 2.9 copy-start.14
  9.3 2.9 copy-start.15
  9.3 2.9 copy-start.16
  9.3 2.9 copy-start.17
  9.3 3.0 copy-start.18
  9.3 3.0 copy-start.19
  9.4 3.0 copy-start.20
  12.5 0.9 copy-start.3
  93.0 5.6 copy-start.1
  95.1 3.6 copy-start.2
  100.5 191.0 %copy-start.5 = (bf16[200,448]{1,0:T(8,128)(2,1)S(1)}, bf16[200,448]{1,0:T(8,128)(2,1)}, u32[]{:S(2)}) copy-start(bf16[200,448]{1,0:T(8,128)(2,1)} %get-tuple-element.198) | copy-start | bytes 537604
  100.5 191.0 %copy-start.6 = (bf16[200,448]{1,0:T(8,128)(2,1)S(1)}, bf16[200,448]{1,0:T(8,128)(2,1)}, u32[]{:S(2)}) copy-start(bf16[200,448]{1,0:T(8,128)(2,1)} %get-tuple-element.199) | copy-start | bytes 537604
  100.5 191.1 %copy-start.7 = (bf16[200,448]{1,0:T(8,128)(2,1)S(1)}, bf16[200,448]{1,0:T(8,128)(2,1)}, u32[]{:S(2)}) copy-start(bf16[200,448]{1,0:T(8,128)(2,1)} %get-tuple-element.200) | copy-start | bytes 537604
  100.5 191.1 %copy-start.8 = (bf16[200,448]{1,0:T(8,128)(2,1)S(1)}, bf16[200,448]{1,0:T(8,128)(2,1)}, u32[]{:S(2)}) copy-start(bf16[200,448]{1,0:T(8,128)(2,1)} %get-tuple-element.227) | copy-start | bytes 537604
  634.3 2.3 copy-start.9
  692.4 202.3 %copy-start.11 = (f32[1,1600]{1,0:T(1,128)S(1)}, f32[1,1600]{1,0:T(1,128)}, u32[]{:S(2)}) copy-start(f32[1,1600]{1,0:T(1,128)} %get-tuple-element.110) | copy-start | bytes 19204
  1003.8 207.5 %copy-start.10 = (f32[1,1600]{1,0:T(1,128)S(1)}, f32[1,1600]{1,0:T(1,128)}, u32[]{:S(2)}) copy-start(f32[1,1600]{1,0:T(1,128)} %get-tuple-element.125) | copy-start | bytes 19204
  1333.6 3.6 copy-start.4

commit v10 on v9

--- a/solution.py
+++ b/solution.py
@@ -489,8 +489,10 @@
         return [
             self.piece(g.member, c, arrives, g.at(g.far_inner, g.y), True, 2),
             self.piece(g.member, c, 1, g.at(g.mate, g.y), True),
-            self.piece(g.member, c, 0, self.partner, True),
         ]
+
+    def own_across(self, c):
+        return self.piece(self.g.member, c, 0, self.partner, True)
 
     def relayed(self, c, k):
         g = self.g
@@ -508,21 +510,33 @@
     def start(self, first=0, last=None):
         if first == 0:
             self.keep().start()
+            for c in range(len(self.columns)):
+                self.own_across(c).start()
         for c in range(len(self.columns))[first:last]:
             for copy in self.own(c):
                 copy.start()
 
+    def arrival(self, c, k):
+        g = self.g
+        self.piece(g.at(self.origins[k - 1], g.y), c, k, self.partner).wait_recv()
+
     def relay(self, c):
-        g = self.g
-        for k in (1, 2, 3):
-            self.piece(g.at(self.origins[k - 1], g.y), c, k, self.partner).wait_recv()
-            if k > 1:
-
-                @pl.when(g.inner)
-                def _(k=k):
-                    self.passed(c, k).start()
-
-            self.relayed(c, k).start()
+        self.arrival(c, 1)
+        self.relayed(c, 1).start()
+
+        @pl.when(self.g.inner)
+        def _():
+            for k in (2, 3):
+                self.arrival(c, k)
+                self.passed(c, k).start()
+                self.relayed(c, k).start()
+
+    def relay_late(self, c):
+        @pl.when(jnp.logical_not(self.g.inner))
+        def _():
+            for k in (2, 3):
+                self.arrival(c, k)
+                self.relayed(c, k).start()
 
     def finish(self):
         g = self.g
@@ -531,7 +545,7 @@
             for k in (1, 2, 3):
                 self.piece(g.at(self.origins[k - 1], 1 - g.y), c, 3 + k, self.partner).wait_recv()
                 self.relayed(c, k).wait_send()
-            for copy in self.own(c):
+            for copy in self.own(c) + [self.own_across(c)]:
                 copy.wait_send()
 
             @pl.when(g.inner)
@@ -557,6 +571,9 @@
     for c in range(len(chunks)):
         spread.relay(c)
         spread.start(c + 2, c + 3)
+        if c:
+            spread.relay_late(c - 1)
+    spread.relay_late(len(chunks) - 1)
     spread.finish()
 
 
@@ -684,6 +701,7 @@
     scatter.send_over()
     if n:
         spread.start(2, 3)
+        spread.relay_late(0)
     down(p.x)
     scatter.near_to_core().start()
     if n:
@@ -697,7 +715,10 @@
     row_chunks(rows, final)
     if n:
         spread.relay(2)
+        spread.relay_late(1)
         spread.relay(3)
+        spread.relay_late(2)
+        spread.relay_late(3)
     gather.finish()
     scatter.finish()
     for copy in (keep_all, keep_pre, keep_hid):
@@ -1186,9 +1207,9 @@
     }
     if n:
         hooks[0, 0] = [lambda: spread.start(2, 3)]
-        hooks[0, 2] += [lambda: spread.relay(1)]
+        hooks[0, 2] += [lambda: spread.relay(1), lambda: spread.relay_late(1)]
         hooks[0, 3] += [lambda: spread.start(3, 4)]
-        hooks[1, 1] += [lambda: spread.relay(2), lambda: spread.start(4)]
+        hooks[1, 1] += [lambda: spread.relay(2), lambda: spread.relay_late(2), lambda: spread.start(4)]
     keep_all = pltpu.make_async_copy(buf, all_hbm, local.at[2])
     keep_own = pltpu.make_async_copy(own, own_hbm, local.at[3])
     keep_all.start()
@@ -1200,6 +1221,7 @@
     share.start(0, 1)
     if n:
         spread.relay(0)
+        spread.relay_late(0)
     share.wait(0, 0)
 
     for micro in range(MICRO):
@@ -1273,6 +1295,7 @@
     scatter.near_to_core().start()
     if n:
         spread.relay(3)
+        spread.relay_late(3)
     scatter.wait()
     mixes.start()
 
@@ -1283,6 +1306,7 @@
     mixes.relay()
     if n:
         spread.relay(4)
+        spread.relay_late(4)
     gather.finish()
     scatter.finish()
     share.finish()
@@ -1344,10 +1368,11 @@
 
 
 def attn_bwd_kernel(n, *refs):
-    g_ref, x_ref, vec_ref, lse_ref, all_hbm, own_hbm, kv_hbm, mix_hbm, wqkv_hbm, wout_hbm = refs[:10]
-    sources, refs = refs[10 : 10 + n], refs[10 + n :]
-    out_ref, sums_ref, cols_ref, dqo_hbm = refs[:4]
-    results, refs = refs[4 : 4 + 2 * n], refs[4 + 2 * n :]
+    g_ref, x_ref, vec_ref, lse_ref, ff_ref, fcb_ref, all_hbm, own_hbm, kv_hbm, mix_hbm, wqkv_hbm, wout_hbm = refs[:12]
+    sources, refs = refs[12 : 12 + n], refs[12 + n :]
+    out_ref, dqo_hbm = refs[:2]
+    results, refs = refs[2 : 2 + 2 * n], refs[2 + 2 * n :]
+    (sums_ref, cols_ref, vectors), refs = refs[:3], refs[3:]
     wqkv, wout, buf, other, mixed, own, kv, gm, dkv, from_y, to_z, from_z, dkc, dqkv, stage, stage_out = refs[:16]
     p_ref, dp_ref, ds_ref, o_ref = refs[16:20]
     part, from_core, over_out, from_over, send, recv, gsend, grecv, local = refs[20:29]
@@ -1498,7 +1523,9 @@
         count = out_step if t < n_tp - 1 else out_width
         value = mm(mixed[t].reshape(n_tp * rows, WIDE), low, TN).astype(bf16)
         stage_out[t * out_step : t * out_step + count, :out_width] = value[:count, :]
-    keep_out = pltpu.make_async_copy(stage_out, dqo_hbm.at[:, 3 * WIDE :], local.at[5])
+    keep_out = pltpu.make_async_copy(
+        stage_out.at[:, :out_step], dqo_hbm.at[:, 3 * WIDE : 3 * WIDE + out_step], local.at[5]
+    )
     keep_out.start()
     reduce.turn(1, 1)
     if n:
@@ -1547,17 +1574,30 @@
         out_ref[at, :] = g_ref[at, :] + dx
 
     row_chunks(rows, final)
+    vectors[...] = jnp.zeros_like(vectors)
+    vectors[0:2, :] = sums_ref[0:2, :]
+    vectors[2:3, columns] = cols_ref[:, :out_width]
+    vectors[3:4, columns] = cols_ref[:, 2 * WIDE : 2 * WIDE + out_width]
+    vectors[4:5, :] = sums_ref[4:5, :]
+    vectors[5:8, :] = ff_ref[5:8, :]
+    vectors[8:9, :] = fcb_ref[...]
+    stage_out[:, out_width : out_width + 16] = vectors[...].T.astype(bf16)
+    keep_rest = pltpu.make_async_copy(
+        stage_out.at[:, out_step:], dqo_hbm.at[:, 3 * WIDE + out_step :], local.at[8]
+    )
+    keep_rest.start()
     gather.finish()
     scatter.finish()
     for micro in range(MICRO):
         reduce.finish(micro)
     keep_out.wait()
+    keep_rest.wait()
     keep_qkv.wait()
     for i, item in enumerate(sums):
         item.finish(i < n - 1)
 
 
-def attn_bwd(grad, x, vecs, lse, all_rows, own, kv, mixed_all, w_a, w_out, n_tp, payload, collective_id):
+def attn_bwd(grad, x, vecs, lse, ff_sums, fc_bias_sums, all_rows, own, kv, mixed_all, w_a, w_out, n_tp, payload, collective_id):
     rows = x.shape[0]
     operands, results, more = reduce_parts(payload)
     pieces = (MICRO, 4, 2, 2, PROMPT_DEV, WIDE)
@@ -1565,14 +1605,15 @@
         functools.partial(attn_bwd_kernel, len(payload)),
         out_shape=(
             jax.ShapeDtypeStruct((rows, D), f32),
-            jax.ShapeDtypeStruct((8, D), f32),
-            jax.ShapeDtypeStruct((1, 3 * WIDE), f32),
             jax.ShapeDtypeStruct((D, 4 * WIDE), bf16),
         )
         + results,
-        in_specs=[IN_VMEM] * 4 + [ANY] * (6 + len(payload)),
-        out_specs=(IN_VMEM, IN_VMEM, IN_VMEM) + (ANY,) * (1 + 2 * len(payload)),
+        in_specs=[IN_VMEM] * 6 + [ANY] * (6 + len(payload)),
+        out_specs=(IN_VMEM,) + (ANY,) * (1 + 2 * len(payload)),
         scratch_shapes=[
+            pltpu.VMEM((8, D), f32),
+            pltpu.VMEM((1, 3 * WIDE), f32),
+            pltpu.VMEM((16, D), f32),
             pltpu.VMEM((D, 3 * WIDE), bf16),
             pltpu.VMEM((WIDE, D), bf16),
             pltpu.VMEM((n_tp, rows, D), bf16),
@@ -1598,12 +1639,12 @@
         + [
             pltpu.SemaphoreType.DMA((8 * MICRO,)),
             pltpu.SemaphoreType.DMA((8 * MICRO,)),
-            pltpu.SemaphoreType.DMA((8,)),
+            pltpu.SemaphoreType.DMA((9,)),
         ]
         + more,
         compiler_params=params(collective_id),
         cost_estimate=pl.CostEstimate(flops=2 * 10**11, bytes_accessed=50 * 2**20, transcendentals=0),
-    )(grad, x, vecs, lse, all_rows, own, kv, mixed_all, w_a, w_out, *operands)
+    )(grad, x, vecs, lse, ff_sums, fc_bias_sums, all_rows, own, kv, mixed_all, w_a, w_out, *operands)
 
 
 def forward_layer(x, layer, fetch, vecs, fc_bias, cols, n_tp):
@@ -1672,24 +1713,7 @@
     return own.astype(f32) + near.astype(f32) + jnp.sum(from_z.astype(f32), 0)
 
 
-def with_vectors(grad_qo, ff_sums, attn_sums, col_sums, fc_bias_sums, cols, width):
-    def placed(part):
-        return lax.dynamic_update_slice_in_dim(jnp.zeros((1, D), f32), part, cols, 1)
-
-    vector_grads = jnp.concatenate(
-        [
-            attn_sums[:2],
-            placed(col_sums[:, :width]),
-            placed(col_sums[:, 2 * WIDE : 2 * WIDE + width]),
-            attn_sums[4:5],
-            ff_sums[5:],
-            fc_bias_sums,
-        ]
-    )
-    return lax.dynamic_update_slice(grad_qo, vector_grads.astype(bf16).T, (0, 3 * WIDE + width))
-
-
-def backward(grad, weights, vecs, saves, cols, n_tp):
+def backward(grad, weights, vecs, saves, n_tp):
     width = D - HEADS // n_tp * HEAD * (n_tp - 1)
     staged = lax.axis_size("fsdp") == GROUP
     done, waiting = {}, {}
@@ -1722,13 +1746,14 @@
         )
         produced((layer, "proj"), grad_proj)
         produced((layer, "fc"), grad_fc)
-        grad, attn_sums, col_sums, grad_qo = during(
+        grad, grad_qo = during(
             [(layer, "proj"), (layer, "fc")],
             lambda payload: attn_bwd(
-                grad, x, vecs[layer], lse, all_rows, own, kv, mixed_all, w_a, w_out, n_tp, payload, 20 + layer
+                grad, x, vecs[layer], lse, ff_sums, fc_bias_sums, all_rows, own, kv, mixed_all,
+                w_a, w_out, n_tp, payload, 20 + layer,
             ),
         )
-        produced((layer, "qo"), with_vectors(grad_qo, ff_sums, attn_sums, col_sums, fc_bias_sums, cols, width))
+        produced((layer, "qo"), grad_qo)
     if staged:
         got = last_sum(waiting[0, "qo"], owned(*done[1, "qo"]).astype(bf16), n_tp, 30)
         return grad, assemble([(got[k],) + done[k, "proj"] + done[k, "fc"] for k in range(LAYERS)])
@@ -1795,7 +1820,7 @@
     out_tokens = state.astype(bf16).reshape(tokens.shape)
     grad = out_grad.astype(f32).reshape(MICRO * row_count, D)
     grad, (qkv_g, out_g, fc_g, proj_g, *vec_g) = backward(
-        grad, fetch.weights, [vectors[:8, layer] for layer in range(LAYERS)], saves, cols, n_tp
+        grad, fetch.weights, [vectors[:8, layer] for layer in range(LAYERS)], saves, n_tp
     )
     return (
         out_tokens,

time: 1350 us -> 1300 us (0.963)
  Pallas kernels: 1280 us -> 1250 us
  local copies, waits for them, and re-layouts: 38.1 us -> 22.1 us
    pallas_call x2, Pallas kernels: 390 us -> 359 us  [attn_fwd(): pl.pallas_call(functools.partial(attn_fwd_kernel, len(operands)), out_sha...]
    pallas_call x2, Pallas kernels: 404 us -> 390 us  [attn_bwd(): pl.pallas_call(functools.partial(attn_bwd_kernel, len(payload)), out_shap...]
where the time goes in v10:
time: 1300 us; the launch traced here: 1290 us
  Pallas kernels  1250 us (96%)
  local copies, waits for them, and re-layouts  22.1 us (2%)
  other arithmetic  14.5 us (1%)
    pallas_call x2, Pallas kernels, attn_bwd(): pl.pallas_call(functools.partial(attn_bwd_kernel, len(payload)), out_shap...  390 us
    pallas_call x2, Pallas kernels, attn_fwd(): pl.pallas_call(functools.partial(attn_fwd_kernel, len(operands)), out_sha...  359 us
    pallas_call x2, Pallas kernels, ff_bwd(): pl.pallas_call(functools.partial(ff_bwd_kernel, len(payload)), out_shape=...  159 us
    pallas_call x2, Pallas kernels, ff_fwd(): pl.pallas_call(functools.partial(ff_fwd_kernel, len(operands)), out_shape...  145 us
    pallas_call x1, Pallas kernels, last_sum(): pl.pallas_call(last_sum_kernel, out_shape=results + (whole, whole), in_sp...  103 us
    pallas_call x1, Pallas kernels, spread_only(): pl.pallas_call(functools.partial(spread_kernel, chunks), out_shape=result...  79.6 us

profile of v10, /device:TPU:9, one launch (start us, length us, event | category | flops | bytes accessed | tf_op | source)
XLA Modules:
  0.0 1287.5 jit_solution(13820202367270955146)
XLA Ops:
  0.6 2.2 bitcast_convert_fusion.1.refs_0_.refs_1_
  2.9 3.6 fusion.21
  6.5 2.7 dynamic-slice_bitcast_fusion.3
  9.3 0.0 copy-start.12
  9.3 0.0 copy-start.13
  9.3 0.0 copy-start.16
  9.3 0.0 copy-start.17
  9.4 0.9 fusion.22
  10.3 1.8 dynamic-slice_bitcast_fusion
  12.4 0.1 copy.35
  12.6 0.9 copy-done.3
  13.5 79.6 %shard_map.262 = bf16[8,200,2176]{2,1,0:T(8,128)(2,1)} custom-call(bf16[200,2176]{1,0:T(8,128)(2,1)} %copy-done.3), custom_call_target="tpu_custom_call" | custom-call | tf_op jit(solution)/shard_map/pallas_call | solution.py:582
  93.0 1.2 convert_bitcast_fusion
  94.2 1.0 copy.36
  95.2 1.1 reshape.137
  96.3 0.1 fusion.23
  96.4 0.6 copy.46
  97.0 0.6 slice_bitcast_fusion.4
  97.6 0.1 fusion.20
  97.7 0.1 fusion.19
  97.8 0.1 pad.76.clone
  97.8 0.1 fusion.18
  97.9 0.1 fusion.17
  98.0 0.1 pad_maximum_fusion.1
  98.1 0.6 pad.54.refs_2_
  98.6 0.1 slice_bitcast_fusion
  98.8 0.1 slice_bitcast_fusion.1
  98.9 1.7 fusion.12
  100.6 178.2 %shard_map.263 = (f32[192,1600]{1,0:T(8,128)}, f32[2,4,8,384]{3,2,1,0:T(8,128)}, bf16[4,192,1600]{2,1,0:T(8,128)(2,1)}, bf16[3,2,384,512]{3,2,1,0:T(8,128)(2,1)}...) custom-call(f32[192,1600]{1,0:T(8,128)} %bitcast_convert_fusion.1.re, ...), custom_call_target="tpu_custom_call" | custom-call | flops 99999997952 | bytes 31457280 | tf_op jit(solution)/shard_map/pallas_call | solution.py:1336
  278.8 1.0 fusion.15.refs_4_
  279.8 92.1 %shard_map.264 = (f32[192,1600]{1,0:T(8,128)}, bf16[4,192,1600]{2,1,0:T(8,128)(2,1)}, f32[4,192,1600]{2,1,0:T(8,128)}, bf16[4,192,1600]{2,1,0:T(8,128)(2,1)}, bf16[8,200,2048]{2,1,0:T(8,128)(2,1)}) custom-call(f32[192,1600]{1,0:T(8,128)} %get-tuple-element.79.refs_0_.refs_1_, f32[8,1600]{1,0:T(8,128)} %bitcast.111, f32[1,1600]{1,0:T(1,128)} %get-tuple-element.190.refs_2_, ...), custom_call_target="tpu_custom_call" | custom-call | flops 7864320000 | bytes 41943040 | tf_op jit(solution)/shard_map/pallas_call | solution.py:749
  371.9 0.6 copy.45
  372.5 0.6 pad.61.refs_2_
  373.1 180.5 %shard_map.265 = (f32[192,1600]{1,0:T(8,128)}, f32[2,4,8,384]{3,2,1,0:T(8,128)}, bf16[4,192,1600]{2,1,0:T(8,128)(2,1)}, bf16[3,2,384,512]{3,2,1,0:T(8,128)(2,1)}...) custom-call(f32[192,1600]{1,0:T(8,128)} %get-tuple-element.81.refs_0, ...), custom_call_target="tpu_custom_call" | custom-call | flops 99999997952 | bytes 31457280 | tf_op jit(solution)/shard_map/pallas_call | solution.py:1336
  553.6 52.9 %shard_map.266 = (f32[192,1600]{1,0:T(8,128)}, bf16[4,192,1600]{2,1,0:T(8,128)(2,1)}, f32[4,192,1600]{2,1,0:T(8,128)}, bf16[4,192,1600]{2,1,0:T(8,128)(2,1)}) custom-call(f32[192,1600]{1,0:T(8,128)} %get-tuple-element.83.refs_0_.refs_1_, f32[8,1600]{1,0:T(8,128)} %bitcast.115, f32[1,1600]{1,0:T(1,128)} %get-tuple-element.187.refs_2_, ...), custom_call_target="tpu_custom_call" | custom-call | flops 7864320000 | bytes 41943040 | tf_op jit(solution)/shard_map/pallas_call | solution.py:749
  606.5 2.3 convert_element_type.47
  608.8 1.2 bitcast_convert_fusion.refs_0_
  609.9 54.5 %shard_map.267 = (f32[192,1600]{1,0:T(8,128)}, f32[8,1600]{1,0:T(8,128)}, f32[1,1600]{1,0:T(1,128)}, bf16[1600,1600]{1,0:T(8,128)(2,1)}, bf16[1600,1600]{1,0:T(8,128)(2,1)}) custom-call(f32[192,1600]{1,0:T(8,128)} %bitcast_convert_fusion.refs_0_, f32[192,1600]{1,0:T(8,128)} %get-tuple-element.83.refs_0_.refs_1_, f32[8,1600]{1,0:T(8,128)} %bitcast.116, ...), custom_call_target="tpu_custom_call" | custom-call | flops 15728640000 | bytes 52428800 | tf_op jit(solution)/shard_map/pallas_call | solution.py:921
  664.5 201.6 %shard_map.268 = (f32[192,1600]{1,0:T(8,128)}, bf16[1600,2048]{1,0:T(8,128)(2,1)}, bf16[4,200,1600]{2,1,0:T(8,128)(2,1)}, bf16[3,200,1600]{2,1,0:T(8,128)(2,1)},...) custom-call(f32[192,1600]{1,0:T(8,128)} %get-tuple-element.89.refs_0_, ...), custom_call_target="tpu_custom_call" | custom-call | flops 199999995904 | bytes 52428800 | tf_op jit(solution)/shard_map/pallas_call | solution.py:1604
  866.1 104.8 %shard_map.269 = (f32[192,1600]{1,0:T(8,128)}, f32[8,1600]{1,0:T(8,128)}, f32[1,1600]{1,0:T(1,128)}, bf16[1600,1600]{1,0:T(8,128)(2,1)}, bf16[1600,1600]{1,0:T(8...) custom-call(f32[192,1600]{1,0:T(8,128)} %get-tuple-element.100.refs_0_, ...), custom_call_target="tpu_custom_call" | custom-call | flops 15728640000 | bytes 52428800 | tf_op jit(solution)/shard_map/pallas_call | solution.py:921
  970.9 188.2 %shard_map.270 = (f32[192,1600]{1,0:T(8,128)}, bf16[1600,2048]{1,0:T(8,128)(2,1)}, bf16[4,200,1600]{2,1,0:T(8,128)(2,1)}, bf16[3,200,1600]{2,1,0:T(8,128)(2,1)},...) custom-call(f32[192,1600]{1,0:T(8,128)} %get-tuple-element.105.refs_0_, ...), custom_call_target="tpu_custom_call" | custom-call | flops 199999995904 | bytes 52428800 | tf_op jit(solution)/shard_map/pallas_call | solution.py:1604
  1159.0 2.3 convert_reduce_fusion
  1161.4 2.6 fusion.5.earlier
  1164.1 102.9 %shard_map.271 = (bf16[4,200,2048]{2,1,0:T(8,128)(2,1)}, bf16[3,200,2048]{2,1,0:T(8,128)(2,1)}, bf16[4,200,2048]{2,1,0:T(8,128)(2,1)}, bf16[4,200,2048]{2,1,0:T(8,128)(2,1)}) custom-call(bf16[4,2,200,2048]{3,2,1,0:T(8,128)(2,1)} %bitcast.96, bf16[200,2048]{1,0:T(8,128)(2,1)} %fusion.5.earlier), custom_call_target="tpu_custom_call" | custom-call | tf_op jit(solution)/shard_map/pallas_call | solution.py:389
  1267.0 14.4 %shard_map.272 = (f32[2,200,4800]{2,1,0:T(8,128)}, f32[2,200,1600]{2,1,0:T(8,128)}, f32[2,200,1600]{2,1,0:T(8,128)}, f32[2,1600,200]{2,1,0:T(8,128)}, f32[2,200]...) custom-call(bf16[4,200,2048]{2,1,0:T(8,128)(2,1)} %get-tuple-element, ...), custom_call_target="tpu_custom_call" | custom-call | tf_op jit(solution)/shard_map/pallas_call | solution.py:458
  1281.4 1.3 copy.39
  1282.7 3.6 copy.40
  1286.2 1.0 copy.60
  (48 shorter events, 0.3 us)
Async XLA Ops:
  6.5 2.8 copy-start
  9.3 2.9 copy-start.10
  9.3 2.9 copy-start.11
  9.3 2.9 copy-start.12
  9.3 2.9 copy-start.13
  9.3 3.0 copy-start.14
  9.3 3.0 copy-start.15
  9.3 3.0 copy-start.16
  9.3 3.0 copy-start.17
  9.4 3.0 copy-start.18
  12.6 0.9 copy-start.3
  93.0 5.6 copy-start.1
  95.2 3.6 copy-start.2
  100.6 178.2 %copy-start.5 = (bf16[200,448]{1,0:T(8,128)(2,1)S(1)}, bf16[200,448]{1,0:T(8,128)(2,1)}, u32[]{:S(2)}) copy-start(bf16[200,448]{1,0:T(8,128)(2,1)} %get-tuple-element.175) | copy-start | bytes 537604
  100.6 178.2 %copy-start.6 = (bf16[200,448]{1,0:T(8,128)(2,1)S(1)}, bf16[200,448]{1,0:T(8,128)(2,1)}, u32[]{:S(2)}) copy-start(bf16[200,448]{1,0:T(8,128)(2,1)} %get-tuple-element.176) | copy-start | bytes 537604
  100.6 178.2 %copy-start.7 = (bf16[200,448]{1,0:T(8,128)(2,1)S(1)}, bf16[200,448]{1,0:T(8,128)(2,1)}, u32[]{:S(2)}) copy-start(bf16[200,448]{1,0:T(8,128)(2,1)} %get-tuple-element.177) | copy-start | bytes 537604
  100.6 178.2 %copy-start.8 = (bf16[200,448]{1,0:T(8,128)(2,1)S(1)}, bf16[200,448]{1,0:T(8,128)(2,1)}, u32[]{:S(2)}) copy-start(bf16[200,448]{1,0:T(8,128)(2,1)} %get-tuple-element.200) | copy-start | bytes 537604
  606.5 2.3 copy-start.9
  1282.7 3.6 copy-start.4

commit v11 on v10

--- a/solution.py
+++ b/solution.py
@@ -621,17 +621,37 @@
     return centred * scale, scale
 
 
+FIRST_CHUNKS = (3, 3, 3, 3, 2, 2)
+FF_CHUNKS = (5, 5, 4, 2)
+ATTN_CHUNKS = (5, 6, 6, 5, 3)
+
+
 def lanes_up(width):
     return -(-width // 128) * 128
 
 
-def proj_part(w_b, width):
-    return w_b.at[:, lanes_up(width) :]
-
-
-FIRST_CHUNKS = (3, 3, 3, 3, 3, 2)
-FF_CHUNKS = (5, 5, 4, 2)
-ATTN_CHUNKS = (5, 6, 6, 5, 4)
+def lanes_down(width):
+    return width // 128 * 128
+
+
+class FeedForward:
+    def __init__(self, w_b, wfc, wproj, width, sems):
+        main, end = lanes_down(width), 2 * (width - lanes_down(width))
+        self.main, self.width, self.wfc, self.wproj = main, width, wfc, wproj
+        self.fc = [
+            pltpu.make_async_copy(w_b.at[:, :main], wfc.at[:, :main], sems[0]),
+            pltpu.make_async_copy(w_b.at[:, 2 * main :], wfc.at[:, main : main + end], sems[1]),
+        ]
+        self.proj = pltpu.make_async_copy(w_b.at[:, main : 2 * main], wproj.at[:, :main], sems[2])
+
+    def start(self):
+        for copy in self.fc + [self.proj]:
+            copy.start()
+
+    def wait(self):
+        for copy in self.fc + [self.proj]:
+            copy.wait()
+        self.wproj[:, self.main : self.width] = self.wfc[:, self.width : 2 * self.width - self.main]
 
 
 def ff_fwd_kernel(n, *refs):
@@ -647,10 +667,8 @@
     gather = Gather(p, buf, sems)
     scatter = Scatter(p, part, from_core, over_out, from_over, sems)
     width = fcb_ref.shape[1]
-    load_fc = pltpu.make_async_copy(wb_hbm.at[:, : wfc.shape[1]], wfc, local.at[0])
-    load_proj = pltpu.make_async_copy(proj_part(wb_hbm, width), wproj, local.at[1])
-    load_fc.start()
-    load_proj.start()
+    weights = FeedForward(wb_hbm, wfc, wproj, width, [local.at[0], local.at[1], local.at[5]])
+    weights.start()
 
     def norm(at):
         hat, _ = norm_stats(x_ref[at, :])
@@ -665,7 +683,7 @@
     if n:
         spread.start(0, 1)
     gather.wait_chip()
-    load_fc.wait()
+    weights.wait()
 
     def up(x):
         def tile(at):
@@ -695,7 +713,6 @@
     keep_hid = pltpu.make_async_copy(hid, hid_hbm, local.at[4])
     keep_pre.start()
     keep_hid.start()
-    load_proj.wait()
     down(1 - p.x)
     scatter.far_to_core().start()
     scatter.send_over()
@@ -765,7 +782,7 @@
             pltpu.VMEM(block + (width,), bf16),
         ]
         + scatter_scratch(n_tp, rows)
-        + [pltpu.SemaphoreType.DMA((5,))]
+        + [pltpu.SemaphoreType.DMA((6,))]
         + sems,
         compiler_params=params(collective_id),
         cost_estimate=pl.CostEstimate(
@@ -805,11 +822,11 @@
     sems = (send, recv)
     gather = Gather(p, buf, sems)
     scatter = Scatter(p, part, from_core, over_out, from_over, sems)
-    load_proj = pltpu.make_async_copy(proj_part(wb_hbm, width), wproj, local.at[0])
+    weights = FeedForward(wb_hbm, wfc, wproj, width, [local.at[0], local.at[2], local.at[7]])
     load_pre = pltpu.make_async_copy(pre_hbm, pre, local.at[1])
-    load_fc = pltpu.make_async_copy(wb_hbm.at[:, : wfc.shape[1]], wfc, local.at[2])
     load_other = pltpu.make_async_copy(hid_hbm, other, local.at[3])
-    for copy in (load_proj, load_pre, load_fc, load_other):
+    weights.start()
+    for copy in (load_pre, load_other):
         copy.start()
     sums_ref[...] = jnp.zeros_like(sums_ref)
     fcb_ref[...] = jnp.zeros_like(fcb_ref)
@@ -833,7 +850,7 @@
 
     advance()
     gather.wait_chip()
-    load_proj.wait()
+    weights.wait()
     load_pre.wait()
 
     def through(x):
@@ -858,7 +875,6 @@
     gather.wait_diag()
     through(1 - p.x)
     advance()
-    load_fc.wait()
     down(1 - p.x)
     scatter.far_to_core().start()
     scatter.send_over()
@@ -940,7 +956,7 @@
             pltpu.VMEM((D, width), bf16),
         ]
         + scatter_scratch(n_tp, rows)
-        + [pltpu.SemaphoreType.DMA((7,))]
+        + [pltpu.SemaphoreType.DMA((8,))]
         + more,
         compiler_params=params(collective_id),
         cost_estimate=pl.CostEstimate(
@@ -1423,14 +1439,14 @@
         first_sum.start(2)
     gather.relay()
     gather.wait_diag()
+    if n:
+        first_sum.pump(1, then=lambda: first_sum.start(3))
     mixed_back(1 - p.x)
     load_own.wait()
     load_kv.wait()
     limit = key_limit(g.member)
     sub = lax.broadcasted_iota(jnp.int32, (CHUNK, TOK_DEV), 0)
 
-    if n:
-        first_sum.pump(1, then=lambda: first_sum.start(3))
 
     for micro in range(MICRO):
 
@@ -1802,15 +1818,17 @@
     shards = {}
     for layer in range(LAYERS):
         sides = [widen(lax.dynamic_slice_in_dim(qkv_weight[layer], cols + i * D, width, 1)) for i in range(3)]
-        sides.append(widen(lax.dynamic_slice_in_dim(out_weight[layer], cols, width, 1)))
+        out_cols = lax.dynamic_slice_in_dim(out_weight[layer], cols, width, 1)
         if layer == 0:
-            sides.append(jnp.pad(vectors.T, ((0, 0), (0, 128 - 9 * LAYERS))))
+            out_cols = jnp.concatenate([out_cols, vectors.T], axis=1)
+        sides.append(widen(out_cols))
         shards[layer, "a"] = jnp.concatenate(sides, axis=1)
         fc, proj = fc_weight[layer], proj_weight[layer].T
-        more = ((0, 0), (0, lanes_up(fc.shape[1]) - fc.shape[1]))
-        shards[layer, "b"] = jnp.concatenate([jnp.pad(fc, more), jnp.pad(proj, more)], axis=1)
+        main = lanes_down(fc.shape[1])
+        shards[layer, "b"] = jnp.concatenate([fc[:, :main], proj[:, :main], fc[:, main:], proj[:, main:]], axis=1)
     fetch = Fetch(shards)
-    vectors = fetch.weights[0, "a"][:, 4 * WIDE : 4 * WIDE + 9 * LAYERS].T.astype(f32).reshape(9, LAYERS, D)
+    beside = 3 * WIDE + width
+    vectors = fetch.weights[0, "a"][:, beside : beside + 9 * LAYERS].T.astype(f32).reshape(9, LAYERS, D)
 
     state = tokens.astype(f32).reshape(MICRO * row_count, D)
     saves = []

time: 1300 us -> 1280 us (0.985)
    pallas_call x2, Pallas kernels: 159 us -> 146 us  [ff_bwd(): pl.pallas_call(functools.partial(ff_bwd_kernel, len(payload)), out_shape=...]
where the time goes in v11:
time: 1280 us; the launch traced here: 1270 us
  Pallas kernels  1240 us (97%)
  local copies, waits for them, and re-layouts  23 us (2%)
  other arithmetic  14 us (1%)
    pallas_call x2, Pallas kernels, attn_bwd(): pl.pallas_call(functools.partial(attn_bwd_kernel, len(payload)), out_shap...  392 us
    pallas_call x2, Pallas kernels, attn_fwd(): pl.pallas_call(functools.partial(attn_fwd_kernel, len(operands)), out_sha...  353 us
    pallas_call x2, Pallas kernels, ff_bwd(): pl.pallas_call(functools.partial(ff_bwd_kernel, len(payload)), out_shape=...  146 us
    pallas_call x2, Pallas kernels, ff_fwd(): pl.pallas_call(functools.partial(ff_fwd_kernel, len(operands)), out_shape...  141 us
    pallas_call x1, Pallas kernels, last_sum(): pl.pallas_call(last_sum_kernel, out_shape=results + (whole, whole), in_sp...  114 us
    pallas_call x1, Pallas kernels, spread_only(): pl.pallas_call(functools.partial(spread_kernel, chunks), out_shape=result...  75.2 us

profile of v11, /device:TPU:9, one launch (start us, length us, event | category | flops | bytes accessed | tf_op | source)
XLA Modules:
  0.0 1274.2 jit_solution(14589067267895935807)
XLA Ops:
  0.6 2.2 bitcast_convert_fusion.1.refs_0_.refs_1_
  2.9 3.6 fusion.24
  6.6 2.8 dynamic-slice_bitcast_fusion.3
  9.6 0.1 copy.35
  9.8 0.1 fusion.25
  9.9 0.9 dynamic-slice_bitcast_fusion
  10.8 0.1 fusion.19
  10.9 0.0 copy-done.8
  10.9 1.0 fusion.13.source
  11.9 75.2 %shard_map.262 = bf16[8,200,2048]{2,1,0:T(8,128)(2,1)} custom-call(bf16[200,2048]{1,0:T(8,128)(2,1)} %fusion.13.source), custom_call_target="tpu_custom_call" | custom-call | tf_op jit(solution)/shard_map/pallas_call | solution.py:582
  87.1 1.3 convert_bitcast_fusion
  88.4 0.3 copy.36
  88.6 0.1 reshape.137
  88.7 0.1 fusion.26
  88.8 0.6 copy.46
  89.5 0.6 slice_bitcast_fusion.4
  90.1 0.1 fusion.23
  90.2 0.1 fusion.22
  90.2 0.1 pad.51.clone
  90.3 0.1 fusion.21
  90.4 0.1 fusion.20
  90.5 0.1 pad_maximum_fusion.1
  90.5 0.6 pad.37.refs_2_
  91.1 0.1 slice_bitcast_fusion.1
  91.3 1.2 copy-done.2
  92.5 0.1 slice_bitcast_fusion
  92.6 1.9 concatenate.17.refs_4_
  94.6 174.5 %shard_map.263 = (f32[192,1600]{1,0:T(8,128)}, f32[2,4,8,384]{3,2,1,0:T(8,128)}, bf16[4,192,1600]{2,1,0:T(8,128)(2,1)}, bf16[3,2,384,512]{3,2,1,0:T(8,128)(2,1)}...) custom-call(f32[192,1600]{1,0:T(8,128)} %bitcast_convert_fusion.1.re, ...), custom_call_target="tpu_custom_call" | custom-call | flops 99999997952 | bytes 31457280 | tf_op jit(solution)/shard_map/pallas_call | solution.py:1352
  269.1 1.0 fusion.16.refs_4_
  270.1 89.1 %shard_map.264 = (f32[192,1600]{1,0:T(8,128)}, bf16[4,192,1600]{2,1,0:T(8,128)(2,1)}, f32[4,192,1600]{2,1,0:T(8,128)}, bf16[4,192,1600]{2,1,0:T(8,128)(2,1)}, bf16[8,200,2048]{2,1,0:T(8,128)(2,1)}) custom-call(f32[192,1600]{1,0:T(8,128)} %get-tuple-element.79.refs_0_.refs_1_, f32[8,1600]{1,0:T(8,128)} %bitcast.111, f32[1,1600]{1,0:T(1,128)} %get-tuple-element.190.refs_2_, ...), custom_call_target="tpu_custom_call" | custom-call | flops 7864320000 | bytes 41943040 | tf_op jit(solution)/shard_map/pallas_call | solution.py:766
  359.2 0.6 copy.45
  359.9 0.6 pad.42.refs_2_
  360.6 1.9 concatenate.19.refs_4_
  362.5 178.7 %shard_map.265 = (f32[192,1600]{1,0:T(8,128)}, f32[2,4,8,384]{3,2,1,0:T(8,128)}, bf16[4,192,1600]{2,1,0:T(8,128)(2,1)}, bf16[3,2,384,512]{3,2,1,0:T(8,128)(2,1)}...) custom-call(f32[192,1600]{1,0:T(8,128)} %get-tuple-element.81.refs_0, ...), custom_call_target="tpu_custom_call" | custom-call | flops 99999997952 | bytes 31457280 | tf_op jit(solution)/shard_map/pallas_call | solution.py:1352
  541.2 52.3 %shard_map.266 = (f32[192,1600]{1,0:T(8,128)}, bf16[4,192,1600]{2,1,0:T(8,128)(2,1)}, f32[4,192,1600]{2,1,0:T(8,128)}, bf16[4,192,1600]{2,1,0:T(8,128)(2,1)}) custom-call(f32[192,1600]{1,0:T(8,128)} %get-tuple-element.83.refs_0_.refs_1_, f32[8,1600]{1,0:T(8,128)} %bitcast.115, f32[1,1600]{1,0:T(1,128)} %get-tuple-element.187.refs_2_, ...), custom_call_target="tpu_custom_call" | custom-call | flops 7864320000 | bytes 41943040 | tf_op jit(solution)/shard_map/pallas_call | solution.py:766
  593.5 2.3 convert_element_type.41
  595.8 1.2 bitcast_convert_fusion.refs_0_
  597.0 54.6 %shard_map.267 = (f32[192,1600]{1,0:T(8,128)}, f32[8,1600]{1,0:T(8,128)}, f32[1,1600]{1,0:T(1,128)}, bf16[1600,1600]{1,0:T(8,128)(2,1)}, bf16[1600,1600]{1,0:T(8,128)(2,1)}) custom-call(f32[192,1600]{1,0:T(8,128)} %bitcast_convert_fusion.refs_0_, f32[192,1600]{1,0:T(8,128)} %get-tuple-element.83.refs_0_.refs_1_, f32[8,1600]{1,0:T(8,128)} %bitcast.116, ...), custom_call_target="tpu_custom_call" | custom-call | flops 15728640000 | bytes 52428800 | tf_op jit(solution)/shard_map/pallas_call | solution.py:937
  651.6 200.5 %shard_map.268 = (f32[192,1600]{1,0:T(8,128)}, bf16[1600,2048]{1,0:T(8,128)(2,1)}, bf16[4,200,1600]{2,1,0:T(8,128)(2,1)}, bf16[3,200,1600]{2,1,0:T(8,128)(2,1)},...) custom-call(f32[192,1600]{1,0:T(8,128)} %get-tuple-element.89.refs_0_, ...), custom_call_target="tpu_custom_call" | custom-call | flops 199999995904 | bytes 52428800 | tf_op jit(solution)/shard_map/pallas_call | solution.py:1620
  852.1 91.2 %shard_map.269 = (f32[192,1600]{1,0:T(8,128)}, f32[8,1600]{1,0:T(8,128)}, f32[1,1600]{1,0:T(1,128)}, bf16[1600,1600]{1,0:T(8,128)(2,1)}, bf16[1600,1600]{1,0:T(8...) custom-call(f32[192,1600]{1,0:T(8,128)} %get-tuple-element.100.refs_0_, ...), custom_call_target="tpu_custom_call" | custom-call | flops 15728640000 | bytes 52428800 | tf_op jit(solution)/shard_map/pallas_call | solution.py:937
  943.3 191.1 %shard_map.270 = (f32[192,1600]{1,0:T(8,128)}, bf16[1600,2048]{1,0:T(8,128)(2,1)}, bf16[4,200,1600]{2,1,0:T(8,128)(2,1)}, bf16[3,200,1600]{2,1,0:T(8,128)(2,1)},...) custom-call(f32[192,1600]{1,0:T(8,128)} %get-tuple-element.105.refs_0_, ...), custom_call_target="tpu_custom_call" | custom-call | flops 199999995904 | bytes 52428800 | tf_op jit(solution)/shard_map/pallas_call | solution.py:1620
  1134.5 2.3 convert_reduce_fusion
  1136.9 2.6 fusion.3.earlier
  1139.5 114.2 %shard_map.271 = (bf16[4,200,2048]{2,1,0:T(8,128)(2,1)}, bf16[3,200,2048]{2,1,0:T(8,128)(2,1)}, bf16[4,200,2048]{2,1,0:T(8,128)(2,1)}, bf16[4,200,2048]{2,1,0:T(8,128)(2,1)}) custom-call(bf16[4,2,200,2048]{3,2,1,0:T(8,128)(2,1)} %bitcast.96, bf16[200,2048]{1,0:T(8,128)(2,1)} %fusion.3.earlier), custom_call_target="tpu_custom_call" | custom-call | tf_op jit(solution)/shard_map/pallas_call | solution.py:389
  1253.7 14.4 %shard_map.272 = (f32[2,200,4800]{2,1,0:T(8,128)}, f32[2,200,1600]{2,1,0:T(8,128)}, f32[2,200,1600]{2,1,0:T(8,128)}, f32[2,1600,200]{2,1,0:T(8,128)}, f32[2,200]...) custom-call(bf16[4,200,2048]{2,1,0:T(8,128)(2,1)} %get-tuple-element, ...), custom_call_target="tpu_custom_call" | custom-call | tf_op jit(solution)/shard_map/pallas_call | solution.py:458
  1268.1 1.3 copy.39
  1269.3 3.6 copy.40
  1272.9 1.0 copy.56
  (56 shorter events, 0.4 us)
Async XLA Ops:
  6.5 2.9 copy-start.11
  6.5 2.9 copy-start.12
  6.5 2.9 copy-start.13
  6.5 3.0 copy-start.14
  6.5 3.0 copy-start.15
  6.5 3.0 copy-start.16
  6.5 3.0 copy-start.17
  6.5 3.0 copy-start.18
  6.6 3.0 copy-start.19
  6.6 3.2 copy-start
  9.8 1.1 copy-start.6
  9.8 1.1 copy-start.7
  9.8 1.1 copy-start.8
  87.1 4.1 copy-start.1
  91.1 1.3 copy-start.2
  94.6 174.5 %copy-start.4 = (bf16[200,448]{1,0:T(8,128)(2,1)S(1)}, bf16[200,448]{1,0:T(8,128)(2,1)}, u32[]{:S(2)}) copy-start(bf16[200,448]{1,0:T(8,128)(2,1)} %get-tuple-element.176) | copy-start | bytes 537604
  94.6 174.5 %copy-start.5 = (bf16[200,448]{1,0:T(8,128)(2,1)S(1)}, bf16[200,448]{1,0:T(8,128)(2,1)}, u32[]{:S(2)}) copy-start(bf16[200,448]{1,0:T(8,128)(2,1)} %get-tuple-element.177) | copy-start | bytes 537604
  94.6 174.6 %copy-start.9 = (bf16[200,448]{1,0:T(8,128)(2,1)S(1)}, bf16[200,448]{1,0:T(8,128)(2,1)}, u32[]{:S(2)}) copy-start(bf16[200,448]{1,0:T(8,128)(2,1)} %get-tuple-element.200) | copy-start | bytes 537604
  593.5 2.3 copy-start.10
  1269.3 3.6 copy-start.3

commit v12 on v11

--- a/solution.py
+++ b/solution.py
@@ -634,6 +634,31 @@
     return width // 128 * 128
 
 
+class Projections:
+    def __init__(self, w_a, wqkv, step, width, sems):
+        self.step, self.width, self.wqkv = step, width, wqkv
+        tail = 4 * step
+        self.loads = [
+            pltpu.make_async_copy(w_a.at[:, i * step : (i + 1) * step], wqkv.at[:, i * WIDE : i * WIDE + step], sems[i])
+            for i in range(3)
+        ]
+        for i, at in ((0, 0), (1, 2)):
+            source = w_a.at[:, tail + 128 * i : tail + 128 * (i + 1)]
+            self.loads.append(pltpu.make_async_copy(source, wqkv.at[:, at * WIDE + step : (at + 1) * WIDE], sems[3 + i]))
+
+    def start(self):
+        for load in self.loads:
+            load.start()
+
+    def wait(self):
+        for load in self.loads:
+            load.wait()
+        step, width, wqkv = self.step, self.width, self.wqkv
+        wqkv[:, WIDE + step : WIDE + width] = wqkv[:, width:WIDE]
+        for i in range(3):
+            wqkv[:, i * WIDE + width : (i + 1) * WIDE] = jnp.zeros((D, WIDE - width), bf16)
+
+
 class FeedForward:
     def __init__(self, w_b, wfc, wproj, width, sems):
         main, end = lanes_down(width), 2 * (width - lanes_down(width))
@@ -1169,17 +1194,24 @@
     gather = Gather(p, buf, sems)
     scatter = Scatter(p, part, from_core, over_out, from_over, sems)
     share = Share(g, kv, (gsend, grecv))
-    load_qkv = pltpu.make_async_copy(wqkv_hbm.at[:, : 3 * WIDE], wqkv, local.at[0])
-    load_qkv.start()
-
-    def rows_for(t):
-        return wqkv_hbm.at[pl.ds(pl.multiple_of(t * step, 128), width), 3 * WIDE : 4 * WIDE]
-
-    keep_part = pltpu.make_async_copy(rows_for(p.t), wparts.at[p.t], local.at[1])
-    keep_part.start()
-    give_parts = [
-        p.copy(rows_for(t), wparts.at[p.t], (wsend, wrecv), i, t) for i, t in enumerate((p.core, p.over, p.diag))
+    projections = Projections(wqkv_hbm, wqkv, step, width, [local.at[k] for k in (0, 7, 8, 9, 10)])
+    projections.start()
+
+    spans = ((3 * step, 4 * step, 0, step), (4 * step + 128, 4 * step + 256, step, WIDE))
+
+    def rows_for(t, k):
+        return wqkv_hbm.at[pl.ds(pl.multiple_of(t * step, 128), width), spans[k][0] : spans[k][1]]
+
+    def part_of(t, k):
+        return wparts.at[t, :, spans[k][2] : spans[k][3]]
+
+    keep_parts = [
+        pltpu.make_async_copy(rows_for(p.t, k), part_of(p.t, k), local.at[1 + 10 * k]) for k in range(2)
     ]
+    for copy in keep_parts:
+        copy.start()
+    near = [(2 * i + k, t, k) for i, t in enumerate((p.core, p.over, p.diag)) for k in range(2)]
+    give_parts = [p.copy(rows_for(t, k), part_of(p.t, k), (wsend, wrecv), i, t) for i, t, k in near]
 
     def norm(at):
         hat, _ = norm_stats(x_ref[at, :])
@@ -1193,7 +1225,7 @@
     if n:
         spread.start(0, 1)
     gather.wait_chip()
-    load_qkv.wait()
+    projections.wait()
 
     def project(x):
         for i in range(3):
@@ -1283,12 +1315,13 @@
 
     keep_kv = pltpu.make_async_copy(kv, kv_hbm, local.at[4])
     keep_kv.start()
-    keep_part.wait()
-    for i, t in enumerate((p.core, p.over, p.diag)):
-        p.copy(rows_for(t), wparts.at[t], (wsend, wrecv), i, t).wait_recv()
+    for copy in keep_parts:
+        copy.wait()
+    for i, t, k in near:
+        p.copy(rows_for(t, k), part_of(t, k), (wsend, wrecv), i, t).wait_recv()
     for t in range(n_tp):
-        count = min(WIDE, D - t * step)
-        wout[:width, t * step : t * step + count] = wparts[t, :, :count]
+        wout[:width, t * step : (t + 1) * step] = wparts[t, :, :step]
+    wout[:width, n_tp * step :] = wparts[n_tp - 1, :, width : 2 * width - step]
     wout[width:, :] = jnp.zeros((WIDE - width, D), bf16)
 
     @pl.when(p.t < n_tp - 1)
@@ -1371,9 +1404,9 @@
         + [
             pltpu.SemaphoreType.DMA((14 * MICRO,)),
             pltpu.SemaphoreType.DMA((14 * MICRO,)),
-            pltpu.SemaphoreType.DMA((3,)),
-            pltpu.SemaphoreType.DMA((3,)),
-            pltpu.SemaphoreType.DMA((7,)),
+            pltpu.SemaphoreType.DMA((6,)),
+            pltpu.SemaphoreType.DMA((6,)),
+            pltpu.SemaphoreType.DMA((12,)),
             pltpu.SemaphoreType.DMA((3,)),
             pltpu.SemaphoreType.DMA((3,)),
         ]
@@ -1405,10 +1438,11 @@
     load_out = pltpu.make_async_copy(wout_hbm, wout, local.at[0])
     load_own = pltpu.make_async_copy(own_hbm, own, local.at[1])
     load_kv = pltpu.make_async_copy(kv_hbm, kv, local.at[2])
-    load_qkv = pltpu.make_async_copy(wqkv_hbm.at[:, : 3 * WIDE], wqkv, local.at[3])
+    projections = Projections(wqkv_hbm, wqkv, out_step, out_width, [local.at[k] for k in (3, 9, 10, 11, 12)])
+    projections.start()
     load_mix = pltpu.make_async_copy(mix_hbm, mixed, local.at[4])
     load_all = pltpu.make_async_copy(all_hbm, other, local.at[6])
-    for copy in (load_out, load_own, load_kv, load_qkv, load_mix, load_all):
+    for copy in (load_out, load_own, load_kv, load_mix, load_all):
         copy.start()
     sums_ref[...] = jnp.zeros_like(sums_ref)
 
@@ -1552,7 +1586,7 @@
             to_slots(dqkv, micro, 0, reduce.total(micro, i), slice((1 + i) * WIDE, (2 + i) * WIDE))
     if n:
         second_sum.pump(2, first_sum, lambda: second_sum.start(3))
-    load_qkv.wait()
+    projections.wait()
 
     def down(x):
         def tile(at):
@@ -1655,7 +1689,7 @@
         + [
             pltpu.SemaphoreType.DMA((8 * MICRO,)),
             pltpu.SemaphoreType.DMA((8 * MICRO,)),
-            pltpu.SemaphoreType.DMA((9,)),
+            pltpu.SemaphoreType.DMA((13,)),
         ]
         + more,
         compiler_params=params(collective_id),
@@ -1817,17 +1851,17 @@
 
     shards = {}
     for layer in range(LAYERS):
-        sides = [widen(lax.dynamic_slice_in_dim(qkv_weight[layer], cols + i * D, width, 1)) for i in range(3)]
-        out_cols = lax.dynamic_slice_in_dim(out_weight[layer], cols, width, 1)
+        sides = [lax.dynamic_slice_in_dim(qkv_weight[layer], cols + i * D, width, 1) for i in range(3)]
+        sides.append(lax.dynamic_slice_in_dim(out_weight[layer], cols, width, 1))
+        sides = [side[:, :step] for side in sides] + [side[:, step:] for side in sides]
         if layer == 0:
-            out_cols = jnp.concatenate([out_cols, vectors.T], axis=1)
-        sides.append(widen(out_cols))
+            sides.append(jnp.pad(vectors.T, ((0, 0), (0, 128 - 9 * LAYERS))))
         shards[layer, "a"] = jnp.concatenate(sides, axis=1)
         fc, proj = fc_weight[layer], proj_weight[layer].T
         main = lanes_down(fc.shape[1])
         shards[layer, "b"] = jnp.concatenate([fc[:, :main], proj[:, :main], fc[:, main:], proj[:, main:]], axis=1)
     fetch = Fetch(shards)
-    beside = 3 * WIDE + width
+    beside = 4 * width
     vectors = fetch.weights[0, "a"][:, beside : beside + 9 * LAYERS].T.astype(f32).reshape(9, LAYERS, D)
 
     state = tokens.astype(f32).reshape(MICRO * row_count, D)

time: 1280 us -> 1270 us (level)
  Pallas kernels: 1240 us -> 1220 us
where the time goes in v12:
time: 1270 us; the launch traced here: 1260 us
  Pallas kernels  1220 us (96%)
  local copies, waits for them, and re-layouts  28.4 us (2%)
    pallas_call x2, Pallas kernels, attn_bwd(): pl.pallas_call(functools.partial(attn_bwd_kernel, len(payload)), out_shap...  386 us
    pallas_call x2, Pallas kernels, attn_fwd(): pl.pallas_call(functools.partial(attn_fwd_kernel, len(operands)), out_sha...  361 us
    pallas_call x2, Pallas kernels, ff_bwd(): pl.pallas_call(functools.partial(ff_bwd_kernel, len(payload)), out_shape=...  150 us
    pallas_call x2, Pallas kernels, ff_fwd(): pl.pallas_call(functools.partial(ff_fwd_kernel, len(operands)), out_shape...  132 us
    pallas_call x1, Pallas kernels, last_sum(): pl.pallas_call(last_sum_kernel, out_shape=results + (whole, whole), in_sp...  103 us
    pallas_call x1, Pallas kernels, spread_only(): pl.pallas_call(functools.partial(spread_kernel, chunks), out_shape=result...  70.8 us

profile of v12, /device:TPU:9, one launch (start us, length us, event | category | flops | bytes accessed | tf_op | source)
XLA Modules:
  0.0 1258.3 jit_solution(5504025567871259687)
XLA Ops:
  0.6 2.2 bitcast_convert_fusion.1.refs_0_.refs_1_
  2.9 3.6 fusion.6
  6.5 2.7 dynamic-slice_bitcast_fusion.1
  9.3 0.5 copy-done.7
  9.8 0.1 copy-done.8
  9.9 0.1 fusion.7
  10.0 0.9 dynamic-slice_bitcast_fusion
  10.9 0.8 slice.182
  11.7 0.8 slice.183
  12.8 0.1 copy.35
  13.0 2.3 concatenate.12.source
  15.2 70.8 %shard_map.262 = bf16[8,200,1920]{2,1,0:T(8,128)(2,1)} custom-call(bf16[200,1920]{1,0:T(8,128)(2,1)} %concatenate.12.source), custom_call_target="tpu_custom_call" | custom-call | tf_op jit(solution)/shard_map/pallas_call | solution.py:582
  86.0 1.2 convert_bitcast_fusion
  87.2 0.3 copy.36
  87.5 0.1 reshape.137
  87.6 0.1 fusion.8
  87.7 0.6 copy.46
  88.3 0.6 slice_bitcast_fusion.4
  88.9 0.1 fusion.5
  89.0 0.1 fusion.4
  89.0 0.1 pad.18.clone
  89.1 0.1 fusion.3
  89.2 0.1 fusion.2
  89.3 0.6 pad.12.refs_2_
  90.0 0.1 slice_bitcast_fusion.1
  90.1 0.1 slice_bitcast_fusion
  90.3 1.9 concatenate.13.refs_4_
  92.2 174.8 %shard_map.263 = (f32[192,1600]{1,0:T(8,128)}, f32[2,4,8,384]{3,2,1,0:T(8,128)}, bf16[4,192,1600]{2,1,0:T(8,128)(2,1)}, bf16[3,2,384,512]{3,2,1,0:T(8,128)(2,1)}...) custom-call(f32[192,1600]{1,0:T(8,128)} %bitcast_convert_fusion.1.re, ...), custom_call_target="tpu_custom_call" | custom-call | flops 99999997952 | bytes 31457280 | tf_op jit(solution)/shard_map/pallas_call | solution.py:1385
  267.2 2.2 concatenate.14.refs_4_
  269.4 82.8 %shard_map.264 = (f32[192,1600]{1,0:T(8,128)}, bf16[4,192,1600]{2,1,0:T(8,128)(2,1)}, f32[4,192,1600]{2,1,0:T(8,128)}, bf16[4,192,1600]{2,1,0:T(8,128)(2,1)}, bf16[8,200,1792]{2,1,0:T(8,128)(2,1)}) custom-call(f32[192,1600]{1,0:T(8,128)} %get-tuple-element.79.refs_0_.refs_1_, f32[8,1600]{1,0:T(8,128)} %bitcast.111, f32[1,1600]{1,0:T(1,128)} %get-tuple-element.190.refs_2_, ...), custom_call_target="tpu_custom_call" | custom-call | flops 7864320000 | bytes 41943040 | tf_op jit(solution)/shard_map/pallas_call | solution.py:791
  352.1 0.6 copy.45
  352.8 0.6 pad.13.refs_2_
  353.5 1.9 concatenate.15.refs_4_
  355.4 186.5 %shard_map.265 = (f32[192,1600]{1,0:T(8,128)}, f32[2,4,8,384]{3,2,1,0:T(8,128)}, bf16[4,192,1600]{2,1,0:T(8,128)(2,1)}, bf16[3,2,384,512]{3,2,1,0:T(8,128)(2,1)}...) custom-call(f32[192,1600]{1,0:T(8,128)} %get-tuple-element.81.refs_0, ...), custom_call_target="tpu_custom_call" | custom-call | flops 99999997952 | bytes 31457280 | tf_op jit(solution)/shard_map/pallas_call | solution.py:1385
  542.0 48.9 %shard_map.266 = (f32[192,1600]{1,0:T(8,128)}, bf16[4,192,1600]{2,1,0:T(8,128)(2,1)}, f32[4,192,1600]{2,1,0:T(8,128)}, bf16[4,192,1600]{2,1,0:T(8,128)(2,1)}) custom-call(f32[192,1600]{1,0:T(8,128)} %get-tuple-element.83.refs_0_.refs_1_, f32[8,1600]{1,0:T(8,128)} %bitcast.115, f32[1,1600]{1,0:T(1,128)} %get-tuple-element.187.refs_2_, ...), custom_call_target="tpu_custom_call" | custom-call | flops 7864320000 | bytes 41943040 | tf_op jit(solution)/shard_map/pallas_call | solution.py:791
  590.8 2.2 convert_element_type.33
  593.0 1.2 bitcast_convert_fusion.refs_0_
  594.2 55.9 %shard_map.267 = (f32[192,1600]{1,0:T(8,128)}, f32[8,1600]{1,0:T(8,128)}, f32[1,1600]{1,0:T(1,128)}, bf16[1600,1600]{1,0:T(8,128)(2,1)}, bf16[1600,1600]{1,0:T(8,128)(2,1)}) custom-call(f32[192,1600]{1,0:T(8,128)} %bitcast_convert_fusion.refs_0_, f32[192,1600]{1,0:T(8,128)} %get-tuple-element.83.refs_0_.refs_1_, f32[8,1600]{1,0:T(8,128)} %bitcast.116, ...), custom_call_target="tpu_custom_call" | custom-call | flops 15728640000 | bytes 52428800 | tf_op jit(solution)/shard_map/pallas_call | solution.py:962
  650.2 195.7 %shard_map.268 = (f32[192,1600]{1,0:T(8,128)}, bf16[1600,2048]{1,0:T(8,128)(2,1)}, bf16[4,200,1600]{2,1,0:T(8,128)(2,1)}, bf16[3,200,1600]{2,1,0:T(8,128)(2,1)},...) custom-call(f32[192,1600]{1,0:T(8,128)} %get-tuple-element.89.refs_0_, ...), custom_call_target="tpu_custom_call" | custom-call | flops 199999995904 | bytes 52428800 | tf_op jit(solution)/shard_map/pallas_call | solution.py:1654
  845.8 94.1 %shard_map.269 = (f32[192,1600]{1,0:T(8,128)}, f32[8,1600]{1,0:T(8,128)}, f32[1,1600]{1,0:T(1,128)}, bf16[1600,1600]{1,0:T(8,128)(2,1)}, bf16[1600,1600]{1,0:T(8...) custom-call(f32[192,1600]{1,0:T(8,128)} %get-tuple-element.100.refs_0_, ...), custom_call_target="tpu_custom_call" | custom-call | flops 15728640000 | bytes 52428800 | tf_op jit(solution)/shard_map/pallas_call | solution.py:962
  939.9 190.0 %shard_map.270 = (f32[192,1600]{1,0:T(8,128)}, bf16[1600,2048]{1,0:T(8,128)(2,1)}, bf16[4,200,1600]{2,1,0:T(8,128)(2,1)}, bf16[3,200,1600]{2,1,0:T(8,128)(2,1)},...) custom-call(f32[192,1600]{1,0:T(8,128)} %get-tuple-element.105.refs_0_, ...), custom_call_target="tpu_custom_call" | custom-call | flops 199999995904 | bytes 52428800 | tf_op jit(solution)/shard_map/pallas_call | solution.py:1654
  1130.0 2.3 convert_reduce_fusion
  1132.3 2.6 fusion.1.earlier
  1135.0 102.6 %shard_map.271 = (bf16[4,200,2048]{2,1,0:T(8,128)(2,1)}, bf16[3,200,2048]{2,1,0:T(8,128)(2,1)}, bf16[4,200,2048]{2,1,0:T(8,128)(2,1)}, bf16[4,200,2048]{2,1,0:T(8,128)(2,1)}) custom-call(bf16[4,2,200,2048]{3,2,1,0:T(8,128)(2,1)} %bitcast.96, bf16[200,2048]{1,0:T(8,128)(2,1)} %fusion.1.earlier), custom_call_target="tpu_custom_call" | custom-call | tf_op jit(solution)/shard_map/pallas_call | solution.py:389
  1237.5 14.4 %shard_map.272 = (f32[2,200,4800]{2,1,0:T(8,128)}, f32[2,200,1600]{2,1,0:T(8,128)}, f32[2,200,1600]{2,1,0:T(8,128)}, f32[2,1600,200]{2,1,0:T(8,128)}, f32[2,200]...) custom-call(bf16[4,200,2048]{2,1,0:T(8,128)(2,1)} %get-tuple-element, ...), custom_call_target="tpu_custom_call" | custom-call | tf_op jit(solution)/shard_map/pallas_call | solution.py:458
  1251.9 1.3 copy.39
  1253.2 3.6 copy.40
  1256.8 1.0 copy.56
  (72 shorter events, 0.7 us)
Async XLA Ops:
  6.5 3.4 copy-start
  9.2 0.7 copy-start.7
  9.2 0.7 copy-start.8
  9.2 3.4 copy-start.11
  9.2 3.4 copy-start.12
  9.2 3.4 copy-start.13
  9.2 3.4 copy-start.14
  9.2 3.4 copy-start.15
  9.2 3.5 copy-start.16
  9.3 3.5 copy-start.17
  9.3 3.5 copy-start.18
  9.3 3.5 copy-start.19
  86.0 3.9 copy-start.1
  87.5 2.6 copy-start.2
  92.2 174.8 %copy-start.6 = (bf16[200,448]{1,0:T(8,128)(2,1)S(1)}, bf16[200,448]{1,0:T(8,128)(2,1)}, u32[]{:S(2)}) copy-start(bf16[200,448]{1,0:T(8,128)(2,1)} %get-tuple-element.177) | copy-start | bytes 537604
  92.2 174.8 %copy-start.5 = (bf16[200,448]{1,0:T(8,128)(2,1)S(1)}, bf16[200,448]{1,0:T(8,128)(2,1)}, u32[]{:S(2)}) copy-start(bf16[200,448]{1,0:T(8,128)(2,1)} %get-tuple-element.176) | copy-start | bytes 537604
  92.2 174.9 %copy-start.4 = (bf16[200,448]{1,0:T(8,128)(2,1)S(1)}, bf16[200,448]{1,0:T(8,128)(2,1)}, u32[]{:S(2)}) copy-start(bf16[200,448]{1,0:T(8,128)(2,1)} %get-tuple-element.175) | copy-start | bytes 537604
  92.2 174.9 %copy-start.9 = (bf16[200,448]{1,0:T(8,128)(2,1)S(1)}, bf16[200,448]{1,0:T(8,128)(2,1)}, u32[]{:S(2)}) copy-start(bf16[200,448]{1,0:T(8,128)(2,1)} %get-tuple-element.200) | copy-start | bytes 537604
  541.9 51.1 %copy-start.10 = (bf16[2,96,1600]{2,1,0:T(8,128)(2,1)S(1)}, bf16[2,96,1600]{2,1,0:T(8,128)(2,1)}, u32[]{:S(2)}) copy-start(bf16[2,96,1600]{2,1,0:T(8,128)(2,1)} %param.29) | copy-start | bytes 1843204
  1253.2 3.6 copy-start.3

commit v13 on v12

--- a/solution.py
+++ b/solution.py
@@ -340,9 +340,9 @@
         target[at] = total.astype(target.dtype)
 
 
-def last_sum_kernel(source, earlier, from_y, from_z, got, got_earlier, *scratch):
+def last_sum_kernel(source, part, near, far, from_y, from_z, got, got_earlier, *scratch):
     p, g = Peers(), Group()
-    scratch, (bsend, brecv, blocal, terms, mine) = scratch[:-5], scratch[-5:]
+    scratch, (bsend, brecv, blocal, terms, mine, earlier) = scratch[:-6], scratch[-6:]
     before = BlockGather(p, earlier, got_earlier, (bsend, brecv), 0, blocal.at[0])
     items = reduces(g, [source], [from_y, from_z], scratch)
     after = [
@@ -352,6 +352,16 @@
     steps = in_turn(items)
     g.greet(p)
     steps[0]()
+    loads = [
+        pltpu.make_async_copy(part.at[g.z, g.y], terms.at[0], blocal.at[3]),
+        pltpu.make_async_copy(near.at[g.z], terms.at[1], blocal.at[4]),
+        pltpu.make_async_copy(far, terms.at[2:5], blocal.at[5]),
+    ]
+    for load in loads:
+        load.start()
+    for load in loads:
+        load.wait()
+    add_up(terms.at[0], [terms.at[k] for k in range(1, 5)], earlier, slice(None))
     before.start()
 
     def total(n):
@@ -385,17 +395,18 @@
 
 def last_sum(part, earlier, n_tp, collective_id):
     operands, results, scratch = reduce_parts([part])
-    whole = jax.ShapeDtypeStruct((n_tp,) + earlier.shape, bf16)
+    rows = part.shape[2:]
+    whole = jax.ShapeDtypeStruct((n_tp,) + rows, bf16)
     _, _, got, got_earlier = pl.pallas_call(
         last_sum_kernel,
         out_shape=results + (whole, whole),
-        in_specs=[ANY, ANY],
+        in_specs=[ANY] * 4,
         out_specs=(ANY,) * 4,
         scratch_shapes=scratch
         + [pltpu.SemaphoreType.DMA((9,))] * 2
-        + [pltpu.SemaphoreType.DMA((8,)), pltpu.VMEM((5,) + earlier.shape, bf16), pltpu.VMEM(earlier.shape, bf16)],
+        + [pltpu.SemaphoreType.DMA((8,)), pltpu.VMEM((5,) + rows, bf16), pltpu.VMEM(rows, bf16), pltpu.VMEM(rows, bf16)],
         compiler_params=params(collective_id),
-    )(part, earlier)
+    )(part, *earlier)
     return got, got_earlier
 
 
@@ -1756,13 +1767,6 @@
     return part.reshape(4, 2, -1, part.shape[1])
 
 
-def owned(part, from_y, from_z):
-    z, y = lax.axis_index("fsdp") // 2, lax.axis_index("fsdp") % 2
-    own = lax.dynamic_index_in_dim(lax.dynamic_index_in_dim(part, z, 0, False), y, 0, False)
-    near = lax.dynamic_index_in_dim(from_y, z, 0, False)
-    return own.astype(f32) + near.astype(f32) + jnp.sum(from_z.astype(f32), 0)
-
-
 def backward(grad, weights, vecs, saves, n_tp):
     width = D - HEADS // n_tp * HEAD * (n_tp - 1)
     staged = lax.axis_size("fsdp") == GROUP
@@ -1805,7 +1809,7 @@
         )
         produced((layer, "qo"), grad_qo)
     if staged:
-        got = last_sum(waiting[0, "qo"], owned(*done[1, "qo"]).astype(bf16), n_tp, 30)
+        got = last_sum(waiting[0, "qo"], done[1, "qo"], n_tp, 30)
         return grad, assemble([(got[k],) + done[k, "proj"] + done[k, "fc"] for k in range(LAYERS)])
     outs = []
     for layer in range(LAYERS):

time: 1270 us -> 1260 us (level)
  no operation moved by 1% of the time
where the time goes in v13:
time: 1260 us; the launch traced here: 1250 us
  Pallas kernels  1220 us (97%)
  local copies, waits for them, and re-layouts  28.5 us (2%)
    pallas_call x2, Pallas kernels, attn_bwd(): pl.pallas_call(functools.partial(attn_bwd_kernel, len(payload)), out_shap...  386 us
    pallas_call x2, Pallas kernels, attn_fwd(): pl.pallas_call(functools.partial(attn_fwd_kernel, len(operands)), out_sha...  361 us
    pallas_call x2, Pallas kernels, ff_bwd(): pl.pallas_call(functools.partial(ff_bwd_kernel, len(payload)), out_shape=...  150 us
    pallas_call x2, Pallas kernels, ff_fwd(): pl.pallas_call(functools.partial(ff_fwd_kernel, len(operands)), out_shape...  131 us
    pallas_call x1, Pallas kernels, last_sum(): pl.pallas_call(last_sum_kernel, out_shape=results + (whole, whole), in_sp...  103 us
    pallas_call x1, Pallas kernels, spread_only(): pl.pallas_call(functools.partial(spread_kernel, chunks), out_shape=result...  70.8 us

profile of v13, /device:TPU:9, one launch (start us, length us, event | category | flops | bytes accessed | tf_op | source)
XLA Modules:
  0.0 1253.5 jit_solution(18156894666079509242)
XLA Ops:
  0.6 2.2 bitcast_convert_fusion.1.refs_0_.refs_1_
  2.9 3.6 fusion.4
  6.5 2.7 dynamic-slice_bitcast_fusion.1
  9.2 0.0 copy-start.14
  9.3 0.5 copy-done.7
  9.8 0.1 copy-done.8
  9.9 0.1 fusion.5
  10.0 0.9 dynamic-slice_bitcast_fusion
  10.9 0.8 slice.182
  11.7 0.8 slice.183
  12.8 0.1 copy.35
  13.0 2.3 concatenate.12.source
  15.2 70.8 %shard_map.262 = bf16[8,200,1920]{2,1,0:T(8,128)(2,1)} custom-call(bf16[200,1920]{1,0:T(8,128)(2,1)} %concatenate.12.source), custom_call_target="tpu_custom_call" | custom-call | tf_op jit(solution)/shard_map/pallas_call | solution.py:593
  86.0 1.2 convert_bitcast_fusion
  87.2 0.3 copy.36
  87.5 0.1 reshape.131
  87.6 0.1 fusion.6
  87.7 0.6 copy.46
  88.3 0.6 slice_bitcast_fusion.4
  88.9 0.1 fusion.3
  89.0 0.1 fusion.2
  89.1 0.1 pad.18.clone
  89.1 0.1 fusion.1
  89.2 0.1 fusion
  89.3 0.1 pad_maximum_fusion.1
  89.4 0.6 pad.12.refs_2_
  90.0 0.1 slice_bitcast_fusion.1
  90.1 0.1 slice_bitcast_fusion
  90.3 1.9 concatenate.13.refs_4_
  92.2 174.8 %shard_map.263 = (f32[192,1600]{1,0:T(8,128)}, f32[2,4,8,384]{3,2,1,0:T(8,128)}, bf16[4,192,1600]{2,1,0:T(8,128)(2,1)}, bf16[3,2,384,512]{3,2,1,0:T(8,128)(2,1)}...) custom-call(f32[192,1600]{1,0:T(8,128)} %bitcast_convert_fusion.1.re, ...), custom_call_target="tpu_custom_call" | custom-call | flops 99999997952 | bytes 31457280 | tf_op jit(solution)/shard_map/pallas_call | solution.py:1396
  267.3 2.2 concatenate.14.refs_4_
  269.4 82.6 %shard_map.264 = (f32[192,1600]{1,0:T(8,128)}, bf16[4,192,1600]{2,1,0:T(8,128)(2,1)}, f32[4,192,1600]{2,1,0:T(8,128)}, bf16[4,192,1600]{2,1,0:T(8,128)(2,1)}, bf16[8,200,1792]{2,1,0:T(8,128)(2,1)}) custom-call(f32[192,1600]{1,0:T(8,128)} %get-tuple-element.79.refs_0_.refs_1_, f32[8,1600]{1,0:T(8,128)} %bitcast.105, f32[1,1600]{1,0:T(1,128)} %get-tuple-element.190.refs_2_, ...), custom_call_target="tpu_custom_call" | custom-call | flops 7864320000 | bytes 41943040 | tf_op jit(solution)/shard_map/pallas_call | solution.py:802
  352.0 0.6 copy.45
  352.7 0.6 pad.13.refs_2_
  353.4 1.9 concatenate.15.refs_4_
  355.3 186.7 %shard_map.265 = (f32[192,1600]{1,0:T(8,128)}, f32[2,4,8,384]{3,2,1,0:T(8,128)}, bf16[4,192,1600]{2,1,0:T(8,128)(2,1)}, bf16[3,2,384,512]{3,2,1,0:T(8,128)(2,1)}...) custom-call(f32[192,1600]{1,0:T(8,128)} %get-tuple-element.81.refs_0, ...), custom_call_target="tpu_custom_call" | custom-call | flops 99999997952 | bytes 31457280 | tf_op jit(solution)/shard_map/pallas_call | solution.py:1396
  542.0 48.9 %shard_map.266 = (f32[192,1600]{1,0:T(8,128)}, bf16[4,192,1600]{2,1,0:T(8,128)(2,1)}, f32[4,192,1600]{2,1,0:T(8,128)}, bf16[4,192,1600]{2,1,0:T(8,128)(2,1)}) custom-call(f32[192,1600]{1,0:T(8,128)} %get-tuple-element.83.refs_0_.refs_1_, f32[8,1600]{1,0:T(8,128)} %bitcast.109, f32[1,1600]{1,0:T(1,128)} %get-tuple-element.187.refs_2_, ...), custom_call_target="tpu_custom_call" | custom-call | flops 7864320000 | bytes 41943040 | tf_op jit(solution)/shard_map/pallas_call | solution.py:802
  590.8 2.2 convert_element_type.15
  593.0 1.2 bitcast_convert_fusion.refs_0_
  594.2 55.9 %shard_map.267 = (f32[192,1600]{1,0:T(8,128)}, f32[8,1600]{1,0:T(8,128)}, f32[1,1600]{1,0:T(1,128)}, bf16[1600,1600]{1,0:T(8,128)(2,1)}, bf16[1600,1600]{1,0:T(8,128)(2,1)}) custom-call(f32[192,1600]{1,0:T(8,128)} %bitcast_convert_fusion.refs_0_, f32[192,1600]{1,0:T(8,128)} %get-tuple-element.83.refs_0_.refs_1_, f32[8,1600]{1,0:T(8,128)} %bitcast.110, ...), custom_call_target="tpu_custom_call" | custom-call | flops 15728640000 | bytes 52428800 | tf_op jit(solution)/shard_map/pallas_call | solution.py:973
  650.2 195.7 %shard_map.268 = (f32[192,1600]{1,0:T(8,128)}, bf16[1600,2048]{1,0:T(8,128)(2,1)}, bf16[4,200,1600]{2,1,0:T(8,128)(2,1)}, bf16[3,200,1600]{2,1,0:T(8,128)(2,1)},...) custom-call(f32[192,1600]{1,0:T(8,128)} %get-tuple-element.89.refs_0_, ...), custom_call_target="tpu_custom_call" | custom-call | flops 199999995904 | bytes 52428800 | tf_op jit(solution)/shard_map/pallas_call | solution.py:1665
  845.9 94.1 %shard_map.269 = (f32[192,1600]{1,0:T(8,128)}, f32[8,1600]{1,0:T(8,128)}, f32[1,1600]{1,0:T(1,128)}, bf16[1600,1600]{1,0:T(8,128)(2,1)}, bf16[1600,1600]{1,0:T(8...) custom-call(f32[192,1600]{1,0:T(8,128)} %get-tuple-element.100.refs_0_, ...), custom_call_target="tpu_custom_call" | custom-call | flops 15728640000 | bytes 52428800 | tf_op jit(solution)/shard_map/pallas_call | solution.py:973
  940.1 190.0 %shard_map.270 = (f32[192,1600]{1,0:T(8,128)}, bf16[1600,2048]{1,0:T(8,128)(2,1)}, bf16[4,200,1600]{2,1,0:T(8,128)(2,1)}, bf16[3,200,1600]{2,1,0:T(8,128)(2,1)},...) custom-call(f32[192,1600]{1,0:T(8,128)} %get-tuple-element.105.refs_0_, ...), custom_call_target="tpu_custom_call" | custom-call | flops 199999995904 | bytes 52428800 | tf_op jit(solution)/shard_map/pallas_call | solution.py:1665
  1130.0 102.7 %shard_map.271 = (bf16[4,200,2048]{2,1,0:T(8,128)(2,1)}, bf16[3,200,2048]{2,1,0:T(8,128)(2,1)}, bf16[4,200,2048]{2,1,0:T(8,128)(2,1)}, bf16[4,200,2048]{2,1,0:T(8,128)(2,1)}) custom-call(bf16[4,2,200,2048]{3,2,1,0:T(8,128)(2,1)} %bitcast.92, bf16[4,2,200,2048]{3,2,1,0:T(8,128)(2,1)} %bitcast.91, bf16[4,200,2048]{2,1,0:T(8,128)(2,1)} %get-tuple-element.118.near, ...), custom_call_target="tpu_custom_call" | custom-call | tf_op jit(solution)/shard_map/pallas_call | solution.py:400
  1232.8 14.4 %shard_map.272 = (f32[2,200,4800]{2,1,0:T(8,128)}, f32[2,200,1600]{2,1,0:T(8,128)}, f32[2,200,1600]{2,1,0:T(8,128)}, f32[2,1600,200]{2,1,0:T(8,128)}, f32[2,200]...) custom-call(bf16[4,200,2048]{2,1,0:T(8,128)(2,1)} %get-tuple-element, ...), custom_call_target="tpu_custom_call" | custom-call | tf_op jit(solution)/shard_map/pallas_call | solution.py:469
  1247.2 1.3 copy.39
  1248.4 3.6 copy.40
  1252.0 1.0 copy.56
  (70 shorter events, 0.6 us)
Async XLA Ops:
  6.5 3.4 copy-start
  9.2 0.7 copy-start.7
  9.2 0.7 copy-start.8
  9.2 3.4 copy-start.11
  9.2 3.4 copy-start.12
  9.2 3.5 copy-start.13
  9.2 3.5 copy-start.14
  9.2 3.5 copy-start.15
  9.2 3.5 copy-start.16
  9.2 3.5 copy-start.17
  9.2 3.5 copy-start.18
  9.2 3.5 copy-start.19
  86.0 4.0 copy-start.1
  87.5 2.6 copy-start.2
  92.2 174.8 %copy-start.6 = (bf16[200,448]{1,0:T(8,128)(2,1)S(1)}, bf16[200,448]{1,0:T(8,128)(2,1)}, u32[]{:S(2)}) copy-start(bf16[200,448]{1,0:T(8,128)(2,1)} %get-tuple-element.177) | copy-start | bytes 537604
  92.2 174.9 %copy-start.5 = (bf16[200,448]{1,0:T(8,128)(2,1)S(1)}, bf16[200,448]{1,0:T(8,128)(2,1)}, u32[]{:S(2)}) copy-start(bf16[200,448]{1,0:T(8,128)(2,1)} %get-tuple-element.176) | copy-start | bytes 537604
  92.2 174.9 %copy-start.4 = (bf16[200,448]{1,0:T(8,128)(2,1)S(1)}, bf16[200,448]{1,0:T(8,128)(2,1)}, u32[]{:S(2)}) copy-start(bf16[200,448]{1,0:T(8,128)(2,1)} %get-tuple-element.175) | copy-start | bytes 537604
  92.2 174.9 %copy-start.9 = (bf16[200,448]{1,0:T(8,128)(2,1)S(1)}, bf16[200,448]{1,0:T(8,128)(2,1)}, u32[]{:S(2)}) copy-start(bf16[200,448]{1,0:T(8,128)(2,1)} %get-tuple-element.200) | copy-start | bytes 537604
  542.0 51.1 %copy-start.10 = (bf16[2,96,1600]{2,1,0:T(8,128)(2,1)S(1)}, bf16[2,96,1600]{2,1,0:T(8,128)(2,1)}, u32[]{:S(2)}) copy-start(bf16[2,96,1600]{2,1,0:T(8,128)(2,1)} %param.29) | copy-start | bytes 1843204
  1248.4 3.6 copy-start.3
